TPU v7x, 32 devices: a whole 2x2x4 slice. The times are simulated.
32 devices in a mesh: dp: 4 (over y, core), seq: 8 (over z, x).
Axes of the slice: x: 2, y: 2, z: 4, core: 2. Of those that a mesh axis runs over, the one named last changes fastest.
Arguments:
- tokens: bfloat16 [4, 3072, 1024], P('dp', 'seq'), may hold values from -6 to 6
- gain_one: bfloat16 [1024], P(('dp', 'seq')), may hold values from 0.5 to 1.5
- w_in: bfloat16 [1024, 3328], P(('dp', 'seq')), may hold values from -0.1875 to 0.1875
- w_step: bfloat16 [1024, 24], P(('dp', 'seq')), may hold values from -0.375 to 0.375
- conv_weight: bfloat16 [4, 1792], P(None, ('dp', 'seq')), may hold values from -3 to 3
- conv_bias: bfloat16 [1792], P(('dp', 'seq')), may hold values from -3 to 3
- mamba_heads: float32 [2, 24], replicated, may hold values from -11.5 to 0.5
- skip_weight: float32 [24], replicated, may hold values from 0.5 to 1.5
- w_query: bfloat16 [1024, 512], P(('dp', 'seq')), may hold values from -0.1875 to 0.1875
- w_keyval: bfloat16 [1024, 256], P(('dp', 'seq')), may hold values from -0.1875 to 0.1875
- w_attn_out: bfloat16 [512, 1024], P(None, ('dp', 'seq')), may hold values from -2 to 2
- w_mix_out: bfloat16 [1536, 1024], P(None, ('dp', 'seq')), may hold values from -0.109375 to 0.109375
- gain_two: bfloat16 [1024], P(('dp', 'seq')), may hold values from 0.5 to 1.5
- w_gate_up: bfloat16 [1024, 4096], P(('dp', 'seq')), may hold values from -0.1875 to 0.1875
- w_down: bfloat16 [2048, 1024], P(None, ('dp', 'seq')), may hold values from -0.125 to 0.125
- cotangent: bfloat16 [4, 3072, 1024], P('dp', 'seq'), may hold values from -6 to 6
Outputs:
- output: bfloat16 [4, 3072, 1024], P('dp', 'seq')
- input_grad: float32 [4, 3072, 1024], P('dp', 'seq')
- grad_gain_one: float32 [1024], P(('dp', 'seq'))
- grad_w_in: float32 [1024, 3328], P(('dp', 'seq'))
- grad_w_step: float32 [1024, 24], P(('dp', 'seq'))
- grad_conv_weight: float32 [4, 1792], P(None, ('dp', 'seq'))
- grad_conv_bias: float32 [1792], P(('dp', 'seq'))
- grad_mamba_heads: float32 [2, 24], replicated
- grad_skip_weight: float32 [24], replicated
- grad_w_query: float32 [1024, 512], P(('dp', 'seq'))
- grad_w_keyval: float32 [1024, 256], P(('dp', 'seq'))
- grad_w_attn_out: float32 [512, 1024], P(None, ('dp', 'seq'))
- grad_w_mix_out: float32 [1536, 1024], P(None, ('dp', 'seq'))
- grad_gain_two: float32 [1024], P(('dp', 'seq'))
- grad_w_gate_up: float32 [1024, 4096], P(('dp', 'seq'))
- grad_w_down: float32 [2048, 1024], P(None, ('dp', 'seq'))
All inputs are finite; a program needn't handle non-finite values.
Results may differ from a plain program's by a relative error of at most 0.017.
Values may be sent and summed in bfloat16 or wider, within the bound.
No kernel may reach another device: no remote copies, remote signals or barrier semaphores. Data moves between devices by JAX's collectives and lax.ppermute only.
A program may use at most 256 MiB of HBM per device.

v0:
```python
from functools import partial
import math

import jax
import jax.numpy as jnp
from jax import lax
from jax.sharding import PartitionSpec as P

MHEADS = 24
MHEAD_DIM = 64
STATE = 128
CONV = 4
QHEADS = 8
KVHEADS = 2
HEAD_DIM = 64
FF = 2048


norm_epsilon = 1e-06
rope_base = 100000000000.0
key_block = 1024
masked_score = -1e30
highest_precision = lax.Precision.HIGHEST


def from_behind(block, axis, distance):
    devices = range(lax.axis_size(axis))
    route = [(i - distance, i) for i in devices if i - distance in devices]
    return lax.ppermute(block, axis, route)


def carried_in(x, axis, join, neutral):
    place = lax.axis_index(axis)
    gathered = jax.tree.map(
        lambda a, kind: lax.all_gather(a.astype(kind), axis), x, (jnp.bfloat16, jnp.bfloat16)
    )
    state = jax.tree.map(lambda a, e: jnp.zeros_like(a) + jnp.asarray(e, a.dtype), x, neutral)

    def one(lap, state):
        return join(
            state,
            jax.tree.map(
                lambda a, own: lax.dynamic_index_in_dim(a, lap, 0, False).astype(own.dtype),
                gathered,
                x,
            ),
        )

    return lax.fori_loop(0, place, one, state)


def carried_in_2(x, axis, join, neutral):
    count = lax.axis_size(axis)
    place = lax.axis_index(axis)
    ahead = count - 1 - place
    gathered = jax.tree.map(
        lambda a, kind: lax.all_gather(a.astype(kind), axis),
        x,
        jax.tree.map(lambda a: jnp.bfloat16 if a.dtype == jnp.float32 else a.dtype, x),
    )
    state = jax.tree.map(lambda a, e: jnp.zeros_like(a) + jnp.asarray(e, a.dtype), x, neutral)

    def one(lap, state):
        source = count - 1 - lap
        return join(
            state,
            jax.tree.map(
                lambda a, own: lax.dynamic_index_in_dim(a, source, 0, False).astype(own.dtype),
                gathered,
                x,
            ),
        )

    return lax.fori_loop(0, ahead, one, state)


def rms_norm(values, gain_vector):
    return (
        values
        * lax.rsqrt(jnp.mean(values * values, axis=-1, keepdims=True) + norm_epsilon)
        * gain_vector
    )


def rope_tables(positions, head_width):
    half_width = head_width // 2
    exponents = jnp.arange(half_width).astype(jnp.float32) * (2.0 / head_width)
    frequency = rope_base ** (-exponents)
    angles = positions.astype(jnp.float32)[:, None] * frequency[None, :]
    return (jnp.cos(angles), jnp.sin(angles))


def rotate(values, cosine, sine_table):
    half_width = values.shape[-1] // 2
    first_half = values[..., :half_width]
    second_half = values[..., half_width:]
    cosine_b = cosine[:, None, :]
    sine_b = sine_table[:, None, :]
    return jnp.concatenate(
        [
            first_half * cosine_b - second_half * sine_b,
            second_half * cosine_b + first_half * sine_b,
        ],
        axis=-1,
    )


def outer_product(left, right):
    return lax.dot_general(
        left, right, (((0,), (0,)), ((), ())), preferred_element_type=jnp.float32
    )


def back_product(grad_rows, weight_matrix):
    return lax.dot_general(
        grad_rows, weight_matrix, (((1,), (1,)), ((), ())), preferred_element_type=jnp.float32
    )


def mamba_inputs(extended, step_raw, conv_weight, conv_bias, head_params):
    row_count = extended.shape[0] - (CONV - 1)
    conv_sum = conv_bias[None, :] + conv_weight[0][None, :] * extended[0:row_count]
    for offset in range(1, CONV):
        conv_sum = conv_sum + conv_weight[offset][None, :] * extended[offset : offset + row_count]
    activated = jax.nn.silu(conv_sum)
    inner_width = MHEADS * MHEAD_DIM
    inputs_x = activated[:, :inner_width].reshape(row_count, MHEADS, MHEAD_DIM)
    input_mat = activated[:, inner_width : inner_width + STATE]
    output_mat = activated[:, inner_width + STATE :]
    step_size = jax.nn.softplus(step_raw + head_params[1][None, :])
    log_decay = -jnp.exp(head_params[0])[None, :] * step_size
    return (inputs_x, input_mat, output_mat, log_decay, step_size)


def ssd_summary(inputs_x, input_mat, log_decay, step_size):
    cumulative = jnp.cumsum(log_decay, axis=0)
    weights_tail = jnp.exp(cumulative[-1][None, :] - cumulative) * step_size
    fresh_state = jnp.einsum(
        "th,thp,tn->hpn", weights_tail, inputs_x, input_mat, precision=highest_precision
    )
    return (jnp.exp(cumulative[-1]), fresh_state)


def ssd_output(inputs_x, input_mat, output_mat, log_decay, step_size, carry_state):
    row_count = inputs_x.shape[0]
    cumulative = jnp.cumsum(log_decay, axis=0)
    by_head = cumulative.T
    indices = jnp.arange(row_count)
    causal_mask = (indices[:, None] >= indices[None, :])[None]
    gap_matrix = jnp.where(causal_mask, by_head[:, :, None] - by_head[:, None, :], 0.0)
    kernel = jnp.where(causal_mask, jnp.exp(gap_matrix), 0.0)
    intersection = jnp.dot(output_mat, input_mat.T, precision=highest_precision)
    mixing = kernel * intersection[None] * step_size.T[:, None, :]
    within = jnp.einsum("hts,shp->thp", mixing, inputs_x, precision=highest_precision)
    carried = (
        jnp.einsum("tn,hpn->thp", output_mat, carry_state, precision=highest_precision)
        * jnp.exp(cumulative)[:, :, None]
    )
    return within + carried


def mamba_mix(
    inputs_x, input_mat, output_mat, log_decay, step_size, carry_state, gate_z, skip_vector
):
    row_count = inputs_x.shape[0]
    mixed_y = (
        ssd_output(inputs_x, input_mat, output_mat, log_decay, step_size, carry_state)
        + skip_vector[None, :, None] * inputs_x
    )
    return mixed_y.reshape(row_count, MHEADS * MHEAD_DIM) * jax.nn.silu(gate_z)


def mamba_local(
    extended, step_raw, gate_z, conv_weight, conv_bias, head_params, skip_vector, carry_state
):
    inputs_x, input_mat, output_mat, log_decay, step_size = mamba_inputs(
        extended, step_raw, conv_weight, conv_bias, head_params
    )
    mixer = mamba_mix(
        inputs_x, input_mat, output_mat, log_decay, step_size, carry_state, gate_z, skip_vector
    )
    factor, fresh_state = ssd_summary(inputs_x, input_mat, log_decay, step_size)
    end_state = factor[:, None, None] * carry_state + fresh_state
    return ((mixer, end_state), (output_mat, jnp.cumsum(log_decay, axis=0)))


def chain_combine(earlier, later):
    return (earlier[0] * later[0], later[0][:, None, None] * earlier[1] + later[1])


def online_block(running, key_rows, first_key, queries, query_pos):
    best_score, weight_total, weighted = running
    row_count = key_rows.shape[0]
    key_width = KVHEADS * HEAD_DIM
    key_heads = key_rows[:, :key_width].reshape(row_count, KVHEADS, HEAD_DIM)
    value_heads = key_rows[:, key_width:].reshape(row_count, KVHEADS, HEAD_DIM)
    score_scale = 1.0 / math.sqrt(HEAD_DIM)
    scores = (
        jnp.einsum("tgjd,sgd->gjts", queries, key_heads, preferred_element_type=jnp.float32)
        * score_scale
    )
    key_pos = first_key + jnp.arange(row_count, dtype=jnp.int32)
    allowed = key_pos[None, :] <= query_pos[:, None]
    scores = jnp.where(allowed, scores, masked_score)
    new_best = jnp.maximum(best_score, jnp.max(scores, axis=-1))
    rescale = jnp.exp(best_score - new_best)
    soft_weights = jnp.where(allowed, jnp.exp(scores - new_best[..., None]), 0.0)
    weight_total = weight_total * rescale + jnp.sum(soft_weights, axis=-1)
    weighted = weighted * rescale[..., None] + jnp.einsum(
        "gjts,sgd->gjtd",
        soft_weights.astype(jnp.bfloat16),
        value_heads,
        preferred_element_type=jnp.float32,
    )
    return (new_best, weight_total, weighted)


def attend_piece(running, key_piece, first_key, queries, query_pos):
    row_count = key_piece.shape[0]
    block_rows = math.gcd(row_count, key_block)
    block_count = row_count // block_rows
    stacked = key_piece.reshape(block_count, block_rows, key_piece.shape[1])
    firsts = block_rows * jnp.arange(block_count, dtype=jnp.int32)
    last_query = query_pos[-1]

    def advance(state_now, item_pair):
        key_rows, block_first = item_pair
        updated = lax.cond(
            block_first <= last_query,
            lambda carried: online_block(carried, key_rows, block_first, queries, query_pos),
            lambda carried: carried,
            state_now,
        )
        return (updated, None)

    running, _ = lax.scan(advance, running, (stacked, firsts))
    return running


def on_device(
    tokens,
    gain_one,
    w_in,
    w_step,
    conv_weight,
    conv_bias,
    mamba_heads,
    skip_weight,
    w_query,
    w_keyval,
    w_attn_out,
    w_mix_out,
    gain_two,
    w_gate_up,
    w_down,
    cotangent,
):
    gathered = (
        lax.all_gather(gain_one, ("dp", "seq"), axis=0, tiled=True),
        lax.all_gather(w_in, ("dp", "seq"), axis=0, tiled=True),
        lax.all_gather(w_step, ("dp", "seq"), axis=0, tiled=True),
        lax.all_gather(conv_weight, ("dp", "seq"), axis=1, tiled=True),
        lax.all_gather(conv_bias, ("dp", "seq"), axis=0, tiled=True),
        lax.all_gather(w_query, ("dp", "seq"), axis=0, tiled=True),
        lax.all_gather(w_keyval, ("dp", "seq"), axis=0, tiled=True),
        lax.all_gather(w_attn_out, ("dp", "seq"), axis=1, tiled=True),
        lax.all_gather(w_mix_out, ("dp", "seq"), axis=1, tiled=True),
        lax.all_gather(gain_two, ("dp", "seq"), axis=0, tiled=True),
        lax.all_gather(w_gate_up, ("dp", "seq"), axis=0, tiled=True),
        lax.all_gather(w_down, ("dp", "seq"), axis=1, tiled=True),
    )
    (
        full_gain_one,
        full_in,
        full_step,
        full_conv,
        full_conv_bias,
        full_query,
        full_keyval,
        full_attn_out,
        full_mix_out,
        full_gain_two,
        full_gate_up,
        full_down,
    ) = gathered
    piece_index = lax.axis_index("seq")
    inputs = tokens[0].astype(jnp.float32)
    row_count = inputs.shape[0]
    inner_width = MHEADS * MHEAD_DIM
    key_width = KVHEADS * HEAD_DIM
    group_size = QHEADS // KVHEADS
    gain_one_float = full_gain_one.astype(jnp.float32)
    normed = rms_norm(inputs, gain_one_float).astype(jnp.bfloat16)
    projected = jnp.dot(normed, full_in, preferred_element_type=jnp.float32)
    step_raw = jnp.dot(normed, full_step, preferred_element_type=jnp.float32)
    gate_z = projected[:, :inner_width]
    conv_input = projected[:, inner_width:].astype(jnp.bfloat16)
    border = from_behind(conv_input[row_count - (CONV - 1) :], "seq", 1)
    extended = jnp.concatenate([border, conv_input], axis=0).astype(jnp.float32)
    conv_float = full_conv.astype(jnp.float32)
    conv_bias_float = full_conv_bias.astype(jnp.float32)
    inputs_x, input_mat, output_mat, log_decay, step_size = mamba_inputs(
        extended, step_raw, conv_float, conv_bias_float, mamba_heads
    )
    factor, fresh_state = ssd_summary(inputs_x, input_mat, log_decay, step_size)
    zero_state = jnp.zeros_like(fresh_state)
    _, carry_state = carried_in(
        (factor, fresh_state), "seq", chain_combine, (jnp.ones_like(factor), zero_state)
    )
    mixer = mamba_mix(
        inputs_x, input_mat, output_mat, log_decay, step_size, carry_state, gate_z, skip_weight
    ).astype(jnp.bfloat16)
    mixed = jnp.dot(mixer, full_mix_out, preferred_element_type=jnp.float32)
    positions = piece_index * row_count + jnp.arange(row_count, dtype=jnp.int32)
    cosine, sine_table = rope_tables(positions, HEAD_DIM)
    query_raw = jnp.dot(normed, full_query, preferred_element_type=jnp.float32)
    keyval_raw = jnp.dot(normed, full_keyval, preferred_element_type=jnp.float32)
    queries = (
        rotate(query_raw.reshape(row_count, QHEADS, HEAD_DIM), cosine, sine_table)
        .astype(jnp.bfloat16)
        .reshape(row_count, KVHEADS, group_size, HEAD_DIM)
    )
    key_rotated = rotate(
        keyval_raw[:, :key_width].reshape(row_count, KVHEADS, HEAD_DIM), cosine, sine_table
    ).reshape(row_count, key_width)
    own_keys = jnp.concatenate([key_rotated, keyval_raw[:, key_width:]], axis=1).astype(
        jnp.bfloat16
    )
    start_state = (
        jnp.full((KVHEADS, group_size, row_count), masked_score, jnp.float32),
        jnp.zeros((KVHEADS, group_size, row_count), jnp.float32),
        jnp.zeros((KVHEADS, group_size, row_count, HEAD_DIM), jnp.float32),
    )
    folding = partial(attend_piece, queries=queries, query_pos=positions)
    best_score, weight_total, weighted = folding(
        start_state, lax.all_gather(own_keys, "seq", axis=0, tiled=True), jnp.int32(0)
    )
    attended_heads = weighted / weight_total[..., None]
    log_total = best_score + jnp.log(weight_total)
    attention_rows = (
        jnp.transpose(attended_heads, (2, 0, 1, 3))
        .reshape(row_count, QHEADS * HEAD_DIM)
        .astype(jnp.bfloat16)
    )
    attended = jnp.dot(attention_rows, full_attn_out, preferred_element_type=jnp.float32)
    hidden = inputs + mixed + attended
    gain_two_float = full_gain_two.astype(jnp.float32)
    normed_two = rms_norm(hidden, gain_two_float).astype(jnp.bfloat16)
    gate_up = jnp.dot(normed_two, full_gate_up, preferred_element_type=jnp.float32)
    gate_part = gate_up[:, :FF]
    up_part = gate_up[:, FF:]
    activated = (jax.nn.silu(gate_part) * up_part).astype(jnp.bfloat16)
    result = hidden + jnp.dot(activated, full_down, preferred_element_type=jnp.float32)
    output = result.astype(jnp.bfloat16)[None]
    regathered = (
        lax.all_gather(gain_one, ("dp", "seq"), axis=0, tiled=True),
        lax.all_gather(w_in, ("dp", "seq"), axis=0, tiled=True),
        lax.all_gather(w_step, ("dp", "seq"), axis=0, tiled=True),
        lax.all_gather(conv_weight, ("dp", "seq"), axis=1, tiled=True),
        lax.all_gather(conv_bias, ("dp", "seq"), axis=0, tiled=True),
        lax.all_gather(w_query, ("dp", "seq"), axis=0, tiled=True),
        lax.all_gather(w_keyval, ("dp", "seq"), axis=0, tiled=True),
        lax.all_gather(w_attn_out, ("dp", "seq"), axis=1, tiled=True),
        lax.all_gather(w_mix_out, ("dp", "seq"), axis=1, tiled=True),
        lax.all_gather(gain_two, ("dp", "seq"), axis=0, tiled=True),
        lax.all_gather(w_gate_up, ("dp", "seq"), axis=0, tiled=True),
        lax.all_gather(w_down, ("dp", "seq"), axis=1, tiled=True),
    )
    (
        full_gain_one,
        full_in,
        full_step,
        full_conv,
        full_conv_bias,
        full_query,
        full_keyval,
        full_attn_out,
        full_mix_out,
        full_gain_two,
        full_gate_up,
        full_down,
    ) = regathered
    gain_one_float = full_gain_one.astype(jnp.float32)
    gain_two_float = full_gain_two.astype(jnp.float32)
    conv_float = full_conv.astype(jnp.float32)
    conv_bias_float = full_conv_bias.astype(jnp.float32)
    grad_output = cotangent[0]
    grad_out_float = grad_output.astype(jnp.float32)
    grad_w_down = outer_product(activated, grad_output)
    grad_activated = back_product(grad_output, full_down)
    gate_sigmoid = jax.nn.sigmoid(gate_part)
    grad_gate = grad_activated * up_part * gate_sigmoid * (1.0 + gate_part * (1.0 - gate_sigmoid))
    grad_up = grad_activated * gate_part * gate_sigmoid
    grad_gate_up = jnp.concatenate([grad_gate, grad_up], axis=1).astype(jnp.bfloat16)
    grad_w_gate_up = outer_product(normed_two, grad_gate_up)
    grad_normed_two = back_product(grad_gate_up, full_gate_up)
    _, pull_two = jax.vjp(rms_norm, hidden, gain_two_float)
    grad_hidden_norm, grad_gain_two = pull_two(grad_normed_two)
    grad_hidden = grad_out_float + grad_hidden_norm
    grad_branch = grad_hidden.astype(jnp.bfloat16)
    grad_w_mix_out = outer_product(mixer, grad_branch)
    grad_w_attn_out = outer_product(attention_rows, grad_branch)
    grad_mixer = back_product(grad_branch, full_mix_out)
    grad_attention = back_product(grad_branch, full_attn_out).astype(jnp.bfloat16)
    grad_heads = grad_attention.reshape(row_count, KVHEADS, group_size, HEAD_DIM)
    row_dots = jnp.einsum("tgjd,gjtd->gjt", grad_heads.astype(jnp.float32), attended_heads)
    keys_back = lax.all_gather(own_keys, "seq", axis=0, tiled=True)
    total_rows = keys_back.shape[0]
    block_rows = min(key_block, total_rows)
    stacked = keys_back.reshape(total_rows // block_rows, block_rows, 2 * key_width)
    firsts = block_rows * jnp.arange(total_rows // block_rows, dtype=jnp.int32)
    score_scale = 1.0 / math.sqrt(HEAD_DIM)
    last_query = positions[-1]

    def backward_block(grad_query_acc, item_pair):
        key_rows, first_key = item_pair

        def compute(acc_now):
            key_heads = key_rows[:, :key_width].reshape(block_rows, KVHEADS, HEAD_DIM)
            value_heads = key_rows[:, key_width:].reshape(block_rows, KVHEADS, HEAD_DIM)
            scores = (
                jnp.einsum("tgjd,sgd->gjts", queries, key_heads, preferred_element_type=jnp.float32)
                * score_scale
            )
            key_pos = first_key + jnp.arange(block_rows, dtype=jnp.int32)
            allowed = key_pos[None, :] <= positions[:, None]
            scores = jnp.where(allowed, scores, masked_score)
            soft_weights = jnp.where(allowed, jnp.exp(scores - log_total[..., None]), 0.0)
            grad_weights = jnp.einsum(
                "tgjd,sgd->gjts", grad_heads, value_heads, preferred_element_type=jnp.float32
            )
            grad_scores = (soft_weights * (grad_weights - row_dots[..., None])).astype(jnp.bfloat16)
            acc_next = (
                acc_now
                + jnp.einsum(
                    "gjts,sgd->gjtd", grad_scores, key_heads, preferred_element_type=jnp.float32
                )
                * score_scale
            )
            grad_key = (
                jnp.einsum(
                    "gjts,tgjd->sgd", grad_scores, queries, preferred_element_type=jnp.float32
                )
                * score_scale
            )
            grad_value = jnp.einsum(
                "gjts,tgjd->sgd",
                soft_weights.astype(jnp.bfloat16),
                grad_heads,
                preferred_element_type=jnp.float32,
            )
            return (
                acc_next,
                jnp.concatenate(
                    [
                        grad_key.reshape(block_rows, key_width),
                        grad_value.reshape(block_rows, key_width),
                    ],
                    axis=1,
                ),
            )

        def skipped(acc_now):
            return (acc_now, jnp.zeros((block_rows, 2 * key_width), jnp.float32))

        return lax.cond(first_key <= last_query, compute, skipped, grad_query_acc)

    grad_query_heads, grad_key_rows = lax.scan(
        backward_block,
        jnp.zeros((KVHEADS, group_size, row_count, HEAD_DIM), jnp.float32),
        (stacked, firsts),
    )
    grad_key_rows = grad_key_rows.reshape(total_rows, 2 * key_width)
    own_grads = lax.psum_scatter(
        grad_key_rows.astype(jnp.bfloat16), "seq", scatter_dimension=0, tiled=True
    ).astype(jnp.float32)
    grad_query_rows = jnp.transpose(grad_query_heads, (2, 0, 1, 3)).reshape(
        row_count, QHEADS, HEAD_DIM
    )
    grad_query = (
        rotate(grad_query_rows, cosine, -sine_table)
        .reshape(row_count, QHEADS * HEAD_DIM)
        .astype(jnp.bfloat16)
    )
    grad_key_raw = rotate(
        own_grads[:, :key_width].reshape(row_count, KVHEADS, HEAD_DIM), cosine, -sine_table
    ).reshape(row_count, key_width)
    grad_keyval = jnp.concatenate([grad_key_raw, own_grads[:, key_width:]], axis=1).astype(
        jnp.bfloat16
    )
    grad_w_query = outer_product(normed, grad_query)
    grad_w_keyval = outer_product(normed, grad_keyval)
    grad_normed = back_product(grad_query, full_query) + back_product(grad_keyval, full_keyval)
    primal_out, pull_mamba, aux_values = jax.vjp(
        mamba_local,
        extended,
        step_raw,
        gate_z,
        conv_float,
        conv_bias_float,
        mamba_heads,
        skip_weight,
        carry_state,
        has_aux=True,
    )
    output_saved, cumulative = aux_values
    grad_y = (grad_mixer * jax.nn.silu(gate_z)).reshape(row_count, MHEADS, MHEAD_DIM)
    from_output = jnp.einsum(
        "th,thp,tn->hpn", jnp.exp(cumulative), grad_y, output_saved, precision=highest_precision
    )
    piece_decay = jnp.exp(cumulative[-1])
    _, grad_end = carried_in_2(
        (piece_decay, from_output),
        "seq",
        chain_combine,
        (jnp.ones_like(piece_decay), jnp.zeros_like(from_output)),
    )
    (
        grad_extended,
        grad_step_raw,
        grad_gate_z,
        grad_conv_weight,
        grad_conv_bias,
        grad_head_params,
        grad_skip,
        _,
    ) = pull_mamba((grad_mixer, grad_end))
    rim_back = from_behind(grad_extended[: CONV - 1], "seq", -1)
    grad_conv_input = grad_extended[CONV - 1 :] + jnp.concatenate(
        [jnp.zeros((row_count - (CONV - 1), grad_extended.shape[1]), jnp.float32), rim_back], axis=0
    )
    grad_projected = jnp.concatenate([grad_gate_z, grad_conv_input], axis=1).astype(jnp.bfloat16)
    grad_step_low = grad_step_raw.astype(jnp.bfloat16)
    grad_w_in = outer_product(normed, grad_projected)
    grad_w_step = outer_product(normed, grad_step_low)
    grad_normed = (
        grad_normed + back_product(grad_projected, full_in) + back_product(grad_step_low, full_step)
    )
    _, pull_one = jax.vjp(rms_norm, inputs, gain_one_float)
    grad_input_norm, grad_gain_one = pull_one(grad_normed)
    input_grad = (grad_hidden + grad_input_norm)[None]
    head_grad, skip_grad = lax.psum((grad_head_params, grad_skip), ("dp", "seq"))
    reduced = (
        lax.psum_scatter(grad_gain_one, ("dp", "seq"), scatter_dimension=0, tiled=True),
        lax.psum_scatter(grad_w_in, ("dp", "seq"), scatter_dimension=0, tiled=True),
        lax.psum_scatter(grad_w_step, ("dp", "seq"), scatter_dimension=0, tiled=True),
        lax.psum_scatter(grad_conv_weight, ("dp", "seq"), scatter_dimension=1, tiled=True),
        lax.psum_scatter(grad_conv_bias, ("dp", "seq"), scatter_dimension=0, tiled=True),
        lax.psum_scatter(grad_w_query, ("dp", "seq"), scatter_dimension=0, tiled=True),
        lax.psum_scatter(grad_w_keyval, ("dp", "seq"), scatter_dimension=0, tiled=True),
        lax.psum_scatter(grad_w_attn_out, ("dp", "seq"), scatter_dimension=1, tiled=True),
        lax.psum_scatter(grad_w_mix_out, ("dp", "seq"), scatter_dimension=1, tiled=True),
        lax.psum_scatter(grad_gain_two, ("dp", "seq"), scatter_dimension=0, tiled=True),
        lax.psum_scatter(grad_w_gate_up, ("dp", "seq"), scatter_dimension=0, tiled=True),
        lax.psum_scatter(grad_w_down, ("dp", "seq"), scatter_dimension=1, tiled=True),
    )
    return (
        output,
        input_grad,
        reduced[0],
        reduced[1],
        reduced[2],
        reduced[3],
        reduced[4],
        head_grad,
        skip_grad,
        reduced[5],
        reduced[6],
        reduced[7],
        reduced[8],
        reduced[9],
        reduced[10],
        reduced[11],
    )


def solution(mesh):
    return jax.shard_map(
        on_device,
        mesh=mesh,
        in_specs=(
            P("dp", "seq", None),
            P(("dp", "seq")),
            P(("dp", "seq"), None),
            P(("dp", "seq"), None),
            P(None, ("dp", "seq")),
            P(("dp", "seq")),
            P(),
            P(),
            P(("dp", "seq"), None),
            P(("dp", "seq"), None),
            P(None, ("dp", "seq")),
            P(None, ("dp", "seq")),
            P(("dp", "seq")),
            P(("dp", "seq"), None),
            P(None, ("dp", "seq")),
            P("dp", "seq", None),
        ),
        out_specs=(
            P("dp", "seq", None),
            P("dp", "seq", None),
            P(("dp", "seq")),
            P(("dp", "seq"), None),
            P(("dp", "seq"), None),
            P(None, ("dp", "seq")),
            P(("dp", "seq")),
            P(),
            P(),
            P(("dp", "seq"), None),
            P(("dp", "seq"), None),
            P(None, ("dp", "seq")),
            P(None, ("dp", "seq")),
            P(("dp", "seq")),
            P(("dp", "seq"), None),
            P(None, ("dp", "seq")),
        ),
        check_vma=False,
    )
```

profile of v0, /device:TPU:0, one launch (start us, length us, event | category | flops | bytes accessed | tf_op | source)
XLA Modules:
  0.0 2336.9 jit_solution(8677083434358670090)
XLA Ops:
  11.3 42.8 %all-reduce.24 = (bf16[1024]{0:T(1024)(128)(2,1)S(1)}, bf16[1792]{0:T(1024)(128)(2,1)S(1)}, bf16[1024]{0:T(1024)(128)(2,1)S(1)}) all-reduce(bf16[1024]{0:T(1024)(128)(2,1)S(1)} %dynamic-update-slice.1, bf16[1792]{0:T(1024)(128)(2,1)S(1)} %dynamic-update-slice, ...), channel_id=1, replica_groups=mesh['dp'=4,'seq'=8] {'dp','seq'}, use_global_device_ids=true, to_apply=%add.17 | all-reduce | flops 3840 | bytes 15360
  56.0 71.2 %all_gather.79 = bf16[1024,256]{1,0:T(8,128)(2,1)S(1)} all-gather(bf16[32,256]{1,0:T(8,128)(2,1)} %param.37), channel_id=1, replica_groups=mesh['dp'=4,'seq'=8] {'dp','seq'}, dimensions={0}, use_global_device_ids=true | all-gather | bytes 540672 | tf_op jit(solution)/shard_map/all_gather | solution.py:265
  131.5 63.9 %all-gather.2 = bf16[32,56,4]{1,2,0:T(4,128)(2,1)S(1)} all-gather(bf16[1,56,4]{1,2,0:T(4,128)(2,1)S(1)} %bitcast.470), channel_id=1, replica_groups=mesh['dp'=4,'seq'=8] {'dp','seq'}, dimensions={0}, use_global_device_ids=true | all-gather | bytes 14784 | tf_op jit(solution)/shard_map/all_gather | solution.py:262
  195.6 66.6 %all-gather.3 = bf16[32,32,24]{1,2,0:T(8,128)(2,1)S(1)} all-gather(bf16[1,32,24]{1,2,0:T(8,128)(2,1)S(1)} %bitcast.464), channel_id=1, replica_groups=mesh['dp'=4,'seq'=8] {'dp','seq'}, dimensions={0}, use_global_device_ids=true | all-gather | bytes 50688 | tf_op jit(solution)/shard_map/all_gather | solution.py:261
  266.2 7.6 fusion.191
  294.0 18.7 all-gather.4
  324.9 21.1 while.59
  328.0 11.7 conditional.6
  354.0 19.6 fusion.58
  380.8 29.2 %all-gather.17.cloned.1.call-done = bf16[1536,1024]{0,1:T(8,128)(2,1)} async-done(((bf16[1536,32]{0,1:T(8,128)(2,1)}), bf16[1536,1024]{0,1:T(8,128)(2,1)}) %all-gather.17.cloned.1.call-update) | async-done | bytes 3145744 | tf_op jit(solution)/shard_map/all_gather | solution.py:267
  414.8 50.7 %all-gather.23.cloned.1.call-done = bf16[512,1024]{0,1:T(8,128)(2,1)} async-done(((bf16[512,32]{0,1:T(8,128)(2,1)}), bf16[512,1024]{0,1:T(8,128)(2,1)}) %all-gather.23.cloned.1.call-update) | async-done | bytes 1048592 | tf_op jit(solution)/shard_map/all_gather | solution.py:266
  470.3 74.6 %all-gather.25.cloned.1.call-done = bf16[1024,4096]{1,0:T(8,128)(2,1)} async-done(((bf16[32,4096]{1,0:T(8,128)(2,1)}), bf16[1024,4096]{1,0:T(8,128)(2,1)}) %all-gather.25.cloned.1.call-update) | async-done | bytes 8388624 | tf_op jit(solution)/shard_map/all_gather | solution.py:269
  544.8 10.1 fusion.174
  554.9 53.6 %all-gather.27.cloned.1.call-done = bf16[2048,1024]{0,1:T(8,128)(2,1)} async-done(((bf16[2048,32]{0,1:T(8,128)(2,1)}), bf16[2048,1024]{0,1:T(8,128)(2,1)}) %all-gather.27.cloned.1.call-update) | async-done | bytes 4194320 | tf_op jit(solution)/shard_map/all_gather | solution.py:270
  608.6 7.4 multiply_convert_fusion.1
  617.1 8.0 multiply_reduce_fusion.9
  646.5 21.8 fusion.38
  674.5 35.2 %while.60 = (s32[]{:T(128)}, f32[2,4,384,64]{2,3,1,0:T(8,128)S(1)}, bf16[3,1024,256]{2,1,0:T(8,128)(2,1)}, s32[3]{0:T(128)S(1)}, s32[]{:T(128)}, /*index=5*/bf16...) while((s32[]{:T(128)}, f32[2,4,384,64]{2,3,1,0:T(8,128)S(1)}, ...), condition=%wide.region_16.17_spmd.clone, body=%wide.region_13.16_spmd.clone.sunk | while | flops 2053113216 | bytes 67554048 | solution.py:468
  676.6 26.0 %conditional.7 = (f32[2,4,384,64]{2,3,1,0:T(8,128)S(1)}, bf16[1,1024,256]{1,2,0:T(8,128)(2,1)S(1)}) conditional(s32[]{:T(128)} %convert_element_type.330, f32[2,4,384,64]{2,3,1,0:T(8,128)S(1)} %get-tuple-element.987, (s32[]{:T(128)}, s32[]{:T(128)}, bf16[3,1024,256]{1,2,0:T(8,128)(2,1)}, s32[]{:T(128)}, bf16[384,2,4,64]{0,3,2,1:T(8,128)(2,1)S(1)}, ...), branch_computations={%region_14.14_spmd, %region_15.15_spmd} | conditional | flops 2053113216 | bytes 65454620 | solution.py:466
  685.1 7.3 fusion.17
  710.8 13.4 while.58
  742.4 83.8 %reduce-scatter.13.cloned.1.call-done = bf16[384,256]{1,0:T(8,128)(2,1)} async-done(((bf16[3072,256]{1,0:T(8,128)(2,1)}), bf16[384,256]{1,0:T(8,128)(2,1)}) %reduce-scatter.13.cloned.1.call-update) | async-done | bytes 196624 | tf_op jit(solution)/shard_map/reduce_scatter | solution.py:474
  852.7 15.2 bitcast_add_fusion
  898.6 10.2 fusion.68
  923.2 41.8 %all-reduce.23 = (f32[1024]{0:T(1024)S(1)}, f32[4,1792]{1,0:T(4,128)S(1)}, f32[1792]{0:T(1024)S(1)}, f32[2,24]{1,0:T(2,128)}, f32[24]{0:T(128)}, /*index=5*/f32[1024]{0:T(1024)S(1)}) all-reduce(f32[1024]{0:T(1024)S(1)} %get-tuple-element.550, f32[4,1792]{1,0:T(4,128)S(1)} %pad_add_fusion.2, ...), channel_id=5, replica_groups=mesh['dp'=4,'seq'=8] {'dp','seq'}, use_global_device_ids=true, to_apply=%region_33.34.clone | all-reduce | flops 11080 | bytes 88640
  972.6 125.7 %reduce-scatter.17.cloned.1.call-done = f32[32,512]{1,0:T(8,128)} async-done(((f32[1024,512]{1,0:T(8,128)}), f32[32,512]{1,0:T(8,128)}) %reduce-scatter.17.cloned.1.call-update) | async-done | bytes 65552 | tf_op jit(solution)/shard_map/reduce_scatter | solution.py:549
  1098.3 137.1 %reduce-scatter.21.cloned.1.call-done = f32[512,32]{0,1:T(8,128)} async-done(((f32[512,1024]{0,1:T(8,128)}), f32[512,32]{0,1:T(8,128)}) %reduce-scatter.21.cloned.1.call-update) | async-done | bytes 65552 | tf_op jit(solution)/shard_map/reduce_scatter | solution.py:551
  1235.5 134.5 %reduce-scatter.19.cloned.1.call-done = f32[32,256]{1,0:T(8,128)} async-done(((f32[1024,256]{1,0:T(8,128)}), f32[32,256]{1,0:T(8,128)}) %reduce-scatter.19.cloned.1.call-update) | async-done | bytes 32784 | tf_op jit(solution)/shard_map/reduce_scatter | solution.py:550
  1369.9 118.0 %reduce-scatter.23.cloned.1.call-done = f32[1536,32]{0,1:T(8,128)} async-done(((f32[1536,1024]{0,1:T(8,128)}), f32[1536,32]{0,1:T(8,128)}) %reduce-scatter.23.cloned.1.call-update) | async-done | bytes 196624 | tf_op jit(solution)/shard_map/reduce_scatter | solution.py:552
  1488.0 186.6 %reduce-scatter.27.cloned.1.call-done = f32[2048,32]{0,1:T(8,128)} async-done(((f32[2048,1024]{0,1:T(8,128)}), f32[2048,32]{0,1:T(8,128)}) %reduce-scatter.27.cloned.1.call-update) | async-done | bytes 262160 | tf_op jit(solution)/shard_map/reduce_scatter | solution.py:555
  1674.6 294.1 %reduce-scatter.15.cloned.1.call-done = f32[32,3328]{1,0:T(8,128)} async-done(((f32[1024,3328]{1,0:T(8,128)}), f32[32,3328]{1,0:T(8,128)}) %reduce-scatter.15.cloned.1.call-update) | async-done | bytes 426000 | tf_op jit(solution)/shard_map/reduce_scatter | solution.py:545
  1968.7 361.1 %reduce-scatter.25.cloned.1.call-done = f32[32,4096]{1,0:T(8,128)} async-done(((f32[1024,4096]{1,0:T(8,128)}), f32[32,4096]{1,0:T(8,128)}) %reduce-scatter.25.cloned.1.call-update) | async-done | bytes 524304 | tf_op jit(solution)/shard_map/reduce_scatter | solution.py:554
  (504 shorter events, 251.3 us)
Async XLA Ops:
  7.2 124.4 %copy-start.117 = (bf16[4,56]{1,0:T(4,128)(2,1)S(1)}, bf16[4,56]{1,0:T(4,128)(2,1)}, u32[]{:S(2)}) copy-start(bf16[4,56]{1,0:T(4,128)(2,1)} %param.32) | copy-start | bytes 1348
  7.2 259.0 %all-gather.15.cloned.1.call-start = ((), (), s32[]{:S(2)}) async-start(), calls=%async_computation.9 | async-start | bytes 7028736 | tf_op jit(solution)/shard_map/all_gather | solution.py:260
  7.9 306.6 %all-gather.21.cloned.1.call-start = ((), (), s32[]{:S(2)}) async-start(), calls=%async_computation.12 | async-start | bytes 1081344 | tf_op jit(solution)/shard_map/all_gather | solution.py:264
  8.7 310.3 %all-gather.19.cloned.1.call-start = ((), (), s32[]{:S(2)}) async-start(), calls=%async_computation.11 | async-start | bytes 1769472 | tf_op jit(solution)/shard_map/all_gather | solution.py:336
  54.0 262.7 %copy-start.51 = (f32[1024]{0:T(1024)}, f32[1024]{0:T(1024)S(1)}, u32[]{:S(2)}) copy-start(f32[1024]{0:T(1024)S(1)} %convert_element_type.188) | copy-start | bytes 12292
  54.0 141.5 %copy-start.111 = (bf16[32,24]{0,1:T(8,128)(2,1)S(1)}, bf16[32,24]{0,1:T(8,128)(2,1)}, u32[]{:S(2)}) copy-start(bf16[32,24]{0,1:T(8,128)(2,1)} %param.31) | copy-start | bytes 4612
  56.0 260.8 %copy-start.77 = (f32[384]{0:T(512)}, f32[384]{0:T(512)S(1)}, u32[]{:S(2)}) copy-start(f32[384]{0:T(512)S(1)} %fusion.162) | copy-start | bytes 4612
  56.0 206.4 %copy-start.118 = (f32[2,24]{1,0:T(2,128)S(1)}, f32[2,24]{1,0:T(2,128)}, u32[]{:S(2)}) copy-start(f32[2,24]{1,0:T(2,128)} %param.34) | copy-start | bytes 580
  56.0 206.4 %copy-start.10 = (bf16[1,384,1024]{2,1,0:T(8,128)(2,1)S(1)}, bf16[1,384,1024]{2,1,0:T(8,128)(2,1)}, u32[]{:S(2)}) copy-start(bf16[1,384,1024]{2,1,0:T(8,128)(2,1)} %param.28) | copy-start | bytes 2359300
  130.7 188.1 %copy-start.38 = (f32[384,32]{0,1:T(8,128)}, f32[384,32]{0,1:T(8,128)S(1)}, u32[]{:S(2)}) copy-start(f32[384,32]{0,1:T(8,128)S(1)} %get-tuple-element.669) | copy-start | bytes 147460
  131.5 218.5 %all-gather.29.cloned.1.call-start = ((), (), s32[]{:S(2)}) async-start(), calls=%async_computation.24 | async-start | bytes 3538944 | tf_op jit(solution)/shard_map/all_gather | solution.py:35
  273.8 3.4 collective-permute-start
  285.7 360.7 %copy-start.4 = (f32[384,1536]{0,1:T(8,128)}, f32[384,1536]{0,1:T(8,128)S(1)}, u32[]{:S(2)}) copy-start(f32[384,1536]{0,1:T(8,128)S(1)} %copy.167) | copy-start | bytes 7077892
  289.8 120.2 %all-gather.17.cloned.1.call-start = ((), (), s32[]{:S(2)}) async-start(), calls=%async_computation.10 | async-start | bytes 3244032 | tf_op jit(solution)/shard_map/all_gather | solution.py:267
  290.4 175.0 %all-gather.23.cloned.1.call-start = ((), (), s32[]{:S(2)}) async-start(), calls=%async_computation.13 | async-start | bytes 1081344 | tf_op jit(solution)/shard_map/all_gather | solution.py:266
  291.0 253.9 %all-gather.25.cloned.1.call-start = ((), (), s32[]{:S(2)}) async-start(), calls=%async_computation.14 | async-start | bytes 8650752 | tf_op jit(solution)/shard_map/all_gather | solution.py:269
  291.7 316.8 %all-gather.27.cloned.1.call-start = ((), (), s32[]{:S(2)}) async-start(), calls=%async_computation.15 | async-start | bytes 4325376 | tf_op jit(solution)/shard_map/all_gather | solution.py:270
  292.5 418.2 %all-gather.31.cloned.1.call-start = ((), (), s32[]{:S(2)}) async-start(), calls=%async_computation.25 | async-start | bytes 3538944 | tf_op jit(solution)/shard_map/all_gather | solution.py:57
  313.3 311.9 %copy-start.53 = (f32[1024]{0:T(1024)}, f32[1024]{0:T(1024)S(1)}, u32[]{:S(2)}) copy-start(f32[1024]{0:T(1024)S(1)} %convert_element_type.202) | copy-start | bytes 12292
  380.8 84.7 %copy-start.11 = (bf16[1,384,1024]{2,1,0:T(8,128)(2,1)S(1)}, bf16[1,384,1024]{2,1,0:T(8,128)(2,1)}, u32[]{:S(2)}) copy-start(bf16[1,384,1024]{2,1,0:T(8,128)(2,1)} %param.28) | copy-start | bytes 2359300
  642.0 184.2 %reduce-scatter.13.cloned.1.call-start = ((), (), s32[]{:S(2)}) async-start(), calls=%async_computation.16 | async-start | bytes 1769472 | tf_op jit(solution)/shard_map/reduce_scatter | solution.py:474
  710.7 260.6 %reduce-scatter.29.cloned.1.call-start = ((), (), s32[]{:S(2)}) async-start(), calls=%async_computation.26 | async-start | bytes 540672
  736.6 361.7 %reduce-scatter.17.cloned.1.call-start = ((), (), s32[]{:S(2)}) async-start(), calls=%async_computation.18 | async-start | bytes 2162688 | tf_op jit(solution)/shard_map/reduce_scatter | solution.py:549
  740.1 495.3 %reduce-scatter.21.cloned.1.call-start = ((), (), s32[]{:S(2)}) async-start(), calls=%async_computation.20 | async-start | bytes 2162688 | tf_op jit(solution)/shard_map/reduce_scatter | solution.py:551
  742.3 86.6 %copy-start.40 = (f32[384,32]{0,1:T(8,128)S(1)}, f32[384,32]{0,1:T(8,128)}, u32[]{:S(2)}) copy-start(f32[384,32]{0,1:T(8,128)} %copy-done.38) | copy-start | bytes 147460
  742.3 86.6 %copy-start.56 = (f32[384,32]{0,1:T(8,128)S(1)}, f32[384,32]{0,1:T(8,128)}, u32[]{:S(2)}) copy-start(f32[384,32]{0,1:T(8,128)} %get-tuple-element.667) | copy-start | bytes 147460
  742.3 627.6 %reduce-scatter.19.cloned.1.call-start = ((), (), s32[]{:S(2)}) async-start(), calls=%async_computation.19 | async-start | bytes 1081344 | tf_op jit(solution)/shard_map/reduce_scatter | solution.py:550
  830.7 657.3 %reduce-scatter.23.cloned.1.call-start = ((), (), s32[]{:S(2)}) async-start(), calls=%async_computation.21 | async-start | bytes 6488064 | tf_op jit(solution)/shard_map/reduce_scatter | solution.py:552
  836.5 838.2 %reduce-scatter.27.cloned.1.call-start = ((), (), s32[]{:S(2)}) async-start(), calls=%async_computation.23 | async-start | bytes 8650752 | tf_op jit(solution)/shard_map/reduce_scatter | solution.py:555
  844.7 1124.0 %reduce-scatter.15.cloned.1.call-start = ((), (), s32[]{:S(2)}) async-start(), calls=%async_computation.17 | async-start | bytes 14057472 | tf_op jit(solution)/shard_map/reduce_scatter | solution.py:545
  883.0 5.8 collective-permute-start.1
  897.2 1432.7 %reduce-scatter.25.cloned.1.call-start = ((), (), s32[]{:S(2)}) async-start(), calls=%async_computation.22 | async-start | bytes 17301504 | tf_op jit(solution)/shard_map/reduce_scatter | solution.py:554
  (116 other events, 954.3 us)
Sparse Core Ops, SparseCore 0:
  10.9 77.4 all-gather.14
  91.3 52.7 all-gather.20
  146.8 44.3 all-gather.18
  289.9 59.4 all-gather.28
  352.2 57.6 all-gather.16
  412.8 52.5 all-gather.22
  468.4 76.3 all-gather.24
  547.8 60.6 all-gather.26
  642.1 58.9 all-gather.30
  710.8 115.3 reduce-scatter.12
  828.5 133.0 reduce-scatter.28
  964.3 133.9 reduce-scatter.16
  1101.2 134.1 reduce-scatter.20
  1238.1 131.7 reduce-scatter.18
  1376.9 111.0 reduce-scatter.22
  1490.7 183.8 reduce-scatter.26
  1677.4 291.3 reduce-scatter.14
  1971.5 358.3 reduce-scatter.24
where the time goes:
time: 2350 us; the launch traced here: 2340 us
  waiting for transfers between devices  1660 us (71%)
  blocking collectives  305 us (13%)
  matrix products  222 us (9%)
  other arithmetic  65 us (3%)
  local copies, waits for them, and re-layouts  57.8 us (2%)
    reduce_scatter x1, waiting for transfers between devices, on_device(): lax.psum_scatter(grad_w_gate_up, ('dp', 'seq'), scatter_dimension=0, tile...  361 us
    reduce_scatter x1, waiting for transfers between devices, on_device(): lax.psum_scatter(grad_w_in, ('dp', 'seq'), scatter_dimension=0, tiled=True)  294 us
    reduce_scatter x1, waiting for transfers between devices, on_device(): lax.psum_scatter(grad_w_down, ('dp', 'seq'), scatter_dimension=1, tiled=T...  187 us
    reduce_scatter x1, waiting for transfers between devices, on_device(): lax.psum_scatter(grad_w_attn_out, ('dp', 'seq'), scatter_dimension=1, til...  137 us
    reduce_scatter x1, waiting for transfers between devices, on_device(): lax.psum_scatter(grad_w_keyval, ('dp', 'seq'), scatter_dimension=0, tiled...  134 us
    reduce_scatter x1, waiting for transfers between devices, on_device(): lax.psum_scatter(grad_w_query, ('dp', 'seq'), scatter_dimension=0, tiled=...  126 us
    reduce_scatter x1, waiting for transfers between devices, on_device(): lax.psum_scatter(grad_w_mix_out, ('dp', 'seq'), scatter_dimension=1, tile...  118 us
    unnamed x2, blocking collectives  84.6 us
  transfers between devices with their start and end apart: 20, of which 14 were waited for; matrix products, arithmetic and copies ran while one was open for 13% of the time, Pallas kernels for 0%

commit v1 on v0

v1 whole, which is shorter than its diff:
```python
from functools import partial
import math

import jax
import jax.numpy as jnp
from jax import lax
from jax.sharding import Mesh
from jax.sharding import PartitionSpec as P

MHEADS = 24
MHEAD_DIM = 64
STATE = 128
CONV = 4
QHEADS = 8
KVHEADS = 2
HEAD_DIM = 64
FF = 2048


norm_epsilon = 1e-06
rope_base = 100000000000.0
key_block = 1024
masked_score = -1e30
highest_precision = lax.Precision.HIGHEST


def rms_norm(values, gain_vector):
    return (
        values
        * lax.rsqrt(jnp.mean(values * values, axis=-1, keepdims=True) + norm_epsilon)
        * gain_vector
    )


def rope_tables(positions, head_width):
    half_width = head_width // 2
    exponents = jnp.arange(half_width).astype(jnp.float32) * (2.0 / head_width)
    frequency = rope_base ** (-exponents)
    angles = positions.astype(jnp.float32)[:, None] * frequency[None, :]
    return (jnp.cos(angles), jnp.sin(angles))


def rotate(values, cosine, sine_table):
    half_width = values.shape[-1] // 2
    first_half = values[..., :half_width]
    second_half = values[..., half_width:]
    cosine_b = cosine[:, None, :]
    sine_b = sine_table[:, None, :]
    return jnp.concatenate(
        [
            first_half * cosine_b - second_half * sine_b,
            second_half * cosine_b + first_half * sine_b,
        ],
        axis=-1,
    )


def outer_product(left, right):
    return lax.dot_general(
        left, right, (((0,), (0,)), ((), ())), preferred_element_type=jnp.float32
    )


def back_product(grad_rows, weight_matrix):
    return lax.dot_general(
        grad_rows, weight_matrix, (((1,), (1,)), ((), ())), preferred_element_type=jnp.float32
    )


def mamba_inputs(extended, step_raw, conv_weight, conv_bias, head_params):
    row_count = extended.shape[0] - (CONV - 1)
    conv_sum = conv_bias[None, :] + conv_weight[0][None, :] * extended[0:row_count]
    for offset in range(1, CONV):
        conv_sum = conv_sum + conv_weight[offset][None, :] * extended[offset : offset + row_count]
    activated = jax.nn.silu(conv_sum)
    inner_width = MHEADS * MHEAD_DIM
    inputs_x = activated[:, :inner_width].reshape(row_count, MHEADS, MHEAD_DIM)
    input_mat = activated[:, inner_width : inner_width + STATE]
    output_mat = activated[:, inner_width + STATE :]
    step_size = jax.nn.softplus(step_raw + head_params[1][None, :])
    log_decay = -jnp.exp(head_params[0])[None, :] * step_size
    return (inputs_x, input_mat, output_mat, log_decay, step_size)


def ssd_summary(inputs_x, input_mat, log_decay, step_size):
    cumulative = jnp.cumsum(log_decay, axis=0)
    weights_tail = jnp.exp(cumulative[-1][None, :] - cumulative) * step_size
    fresh_state = jnp.einsum(
        "th,thp,tn->hpn", weights_tail, inputs_x, input_mat, precision=highest_precision
    )
    return (jnp.exp(cumulative[-1]), fresh_state)


def ssd_output(inputs_x, input_mat, output_mat, log_decay, step_size, carry_state):
    row_count = inputs_x.shape[0]
    cumulative = jnp.cumsum(log_decay, axis=0)
    by_head = cumulative.T
    indices = jnp.arange(row_count)
    causal_mask = (indices[:, None] >= indices[None, :])[None]
    gap_matrix = jnp.where(causal_mask, by_head[:, :, None] - by_head[:, None, :], 0.0)
    kernel = jnp.where(causal_mask, jnp.exp(gap_matrix), 0.0)
    intersection = jnp.dot(output_mat, input_mat.T, precision=highest_precision)
    mixing = kernel * intersection[None] * step_size.T[:, None, :]
    within = jnp.einsum("hts,shp->thp", mixing, inputs_x, precision=highest_precision)
    carried = (
        jnp.einsum("tn,hpn->thp", output_mat, carry_state, precision=highest_precision)
        * jnp.exp(cumulative)[:, :, None]
    )
    return within + carried


def mamba_mix(
    inputs_x, input_mat, output_mat, log_decay, step_size, carry_state, gate_z, skip_vector
):
    row_count = inputs_x.shape[0]
    mixed_y = (
        ssd_output(inputs_x, input_mat, output_mat, log_decay, step_size, carry_state)
        + skip_vector[None, :, None] * inputs_x
    )
    return mixed_y.reshape(row_count, MHEADS * MHEAD_DIM) * jax.nn.silu(gate_z)


def mamba_local(
    extended, step_raw, gate_z, conv_weight, conv_bias, head_params, skip_vector, carry_state
):
    inputs_x, input_mat, output_mat, log_decay, step_size = mamba_inputs(
        extended, step_raw, conv_weight, conv_bias, head_params
    )
    mixer = mamba_mix(
        inputs_x, input_mat, output_mat, log_decay, step_size, carry_state, gate_z, skip_vector
    )
    factor, fresh_state = ssd_summary(inputs_x, input_mat, log_decay, step_size)
    end_state = factor[:, None, None] * carry_state + fresh_state
    return ((mixer, end_state), (output_mat, jnp.cumsum(log_decay, axis=0)))


def online_block(running, key_rows, first_key, queries, query_pos):
    best_score, weight_total, weighted = running
    row_count = key_rows.shape[0]
    key_width = KVHEADS * HEAD_DIM
    key_heads = key_rows[:, :key_width].reshape(row_count, KVHEADS, HEAD_DIM)
    value_heads = key_rows[:, key_width:].reshape(row_count, KVHEADS, HEAD_DIM)
    score_scale = 1.0 / math.sqrt(HEAD_DIM)
    scores = (
        jnp.einsum("tgjd,sgd->gjts", queries, key_heads, preferred_element_type=jnp.float32)
        * score_scale
    )
    key_pos = first_key + jnp.arange(row_count, dtype=jnp.int32)
    allowed = key_pos[None, :] <= query_pos[:, None]
    scores = jnp.where(allowed, scores, masked_score)
    new_best = jnp.maximum(best_score, jnp.max(scores, axis=-1))
    rescale = jnp.exp(best_score - new_best)
    soft_weights = jnp.where(allowed, jnp.exp(scores - new_best[..., None]), 0.0)
    weight_total = weight_total * rescale + jnp.sum(soft_weights, axis=-1)
    weighted = weighted * rescale[..., None] + jnp.einsum(
        "gjts,sgd->gjtd",
        soft_weights.astype(jnp.bfloat16),
        value_heads,
        preferred_element_type=jnp.float32,
    )
    return (new_best, weight_total, weighted)


def attend_piece(running, key_piece, first_key, queries, query_pos):
    row_count = key_piece.shape[0]
    block_rows = math.gcd(row_count, key_block)
    block_count = row_count // block_rows
    stacked = key_piece.reshape(block_count, block_rows, key_piece.shape[1])
    firsts = block_rows * jnp.arange(block_count, dtype=jnp.int32)
    last_query = query_pos[-1]

    def advance(state_now, item_pair):
        key_rows, block_first = item_pair
        updated = lax.cond(
            block_first <= last_query,
            lambda carried: online_block(carried, key_rows, block_first, queries, query_pos),
            lambda carried: carried,
            state_now,
        )
        return (updated, None)

    running, _ = lax.scan(advance, running, (stacked, firsts))
    return running


seq_axes = ("z", "x")
chip_axes = ("y", "z", "x")


def shifted(block, axis, distance):
    count = lax.axis_size(axis)
    return lax.ppermute(block, axis, [(i, (i + distance) % count) for i in range(count)])


def from_behind(block, distance):
    devices = range(lax.axis_size(seq_axes))
    route = [(i - distance, i) for i in devices if i - distance in devices]
    return lax.ppermute(block, seq_axes, route)


def own_half_first(values):
    cuts = 2 * lax.axis_size("y")
    width = values.shape[1] // cuts
    blocks = [values[:, i * width : (i + 1) * width] for i in range(cuts)]
    first = lax.axis_index("core") == 0
    own = [jnp.where(first, a, b) for a, b in zip(blocks[0::2], blocks[1::2])]
    other = [jnp.where(first, b, a) for a, b in zip(blocks[0::2], blocks[1::2])]
    return jnp.concatenate(own + other, axis=1)


def usual_order(values):
    cuts = 2 * lax.axis_size("y")
    width = values.shape[1] // cuts
    blocks = [values[:, i * width : (i + 1) * width] for i in range(cuts)]
    first = lax.axis_index("core") == 0
    merged = []
    for own, other in zip(blocks[: cuts // 2], blocks[cuts // 2 :]):
        merged += [jnp.where(first, own, other), jnp.where(first, other, own)]
    return jnp.concatenate(merged, axis=1)


def gather_rows(shard):
    own = lax.all_gather(shard, chip_axes, axis=0, tiled=True)
    return own, shifted(own, "core", 1)


def times_rows(values, pair):
    half = values.shape[1] // 2
    return jnp.dot(values[:, :half], pair[0], preferred_element_type=jnp.float32) + jnp.dot(
        values[:, half:], pair[1], preferred_element_type=jnp.float32
    )


def times_rows_back(values, pair):
    return jnp.concatenate([back_product(values, pair[0]), back_product(values, pair[1])], axis=1)


def swap_sum(total, axis, dim):
    count = lax.axis_size(axis)
    place = lax.axis_index(axis)
    kept = lax.dynamic_index_in_dim(total, place, dim, False)
    for step in range(1, count):
        part = lax.dynamic_index_in_dim(total, (place + step) % count, dim, False)
        kept = kept + shifted(part.astype(jnp.bfloat16), axis, step).astype(jnp.float32)
    return kept


def scatter_product(left, right):
    half = left.shape[1] // 2
    sizes = [lax.axis_size(axis) for axis in chip_axes]
    rows = half // math.prod(sizes)
    middle = right.shape[1] // 256 * 128
    pieces = []
    for columns, order in (
        (right[:, :middle], (("x", 2), ("y", 0), ("z", 0))),
        (right[:, middle:], (("y", 0), ("x", 1), ("z", 0))),
    ):
        sent = outer_product(left[:, half:], columns).astype(jnp.bfloat16)
        received = shifted(sent, "core", 1)
        total = outer_product(left[:, :half], columns) + received.astype(jnp.float32)
        total = total.reshape(*sizes, rows, columns.shape[1])
        for axis, dim in order:
            total = swap_sum(total, axis, dim)
        pieces.append(total)
    return jnp.concatenate(pieces, axis=1)


def sum_everywhere(values):
    for axis in ("core", "x", "y", "z"):
        count = lax.axis_size(axis)
        step = 1
        while step < count:
            values = values + lax.ppermute(values, axis, [(i, i ^ step) for i in range(count)])
            step *= 2
    return values


def spread_states(states, factor):
    width = states.shape[-1]
    rows = states.reshape(-1, width)
    last = jnp.zeros((16, width), jnp.float32).at[0, : factor.shape[0]].set(factor)
    packed = jnp.concatenate([rows, last], axis=0).astype(jnp.bfloat16)
    gathered = lax.all_gather(packed, seq_axes)
    decays = gathered[:, rows.shape[0], : factor.shape[0]].astype(jnp.float32)
    return gathered[:, : rows.shape[0]].reshape(-1, *states.shape), decays


def carried_from_before(gathered, decays):
    place = lax.axis_index(seq_axes)
    order = jnp.arange(decays.shape[0])[:, None]
    between = jnp.where(order < place, decays, 1.0)
    after = lax.cumprod(between, axis=0, reverse=True)
    after = jnp.concatenate([after[1:], jnp.ones_like(after[:1])], axis=0)
    weights = jnp.where(order < place, after, 0.0)
    return jnp.sum(weights[:, :, None, None] * gathered.astype(jnp.float32), axis=0)


def carried_from_after(gathered, decays):
    place = lax.axis_index(seq_axes)
    order = jnp.arange(decays.shape[0])[:, None]
    between = jnp.where(order > place, decays, 1.0)
    before = lax.cumprod(between, axis=0)
    before = jnp.concatenate([jnp.ones_like(before[:1]), before[:-1]], axis=0)
    weights = jnp.where(order > place, before, 0.0)
    return jnp.sum(weights[:, :, None, None] * gathered.astype(jnp.float32), axis=0)


def sum_key_grads(grad_rows):
    sizes = [lax.axis_size(axis) for axis in seq_axes]
    total = grad_rows.reshape(*sizes, -1, grad_rows.shape[1])
    return swap_sum(swap_sum(total, "x", 1), "z", 0)


def on_device(
    tokens,
    gain_one,
    w_in,
    w_step,
    conv_weight,
    conv_bias,
    mamba_heads,
    skip_weight,
    w_query,
    w_keyval,
    w_attn_out,
    w_mix_out,
    gain_two,
    w_gate_up,
    w_down,
    cotangent,
):
    inputs = own_half_first(tokens[0]).astype(jnp.float32)
    grad_output = own_half_first(cotangent[0])
    row_count = inputs.shape[0]
    inner_width = MHEADS * MHEAD_DIM
    channels = conv_weight.shape[1] * lax.axis_size(("y", "core", "z", "x"))
    key_width = KVHEADS * HEAD_DIM
    group_size = QHEADS // KVHEADS
    own_rows = gain_one.shape[0]
    taps = jnp.concatenate([conv_weight, conv_bias[None]], axis=0)
    tap_columns = -(-taps.size // own_rows)
    tap_shard = jnp.pad(taps.reshape(-1), (0, tap_columns * own_rows - taps.size))
    small_width = w_step.shape[1] + 2 + tap_columns
    first_shard = jnp.concatenate(
        [
            w_in,
            w_query,
            w_keyval,
            w_step,
            gain_one[:, None],
            gain_two[:, None],
            tap_shard.reshape(tap_columns, own_rows).T,
            jnp.zeros((own_rows, -small_width % 128), jnp.bfloat16),
        ],
        axis=1,
    )
    first_pair = gather_rows(first_shard)
    small_at = w_in.shape[1] + w_query.shape[1] + w_keyval.shape[1]
    gain_at = small_at + w_step.shape[1]
    gains = jnp.concatenate([half[:, gain_at : gain_at + 2] for half in first_pair], axis=0)
    gain_one_float = gains[:, 0].astype(jnp.float32)
    gain_two_float = gains[:, 1].astype(jnp.float32)
    tap_own, tap_other = (half[:, gain_at + 2 : gain_at + 2 + tap_columns] for half in first_pair)
    first_core = lax.axis_index("core") == 0
    y_size = lax.axis_size("y")
    tap_both = jnp.stack(
        [
            jnp.where(first_core, tap_own, tap_other).reshape(y_size, -1, own_rows, tap_columns),
            jnp.where(first_core, tap_other, tap_own).reshape(y_size, -1, own_rows, tap_columns),
        ],
        axis=1,
    )
    tap_both = jnp.swapaxes(tap_both, 3, 4).reshape(-1, tap_columns * own_rows)[:, : taps.size]
    tap_all = jnp.swapaxes(tap_both.reshape(-1, *taps.shape), 0, 1).reshape(taps.shape[0], channels)
    tap_all = tap_all.astype(jnp.float32)
    conv_float = tap_all[:CONV]
    conv_bias_float = tap_all[CONV]
    out_pair = gather_rows(jnp.concatenate([w_mix_out.T, w_attn_out.T], axis=1))
    up_pair = gather_rows(w_gate_up)
    down_pair = gather_rows(w_down.T)
    piece_index = lax.axis_index(seq_axes)

    normed = rms_norm(inputs, gain_one_float).astype(jnp.bfloat16)
    projected = times_rows(normed, first_pair)
    gate_z = projected[:, :inner_width]
    conv_input = projected[:, inner_width : inner_width + channels].astype(jnp.bfloat16)
    query_at = inner_width + channels
    query_raw = projected[:, query_at : query_at + QHEADS * HEAD_DIM]
    keyval_raw = projected[:, query_at + QHEADS * HEAD_DIM : small_at]
    step_raw = projected[:, small_at:gain_at]
    positions = piece_index * row_count + jnp.arange(row_count, dtype=jnp.int32)
    cosine, sine_table = rope_tables(positions, HEAD_DIM)
    queries = (
        rotate(query_raw.reshape(row_count, QHEADS, HEAD_DIM), cosine, sine_table)
        .astype(jnp.bfloat16)
        .reshape(row_count, KVHEADS, group_size, HEAD_DIM)
    )
    key_rotated = rotate(
        keyval_raw[:, :key_width].reshape(row_count, KVHEADS, HEAD_DIM), cosine, sine_table
    ).reshape(row_count, key_width)
    own_keys = jnp.concatenate([key_rotated, keyval_raw[:, key_width:]], axis=1).astype(
        jnp.bfloat16
    )
    all_keys = lax.all_gather(own_keys, seq_axes, axis=0, tiled=True)

    border = from_behind(conv_input[row_count - (CONV - 1) :], 1)
    extended = jnp.concatenate([border, conv_input], axis=0).astype(jnp.float32)
    inputs_x, input_mat, output_mat, log_decay, step_size = mamba_inputs(
        extended, step_raw, conv_float, conv_bias_float, mamba_heads
    )
    factor, fresh_state = ssd_summary(inputs_x, input_mat, log_decay, step_size)
    carry_state = carried_from_before(*spread_states(fresh_state, factor))
    mixer = mamba_mix(
        inputs_x, input_mat, output_mat, log_decay, step_size, carry_state, gate_z, skip_weight
    ).astype(jnp.bfloat16)
    start_state = (
        jnp.full((KVHEADS, group_size, row_count), masked_score, jnp.float32),
        jnp.zeros((KVHEADS, group_size, row_count), jnp.float32),
        jnp.zeros((KVHEADS, group_size, row_count, HEAD_DIM), jnp.float32),
    )
    best_score, weight_total, weighted = attend_piece(
        start_state, all_keys, jnp.int32(0), queries=queries, query_pos=positions
    )
    attended_heads = weighted / weight_total[..., None]
    log_total = best_score + jnp.log(weight_total)
    attention_rows = (
        jnp.transpose(attended_heads, (2, 0, 1, 3))
        .reshape(row_count, QHEADS * HEAD_DIM)
        .astype(jnp.bfloat16)
    )
    branches = jnp.concatenate([mixer, attention_rows], axis=1)
    hidden = inputs + times_rows_back(branches, out_pair)
    normed_two = rms_norm(hidden, gain_two_float).astype(jnp.bfloat16)
    gate_up = times_rows(normed_two, up_pair)
    gate_part = gate_up[:, :FF]
    up_part = gate_up[:, FF:]
    activated = (jax.nn.silu(gate_part) * up_part).astype(jnp.bfloat16)
    result = hidden + times_rows_back(activated, down_pair)
    output = usual_order(result.astype(jnp.bfloat16))[None]

    grad_out_float = grad_output.astype(jnp.float32)
    grad_activated = times_rows(grad_output, down_pair)
    grad_w_down = scatter_product(grad_output, activated)
    gate_sigmoid = jax.nn.sigmoid(gate_part)
    grad_gate = grad_activated * up_part * gate_sigmoid * (1.0 + gate_part * (1.0 - gate_sigmoid))
    grad_up = grad_activated * gate_part * gate_sigmoid
    grad_gate_up = jnp.concatenate([grad_gate, grad_up], axis=1).astype(jnp.bfloat16)
    grad_w_gate_up = scatter_product(normed_two, grad_gate_up)
    grad_normed_two = times_rows_back(grad_gate_up, up_pair)
    _, pull_two = jax.vjp(rms_norm, hidden, gain_two_float)
    grad_hidden_norm, grad_gain_two = pull_two(grad_normed_two)
    grad_hidden = grad_out_float + grad_hidden_norm
    grad_branch = grad_hidden.astype(jnp.bfloat16)
    grad_w_out = scatter_product(grad_branch, branches)
    grad_branches = times_rows(grad_branch, out_pair)
    grad_mixer = grad_branches[:, :inner_width]
    grad_attention = grad_branches[:, inner_width:].astype(jnp.bfloat16)
    grad_heads = grad_attention.reshape(row_count, KVHEADS, group_size, HEAD_DIM)
    row_dots = jnp.einsum("tgjd,gjtd->gjt", grad_heads.astype(jnp.float32), attended_heads)
    total_rows = all_keys.shape[0]
    block_rows = min(key_block, total_rows)
    stacked = all_keys.reshape(total_rows // block_rows, block_rows, 2 * key_width)
    firsts = block_rows * jnp.arange(total_rows // block_rows, dtype=jnp.int32)
    score_scale = 1.0 / math.sqrt(HEAD_DIM)
    last_query = positions[-1]

    def backward_block(grad_query_acc, item_pair):
        key_rows, first_key = item_pair

        def compute(acc_now):
            key_heads = key_rows[:, :key_width].reshape(block_rows, KVHEADS, HEAD_DIM)
            value_heads = key_rows[:, key_width:].reshape(block_rows, KVHEADS, HEAD_DIM)
            scores = (
                jnp.einsum("tgjd,sgd->gjts", queries, key_heads, preferred_element_type=jnp.float32)
                * score_scale
            )
            key_pos = first_key + jnp.arange(block_rows, dtype=jnp.int32)
            allowed = key_pos[None, :] <= positions[:, None]
            scores = jnp.where(allowed, scores, masked_score)
            soft_weights = jnp.where(allowed, jnp.exp(scores - log_total[..., None]), 0.0)
            grad_weights = jnp.einsum(
                "tgjd,sgd->gjts", grad_heads, value_heads, preferred_element_type=jnp.float32
            )
            grad_scores = (soft_weights * (grad_weights - row_dots[..., None])).astype(jnp.bfloat16)
            acc_next = (
                acc_now
                + jnp.einsum(
                    "gjts,sgd->gjtd", grad_scores, key_heads, preferred_element_type=jnp.float32
                )
                * score_scale
            )
            grad_key = (
                jnp.einsum(
                    "gjts,tgjd->sgd", grad_scores, queries, preferred_element_type=jnp.float32
                )
                * score_scale
            )
            grad_value = jnp.einsum(
                "gjts,tgjd->sgd",
                soft_weights.astype(jnp.bfloat16),
                grad_heads,
                preferred_element_type=jnp.float32,
            )
            return (
                acc_next,
                jnp.concatenate(
                    [
                        grad_key.reshape(block_rows, key_width),
                        grad_value.reshape(block_rows, key_width),
                    ],
                    axis=1,
                ),
            )

        def skipped(acc_now):
            return (acc_now, jnp.zeros((block_rows, 2 * key_width), jnp.float32))

        return lax.cond(first_key <= last_query, compute, skipped, grad_query_acc)

    grad_query_heads, grad_key_rows = lax.scan(
        backward_block,
        jnp.zeros((KVHEADS, group_size, row_count, HEAD_DIM), jnp.float32),
        (stacked, firsts),
    )
    own_grads = sum_key_grads(grad_key_rows.reshape(total_rows, 2 * key_width))
    grad_query_rows = jnp.transpose(grad_query_heads, (2, 0, 1, 3)).reshape(
        row_count, QHEADS, HEAD_DIM
    )
    grad_query = (
        rotate(grad_query_rows, cosine, -sine_table)
        .reshape(row_count, QHEADS * HEAD_DIM)
        .astype(jnp.bfloat16)
    )
    grad_key_raw = rotate(
        own_grads[:, :key_width].reshape(row_count, KVHEADS, HEAD_DIM), cosine, -sine_table
    ).reshape(row_count, key_width)
    grad_keyval = jnp.concatenate([grad_key_raw, own_grads[:, key_width:]], axis=1).astype(
        jnp.bfloat16
    )
    primal_out, pull_mamba, aux_values = jax.vjp(
        mamba_local,
        extended,
        step_raw,
        gate_z,
        conv_float,
        conv_bias_float,
        mamba_heads,
        skip_weight,
        carry_state,
        has_aux=True,
    )
    output_saved, cumulative = aux_values
    grad_y = (grad_mixer * jax.nn.silu(gate_z)).reshape(row_count, MHEADS, MHEAD_DIM)
    from_output = jnp.einsum(
        "th,thp,tn->hpn", jnp.exp(cumulative), grad_y, output_saved, precision=highest_precision
    )
    grad_end = carried_from_after(*spread_states(from_output, jnp.exp(cumulative[-1])))
    (
        grad_extended,
        grad_step_raw,
        grad_gate_z,
        grad_conv_weight,
        grad_conv_bias,
        grad_head_params,
        grad_skip,
        _,
    ) = pull_mamba((grad_mixer, grad_end))
    rim_back = from_behind(grad_extended[: CONV - 1], -1)
    grad_conv_input = grad_extended[CONV - 1 :] + jnp.concatenate(
        [jnp.zeros((row_count - (CONV - 1), grad_extended.shape[1]), jnp.float32), rim_back], axis=0
    )
    grad_gate_low = grad_gate_z.astype(jnp.bfloat16)
    grad_rest = jnp.concatenate(
        [
            grad_conv_input.astype(jnp.bfloat16),
            grad_query,
            grad_keyval,
            grad_step_raw.astype(jnp.bfloat16),
        ],
        axis=1,
    )
    grad_w_gate = scatter_product(normed, grad_gate_low)
    grad_w_rest = scatter_product(normed, grad_rest)
    grad_all = jnp.concatenate(
        [
            grad_gate_low,
            grad_rest,
            jnp.zeros((row_count, first_shard.shape[1] - gain_at), jnp.bfloat16),
        ],
        axis=1,
    )
    grad_normed = times_rows_back(grad_all, first_pair)
    _, pull_one = jax.vjp(rms_norm, inputs, gain_one_float)
    grad_input_norm, grad_gain_one = pull_one(grad_normed)
    input_grad = usual_order(grad_hidden + grad_input_norm)[None]

    gain_grads = usual_order(jnp.stack([grad_gain_one, grad_gain_two]))
    tap_grads = jnp.concatenate([grad_conv_weight, grad_conv_bias[None]], axis=0)
    summed_taps = sum_everywhere(
        (jnp.concatenate([tap_grads.reshape(-1), grad_head_params.reshape(-1), grad_skip]))
    )
    summed_gains = sum_everywhere(gain_grads)
    place = lax.axis_index(("y", "core", "z", "x"))
    own_gains = lax.dynamic_slice_in_dim(summed_gains, place * own_rows, own_rows, 1)
    own_channels = conv_weight.shape[1]
    own_taps = lax.dynamic_slice_in_dim(
        summed_taps[: tap_grads.size].reshape(tap_grads.shape),
        place * own_channels,
        own_channels,
        1,
    )
    head_grad = summed_taps[tap_grads.size : tap_grads.size + mamba_heads.size]
    skip_grad = summed_taps[tap_grads.size + mamba_heads.size :]
    rest_query = channels + w_query.shape[1]
    rest_keyval = rest_query + w_keyval.shape[1]
    return (
        output,
        input_grad,
        own_gains[0],
        jnp.concatenate([grad_w_gate, grad_w_rest[:, :channels]], axis=1),
        grad_w_rest[:, rest_keyval:],
        own_taps[:CONV],
        own_taps[CONV],
        head_grad.reshape(mamba_heads.shape),
        skip_grad,
        grad_w_rest[:, channels:rest_query],
        grad_w_rest[:, rest_query:rest_keyval],
        grad_w_out[:, inner_width:].T,
        grad_w_out[:, :inner_width].T,
        own_gains[1],
        grad_w_gate_up,
        grad_w_down.T,
    )


def solution(mesh):
    dp, seq = mesh.shape["dp"], mesh.shape["seq"]
    by_axis = Mesh(mesh.devices.reshape(dp // 2, 2, seq // 2, 2), ("y", "core", "z", "x"))
    every = ("y", "core", "z", "x")
    pieces = P(("y", "core"), seq_axes, None)
    rows = P(every, None)
    columns = P(None, every)
    return jax.shard_map(
        on_device,
        mesh=by_axis,
        in_specs=(
            pieces,
            P(every),
            rows,
            rows,
            columns,
            P(every),
            P(),
            P(),
            rows,
            rows,
            columns,
            columns,
            P(every),
            rows,
            columns,
            pieces,
        ),
        out_specs=(
            pieces,
            pieces,
            P(every),
            rows,
            rows,
            columns,
            P(every),
            P(),
            P(),
            rows,
            rows,
            columns,
            columns,
            P(every),
            rows,
            columns,
        ),
        check_vma=False,
    )
```

time: 2350 us -> 973 us (0.41)
  waiting for transfers between devices: 1660 us -> 414 us
  blocking collectives: 305 us -> 0 us
  starting transfers between devices: 4.19 us -> 154 us
  other arithmetic: 65 us -> 104 us
  matrix products: 222 us -> 197 us
    reduce_scatter x8 -> x0, waiting for transfers between devices: 1440 us -> none  [the longest x1 361 us: on_device(): lax.psum_scatter(grad_w_gate_up, ('dp', 'seq'), scatter_dimension=0, tile...]
    all_gather x4 -> x0, blocking collectives: 220 us -> none  [the longest x1 71.2 us: on_device(): lax.all_gather(w_keyval, ('dp', 'seq'), axis=0, tiled=True)]
    ppermute x2 -> x80, starting transfers between devices: 3.25 us -> 153 us  [the longest x68 133 us: shifted(): lax.ppermute(block, axis, [(i, (i + distance) % count) for i in range(cou...]
    ppermute x2 -> x80, waiting for transfers between devices: 4.8 us -> 122 us  [the longest x68 109 us: shifted(): lax.ppermute(block, axis, [(i, (i + distance) % count) for i in range(cou...]
    unnamed x2 -> x0, blocking collectives: 84.6 us -> none
    all_gather x9 -> x7, waiting for transfers between devices: 208 us -> 290 us  [the longest x4 213 us: gather_rows(): own = lax.all_gather(shard, chip_axes, axis=0, tiled=True)]
  transfers between devices with their start and end apart: 20 -> 87, of which waited for: 14 -> 45; matrix products, arithmetic and copies ran while one was open for 13% -> 28% of each run, Pallas kernels for 0% -> 0%
where the time goes in v1:
time: 973 us; the launch traced here: 964 us
  waiting for transfers between devices  414 us (43%)
  matrix products  197 us (20%)
  starting transfers between devices  154 us (16%)
  other arithmetic  104 us (11%)
  local copies, waits for them, and re-layouts  70.6 us (7%)
  between operations  17.3 us (2%)
    all_gather x4, waiting for transfers between devices, gather_rows(): own = lax.all_gather(shard, chip_axes, axis=0, tiled=True)  213 us
    ppermute x68, starting transfers between devices, shifted(): lax.ppermute(block, axis, [(i, (i + distance) % count) for i in range(cou...  133 us
    ppermute x68, waiting for transfers between devices, shifted(): lax.ppermute(block, axis, [(i, (i + distance) % count) for i in range(cou...  109 us
    dot_general x3, matrix products, ssd_output(): jnp.einsum('hts,shp->thp', mixing, inputs_x, precision=highest_precision)  55.9 us
    all_gather x1, waiting for transfers between devices, on_device(): all_keys = lax.all_gather(own_keys, seq_axes, axis=0, tiled=True)  42.5 us
    dot_general x20, matrix products, outer_product(): lax.dot_general(left, right, (((0,), (0,)), ((), ())), preferred_element_...  35.8 us
    all_gather x2, waiting for transfers between devices, spread_states(): gathered = lax.all_gather(packed, seq_axes)  34.6 us
    dot_general x4, matrix products, times_rows(): jnp.dot(values[:, half:], pair[1], preferred_element_type=jnp.float32)  23.3 us
  transfers between devices with their start and end apart: 87, of which 45 were waited for; matrix products, arithmetic and copies ran while one was open for 28% of the time, Pallas kernels for 0%

profile of v1, /device:TPU:0, one launch (start us, length us, event | category | flops | bytes accessed | tf_op | source)
XLA Modules:
  0.0 964.1 jit_solution(6390663401344343713)
XLA Ops:
  15.3 77.0 %all-gather.8.cloned.1.call-done = bf16[512,4224]{1,0:T(8,128)(2,1)} async-done(((bf16[32,4224]{1,0:T(8,128)(2,1)}), bf16[512,4224]{1,0:T(8,128)(2,1)}) %all-gather.8.cloned.1.call-update) | async-done | bytes 4325392 | tf_op jit(solution)/shard_map/all_gather | solution.py:223
  102.3 5.0 fusion.190
  107.3 7.4 fusion.311
  142.0 4.9 fusion.54
  157.7 62.1 %all-gather.18.cloned.1.call-done = bf16[512,2048]{1,0:T(8,128)(2,1)} async-done(((bf16[32,2048]{1,0:T(8,128)(2,1)}), bf16[512,2048]{1,0:T(8,128)(2,1)}) %all-gather.18.cloned.1.call-update) | async-done | bytes 2097168 | tf_op jit(solution)/shard_map/all_gather | solution.py:223
  224.0 73.0 %all-gather.16.cloned.1.call-done = bf16[512,4096]{1,0:T(8,128)(2,1)} async-done(((bf16[32,4096]{1,0:T(8,128)(2,1)}), bf16[512,4096]{1,0:T(8,128)(2,1)}) %all-gather.16.cloned.1.call-update) | async-done | bytes 4194320 | tf_op jit(solution)/shard_map/all_gather | solution.py:223
  300.9 42.5 %all-gather.12.cloned.1.call-done = bf16[3072,256]{0,1:T(8,128)(2,1)} async-done(((bf16[384,256]{0,1:T(8,128)(2,1)}), bf16[3072,256]{0,1:T(8,128)(2,1)}) %all-gather.12.cloned.1.call-update) | async-done | bytes 1572880 | tf_op jit(solution)/shard_map/all_gather | solution.py:404
  349.2 18.2 %while.33 = (s32[]{:T(128)}, f32[2,4,384]{2,1,0:T(4,128)S(1)}, f32[2,4,384]{2,1,0:T(4,128)}, f32[2,4,384,64]{2,3,1,0:T(8,128)S(1)}, s32[3]{0:T(128)}, /*index=5*...) while((s32[]{:T(128)}, f32[2,4,384]{2,1,0:T(4,128)S(1)}, ...), condition=%wide.region_10.11_spmd.clone, body=%wide.region_5.10_spmd.clone.sunk | while | flops 846994816 | bytes 44218688 | solution.py:182
  351.8 10.5 %conditional.6 = ((f32[2,4,384]{2,1,0:T(4,128)S(1)}, f32[2,4,384]{2,1,0:T(4,128)}, f32[2,4,384,64]{2,3,1,0:T(8,128)S(1)})) conditional(s32[]{:T(128)} %convert_element_type.1210, (f32[2,4,384]{2,1,0:T(4,128)S(1)}, f32[2,4,384]{2,1,0:T(4,128)}, f32[2,4,384,64]{2,3,1,0:T(8,128)S(1)}) %tuple.206, (s32[]{:T(128)}, s32[]{:T(128)}, ...), branch_computations={%region_6.6_spmd, %region_7.9_spmd} | conditional | flops 846994816 | bytes 44216932 | solution.py:174
  370.3 34.6 %all-gather.10.cloned.1.call-done = bf16[8,1552,128]{2,1,0:T(8,128)(2,1)} async-done(((bf16[1,1552,128]{2,1,0:T(8,128)(2,1)}), bf16[8,1552,128]{2,1,0:T(8,128)(2,1)}) %all-gather.10.cloned.1.call-update) | async-done | bytes 3178512 | tf_op jit(solution)/shard_map/all_gather | solution.py:283
  409.5 4.8 multiply_reduce_fusion.3
  416.6 19.4 %fusion.59 = f32[384,24,64]{0,2,1:T(8,128)S(1)} fusion(f32[384,24,64]{0,2,1:T(8,128)S(1)} %bitcast.594, f32[384,24,64]{0,2,1:T(8,128)S(1)} %fusion.202, f32[24,384]{1,0:T(8,128)S(1)} %copy-done.112, f32[384,384]{1,0:T(8,128)} %fusion.211, f32[24,384]{1,0:T(8,128)S(1)} %copy-done.110, pred[384,384]{1,0:T(8,128)(4,1)S(1)} %copy-done.91, ...), kind=kOutput, calls=%fused_computation.114 | convolution fusion | flops 2737963008 | bytes 7925856 | tf_op jit(solution)/shard_map/hts,shp->thp/dot_general | solution.py:104
  445.7 6.9 convolution_add_fusion.1
  452.6 6.1 multiply_convert_fusion.1
  499.2 23.1 %fusion.38 = (f32[24,384]{1,0:T(8,128)}, f32[24,384]{1,0:T(8,128)}, f32[24,384]{1,0:T(8,128)}, f32[384,384]{1,0:T(8,128)}) fusion(f32[24,384]{1,0:T(8,128)} %get-tuple-element.696, f32[384,384]{1,0:T(8,128)} %fusion.211, f32[24,384]{1,0:T(8,128)} %get-tuple-element.770, pred[384,384]{1,0:T(8,128)(4,1)} %iota_compare_fusion, f32[24,64,384]{2,1,0:T(8,128)} %bitcast.600, ...), kind=kOutput, calls=%fused_computation.53 | convolution fusion | flops 2770818048 | bytes 6230016 | tf_op jit(solution)/shard_map/transpose(jvp(hts,shp->thp))/dot_general | solution.py:104
  525.4 38.2 %while.34 = (s32[]{:T(128)}, f32[2,4,384,64]{2,3,1,0:T(8,128)S(1)}, f32[3,1024,256]{2,1,0:T(8,128)}, s32[3]{0:T(128)}, s32[]{:T(128)}, /*index=5*/bf16[3,1024,25...) while((s32[]{:T(128)}, f32[2,4,384,64]{2,3,1,0:T(8,128)S(1)}, ...), condition=%wide.region_19.20_spmd.clone, body=%wide.region_16.19_spmd.clone.sunk | while | flops 2052195712 | bytes 71224056 | solution.py:520
  528.1 25.9 %conditional.7 = (f32[2,4,384,64]{2,3,1,0:T(8,128)S(1)}, f32[1,1024,256]{1,2,0:T(8,128)S(1)}) conditional(s32[]{:T(128)} %convert_element_type.1211, f32[2,4,384,64]{2,3,1,0:T(8,128)S(1)} %get-tuple-element.980, (s32[]{:T(128)}, s32[]{:T(128)}, bf16[3,1024,256]{1,2,0:T(8,128)(2,1)}, s32[]{:T(128)}, bf16[384,2,4,64]{0,3,2,1:T(8,128)(2,1)S(1)}, ...), branch_computations={%region_17.17_spmd, %region_18.18_spmd} | conditional | flops 2052195712 | bytes 67027484 | solution.py:518
  529.3 6.5 fusion.312
  536.7 7.3 fusion.17
  546.0 6.6 fusion.22
  589.5 27.2 %collective-permute-start.7 = (bf16[384,256]{0,1:T(8,128)(2,1)S(1)}, bf16[384,256]{0,1:T(8,128)(2,1)S(1)}, u32[]{:S(2)}, u32[]{:S(2)}) collective-permute-start(bf16[384,256]{0,1:T(8,128)(2,1)S(1)} %get-tuple-element.707), channel_id=1, source_target_pairs={{0,2},{2,4},{4,6},{6,0},{1,3},{3,5},{5,7},{7,1},{8,10},{10,12},{12... | collective-permute-start | bytes 589832 | tf_op jit(solution)/shard_map/ppermute | solution.py:192
  616.7 26.6 %collective-permute-start.8 = (bf16[384,256]{0,1:T(8,128)(2,1)S(1)}, bf16[384,256]{0,1:T(8,128)(2,1)S(1)}, u32[]{:S(2)}, u32[]{:S(2)}) collective-permute-start(bf16[384,256]{0,1:T(8,128)(2,1)S(1)} %get-tuple-element.709), channel_id=1, source_target_pairs={{0,4},{2,6},{4,0},{6,2},{1,5},{3,7},{5,1},{7,3},{8,12},{10,14},{12... | collective-permute-start | bytes 589832 | tf_op jit(solution)/shard_map/ppermute | solution.py:192
  648.6 6.9 collective-permute-done.8
  683.7 5.7 collective-permute-start.20
  700.7 9.7 %collective-permute-done.75 = bf16[4,2,32,1024]{3,2,0,1:T(8,128)(2,1)S(1)} collective-permute-done((bf16[4,2,32,1024]{3,2,0,1:T(8,128)(2,1)S(1)}, bf16[4,2,32,1024]{3,2,0,1:T(8,128)(2,1)S(1)}, u32[]{:S(2)}, u32[]{:S(2)}) %collective-permute-start.75) | collective-permute-done | bytes 524320 | tf_op jit(solution)/shard_map/ppermute | solution.py:192
  713.6 7.9 collective-permute-done.45
  764.8 14.6 %collective-permute-done.57 = bf16[2,4,32,2048]{3,2,1,0:T(8,128)(2,1)S(1)} collective-permute-done((bf16[2,4,32,2048]{3,2,1,0:T(8,128)(2,1)S(1)}, bf16[2,4,32,2048]{3,2,1,0:T(8,128)(2,1)S(1)}, u32[]{:S(2)}, u32[]{:S(2)}) %collective-permute-start.57) | collective-permute-done | bytes 1048608 | tf_op jit(solution)/shard_map/ppermute | solution.py:192
  781.3 6.1 collective-permute-done.63
  802.3 6.0 collective-permute-done.60
  808.4 4.8 collective-permute-done.66
  827.2 13.4 %bitcast_add_fusion = f32[384,24,64]{0,2,1:T(8,128)S(1)} fusion(f32[384,24,64]{0,2,1:T(8,128)S(1)} %bitcast.601, f32[384,24,64]{0,2,1:T(8,128)S(1)} %get-tuple-element.787, f32[24,64,384]{2,1,0:T(8,128)S(1)} %bitcast.602, f32[24,384]{1,0:T(8,128)S(1)} %copy-done.113, f32[384,384]{1,0:T(8,128)S(1)} %copy-done.78, f32[24,384]{1,0:T(8,128)S(1)} %copy-done.111, ...), kind=kOutput, calls=%fused_computation.108 | convolution fusion | flops 2737963008 | bytes 10285152 | tf_op jit(solution)/shard_map/transpose(jvp(hts,shp->thp))/dot_general | solution.py:104
  926.6 10.1 %collective-permute-done.34 = bf16[4,2,32,1304]{3,2,1,0:T(8,128)(2,1)S(1)} collective-permute-done((bf16[4,2,32,1304]{3,2,1,0:T(8,128)(2,1)S(1)}, bf16[4,2,32,1304]{3,2,1,0:T(8,128)(2,1)S(1)}, u32[]{:S(2)}, u32[]{:S(2)}) %collective-permute-start.34) | collective-permute-done | bytes 667680 | tf_op jit(solution)/shard_map/ppermute | solution.py:192
  (797 shorter events, 412.6 us)
Async XLA Ops:
  7.2 85.1 %all-gather.8.cloned.1.call-start = ((), (), s32[]{:S(2)}) async-start(), calls=%async_computation | async-start | bytes 4595712 | tf_op jit(solution)/shard_map/all_gather | solution.py:223
  12.3 145.4 %all-gather.14.cloned.1.call-start = ((), (), s32[]{:S(2)}) async-start(), calls=%async_computation.3 | async-start | bytes 2228224 | tf_op jit(solution)/shard_map/all_gather | solution.py:223
  13.9 205.8 %all-gather.18.cloned.1.call-start = ((), (), s32[]{:S(2)}) async-start(), calls=%async_computation.5 | async-start | bytes 2228224 | tf_op jit(solution)/shard_map/all_gather | solution.py:223
  14.7 282.3 %all-gather.16.cloned.1.call-start = ((), (), s32[]{:S(2)}) async-start(), calls=%async_computation.4 | async-start | bytes 4456448 | tf_op jit(solution)/shard_map/all_gather | solution.py:223
  15.3 328.2 %all-gather.12.cloned.1.call-start = ((), (), s32[]{:S(2)}) async-start(), calls=%async_computation.2 | async-start | bytes 1769472 | tf_op jit(solution)/shard_map/all_gather | solution.py:404
  116.3 23.1 %collective-permute-start.1 = (bf16[3,1792]{0,1:T(8,128)(2,1)}, bf16[3,1792]{0,1:T(8,128)(2,1)}, u32[]{:S(2)}, u32[]{:S(2)}) collective-permute-start(bf16[3,1792]{0,1:T(8,128)(2,1)} %slice.555), channel_id=1, source_target_pairs={{0,1},{1,2},{2,3},{3,4},{4,5},{5,6},{6,7},{8,9},{9,10},{10,11},{11... | collective-permute-start | bytes 32264 | tf_op jit(solution)/shard_map/ppermute | solution.py:198
  132.8 272.2 %all-gather.10.cloned.1.call-start = ((), (), s32[]{:S(2)}) async-start(), calls=%async_computation.1 | async-start | bytes 3575808 | tf_op jit(solution)/shard_map/all_gather | solution.py:283
  151.4 662.7 %all-gather.20.cloned.1.call-start = ((), (), s32[]{:S(2)}) async-start(), calls=%async_computation.6 | async-start | bytes 3575808 | tf_op jit(solution)/shard_map/all_gather | solution.py:283
  157.7 281.2 %collective-permute-start.2 = (bf16[512,2048]{1,0:T(8,128)(2,1)}, bf16[512,2048]{1,0:T(8,128)(2,1)}, u32[]{:S(2)}, u32[]{:S(2)}) collective-permute-start(bf16[512,2048]{1,0:T(8,128)(2,1)} %all-gather.14.cloned.1.call-done), channel_id=1, source_target_pairs={{0,8},{8,0},{1,9},{9,1},{2,10},{10,2},{3,11},{11,3},{4,12},{12,4},... | collective-permute-start | bytes 6291464 | tf_op jit(solution)/shard_map/ppermute | solution.py:192
  219.8 232.8 %collective-permute-start.4 = (bf16[512,2048]{1,0:T(8,128)(2,1)}, bf16[512,2048]{1,0:T(8,128)(2,1)}, u32[]{:S(2)}, u32[]{:S(2)}) collective-permute-start(bf16[512,2048]{1,0:T(8,128)(2,1)} %all-gather.18.cloned.1.call-done), channel_id=1, source_target_pairs={{0,8},{8,0},{1,9},{9,1},{2,10},{10,2},{3,11},{11,3},{4,12},{12,4},... | collective-permute-start | bytes 6291464 | tf_op jit(solution)/shard_map/ppermute | solution.py:192
  297.0 148.7 %collective-permute-start.3 = (bf16[512,4096]{1,0:T(8,128)(2,1)}, bf16[512,4096]{1,0:T(8,128)(2,1)}, u32[]{:S(2)}, u32[]{:S(2)}) collective-permute-start(bf16[512,4096]{1,0:T(8,128)(2,1)} %all-gather.16.cloned.1.call-done), channel_id=1, source_target_pairs={{0,8},{8,0},{1,9},{9,1},{2,10},{10,2},{3,11},{11,3},{4,12},{12,4},... | collective-permute-start | bytes 12582920 | tf_op jit(solution)/shard_map/ppermute | solution.py:192
  497.9 159.0 %collective-permute-start.68 = (bf16[512,1024]{1,0:T(8,128)(2,1)}, bf16[512,1024]{1,0:T(8,128)(2,1)}, u32[]{:S(2)}, u32[]{:S(2)}) collective-permute-start(bf16[512,1024]{1,0:T(8,128)(2,1)} %convolution_convert_fusion.5), channel_id=1, source_target_pairs={{0,8},{8,0},{1,9},{9,1},{2,10},{10,2},{3,11},{11,3},{4,12},{12,4},... | collective-permute-start | bytes 3145736 | tf_op jit(solution)/shard_map/ppermute | solution.py:192
  497.9 161.8 %collective-permute-start.74 = (bf16[512,1024]{1,0:T(8,128)(2,1)}, bf16[512,1024]{1,0:T(8,128)(2,1)}, u32[]{:S(2)}, u32[]{:S(2)}) collective-permute-start(bf16[512,1024]{1,0:T(8,128)(2,1)} %convolution_convert_fusion.4), channel_id=1, source_target_pairs={{0,8},{8,0},{1,9},{9,1},{2,10},{10,2},{3,11},{11,3},{4,12},{12,4},... | collective-permute-start | bytes 3145736 | tf_op jit(solution)/shard_map/ppermute | solution.py:192
  524.8 91.8 %collective-permute-start.15 = (bf16[512,768]{1,0:T(8,128)(2,1)}, bf16[512,768]{1,0:T(8,128)(2,1)}, u32[]{:S(2)}, u32[]{:S(2)}) collective-permute-start(bf16[512,768]{1,0:T(8,128)(2,1)} %convolution_convert_fusion.9), channel_id=1, source_target_pairs={{0,8},{8,0},{1,9},{9,1},{2,10},{10,2},{3,11},{11,3},{4,12},{12,4},... | collective-permute-start | bytes 2359304 | tf_op jit(solution)/shard_map/ppermute | solution.py:192
  524.8 120.2 %collective-permute-start.21 = (bf16[512,768]{1,0:T(8,128)(2,1)}, bf16[512,768]{1,0:T(8,128)(2,1)}, u32[]{:S(2)}, u32[]{:S(2)}) collective-permute-start(bf16[512,768]{1,0:T(8,128)(2,1)} %convolution_convert_fusion.8), channel_id=1, source_target_pairs={{0,8},{8,0},{1,9},{9,1},{2,10},{10,2},{3,11},{11,3},{4,12},{12,4},... | collective-permute-start | bytes 2359304 | tf_op jit(solution)/shard_map/ppermute | solution.py:192
  567.9 19.8 %collective-permute-start.6 = (bf16[4,384,256]{1,2,0:T(8,128)(2,1)}, bf16[4,384,256]{1,2,0:T(8,128)(2,1)}, u32[]{:S(2)}, u32[]{:S(2)}) collective-permute-start(bf16[4,384,256]{1,2,0:T(8,128)(2,1)} %bitcast.655), channel_id=1, source_target_pairs={{0,1},{1,0},{2,3},{3,2},{4,5},{5,4},{6,7},{7,6},{8,9},{9,8},{10,11... | collective-permute-start | bytes 2359304 | tf_op jit(solution)/shard_map/ppermute | solution.py:192
  589.5 59.1 %collective-permute-start.7 = (bf16[384,256]{0,1:T(8,128)(2,1)S(1)}, bf16[384,256]{0,1:T(8,128)(2,1)S(1)}, u32[]{:S(2)}, u32[]{:S(2)}) collective-permute-start(bf16[384,256]{0,1:T(8,128)(2,1)S(1)} %get-tuple-element.707), channel_id=1, source_target_pairs={{0,2},{2,4},{4,6},{6,0},{1,3},{3,5},{5,7},{7,1},{8,10},{10,12},{12... | collective-permute-start | bytes 589832 | tf_op jit(solution)/shard_map/ppermute | solution.py:192
  616.7 38.8 %collective-permute-start.8 = (bf16[384,256]{0,1:T(8,128)(2,1)S(1)}, bf16[384,256]{0,1:T(8,128)(2,1)S(1)}, u32[]{:S(2)}, u32[]{:S(2)}) collective-permute-start(bf16[384,256]{0,1:T(8,128)(2,1)S(1)} %get-tuple-element.709), channel_id=1, source_target_pairs={{0,4},{2,6},{4,0},{6,2},{1,5},{3,7},{5,1},{7,3},{8,12},{10,14},{12... | collective-permute-start | bytes 589832 | tf_op jit(solution)/shard_map/ppermute | solution.py:192
  648.6 109.1 %collective-permute-start.56 = (bf16[512,2048]{1,0:T(8,128)(2,1)S(1)}, bf16[512,2048]{1,0:T(8,128)(2,1)S(1)}, u32[]{:S(2)}, u32[]{:S(2)}) collective-permute-start(bf16[512,2048]{1,0:T(8,128)(2,1)S(1)} %copy-done.135), channel_id=1, source_target_pairs={{0,8},{8,0},{1,9},{9,1},{2,10},{10,2},{3,11},{11,3},{4,12},{12,4},... | collective-permute-start | bytes 6291464 | tf_op jit(solution)/shard_map/ppermute | solution.py:192
  663.3 35.7 %collective-permute-start.69 = (bf16[2,4,32,1024]{3,2,1,0:T(8,128)(2,1)S(1)}, bf16[2,4,32,1024]{3,2,1,0:T(8,128)(2,1)S(1)}, u32[]{:S(2)}, u32[]{:S(2)}) collective-permute-start(bf16[2,4,32,1024]{3,2,1,0:T(8,128)(2,1)S(1)} %fusion.131), channel_id=1, source_target_pairs={{0,1},{1,0},{2,3},{3,2},{4,5},{5,4},{6,7},{7,6},{8,9},{9,8},{10,11... | collective-permute-start | bytes 1572872 | tf_op jit(solution)/shard_map/ppermute | solution.py:192
  695.5 64.9 %collective-permute-start.62 = (bf16[512,2048]{1,0:T(8,128)(2,1)S(1)}, bf16[512,2048]{1,0:T(8,128)(2,1)S(1)}, u32[]{:S(2)}, u32[]{:S(2)}) collective-permute-start(bf16[512,2048]{1,0:T(8,128)(2,1)S(1)} %copy-done.136), channel_id=1, source_target_pairs={{0,8},{8,0},{1,9},{9,1},{2,10},{10,2},{3,11},{11,3},{4,12},{12,4},... | collective-permute-start | bytes 6291464 | tf_op jit(solution)/shard_map/ppermute | solution.py:192
  695.5 14.8 %collective-permute-start.75 = (bf16[4,2,32,1024]{3,2,0,1:T(8,128)(2,1)S(1)}, bf16[4,2,32,1024]{3,2,0,1:T(8,128)(2,1)S(1)}, u32[]{:S(2)}, u32[]{:S(2)}) collective-permute-start(bf16[4,2,32,1024]{3,2,0,1:T(8,128)(2,1)S(1)} %fusion.129), channel_id=1, source_target_pairs={{0,16},{16,0},{1,17},{17,1},{2,18},{18,2},{3,19},{19,3},{4,20},{20... | collective-permute-start | bytes 1572872 | tf_op jit(solution)/shard_map/ppermute | solution.py:192
  697.1 14.9 %collective-permute-start.51 = (bf16[2,4,32,1024]{3,2,1,0:T(8,128)(2,1)S(1)}, bf16[2,4,32,1024]{3,2,1,0:T(8,128)(2,1)S(1)}, u32[]{:S(2)}, u32[]{:S(2)}) collective-permute-start(bf16[2,4,32,1024]{3,2,1,0:T(8,128)(2,1)S(1)} %fusion.130), channel_id=1, source_target_pairs={{0,1},{1,0},{2,3},{3,2},{4,5},{5,4},{6,7},{7,6},{8,9},{9,8},{10,11... | collective-permute-start | bytes 1572872 | tf_op jit(solution)/shard_map/ppermute | solution.py:192
  699.0 22.6 %collective-permute-start.45 = (bf16[4,2,32,1024]{3,2,0,1:T(8,128)(2,1)S(1)}, bf16[4,2,32,1024]{3,2,0,1:T(8,128)(2,1)S(1)}, u32[]{:S(2)}, u32[]{:S(2)}) collective-permute-start(bf16[4,2,32,1024]{3,2,0,1:T(8,128)(2,1)S(1)} %fusion.128), channel_id=1, source_target_pairs={{0,16},{16,0},{1,17},{17,1},{2,18},{18,2},{3,19},{19,3},{4,20},{20... | collective-permute-start | bytes 1572872 | tf_op jit(solution)/shard_map/ppermute | solution.py:192
  710.3 16.9 %collective-permute-start.70 = (bf16[4,32,1024]{2,1,0:T(8,128)(2,1)S(1)}, bf16[4,32,1024]{2,1,0:T(8,128)(2,1)S(1)}, u32[]{:S(2)}, u32[]{:S(2)}) collective-permute-start(bf16[4,32,1024]{2,1,0:T(8,128)(2,1)S(1)} %fusion.175), channel_id=1, source_target_pairs={{0,16},{16,0},{1,17},{17,1},{2,18},{18,2},{3,19},{19,3},{4,20},{20... | collective-permute-start | bytes 786440 | tf_op jit(solution)/shard_map/ppermute | solution.py:192
  712.0 16.6 %collective-permute-start.76 = (bf16[4,32,1024]{2,1,0:T(8,128)(2,1)S(1)}, bf16[4,32,1024]{2,1,0:T(8,128)(2,1)S(1)}, u32[]{:S(2)}, u32[]{:S(2)}) collective-permute-start(bf16[4,32,1024]{2,1,0:T(8,128)(2,1)S(1)} %fusion.176), channel_id=1, source_target_pairs={{0,1},{1,0},{2,3},{3,2},{4,5},{5,4},{6,7},{7,6},{8,9},{9,8},{10,11... | collective-permute-start | bytes 786440 | tf_op jit(solution)/shard_map/ppermute | solution.py:192
  759.2 20.2 %collective-permute-start.57 = (bf16[2,4,32,2048]{3,2,1,0:T(8,128)(2,1)S(1)}, bf16[2,4,32,2048]{3,2,1,0:T(8,128)(2,1)S(1)}, u32[]{:S(2)}, u32[]{:S(2)}) collective-permute-start(bf16[2,4,32,2048]{3,2,1,0:T(8,128)(2,1)S(1)} %fusion.95), channel_id=1, source_target_pairs={{0,1},{1,0},{2,3},{3,2},{4,5},{5,4},{6,7},{7,6},{8,9},{9,8},{10,11... | collective-permute-start | bytes 3145736 | tf_op jit(solution)/shard_map/ppermute | solution.py:192
  761.9 25.5 %collective-permute-start.63 = (bf16[4,2,32,2048]{3,2,0,1:T(8,128)(2,1)S(1)}, bf16[4,2,32,2048]{3,2,0,1:T(8,128)(2,1)S(1)}, u32[]{:S(2)}, u32[]{:S(2)}) collective-permute-start(bf16[4,2,32,2048]{3,2,0,1:T(8,128)(2,1)S(1)} %fusion.94), channel_id=1, source_target_pairs={{0,16},{16,0},{1,17},{17,1},{2,18},{18,2},{3,19},{19,3},{4,20},{20... | collective-permute-start | bytes 3145736 | tf_op jit(solution)/shard_map/ppermute | solution.py:192
  861.1 26.7 %collective-permute-start.39 = (f32[9032]{0:T(1024)S(1)}, f32[9032]{0:T(1024)S(1)}, u32[]{:S(2)}, u32[]{:S(2)}) collective-permute-start(f32[9032]{0:T(1024)S(1)} %concatenate.195), channel_id=1, source_target_pairs={{0,8},{8,0},{1,9},{9,1},{2,10},{10,2},{3,11},{11,3},{4,12},{12,4},... | collective-permute-start | bytes 108392 | tf_op jit(solution)/shard_map/ppermute | solution.py:273
  870.6 37.3 %collective-permute-start.27 = (bf16[512,1280]{1,0:T(8,128)(2,1)}, bf16[512,1280]{1,0:T(8,128)(2,1)}, u32[]{:S(2)}, u32[]{:S(2)}) collective-permute-start(bf16[512,1280]{1,0:T(8,128)(2,1)} %convolution_convert_fusion.2), channel_id=1, source_target_pairs={{0,8},{8,0},{1,9},{9,1},{2,10},{10,2},{3,11},{11,3},{4,12},{12,4},... | collective-permute-start | bytes 3932168 | tf_op jit(solution)/shard_map/ppermute | solution.py:192
  881.7 34.3 %collective-permute-start.33 = (bf16[512,1304]{0,1:T(8,128)(2,1)}, bf16[512,1304]{0,1:T(8,128)(2,1)}, u32[]{:S(2)}, u32[]{:S(2)}) collective-permute-start(bf16[512,1304]{0,1:T(8,128)(2,1)} %convolution_convert_fusion.3), channel_id=1, source_target_pairs={{0,8},{8,0},{1,9},{9,1},{2,10},{10,2},{3,11},{11,3},{4,12},{12,4},... | collective-permute-start | bytes 4005896 | tf_op jit(solution)/shard_map/ppermute | solution.py:192
  925.7 14.5 %collective-permute-start.29 = (bf16[4,32,1280]{2,1,0:T(8,128)(2,1)S(1)}, bf16[4,32,1280]{2,1,0:T(8,128)(2,1)S(1)}, u32[]{:S(2)}, u32[]{:S(2)}) collective-permute-start(bf16[4,32,1280]{2,1,0:T(8,128)(2,1)S(1)} %fusion.148), channel_id=1, source_target_pairs={{0,16},{16,0},{1,17},{17,1},{2,18},{18,2},{3,19},{19,3},{4,20},{20... | collective-permute-start | bytes 983048 | tf_op jit(solution)/shard_map/ppermute | solution.py:192
  (199 other events, 2469.0 us)
Sparse Core Ops, SparseCore 0:
  12.4 79.8 all-gather.7
  95.1 62.5 all-gather.13
  160.5 59.2 all-gather.17
  222.4 74.5 all-gather.15
  299.5 43.8 all-gather.11
  346.0 58.8 all-gather.9
  499.3 59.3 all-gather.19

commit v2 on v1

v2 whole, which is shorter than its diff:
```python
import math

import jax
import jax.experimental.pallas as pl
import jax.experimental.pallas.tpu as pltpu
import jax.numpy as jnp
from jax import lax
from jax.sharding import Mesh
from jax.sharding import PartitionSpec as P

MHEADS = 24
MHEAD_DIM = 64
STATE = 128
CONV = 4
QHEADS = 8
KVHEADS = 2
HEAD_DIM = 64
FF = 2048


norm_epsilon = 1e-06
rope_base = 100000000000.0
masked_score = -1e30
highest_precision = lax.Precision.HIGHEST
seq_axes = ("z", "x")
every_axis = ("y", "core", "z", "x")


def rms_norm(values, gain_vector):
    return (
        values
        * lax.rsqrt(jnp.mean(values * values, axis=-1, keepdims=True) + norm_epsilon)
        * gain_vector
    )


def outer_product(left, right):
    return lax.dot_general(
        left, right, (((0,), (0,)), ((), ())), preferred_element_type=jnp.float32
    )


def back_product(grad_rows, weight_matrix):
    return lax.dot_general(
        grad_rows, weight_matrix, (((1,), (1,)), ((), ())), preferred_element_type=jnp.float32
    )


def turn_columns(positions):
    half = HEAD_DIM // 2
    exponents = jnp.arange(half).astype(jnp.float32) * (2.0 / HEAD_DIM)
    frequency = rope_base ** (-exponents)
    angles = frequency[:, None] * positions.astype(jnp.float32)[None, :]
    return (jnp.cos(angles), jnp.sin(angles))


def turn_rows(values, cosine, sine):
    half = HEAD_DIM // 2
    heads = values.reshape(-1, 2, half, values.shape[1])
    first, second = heads[:, 0], heads[:, 1]
    turned = [first * cosine - second * sine, second * cosine + first * sine]
    return jnp.stack(turned, axis=1).reshape(values.shape)


def conv_act(extended, conv_weight, conv_bias):
    row_count = extended.shape[0] - (CONV - 1)
    conv_sum = conv_bias[None, :] + conv_weight[0][None, :] * extended[0:row_count]
    for offset in range(1, CONV):
        conv_sum = conv_sum + conv_weight[offset][None, :] * extended[offset : offset + row_count]
    return jax.nn.silu(conv_sum)


log2_e = math.log2(math.e)
compiler_room = pltpu.CompilerParams(vmem_limit_bytes=48 * 1024 * 1024)


def group_rows(rows, head):
    group = head // (QHEADS // KVHEADS)
    own = rows[head * HEAD_DIM : (head + 1) * HEAD_DIM]
    blank = jnp.zeros_like(own)
    return jnp.concatenate([own if g == group else blank for g in range(KVHEADS)], axis=0)


def plain_dot(left, right):
    return jnp.dot(left, right, preferred_element_type=jnp.float32)


def hidden_keys(rows):
    key_at = lax.broadcasted_iota(jnp.int32, (rows, rows), 0)
    query_at = lax.broadcasted_iota(jnp.int32, (rows, rows), 1)
    return key_at > query_at


def slot_of(index, place_ref):
    z, x = lax.shift_right_logical(index, 1), lax.bitwise_and(index, 1)
    return 2 * (place_ref[0] - z) + lax.bitwise_xor(x, place_ref[1])


def attend_kernel(place_ref, query_ref, key_ref, value_ref, out_ref, log_ref, best_ref, sum_ref):
    rows = query_ref.shape[1]
    scale = log2_e / math.sqrt(HEAD_DIM)
    group_size = QHEADS // KVHEADS

    def scores_of(keys, head):
        return plain_dot(keys, group_rows(query_ref, head)) * scale

    def values_of(piece, head):
        group = head // group_size
        return value_ref[piece, group * HEAD_DIM : (group + 1) * HEAD_DIM, :]

    own = key_ref[0]
    for head in range(QHEADS):
        scores = jnp.where(hidden_keys(rows), masked_score, scores_of(own, head))
        best = jnp.max(scores, axis=0, keepdims=True)
        weights = jnp.exp2(scores - best)
        best_ref[head : head + 1, :] = best
        sum_ref[head : head + 1, :] = jnp.sum(weights, axis=0, keepdims=True)
        out_ref[head * HEAD_DIM : (head + 1) * HEAD_DIM, :] = plain_dot(
            values_of(0, head), weights.astype(jnp.bfloat16)
        )

    def piece_step(index, carry):
        piece = slot_of(index, place_ref)
        keys = key_ref[piece]
        for head in range(QHEADS):
            scores = scores_of(keys, head)
            old = best_ref[head : head + 1, :]
            best = jnp.maximum(old, jnp.max(scores, axis=0, keepdims=True))
            fade = jnp.exp2(old - best)
            weights = jnp.exp2(scores - best)
            best_ref[head : head + 1, :] = best
            sum_ref[head : head + 1, :] = sum_ref[head : head + 1, :] * fade + jnp.sum(
                weights, axis=0, keepdims=True
            )
            span = slice(head * HEAD_DIM, (head + 1) * HEAD_DIM)
            out_ref[span, :] = out_ref[span, :] * fade + plain_dot(
                values_of(piece, head), weights.astype(jnp.bfloat16)
            )
        return carry

    lax.fori_loop(0, 2 * place_ref[0] + place_ref[1], piece_step, 0)
    total = sum_ref[...]
    log_ref[...] = best_ref[...] + jnp.log2(total)
    for head in range(QHEADS):
        span = slice(head * HEAD_DIM, (head + 1) * HEAD_DIM)
        out_ref[span, :] = out_ref[span, :] / total[head : head + 1, :]


def in_vmem(count):
    return [pl.BlockSpec(memory_space=pltpu.VMEM)] * count


def attend(place, queries, keys, values):
    rows = queries.shape[1]
    flops = 4 * queries.size * rows * keys.shape[0]
    return pl.pallas_call(
        attend_kernel,
        out_shape=(
            jax.ShapeDtypeStruct(queries.shape, jnp.float32),
            jax.ShapeDtypeStruct((QHEADS, rows), jnp.float32),
        ),
        in_specs=[pl.BlockSpec(memory_space=pltpu.SMEM)] + in_vmem(3),
        out_specs=tuple(in_vmem(2)),
        scratch_shapes=[pltpu.VMEM((QHEADS, rows), jnp.float32)] * 2,
        compiler_params=compiler_room,
        cost_estimate=pl.CostEstimate(
            flops=flops,
            bytes_accessed=2 * (keys.size + values.size),
            transcendentals=flops // 256,
        ),
        name="attend",
    )(place, queries, keys, values)


def attend_back_kernel(
    place_ref,
    query_ref,
    query_rows_ref,
    grad_ref,
    grad_rows_ref,
    out_ref,
    log_ref,
    key_ref,
    key_cols_ref,
    value_ref,
    grad_query_ref,
    grad_key_ref,
    dots_ref,
):
    rows = query_ref.shape[1]
    key_width = KVHEADS * HEAD_DIM
    group_size = QHEADS // KVHEADS
    scale = log2_e / math.sqrt(HEAD_DIM)
    grad_query_ref[...] = jnp.zeros_like(grad_query_ref)
    for head in range(QHEADS):
        span = slice(head * HEAD_DIM, (head + 1) * HEAD_DIM)
        dots_ref[head : head + 1, :] = jnp.sum(
            grad_ref[span, :].astype(jnp.float32) * out_ref[span, :], axis=0, keepdims=True
        )

    def one_piece(piece, own):
        keys = key_ref[piece]
        values = value_ref[piece]
        grad_keys = jnp.zeros((rows, key_width), jnp.float32)
        grad_values = jnp.zeros((rows, key_width), jnp.float32)
        for head in range(QHEADS):
            group = head // group_size
            scores = plain_dot(keys, group_rows(query_ref, head)) * scale
            weights = jnp.exp2(scores - log_ref[head : head + 1, :])
            if own:
                weights = jnp.where(hidden_keys(rows), 0.0, weights)
            grad_weights = plain_dot(values, group_rows(grad_ref, head))
            grad_scores = (weights * (grad_weights - dots_ref[head : head + 1, :])).astype(
                jnp.bfloat16
            )
            span = slice(head * HEAD_DIM, (head + 1) * HEAD_DIM)
            grad_query_ref[span, :] += plain_dot(
                key_cols_ref[piece, group * HEAD_DIM : (group + 1) * HEAD_DIM, :], grad_scores
            )
            grad_keys += plain_dot(grad_scores, query_rows_ref[head])
            grad_values += plain_dot(weights.astype(jnp.bfloat16), grad_rows_ref[head])
        grad_key_ref[piece, :, :key_width] = grad_keys * (1.0 / math.sqrt(HEAD_DIM))
        grad_key_ref[piece, :, key_width:] = grad_values

    def clear(piece, carry):
        grad_key_ref[piece] = jnp.zeros(grad_key_ref.shape[1:], jnp.float32)
        return carry

    def earlier(index, carry):
        one_piece(slot_of(index, place_ref), False)
        return carry

    lax.fori_loop(1, key_ref.shape[0], clear, 0)
    one_piece(0, True)
    lax.fori_loop(0, 2 * place_ref[0] + place_ref[1], earlier, 0)
    grad_query_ref[...] = grad_query_ref[...] * (1.0 / math.sqrt(HEAD_DIM))


def padded_heads(rows):
    group_size = QHEADS // KVHEADS
    heads = []
    for head in range(QHEADS):
        group = head // group_size
        own = rows[:, head * HEAD_DIM : (head + 1) * HEAD_DIM]
        after = (KVHEADS - 1 - group) * HEAD_DIM
        heads.append(jnp.pad(own, ((0, 0), (group * HEAD_DIM, after))))
    return jnp.stack(heads)


def attend_back(place, queries, grads, grad_rows, outs, logs, keys, key_cols, values):
    rows = queries.shape[1]
    flops = 10 * queries.size * rows * keys.shape[0]
    return pl.pallas_call(
        attend_back_kernel,
        out_shape=(
            jax.ShapeDtypeStruct(queries.shape, jnp.float32),
            jax.ShapeDtypeStruct((*keys.shape[:2], 2 * keys.shape[2]), jnp.float32),
        ),
        in_specs=[pl.BlockSpec(memory_space=pltpu.SMEM)] + in_vmem(9),
        out_specs=tuple(in_vmem(2)),
        scratch_shapes=[pltpu.VMEM((QHEADS, rows), jnp.float32)],
        compiler_params=compiler_room,
        cost_estimate=pl.CostEstimate(
            flops=flops,
            bytes_accessed=8 * keys.size,
            transcendentals=flops // 640,
        ),
        name="attend_back",
    )(
        place,
        queries,
        padded_heads(queries.T),
        grads,
        padded_heads(grad_rows),
        outs,
        logs,
        keys,
        key_cols,
        values,
    )


ssd_rows = 128


def two_parts(values):
    high = values.astype(jnp.bfloat16)
    rest = values - high.astype(jnp.float32)
    middle = rest.astype(jnp.bfloat16)
    low = (rest - middle.astype(jnp.float32)).astype(jnp.bfloat16)
    return jnp.concatenate([high, middle, low], axis=1)


def head_columns(heads, parts):
    shape = (heads * parts, heads * MHEAD_DIM)
    head = lax.broadcasted_iota(jnp.int32, shape, 0) % heads
    channel = lax.broadcasted_iota(jnp.int32, shape, 1) // MHEAD_DIM
    return jnp.where(head == channel, 1.0, 0.0).astype(jnp.bfloat16)


def widen(values, spread):
    return plain_dot(two_parts(values), spread)


def head_sums(values, spread):
    heads = spread.shape[0]
    high = values.astype(jnp.bfloat16)
    low = (values - high.astype(jnp.float32)).astype(jnp.bfloat16)
    total = nt_dot(high, spread) + nt_dot(low, spread)
    return total


def nt_dot(left, right):
    return lax.dot_general(
        left, right, (((1,), (1,)), ((), ())), preferred_element_type=jnp.float32
    )


def split_pair(pair, axis):
    lane = lax.broadcasted_iota(jnp.int32, pair.shape, 1)
    blank = jnp.zeros_like(pair)
    return jnp.concatenate(
        [jnp.where(lane < MHEAD_DIM, pair, blank), jnp.where(lane < MHEAD_DIM, blank, pair)],
        axis=axis,
    )


def bf(values):
    return values.astype(jnp.bfloat16)


def ssd_kernel(act_ref, cum_ref, cum_rows_ref, step_ref, spread_ref, y_ref, grown_ref, state_ref, tail_ref):
    chunks, rows, inner = y_ref.shape
    spread = spread_ref[...]
    state_ref[...] = jnp.zeros_like(state_ref)
    tail_ref[...] = jnp.zeros_like(tail_ref)
    late = lax.broadcasted_iota(jnp.int32, (rows, rows), 0) >= lax.broadcasted_iota(
        jnp.int32, (rows, rows), 1
    )

    def one_chunk(chunk, before):
        act = act_ref[chunk]
        cum = cum_ref[chunk]
        cum_rows = cum_rows_ref[chunk]
        scaled = act[:, :inner] * widen(step_ref[chunk], spread)
        input_mat = act[:, inner : inner + STATE]
        output_low = bf(act[:, inner + STATE :])
        last = cum[rows - 1 : rows, :]
        grown_ref[chunk] = widen(jnp.exp(cum + before), spread)
        mixing = nt_dot(output_low, bf(input_mat))
        state = state_ref[...]
        from_state = plain_dot(output_low, bf(state)) * widen(jnp.exp(cum), spread)
        scaled_low = bf(scaled)
        for pair in range(MHEADS // 2):
            kernels = []
            for head in (2 * pair, 2 * pair + 1):
                gap = cum[:, head : head + 1] - cum_rows[head : head + 1, :]
                kernels.append(bf(jnp.exp(jnp.where(late, gap, masked_score)) * mixing))
            span = slice(2 * pair * MHEAD_DIM, (2 * pair + 2) * MHEAD_DIM)
            y_ref[chunk, :, span] = from_state[:, span] + plain_dot(
                jnp.concatenate(kernels, axis=1), split_pair(scaled_low[:, span], 0)
            )
        weighted = scaled * widen(jnp.exp(last - cum), spread)
        fade = widen(jnp.exp(jnp.broadcast_to(last, (8, last.shape[1]))), spread)[:1]
        state_ref[...] = state * fade + plain_dot(bf(input_mat.T), bf(weighted))
        return before + last

    total = lax.fori_loop(0, chunks, one_chunk, jnp.zeros((1, cum_ref.shape[2]), jnp.float32))
    tail_ref[...] = widen(jnp.exp(jnp.broadcast_to(total, (8, total.shape[1]))), spread)


def by_chunks(values):
    return values.reshape(-1, math.gcd(values.shape[0], ssd_rows), values.shape[1])


def ssd_local(act, cum, step_size):
    act, cum, step_size = by_chunks(act), by_chunks(cum), by_chunks(step_size)
    chunks, rows, _ = act.shape
    inner = MHEADS * MHEAD_DIM
    return pl.pallas_call(
        ssd_kernel,
        out_shape=(
            jax.ShapeDtypeStruct((chunks, rows, inner), jnp.float32),
            jax.ShapeDtypeStruct((chunks, rows, inner), jnp.float32),
            jax.ShapeDtypeStruct((STATE, inner), jnp.float32),
            jax.ShapeDtypeStruct((8, inner), jnp.float32),
        ),
        in_specs=in_vmem(5),
        out_specs=tuple(in_vmem(4)),
        compiler_params=compiler_room,
        cost_estimate=pl.CostEstimate(
            flops=chunks * rows * inner * 2000, bytes_accessed=act.size * 16, transcendentals=0
        ),
        name="ssd",
    )(act, cum, jnp.swapaxes(cum, 1, 2), step_size, head_columns(MHEADS, 3))


def ssd_back_kernel(
    act_ref,
    cum_ref,
    cum_rows_ref,
    step_ref,
    grad_ref,
    carry_ref,
    grad_end_ref,
    skip_ref,
    spread_ref,
    grad_act_ref,
    grad_step_ref,
    grad_log_ref,
    grad_skip_ref,
    states_ref,
    grad_state_ref,
    sums_ref,
):
    chunks, rows, _ = act_ref.shape
    inner = grad_ref.shape[2]
    heads = cum_ref.shape[2]
    spread = spread_ref[...]
    one_spread = spread[:heads]
    at_row = lax.broadcasted_iota(jnp.int32, (rows, rows), 0)
    at_column = lax.broadcasted_iota(jnp.int32, (rows, rows), 1)

    def fade_of(last):
        return widen(jnp.exp(jnp.broadcast_to(last, (8, heads))), spread)[:1]

    states_ref[0] = carry_ref[...]
    for chunk in range(chunks - 1):
        cum = cum_ref[chunk]
        last = cum[rows - 1 : rows, :]
        act = act_ref[chunk]
        weighted = act[:, :inner] * widen(jnp.exp(last - cum) * step_ref[chunk], spread)
        states_ref[chunk + 1] = states_ref[chunk] * fade_of(last) + plain_dot(
            bf(act[:, inner : inner + STATE].T), bf(weighted)
        )
    grad_state_ref[...] = grad_end_ref[...]
    grad_skip_ref[...] = jnp.zeros_like(grad_skip_ref)
    sums_ref[...] = jnp.zeros_like(sums_ref)

    def one_chunk(turn, carried):
        chunk = chunks - 1 - turn
        act = act_ref[chunk]
        cum = cum_ref[chunk]
        cum_rows = cum_rows_ref[chunk]
        step = step_ref[chunk]
        grad_y = grad_ref[chunk]
        last = cum[rows - 1 : rows, :]
        inputs_x = act[:, :inner]
        step_wide = widen(step, spread)
        tail = jnp.exp(last - cum)
        tail_wide = widen(tail, spread)
        scaled = inputs_x * step_wide
        scaled_low = bf(scaled)
        grad_low = bf(grad_y)
        input_low = bf(act[:, inner : inner + STATE])
        output_mat = act[:, inner + STATE :]
        output_low = bf(output_mat)
        state = states_ref[chunk]
        state_low = bf(state)
        grad_state = grad_state_ref[...]
        grad_state_low = bf(grad_state)

        grown_grad = grad_y * widen(jnp.exp(cum), spread)
        grown_low = bf(grown_grad)
        from_row = head_sums(grown_grad * plain_dot(output_low, state_low), one_spread)
        grad_output = nt_dot(grown_low, state_low)
        back = plain_dot(input_low, grad_state_low)
        from_column = head_sums(scaled * back, one_spread) * tail
        grad_input = nt_dot(bf(scaled * tail_wide), grad_state_low)
        fade = fade_of(last)
        both = jnp.sum(grad_state * state, axis=0, keepdims=True) * fade
        from_last = head_sums(jnp.broadcast_to(both, (8, inner)), one_spread)[:1]
        grad_state_ref[...] = grad_state * fade + plain_dot(bf(output_mat.T), grown_low)

        mixing = nt_dot(input_low, output_low)
        grad_mixing = jnp.zeros((rows, rows), jnp.float32)
        column_sums = jnp.zeros((rows, rows), jnp.float32)
        grad_step = jnp.zeros((rows, rows), jnp.float32)
        for pair in range(heads // 2):
            span = slice(2 * pair * MHEAD_DIM, (2 * pair + 2) * MHEAD_DIM)
            apart = split_pair(grad_low[:, span], 0)
            grad_kernels = nt_dot(scaled_low[:, span], apart)
            kernels = []
            for side in range(2):
                head = 2 * pair + side
                gap = cum_rows[head : head + 1, :] - cum[:, head : head + 1]
                decay = jnp.exp(jnp.where(at_row <= at_column, gap, masked_score))
                part = grad_kernels[:, side * rows : (side + 1) * rows] * decay
                grad_mixing = grad_mixing + part
                moved = part * mixing
                sums_ref[head : head + 1, :] = jnp.sum(moved, axis=0, keepdims=True)
                column = jnp.sum(moved, axis=1, keepdims=True)
                column_sums = jnp.where(at_column == head, column, column_sums)
                kernels.append(bf(decay * mixing))
            grad_scaled = plain_dot(jnp.concatenate(kernels, axis=1), apart)
            grad_scaled = grad_scaled + back[:, span] * tail_wide[:, span]
            grad_act_ref[chunk, :, span] = (
                grad_scaled * step_wide[:, span] + skip_ref[:, span] * grad_y[:, span]
            )
            by_step = grad_scaled * inputs_x[:, span]
            lane = lax.broadcasted_iota(jnp.int32, by_step.shape, 1)
            for side in range(2):
                mine = jnp.where((lane < MHEAD_DIM) == (side == 0), by_step, 0.0)
                column = jnp.sum(mine, axis=1, keepdims=True)
                grad_step = jnp.where(at_column == 2 * pair + side, column, grad_step)
        grad_mixing_low = bf(grad_mixing)
        grad_act_ref[chunk, :, inner : inner + STATE] = grad_input + plain_dot(
            grad_mixing_low, output_low
        )
        grad_act_ref[chunk, :, inner + STATE :] = grad_output + plain_dot(
            bf(grad_mixing.T), input_low
        )
        grad_step_ref[chunk] = grad_step[:, :heads]
        row_sums = sums_ref[...].T[:, :heads]
        ahead = row_sums - column_sums[:, :heads] + from_row
        from_here = jnp.where(at_row <= at_column, 1.0, 0.0)
        before = jnp.where(at_row > at_column, 1.0, 0.0)
        grad_log_ref[chunk] = (
            jnp.dot(from_here, ahead, precision=highest_precision)
            + jnp.dot(before, from_column, precision=highest_precision)
            + from_last
        )
        grad_skip_ref[...] += jnp.sum(inputs_x * grad_y, axis=0, keepdims=True)
        return carried

    lax.fori_loop(0, chunks, one_chunk, 0)


def ssd_back(act, cum, step_size, grad_y, carry_state, grad_end, skip_row):
    shape = act.shape
    act, cum, step_size, grad_y = (by_chunks(a) for a in (act, cum, step_size, grad_y))
    chunks, rows, width = act.shape
    inner = MHEADS * MHEAD_DIM
    grad_act, grad_step, grad_log, grad_skip = pl.pallas_call(
        ssd_back_kernel,
        out_shape=(
            jax.ShapeDtypeStruct(act.shape, jnp.float32),
            jax.ShapeDtypeStruct(cum.shape, jnp.float32),
            jax.ShapeDtypeStruct(cum.shape, jnp.float32),
            jax.ShapeDtypeStruct((1, inner), jnp.float32),
        ),
        in_specs=in_vmem(9),
        out_specs=tuple(in_vmem(4)),
        scratch_shapes=[
            pltpu.VMEM((chunks, STATE, inner), jnp.float32),
            pltpu.VMEM((STATE, inner), jnp.float32),
            pltpu.VMEM((rows, rows), jnp.float32),
        ],
        compiler_params=compiler_room,
        cost_estimate=pl.CostEstimate(
            flops=chunks * rows * inner * 5000, bytes_accessed=act.size * 16, transcendentals=0
        ),
        name="ssd_back",
    )(
        act,
        cum,
        jnp.swapaxes(cum, 1, 2),
        step_size,
        grad_y,
        carry_state,
        grad_end,
        skip_row,
        head_columns(MHEADS, 3),
    )
    flat = (shape[0], MHEADS)
    return grad_act.reshape(shape), grad_step.reshape(flat), grad_log.reshape(flat), grad_skip


def shifted(block, axis, distance):
    count = lax.axis_size(axis)
    return lax.ppermute(block, axis, [(i, (i + distance) % count) for i in range(count)])


def moved_along(block, axis, distance):
    count = lax.axis_size(axis)
    route = [(i, i + distance) for i in range(count) if 0 <= i + distance < count]
    return lax.ppermute(block, axis, route)


def width_order(width):
    sizes = {axis: lax.axis_size(axis) for axis in every_axis}
    rows = width // math.prod(sizes.values())
    rest = lax.broadcasted_iota(jnp.int32, (width, width), 1)
    inside, rest = rest % rows, rest // rows
    owner = {}
    for axis in ("z", "x", "y", "core"):
        owner[axis] = (rest % sizes[axis] + lax.axis_index(axis)) % sizes[axis]
        rest = rest // sizes[axis]
    usual = owner["y"]
    for axis in ("core", "z", "x"):
        usual = usual * sizes[axis] + owner[axis]
    usual = usual * rows + inside
    return (lax.broadcasted_iota(jnp.int32, (width, width), 0) == usual).astype(jnp.bfloat16)


def gather_stages(shard, first, after=None):
    if after is not None:
        shard, _ = lax.optimization_barrier((shard, after))
    parts = [shard] + [shifted(shard, "z", -k) for k in range(1, lax.axis_size("z"))]
    started = parts[-1]
    block = jnp.concatenate(parts, axis=0)[None, None]
    for axis in (first, "xy".replace(first, "")):
        parts = [block] + [shifted(block, axis, -k) for k in range(1, lax.axis_size(axis))]
        block = jnp.concatenate(parts, axis="yx".index(axis))
    own = block.reshape(-1, shard.shape[1])
    return (own, shifted(own, "core", 1)), started


def times_rows(values, pair):
    half = values.shape[1] // 2
    return plain_dot(values[:, :half], pair[0]) + plain_dot(values[:, half:], pair[1])


def times_rows_back(values, pair):
    return jnp.concatenate([back_product(values, pair[0]), back_product(values, pair[1])], axis=1)


def keep_own(total, axis, dim):
    kept = lax.index_in_dim(total, 0, dim, False)
    for step in range(1, lax.axis_size(axis)):
        part = lax.index_in_dim(total, step, dim, False)
        kept = kept + shifted(part.astype(jnp.bfloat16), axis, step).astype(jnp.float32)
    return kept


def scatter_product(left, right, first):
    half = left.shape[1] // 2
    sizes = [lax.axis_size(axis) for axis in ("y", "x", "z")]
    sent = outer_product(left[:, half:], right).astype(jnp.bfloat16)
    received = shifted(sent, "core", 1)
    total = outer_product(left[:, :half], right) + received.astype(jnp.float32)
    total = total.reshape(*sizes, -1, right.shape[1])
    for axis, dim in ((("x", 1), ("y", 0)) if first == "x" else (("y", 0), ("x", 0))):
        total = keep_own(total, axis, dim)
    return keep_own(total, "z", 0)


def sum_everywhere(values):
    for axis in ("core", "x", "y", "z"):
        count = lax.axis_size(axis)
        step = 1
        while step < count:
            values = values + lax.ppermute(values, axis, [(i, i ^ step) for i in range(count)])
            step *= 2
    return values


def carried(state, tail, direction):
    depth, width = state.shape
    half = width // 2
    at_x = lax.axis_index("x")
    is_second = (at_x == 1) if direction == 1 else (at_x == 0)
    packed = jnp.concatenate([state, tail], axis=0).astype(jnp.bfloat16)
    other = shifted(packed, "x", 1).astype(jnp.float32)
    own = packed.astype(jnp.float32)
    first = jnp.where(is_second, other, own)
    second = jnp.where(is_second, own, other)
    first_state, first_tail = first[:depth], first[depth : depth + 1]
    second_tail = second[depth : depth + 1]
    pair = jnp.concatenate(
        [second_tail * first_state + second[:depth], first[depth:] * second[depth:]], axis=0
    )
    mine = jnp.where(at_x == 0, pair[:, :half], pair[:, half:]).astype(jnp.bfloat16)
    total = jnp.zeros((depth, half), jnp.float32)
    fade = jnp.ones((1, half), jnp.float32)
    for step in range(1, lax.axis_size("z")):
        got = moved_along(mine, "z", direction * step).astype(jnp.float32)
        total = total + fade * got[:depth]
        fade = fade * got[depth : depth + 1]
    total = total.astype(jnp.bfloat16)
    rest = shifted(total, "x", 1)
    left, right = jnp.where(at_x == 0, total, rest), jnp.where(at_x == 0, rest, total)
    carry = jnp.concatenate([left, right], axis=1).astype(jnp.float32)
    return jnp.where(is_second, first_tail * carry + first_state, carry)


def gather_keys(own):
    slots = []
    for step in range(lax.axis_size("z")):
        block = moved_along(own, "z", step) if step else own
        slots += [block, shifted(block, "x", 1)]
    return jnp.stack(slots)


def sum_key_grads(slots):
    total = slots.reshape(-1, 2, *slots.shape[1:])
    swapped = shifted(total[:, 1].astype(jnp.bfloat16), "x", 1)
    kept = total[:, 0] + swapped.astype(jnp.float32)
    own = kept[0]
    for step in range(1, kept.shape[0]):
        own = own + moved_along(kept[step].astype(jnp.bfloat16), "z", -step).astype(jnp.float32)
    return own


def on_device(
    tokens,
    gain_one,
    w_in,
    w_step,
    conv_weight,
    conv_bias,
    mamba_heads,
    skip_weight,
    w_query,
    w_keyval,
    w_attn_out,
    w_mix_out,
    gain_two,
    w_gate_up,
    w_down,
    cotangent,
):
    width = tokens.shape[2]
    row_count = tokens.shape[1]
    inner_width = MHEADS * MHEAD_DIM
    device_count = math.prod(lax.axis_size(axis) for axis in every_axis)
    channels = conv_weight.shape[1] * device_count
    key_width = KVHEADS * HEAD_DIM
    query_width = QHEADS * HEAD_DIM
    own_rows = gain_one.shape[0]
    at_z, at_x = lax.axis_index("z"), lax.axis_index("x")
    place = jnp.stack([at_z, at_x]).astype(jnp.int32)

    taps = jnp.concatenate([conv_weight, conv_bias[None]], axis=0)
    tap_columns = -(-taps.size // own_rows)
    tap_shard = jnp.pad(taps.reshape(-1), (0, tap_columns * own_rows - taps.size))
    step_at = channels + w_keyval.shape[1]
    gain_at = step_at + w_step.shape[1]
    tap_at = gain_at + 2
    conv_shard = jnp.concatenate(
        [
            w_in[:, inner_width:],
            w_keyval,
            w_step,
            gain_one[:, None],
            gain_two[:, None],
            tap_shard.reshape(tap_columns, own_rows).T,
            jnp.zeros((own_rows, -(tap_at + tap_columns) % 128), jnp.bfloat16),
        ],
        axis=1,
    )
    gate_shard = jnp.concatenate([w_in[:, :inner_width], w_query], axis=1)
    out_shard = jnp.concatenate([w_mix_out.T, w_attn_out.T], axis=1)
    out_half = out_shard.shape[1] // 2
    down_shard = w_down.T
    down_half = down_shard.shape[1] // 2
    conv_pair, conv_started = gather_stages(conv_shard, "x")
    gate_pair, gate_started = gather_stages(gate_shard, "y")
    started = (conv_started, gate_started)
    out_pair_a, out_started = gather_stages(out_shard[:, :out_half], "x", started)
    out_pair_b, out_started_b = gather_stages(out_shard[:, out_half:], "y", started)
    started = (out_started, out_started_b)
    ff_pair_a, ff_started = gather_stages(w_gate_up[:, :FF], "x", started)
    ff_pair_b, ff_started_b = gather_stages(w_gate_up[:, FF:], "y", started)
    started = (ff_started, ff_started_b)
    down_pair_a, _ = gather_stages(down_shard[:, :down_half], "x", started)
    down_pair_b, _ = gather_stages(down_shard[:, down_half:], "y", started)

    order = width_order(width)
    inputs = plain_dot(tokens[0], order)
    grad_output = plain_dot(cotangent[0], order).astype(jnp.bfloat16)
    small = jnp.concatenate([half[:, gain_at : tap_at + tap_columns] for half in conv_pair], axis=0)
    gain_one_float = small[:, 0].astype(jnp.float32)
    gain_two_float = small[:, 1].astype(jnp.float32)
    tap_all = plain_dot(order, small[:, 2:]).reshape(device_count, own_rows, tap_columns)
    tap_all = jnp.swapaxes(tap_all, 1, 2).reshape(device_count, -1)[:, : taps.size]
    tap_all = jnp.swapaxes(tap_all.reshape(-1, *taps.shape), 0, 1).reshape(taps.shape[0], channels)

    normed = rms_norm(inputs, gain_one_float).astype(jnp.bfloat16)
    conv_projected = times_rows(normed, conv_pair)
    conv_input = conv_projected[:, :channels].astype(jnp.bfloat16)
    keyval_raw = conv_projected[:, channels:step_at]
    step_raw = conv_projected[:, step_at:gain_at]
    positions = (at_z * lax.axis_size("x") + at_x) * row_count + jnp.arange(
        row_count, dtype=jnp.int32
    )
    cosine, sine = turn_columns(positions)
    own_keys = turn_rows(keyval_raw[:, :key_width].T, cosine, sine).T
    own_keyval = jnp.concatenate([own_keys, keyval_raw[:, key_width:]], axis=1).astype(jnp.bfloat16)
    all_keyval = gather_keys(own_keyval)
    border = lax.ppermute(
        conv_input[row_count - (CONV - 1) :],
        seq_axes,
        [(i, i + 1) for i in range(lax.axis_size(seq_axes) - 1)],
    )
    extended = jnp.concatenate([border, conv_input], axis=0).astype(jnp.float32)
    act, pull_conv = jax.vjp(conv_act, extended, tap_all[:CONV], tap_all[CONV])
    step_size = jax.nn.softplus(step_raw + mamba_heads[1][None, :])
    log_decay = -jnp.exp(mamba_heads[0])[None, :] * step_size
    by_chunk = by_chunks(log_decay)
    chunk_rows = by_chunk.shape[1]
    lower = jnp.tril(jnp.ones((chunk_rows, chunk_rows), jnp.float32))
    cum = jnp.stack([jnp.dot(lower, c, precision=highest_precision) for c in by_chunk])
    cum = cum.reshape(log_decay.shape)
    y_local, grown, fresh_state, tail = ssd_local(act, cum, step_size)
    y_local = y_local.reshape(row_count, inner_width)
    grown = grown.reshape(row_count, inner_width)
    carry_state = carried(fresh_state, tail, 1)

    gate_projected = times_rows(normed, gate_pair)
    gate_z = gate_projected[:, :inner_width]
    query_cols = turn_rows(gate_projected[:, inner_width:].T, cosine, sine).astype(jnp.bfloat16)
    all_keys = all_keyval[:, :, :key_width]
    all_values = all_keyval[:, :, key_width:]
    attended_cols, logs = attend(place, query_cols, all_keys, jnp.swapaxes(all_values, 1, 2))
    attention_rows = attended_cols.T.astype(jnp.bfloat16)

    skip_row = jnp.repeat(skip_weight, MHEAD_DIM)[None, :]
    output_low = act[:, inner_width + STATE :].astype(jnp.bfloat16)
    ssm_y = (
        y_local
        + grown * plain_dot(output_low, carry_state.astype(jnp.bfloat16))
        + skip_row * act[:, :inner_width]
    )
    gate_sigmoid = jax.nn.sigmoid(gate_z)
    mixer = (ssm_y * gate_z * gate_sigmoid).astype(jnp.bfloat16)
    branches = jnp.concatenate([mixer, attention_rows], axis=1)
    branches_a, branches_b = branches[:, :out_half], branches[:, out_half:]
    hidden = (
        inputs + times_rows_back(branches_a, out_pair_a) + times_rows_back(branches_b, out_pair_b)
    )
    normed_two = rms_norm(hidden, gain_two_float).astype(jnp.bfloat16)
    gate_part = times_rows(normed_two, ff_pair_a)
    up_part = times_rows(normed_two, ff_pair_b)
    activated = (jax.nn.silu(gate_part) * up_part).astype(jnp.bfloat16)
    active_a, active_b = activated[:, :down_half], activated[:, down_half:]
    result = (
        hidden + times_rows_back(active_a, down_pair_a) + times_rows_back(active_b, down_pair_b)
    )
    output = back_product(result.astype(jnp.bfloat16), order).astype(jnp.bfloat16)[None]

    grad_activated = jnp.concatenate(
        [times_rows(grad_output, down_pair_a), times_rows(grad_output, down_pair_b)], axis=1
    )
    grad_down_a = scatter_product(grad_output, active_a, "x")
    grad_down_b = scatter_product(grad_output, active_b, "y")
    ff_sigmoid = jax.nn.sigmoid(gate_part)
    grad_gate = grad_activated * up_part * ff_sigmoid * (1.0 + gate_part * (1.0 - ff_sigmoid))
    grad_gate = grad_gate.astype(jnp.bfloat16)
    grad_up = (grad_activated * gate_part * ff_sigmoid).astype(jnp.bfloat16)
    grad_ff_a = scatter_product(normed_two, grad_gate, "x")
    grad_ff_b = scatter_product(normed_two, grad_up, "y")
    grad_normed_two = times_rows_back(grad_gate, ff_pair_a) + times_rows_back(grad_up, ff_pair_b)
    _, pull_two = jax.vjp(rms_norm, hidden, gain_two_float)
    grad_hidden_norm, grad_gain_two = pull_two(grad_normed_two)
    grad_hidden = grad_output.astype(jnp.float32) + grad_hidden_norm
    grad_branch = grad_hidden.astype(jnp.bfloat16)
    grad_branches = jnp.concatenate(
        [times_rows(grad_branch, out_pair_a), times_rows(grad_branch, out_pair_b)], axis=1
    )
    grad_out_a = scatter_product(grad_branch, branches_a, "x")
    grad_out_b = scatter_product(grad_branch, branches_b, "y")
    grad_mixer = grad_branches[:, :inner_width]
    grad_y = grad_mixer * gate_z * gate_sigmoid
    grad_gate_z = grad_mixer * ssm_y * gate_sigmoid * (1.0 + gate_z * (1.0 - gate_sigmoid))
    from_output = outer_product(output_low, (grown * grad_y).astype(jnp.bfloat16))
    grad_end = carried(from_output, tail, -1)

    grad_attention = grad_branches[:, inner_width:].astype(jnp.bfloat16)
    grad_query_cols, grad_slots = attend_back(
        place,
        query_cols,
        grad_attention.T,
        grad_attention,
        attended_cols,
        logs,
        all_keys,
        jnp.swapaxes(all_keys, 1, 2),
        all_values,
    )
    own_grads = sum_key_grads(grad_slots)
    grad_query = turn_rows(grad_query_cols, cosine, -sine).T.astype(jnp.bfloat16)
    grad_keys = turn_rows(own_grads[:, :key_width].T, cosine, -sine).T
    grad_keyval = jnp.concatenate([grad_keys, own_grads[:, key_width:]], axis=1).astype(
        jnp.bfloat16
    )

    grad_act, grad_step_size, grad_log, grad_skip = ssd_back(
        act, cum, step_size, grad_y, carry_state, grad_end, skip_row
    )
    grad_step_size = grad_step_size - grad_log * jnp.exp(mamba_heads[0])[None, :]
    grad_step_raw = grad_step_size * jax.nn.sigmoid(step_raw + mamba_heads[1][None, :])
    grad_heads = jnp.stack([jnp.sum(grad_log * log_decay, axis=0), jnp.sum(grad_step_raw, axis=0)])
    grad_extended, grad_conv_weight, grad_conv_bias = pull_conv(grad_act)
    rim_back = lax.ppermute(
        grad_extended[: CONV - 1],
        seq_axes,
        [(i + 1, i) for i in range(lax.axis_size(seq_axes) - 1)],
    )
    grad_conv_input = grad_extended[CONV - 1 :] + jnp.pad(
        rim_back, ((row_count - (CONV - 1), 0), (0, 0))
    )
    grad_gate_half = jnp.concatenate([grad_gate_z.astype(jnp.bfloat16), grad_query], axis=1)
    grad_conv_half = jnp.concatenate(
        [
            grad_conv_input.astype(jnp.bfloat16),
            grad_keyval,
            grad_step_raw.astype(jnp.bfloat16),
            jnp.zeros((row_count, conv_shard.shape[1] - gain_at), jnp.bfloat16),
        ],
        axis=1,
    )
    grad_in_gate = scatter_product(normed, grad_gate_half, "y")
    grad_in_conv = scatter_product(normed, grad_conv_half, "x")
    grad_normed = times_rows_back(grad_gate_half, gate_pair) + times_rows_back(
        grad_conv_half, conv_pair
    )
    _, pull_one = jax.vjp(rms_norm, inputs, gain_one_float)
    grad_input_norm, grad_gain_one = pull_one(grad_normed)
    input_grad = lax.dot_general(
        grad_hidden + grad_input_norm,
        order.astype(jnp.float32),
        (((1,), (1,)), ((), ())),
        precision=lax.Precision.HIGH,
        preferred_element_type=jnp.float32,
    )[None]

    def usual_gain(grad):
        rows = jnp.broadcast_to(grad[None], (8, width))
        return lax.dot_general(
            rows,
            order.astype(jnp.float32),
            (((1,), (1,)), ((), ())),
            precision=highest_precision,
        )[:1]

    def padded(row):
        return jnp.pad(row, ((0, 0), (0, channels - row.shape[1])))

    head_row = jnp.concatenate(
        [grad_heads[:1], grad_heads[1:], jnp.sum(grad_skip.reshape(MHEADS, -1), axis=1)[None]],
        axis=1,
    )
    summed = sum_everywhere(
        jnp.concatenate(
            [
                grad_conv_weight,
                grad_conv_bias[None],
                padded(usual_gain(grad_gain_two)),
                padded(head_row),
            ],
            axis=0,
        )
    )
    summed_gain = sum_everywhere(usual_gain(grad_gain_one))
    device = lax.axis_index(every_axis)
    own_channels = conv_weight.shape[1]
    own_taps = lax.dynamic_slice_in_dim(summed[: CONV + 1], device * own_channels, own_channels, 1)
    own_gain_two = lax.dynamic_slice_in_dim(summed[CONV + 1], device * own_rows, own_rows)
    own_gain_one = lax.dynamic_slice_in_dim(summed_gain[0], device * own_rows, own_rows)
    head_sums_row = summed[CONV + 2]
    return (
        output,
        input_grad,
        own_gain_one,
        jnp.concatenate([grad_in_gate[:, :inner_width], grad_in_conv[:, :channels]], axis=1),
        grad_in_conv[:, step_at:gain_at],
        own_taps[:CONV],
        own_taps[CONV],
        head_sums_row[: 2 * MHEADS].reshape(2, MHEADS),
        head_sums_row[2 * MHEADS : 3 * MHEADS],
        grad_in_gate[:, inner_width:],
        grad_in_conv[:, channels:step_at],
        jnp.concatenate([grad_out_a, grad_out_b], axis=1)[:, inner_width:].T,
        jnp.concatenate([grad_out_a, grad_out_b], axis=1)[:, :inner_width].T,
        own_gain_two,
        jnp.concatenate([grad_ff_a, grad_ff_b], axis=1),
        jnp.concatenate([grad_down_a, grad_down_b], axis=1).T,
    )


def solution(mesh):
    dp, seq = mesh.shape["dp"], mesh.shape["seq"]
    by_axis = Mesh(mesh.devices.reshape(dp // 2, 2, seq // 2, 2), every_axis)
    pieces = P(("y", "core"), seq_axes, None)
    rows = P(every_axis, None)
    columns = P(None, every_axis)
    vector = P(every_axis)
    weights = (rows, rows, columns, columns, vector, rows, columns)
    return jax.shard_map(
        on_device,
        mesh=by_axis,
        in_specs=(pieces, vector, rows, rows, columns, vector, P(), P(), *weights, pieces),
        out_specs=(pieces, pieces, vector, rows, rows, columns, vector, P(), P(), *weights),
        check_vma=False,
    )
```

time: 973 us -> 793 us (0.82)
  waiting for transfers between devices: 414 us -> 292 us
  matrix products: 197 us -> 133 us
  Pallas kernels: 0 us -> 31.4 us
  other arithmetic: 104 us -> 75.4 us
  local copies, waits for them, and re-layouts: 70.6 us -> 91 us
  between operations: 17.3 us -> 4.8 us
    all_gather x7 -> x0, waiting for transfers between devices: 290 us -> none  [the longest x4 213 us: gather_rows(): own = lax.all_gather(shard, chip_axes, axis=0, tiled=True)]
    ppermute x68 -> x105, waiting for transfers between devices: 109 us -> 215 us  [shifted(): lax.ppermute(block, axis, [(i, (i + distance) % count) for i in range(cou...]
    dot_general x27 -> x26, matrix products: 141 us -> 59.6 us  [the longest x20 45.7 us: plain_dot(): return jnp.dot(left, right, preferred_element_type=jnp.float32)]
    ppermute x2 -> x14, waiting for transfers between devices: 4.19 us -> 70.3 us  [the longest x12 70.3 us: moved_along(): return lax.ppermute(block, axis, route)]
    pallas_call x0 -> x4, Pallas kernels: none -> 31.4 us  [the longest x1 14.2 us: ssd_back(): pl.pallas_call(ssd_back_kernel, out_shape=(jax.ShapeDtypeStruct(act.shape...]
    dot_general x8 -> x17, matrix products: 19.9 us -> 40.1 us  [back_product(): lax.dot_general(grad_rows, weight_matrix, (((1,), (1,)), ((), ())), prefe...]
    ppermute x2 -> x14, starting transfers between devices: 5.45 us -> 24.7 us  [the longest x12 18.9 us: moved_along(): return lax.ppermute(block, axis, route)]
    unnamed x293 -> x380, local copies, waits for them, and re-layouts: 15.4 us -> 34.2 us
  transfers between devices with their start and end apart: 87 -> 129, of which waited for: 45 -> 55; matrix products, arithmetic and copies ran while one was open for 28% -> 31% of each run, Pallas kernels for 0% -> 4%
where the time goes in v2:
time: 793 us; the launch traced here: 785 us
  waiting for transfers between devices  292 us (37%)
  starting transfers between devices  158 us (20%)
  matrix products  133 us (17%)
  local copies, waits for them, and re-layouts  91 us (11%)
  other arithmetic  75.4 us (10%)
  Pallas kernels  31.4 us (4%)
    ppermute x105, waiting for transfers between devices, shifted(): lax.ppermute(block, axis, [(i, (i + distance) % count) for i in range(cou...  215 us
    ppermute x105, starting transfers between devices, shifted(): lax.ppermute(block, axis, [(i, (i + distance) % count) for i in range(cou...  124 us
    ppermute x12, waiting for transfers between devices, moved_along(): return lax.ppermute(block, axis, route)  70.3 us
    dot_general x20, matrix products, plain_dot(): return jnp.dot(left, right, preferred_element_type=jnp.float32)  45.7 us
    dot_general x17, matrix products, back_product(): lax.dot_general(grad_rows, weight_matrix, (((1,), (1,)), ((), ())), prefe...  40.1 us
    unnamed x380, local copies, waits for them, and re-layouts  34.2 us
    dot_general x17, matrix products, outer_product(): lax.dot_general(left, right, (((0,), (0,)), ((), ())), preferred_element_...  33.1 us
    ppermute x12, starting transfers between devices, moved_along(): return lax.ppermute(block, axis, route)  18.9 us
  transfers between devices with their start and end apart: 129, of which 55 were waited for; matrix products, arithmetic and copies ran while one was open for 31% of the time, Pallas kernels for 4%

profile of v2, /device:TPU:0, one launch (start us, length us, event | category | flops | bytes accessed | tf_op | source)
XLA Modules:
  0.0 785.4 jit_solution(4666190838329548150)
XLA Ops:
  47.3 4.7 collective-permute-done.32
  54.8 8.7 %collective-permute-start.44 = (bf16[32,2048]{1,0:T(8,128)(2,1)S(1)}, bf16[32,2048]{1,0:T(8,128)(2,1)S(1)}, u32[]{:S(2)}, u32[]{:S(2)}) collective-permute-start(bf16[32,2048]{1,0:T(8,128)(2,1)S(1)} %get-tuple-element.42), channel_id=1, source_target_pairs={{0,4},{2,6},{4,0},{6,2},{1,5},{3,7},{5,1},{7,3},{8,12},{10,14},{12... | collective-permute-start | bytes 393224 | tf_op jit(solution)/shard_map/ppermute | solution.py:571
  65.7 4.9 collective-permute-done.44
  89.7 8.0 %collective-permute-done.3 = bf16[1,1,128,2176]{3,2,1,0:T(8,128)(2,1)S(1)} collective-permute-done((bf16[1,1,128,2176]{3,2,1,0:T(8,128)(2,1)S(1)}, bf16[1,1,128,2176]{3,2,1,0:T(8,128)(2,1)S(1)}, u32[]{:S(2)}, u32[]{:S(2)}) %collective-permute-start.3) | collective-permute-done | bytes 557088 | tf_op jit(solution)/shard_map/ppermute | solution.py:571
  99.7 12.2 %collective-permute-done.52 = bf16[1,1,128,1024]{3,2,1,0:T(8,128)(2,1)S(1)} collective-permute-done((bf16[1,1,128,1024]{3,2,1,0:T(8,128)(2,1)S(1)}, bf16[1,1,128,1024]{3,2,1,0:T(8,128)(2,1)S(1)}, u32[]{:S(2)}, u32[]{:S(2)}) %collective-permute-start.52) | collective-permute-done | bytes 262176 | tf_op jit(solution)/shard_map/ppermute | solution.py:571
  120.6 7.7 collective-permute-done.35
  130.0 20.6 %collective-permute-done.53 = bf16[1,2,128,1024]{3,2,1,0:T(8,128)(2,1)S(1)} collective-permute-done((bf16[1,2,128,1024]{3,2,1,0:T(8,128)(2,1)S(1)}, bf16[1,2,128,1024]{3,2,1,0:T(8,128)(2,1)S(1)}, u32[]{:S(2)}, u32[]{:S(2)}) %collective-permute-start.53) | collective-permute-done | bytes 524320 | tf_op jit(solution)/shard_map/ppermute | solution.py:571
  155.0 7.0 collective-permute-done.59
  173.3 6.9 collective-permute-done.47
  209.6 4.5 collective-permute-start.6
  238.5 6.3 ssd.1
  254.4 13.1 %collective-permute-done.28 = bf16[384,256]{1,0:T(8,128)(2,1)S(1)} collective-permute-done((bf16[384,256]{1,0:T(8,128)(2,1)S(1)}, bf16[384,256]{1,0:T(8,128)(2,1)S(1)}, u32[]{:S(2)}, u32[]{:S(2)}) %collective-permute-start.28) | collective-permute-done | bytes 196640 | tf_op jit(solution)/shard_map/ppermute | solution.py:571
  301.4 4.4 multiply_convert_fusion.4
  399.3 7.3 attend_back.1
  408.6 4.0 collective-permute-start.67
  432.1 21.6 %collective-permute-done.62 = bf16[136,768]{1,0:T(8,128)(2,1)S(1)} collective-permute-done((bf16[136,768]{1,0:T(8,128)(2,1)S(1)}, bf16[136,768]{1,0:T(8,128)(2,1)S(1)}, u32[]{:S(2)}, u32[]{:S(2)}) %collective-permute-start.62) | collective-permute-done | bytes 208928 | tf_op jit(solution)/shard_map/ppermute | solution.py:577
  453.7 19.7 %collective-permute-done.63 = bf16[136,768]{1,0:T(8,128)(2,1)S(1)} collective-permute-done((bf16[136,768]{1,0:T(8,128)(2,1)S(1)}, bf16[136,768]{1,0:T(8,128)(2,1)S(1)}, u32[]{:S(2)}, u32[]{:S(2)}) %collective-permute-start.63) | collective-permute-done | bytes 208928 | tf_op jit(solution)/shard_map/ppermute | solution.py:577
  473.5 19.4 %collective-permute-done.64 = bf16[136,768]{1,0:T(8,128)(2,1)S(1)} collective-permute-done((bf16[136,768]{1,0:T(8,128)(2,1)S(1)}, bf16[136,768]{1,0:T(8,128)(2,1)S(1)}, u32[]{:S(2)}, u32[]{:S(2)}) %collective-permute-start.64) | collective-permute-done | bytes 208928 | tf_op jit(solution)/shard_map/ppermute | solution.py:577
  499.6 14.2 %ssd_back.1 = (f32[3,128,1792]{2,1,0:T(8,128)}, f32[3,128,24]{2,1,0:T(8,128)S(1)}, f32[3,128,24]{2,1,0:T(8,128)S(1)}, f32[1,1536]{1,0:T(1,128)S(1)}) custom-call(f32[3,128,1792]{2,1,0:T(8,128)} %bitcast.530, f32[3,128,24]{2,1,0:T(8,128)S(1)} %copy-done.13, f32[3,24,128]{2,1,0:T(8,128)S(1)} %copy-done.17, f32[3,128,24]{2,1,0:T(8,128)S(1)} %bitcast.504, ...), custom_call_target="tpu_custom_call" | custom-call | flops 2949120000 | bytes 11010048 | tf_op jit(solution)/shard_map/ssd_back/pallas_call | solution.py:534
  535.2 8.1 %collective-permute-done.70 = bf16[384,256]{1,0:T(8,128)(2,1)S(1)} collective-permute-done((bf16[384,256]{1,0:T(8,128)(2,1)S(1)}, bf16[384,256]{1,0:T(8,128)(2,1)S(1)}, u32[]{:S(2)}, u32[]{:S(2)}) %collective-permute-start.70) | collective-permute-done | bytes 196640 | tf_op jit(solution)/shard_map/ppermute | solution.py:577
  570.4 5.5 fusion.49
  602.1 9.7 %collective-permute-done.118 = bf16[2,4,32,1024]{3,2,1,0:T(8,128)(2,1)} collective-permute-done((bf16[2,4,32,1024]{3,2,1,0:T(8,128)(2,1)}, bf16[2,4,32,1024]{3,2,1,0:T(8,128)(2,1)}, u32[]{:S(2)}, u32[]{:S(2)}) %collective-permute-start.118) | collective-permute-done | bytes 524320 | tf_op jit(solution)/shard_map/ppermute | solution.py:571
  617.1 4.9 collective-permute-done.100
  627.5 4.7 collective-permute-done.119
  644.2 4.3 collective-permute-start.128
  650.4 4.2 collective-permute-start.104
  658.2 4.3 collective-permute-done.96
  680.8 12.8 %collective-permute-done.106 = bf16[2,4,32,2048]{3,2,1,0:T(8,128)(2,1)S(1)} collective-permute-done((bf16[2,4,32,2048]{3,2,1,0:T(8,128)(2,1)S(1)}, bf16[2,4,32,2048]{3,2,1,0:T(8,128)(2,1)S(1)}, u32[]{:S(2)}, u32[]{:S(2)}) %collective-permute-start.106) | collective-permute-done | bytes 1048608 | tf_op jit(solution)/shard_map/ppermute | solution.py:571
  694.5 10.4 %collective-permute-done.112 = bf16[2,4,32,2048]{3,2,1,0:T(8,128)(2,1)S(1)} collective-permute-done((bf16[2,4,32,2048]{3,2,1,0:T(8,128)(2,1)S(1)}, bf16[2,4,32,2048]{3,2,1,0:T(8,128)(2,1)S(1)}, u32[]{:S(2)}, u32[]{:S(2)}) %collective-permute-start.112) | collective-permute-done | bytes 1048608 | tf_op jit(solution)/shard_map/ppermute | solution.py:571
  706.6 20.8 %collective-permute-done.77 = bf16[2,4,32,2048]{3,2,1,0:T(8,128)(2,1)S(1)} collective-permute-done((bf16[2,4,32,2048]{3,2,1,0:T(8,128)(2,1)S(1)}, bf16[2,4,32,2048]{3,2,1,0:T(8,128)(2,1)S(1)}, u32[]{:S(2)}, u32[]{:S(2)}) %collective-permute-start.77) | collective-permute-done | bytes 1048608 | tf_op jit(solution)/shard_map/ppermute | solution.py:571
  746.6 7.0 collective-permute-done.109
  768.8 4.8 collective-permute-done.84
  (927 shorter events, 484.0 us)
Async XLA Ops:
  52.0 36.3 %collective-permute-start.15 = (bf16[1,1,128,2048]{3,2,1,0:T(8,128)(2,1)S(1)}, bf16[1,1,128,2048]{3,2,1,0:T(8,128)(2,1)S(1)}, u32[]{:S(2)}, u32[]{:S(2)}) collective-permute-start(bf16[1,1,128,2048]{3,2,1,0:T(8,128)(2,1)S(1)} %maximum_bitcast_fusion.1), channel_id=1, source_target_pairs={{0,16},{16,0},{1,17},{17,1},{2,18},{18,2},{3,19},{19,3},{4,20},{20... | collective-permute-start | bytes 1572872 | tf_op jit(solution)/shard_map/ppermute | solution.py:571
  84.2 30.4 %collective-permute-start.40 = (bf16[1,1,128,2048]{3,2,1,0:T(8,128)(2,1)S(1)}, bf16[1,1,128,2048]{3,2,1,0:T(8,128)(2,1)S(1)}, u32[]{:S(2)}, u32[]{:S(2)}) collective-permute-start(bf16[1,1,128,2048]{3,2,1,0:T(8,128)(2,1)S(1)} %maximum_bitcast_fusion.2), channel_id=1, source_target_pairs={{0,1},{1,0},{2,3},{3,2},{4,5},{5,4},{6,7},{7,6},{8,9},{9,8},{10,11... | collective-permute-start | bytes 1572872 | tf_op jit(solution)/shard_map/ppermute | solution.py:571
  85.5 31.9 %collective-permute-start.46 = (bf16[1,1,128,2048]{3,2,1,0:T(8,128)(2,1)S(1)}, bf16[1,1,128,2048]{3,2,1,0:T(8,128)(2,1)S(1)}, u32[]{:S(2)}, u32[]{:S(2)}) collective-permute-start(bf16[1,1,128,2048]{3,2,1,0:T(8,128)(2,1)S(1)} %maximum_bitcast_fusion.3), channel_id=1, source_target_pairs={{0,16},{16,0},{1,17},{17,1},{2,18},{18,2},{3,19},{19,3},{4,20},{20... | collective-permute-start | bytes 1572872 | tf_op jit(solution)/shard_map/ppermute | solution.py:571
  111.9 40.1 %collective-permute-start.4 = (bf16[1,2,128,2176]{3,2,1,0:T(8,128)(2,1)S(1)}, bf16[1,2,128,2176]{3,2,1,0:T(8,128)(2,1)S(1)}, u32[]{:S(2)}, u32[]{:S(2)}) collective-permute-start(bf16[1,2,128,2176]{3,2,1,0:T(8,128)(2,1)S(1)} %pad_maximum_fusion.7), channel_id=1, source_target_pairs={{0,16},{16,0},{1,17},{17,1},{2,18},{18,2},{3,19},{19,3},{4,20},{20... | collective-permute-start | bytes 3342344 | tf_op jit(solution)/shard_map/ppermute | solution.py:571
  114.6 48.8 %collective-permute-start.16 = (bf16[2,1,128,2048]{3,2,1,0:T(8,128)(2,1)}, bf16[2,1,128,2048]{3,2,1,0:T(8,128)(2,1)}, u32[]{:S(2)}, u32[]{:S(2)}) collective-permute-start(bf16[2,1,128,2048]{3,2,1,0:T(8,128)(2,1)} %pad_maximum_fusion.8), channel_id=1, source_target_pairs={{0,1},{1,0},{2,3},{3,2},{4,5},{5,4},{6,7},{7,6},{8,9},{9,8},{10,11... | collective-permute-start | bytes 3145736 | tf_op jit(solution)/shard_map/ppermute | solution.py:571
  117.5 33.2 %collective-permute-start.53 = (bf16[1,2,128,1024]{3,2,1,0:T(8,128)(2,1)S(1)}, bf16[1,2,128,1024]{3,2,1,0:T(8,128)(2,1)S(1)}, u32[]{:S(2)}, u32[]{:S(2)}) collective-permute-start(bf16[1,2,128,1024]{3,2,1,0:T(8,128)(2,1)S(1)} %pad_maximum_fusion.20), channel_id=1, source_target_pairs={{0,16},{16,0},{1,17},{17,1},{2,18},{18,2},{3,19},{19,3},{4,20},{20... | collective-permute-start | bytes 1572872 | tf_op jit(solution)/shard_map/ppermute | solution.py:571
  119.2 42.9 %collective-permute-start.59 = (bf16[2,1,128,1024]{3,2,1,0:T(8,128)(2,1)}, bf16[2,1,128,1024]{3,2,1,0:T(8,128)(2,1)}, u32[]{:S(2)}, u32[]{:S(2)}) collective-permute-start(bf16[2,1,128,1024]{3,2,1,0:T(8,128)(2,1)} %pad_maximum_fusion.21), channel_id=1, source_target_pairs={{0,1},{1,0},{2,3},{3,2},{4,5},{5,4},{6,7},{7,6},{8,9},{9,8},{10,11... | collective-permute-start | bytes 1572872 | tf_op jit(solution)/shard_map/ppermute | solution.py:571
  128.3 42.2 %collective-permute-start.41 = (bf16[1,2,128,2048]{3,2,1,0:T(8,128)(2,1)}, bf16[1,2,128,2048]{3,2,1,0:T(8,128)(2,1)}, u32[]{:S(2)}, u32[]{:S(2)}) collective-permute-start(bf16[1,2,128,2048]{3,2,1,0:T(8,128)(2,1)} %pad_maximum_fusion.11), channel_id=1, source_target_pairs={{0,16},{16,0},{1,17},{17,1},{2,18},{18,2},{3,19},{19,3},{4,20},{20... | collective-permute-start | bytes 3145736 | tf_op jit(solution)/shard_map/ppermute | solution.py:571
  150.7 29.6 %collective-permute-start.47 = (bf16[2,1,128,2048]{3,2,1,0:T(8,128)(2,1)}, bf16[2,1,128,2048]{3,2,1,0:T(8,128)(2,1)}, u32[]{:S(2)}, u32[]{:S(2)}) collective-permute-start(bf16[2,1,128,2048]{3,2,1,0:T(8,128)(2,1)} %pad_maximum_fusion.12), channel_id=1, source_target_pairs={{0,1},{1,0},{2,3},{3,2},{4,5},{5,4},{6,7},{7,6},{8,9},{9,8},{10,11... | collective-permute-start | bytes 3145736 | tf_op jit(solution)/shard_map/ppermute | solution.py:571
  152.0 31.1 %collective-permute-start.54 = (bf16[512,1024]{1,0:T(8,128)(2,1)}, bf16[512,1024]{1,0:T(8,128)(2,1)}, u32[]{:S(2)}, u32[]{:S(2)}) collective-permute-start(bf16[512,1024]{1,0:T(8,128)(2,1)} %bitcast.58), channel_id=1, source_target_pairs={{0,8},{8,0},{1,9},{9,1},{2,10},{10,2},{3,11},{11,3},{4,12},{12,4},... | collective-permute-start | bytes 3145736 | tf_op jit(solution)/shard_map/ppermute | solution.py:571
  162.1 28.8 %collective-permute-start.5 = (bf16[512,2176]{0,1:T(8,128)(2,1)}, bf16[512,2176]{0,1:T(8,128)(2,1)S(1)}, u32[]{:S(2)}, u32[]{:S(2)}) collective-permute-start(bf16[512,2176]{0,1:T(8,128)(2,1)} %copy.70), channel_id=1, source_target_pairs={{0,8},{8,0},{1,9},{9,1},{2,10},{10,2},{3,11},{11,3},{4,12},{12,4},... | collective-permute-start | bytes 6684680 | tf_op jit(solution)/shard_map/ppermute | solution.py:571
  170.5 140.1 %collective-permute-start.23 = (bf16[512,1024]{1,0:T(8,128)(2,1)}, bf16[512,1024]{1,0:T(8,128)(2,1)}, u32[]{:S(2)}, u32[]{:S(2)}) collective-permute-start(bf16[512,1024]{1,0:T(8,128)(2,1)} %bitcast.27), channel_id=1, source_target_pairs={{0,8},{8,0},{1,9},{9,1},{2,10},{10,2},{3,11},{11,3},{4,12},{12,4},... | collective-permute-start | bytes 3145736 | tf_op jit(solution)/shard_map/ppermute | solution.py:571
  180.2 132.3 %collective-permute-start.36 = (bf16[512,1024]{1,0:T(8,128)(2,1)}, bf16[512,1024]{1,0:T(8,128)(2,1)}, u32[]{:S(2)}, u32[]{:S(2)}) collective-permute-start(bf16[512,1024]{1,0:T(8,128)(2,1)} %bitcast.50), channel_id=1, source_target_pairs={{0,8},{8,0},{1,9},{9,1},{2,10},{10,2},{3,11},{11,3},{4,12},{12,4},... | collective-permute-start | bytes 3145736 | tf_op jit(solution)/shard_map/ppermute | solution.py:571
  199.6 45.4 %collective-permute-start.24 = (bf16[384,256]{1,0:T(8,128)(2,1)}, bf16[384,256]{1,0:T(8,128)(2,1)}, u32[]{:S(2)}, u32[]{:S(2)}) collective-permute-start(bf16[384,256]{1,0:T(8,128)(2,1)} %pad_maximum_fusion.29), channel_id=1, source_target_pairs={{0,1},{1,0},{2,3},{3,2},{4,5},{5,4},{6,7},{7,6},{8,9},{9,8},{10,11... | collective-permute-start | bytes 589832 | tf_op jit(solution)/shard_map/ppermute | solution.py:571
  199.9 46.4 %collective-permute-start.25 = (bf16[384,256]{1,0:T(8,128)(2,1)}, bf16[384,256]{1,0:T(8,128)(2,1)}, u32[]{:S(2)}, u32[]{:S(2)}) collective-permute-start(bf16[384,256]{1,0:T(8,128)(2,1)} %pad_maximum_fusion.29), channel_id=1, source_target_pairs={{0,2},{2,4},{4,6},{1,3},{3,5},{5,7},{8,10},{10,12},{12,14},{9,11},... | collective-permute-start | bytes 589832 | tf_op jit(solution)/shard_map/ppermute | solution.py:577
  281.1 38.7 %collective-permute-start.42 = (bf16[512,2048]{1,0:T(8,128)(2,1)}, bf16[512,2048]{1,0:T(8,128)(2,1)}, u32[]{:S(2)}, u32[]{:S(2)}) collective-permute-start(bf16[512,2048]{1,0:T(8,128)(2,1)} %bitcast.532), channel_id=1, source_target_pairs={{0,8},{8,0},{1,9},{9,1},{2,10},{10,2},{3,11},{11,3},{4,12},{12,4},... | collective-permute-start | bytes 6291464 | tf_op jit(solution)/shard_map/ppermute | solution.py:571
  282.5 32.6 %collective-permute-start.48 = (bf16[512,2048]{1,0:T(8,128)(2,1)}, bf16[512,2048]{1,0:T(8,128)(2,1)}, u32[]{:S(2)}, u32[]{:S(2)}) collective-permute-start(bf16[512,2048]{1,0:T(8,128)(2,1)} %bitcast.515), channel_id=1, source_target_pairs={{0,8},{8,0},{1,9},{9,1},{2,10},{10,2},{3,11},{11,3},{4,12},{12,4},... | collective-permute-start | bytes 6291464 | tf_op jit(solution)/shard_map/ppermute | solution.py:571
  356.3 228.4 %collective-permute-start.117 = (bf16[512,1024]{1,0:T(8,128)(2,1)}, bf16[512,1024]{1,0:T(8,128)(2,1)}, u32[]{:S(2)}, u32[]{:S(2)}) collective-permute-start(bf16[512,1024]{1,0:T(8,128)(2,1)} %convolution_convert_fusion.6), channel_id=1, source_target_pairs={{0,8},{8,0},{1,9},{9,1},{2,10},{10,2},{3,11},{11,3},{4,12},{12,4},... | collective-permute-start | bytes 3145736 | tf_op jit(solution)/shard_map/ppermute | solution.py:571
  365.9 58.9 %collective-permute-start.61 = (bf16[136,1536]{1,0:T(8,128)(2,1)}, bf16[136,1536]{1,0:T(8,128)(2,1)}, u32[]{:S(2)}, u32[]{:S(2)}) collective-permute-start(bf16[136,1536]{1,0:T(8,128)(2,1)} %pad_maximum_fusion.16), channel_id=1, source_target_pairs={{0,1},{1,0},{2,3},{3,2},{4,5},{5,4},{6,7},{7,6},{8,9},{9,8},{10,11... | collective-permute-start | bytes 1253384 | tf_op jit(solution)/shard_map/ppermute | solution.py:571
  408.6 84.8 %collective-permute-start.67 = (bf16[4,384,256]{2,1,0:T(8,128)(2,1)S(1)}, bf16[4,384,256]{2,1,0:T(8,128)(2,1)S(1)}, u32[]{:S(2)}, u32[]{:S(2)}) collective-permute-start(bf16[4,384,256]{2,1,0:T(8,128)(2,1)S(1)} %fusion.71), channel_id=1, source_target_pairs={{0,1},{1,0},{2,3},{3,2},{4,5},{5,4},{6,7},{7,6},{8,9},{9,8},{10,11... | collective-permute-start | bytes 2359304 | tf_op jit(solution)/shard_map/ppermute | solution.py:571
  427.8 45.6 %collective-permute-start.63 = (bf16[136,768]{1,0:T(8,128)(2,1)S(1)}, bf16[136,768]{1,0:T(8,128)(2,1)S(1)}, u32[]{:S(2)}, u32[]{:S(2)}) collective-permute-start(bf16[136,768]{1,0:T(8,128)(2,1)S(1)} %fusion.116), channel_id=1, source_target_pairs={{4,0},{6,2},{5,1},{7,3},{12,8},{14,10},{13,9},{15,11},{20,16},{22,... | collective-permute-start | bytes 626696 | tf_op jit(solution)/shard_map/ppermute | solution.py:577
  430.8 62.1 %collective-permute-start.64 = (bf16[136,768]{1,0:T(8,128)(2,1)S(1)}, bf16[136,768]{1,0:T(8,128)(2,1)S(1)}, u32[]{:S(2)}, u32[]{:S(2)}) collective-permute-start(bf16[136,768]{1,0:T(8,128)(2,1)S(1)} %fusion.116), channel_id=1, source_target_pairs={{6,0},{7,1},{14,8},{15,9},{22,16},{23,17},{30,24},{31,25}} | collective-permute-start | bytes 626696 | tf_op jit(solution)/shard_map/ppermute | solution.py:577
  453.6 134.6 %collective-permute-start.123 = (bf16[512,1024]{1,0:T(8,128)(2,1)}, bf16[512,1024]{1,0:T(8,128)(2,1)}, u32[]{:S(2)}, u32[]{:S(2)}) collective-permute-start(bf16[512,1024]{1,0:T(8,128)(2,1)} %convolution_convert_fusion.5), channel_id=1, source_target_pairs={{0,8},{8,0},{1,9},{9,1},{2,10},{10,2},{3,11},{11,3},{4,12},{12,4},... | collective-permute-start | bytes 3145736 | tf_op jit(solution)/shard_map/ppermute | solution.py:571
  495.7 36.3 %collective-permute-start.68 = (bf16[384,256]{1,0:T(8,128)(2,1)}, bf16[384,256]{1,0:T(8,128)(2,1)}, u32[]{:S(2)}, u32[]{:S(2)}) collective-permute-start(bf16[384,256]{1,0:T(8,128)(2,1)} %get-tuple-element.152), channel_id=1, source_target_pairs={{2,0},{4,2},{6,4},{3,1},{5,3},{7,5},{10,8},{12,10},{14,12},{11,9},... | collective-permute-start | bytes 589832 | tf_op jit(solution)/shard_map/ppermute | solution.py:577
  497.0 35.6 %collective-permute-start.69 = (bf16[384,256]{1,0:T(8,128)(2,1)}, bf16[384,256]{1,0:T(8,128)(2,1)}, u32[]{:S(2)}, u32[]{:S(2)}) collective-permute-start(bf16[384,256]{1,0:T(8,128)(2,1)} %get-tuple-element.154), channel_id=1, source_target_pairs={{4,0},{6,2},{5,1},{7,3},{12,8},{14,10},{13,9},{15,11},{20,16},{22,... | collective-permute-start | bytes 589832 | tf_op jit(solution)/shard_map/ppermute | solution.py:577
  532.0 135.5 %collective-permute-start.105 = (bf16[512,2048]{1,0:T(8,128)(2,1)}, bf16[512,2048]{1,0:T(8,128)(2,1)}, u32[]{:S(2)}, u32[]{:S(2)}) collective-permute-start(bf16[512,2048]{1,0:T(8,128)(2,1)} %convolution_convert_fusion.2), channel_id=1, source_target_pairs={{0,8},{8,0},{1,9},{9,1},{2,10},{10,2},{3,11},{11,3},{4,12},{12,4},... | collective-permute-start | bytes 6291464 | tf_op jit(solution)/shard_map/ppermute | solution.py:571
  584.7 87.5 %collective-permute-start.111 = (bf16[512,2048]{1,0:T(8,128)(2,1)}, bf16[512,2048]{1,0:T(8,128)(2,1)}, u32[]{:S(2)}, u32[]{:S(2)}) collective-permute-start(bf16[512,2048]{1,0:T(8,128)(2,1)} %convolution_convert_fusion.1), channel_id=1, source_target_pairs={{0,8},{8,0},{1,9},{9,1},{2,10},{10,2},{3,11},{11,3},{4,12},{12,4},... | collective-permute-start | bytes 6291464 | tf_op jit(solution)/shard_map/ppermute | solution.py:571
  664.1 64.9 %collective-permute-start.82 = (bf16[512,2176]{1,0:T(8,128)(2,1)S(1)}, bf16[512,2176]{1,0:T(8,128)(2,1)S(1)}, u32[]{:S(2)}, u32[]{:S(2)}) collective-permute-start(bf16[512,2176]{1,0:T(8,128)(2,1)S(1)} %copy-done.172), channel_id=1, source_target_pairs={{0,8},{8,0},{1,9},{9,1},{2,10},{10,2},{3,11},{11,3},{4,12},{12,4},... | collective-permute-start | bytes 6684680 | tf_op jit(solution)/shard_map/ppermute | solution.py:571
  679.5 47.9 %collective-permute-start.77 = (bf16[2,4,32,2048]{3,2,1,0:T(8,128)(2,1)S(1)}, bf16[2,4,32,2048]{3,2,1,0:T(8,128)(2,1)S(1)}, u32[]{:S(2)}, u32[]{:S(2)}) collective-permute-start(bf16[2,4,32,2048]{3,2,1,0:T(8,128)(2,1)S(1)} %bitcast.543), channel_id=1, source_target_pairs={{0,16},{16,0},{1,17},{17,1},{2,18},{18,2},{3,19},{19,3},{4,20},{20... | collective-permute-start | bytes 3145736 | tf_op jit(solution)/shard_map/ppermute | solution.py:571
  694.1 41.1 %collective-permute-start.107 = (bf16[4,32,2048]{2,1,0:T(8,128)(2,1)S(1)}, bf16[4,32,2048]{2,1,0:T(8,128)(2,1)S(1)}, u32[]{:S(2)}, u32[]{:S(2)}) collective-permute-start(bf16[4,32,2048]{2,1,0:T(8,128)(2,1)S(1)} %fusion.79), channel_id=1, source_target_pairs={{0,16},{16,0},{1,17},{17,1},{2,18},{18,2},{3,19},{19,3},{4,20},{20... | collective-permute-start | bytes 1572872 | tf_op jit(solution)/shard_map/ppermute | solution.py:571
  705.3 33.1 %collective-permute-start.113 = (bf16[4,32,2048]{2,1,0:T(8,128)(2,1)S(1)}, bf16[4,32,2048]{2,1,0:T(8,128)(2,1)S(1)}, u32[]{:S(2)}, u32[]{:S(2)}) collective-permute-start(bf16[4,32,2048]{2,1,0:T(8,128)(2,1)S(1)} %fusion.80), channel_id=1, source_target_pairs={{0,1},{1,0},{2,3},{3,2},{4,5},{5,4},{6,7},{7,6},{8,9},{9,8},{10,11... | collective-permute-start | bytes 1572872 | tf_op jit(solution)/shard_map/ppermute | solution.py:571
  730.4 28.2 %collective-permute-start.83 = (bf16[2,4,32,2176]{3,2,1,0:T(8,128)(2,1)S(1)}, bf16[2,4,32,2176]{3,2,1,0:T(8,128)(2,1)S(1)}, u32[]{:S(2)}, u32[]{:S(2)}) collective-permute-start(bf16[2,4,32,2176]{3,2,1,0:T(8,128)(2,1)S(1)} %fusion.60), channel_id=1, source_target_pairs={{0,1},{1,0},{2,3},{3,2},{4,5},{5,4},{6,7},{7,6},{8,9},{9,8},{10,11... | collective-permute-start | bytes 3342344 | tf_op jit(solution)/shard_map/ppermute | solution.py:571
  (280 other events, 3581.5 us)

commit v3 on v2

--- a/solution.py
+++ b/solution.py
@@ -1,4 +1,5 @@
 import math
+from functools import partial
 
 import jax
 import jax.experimental.pallas as pl
@@ -71,18 +72,17 @@
 
 
 log2_e = math.log2(math.e)
+group_size = QHEADS // KVHEADS
+score_scale = 1.0 / math.sqrt(HEAD_DIM)
 compiler_room = pltpu.CompilerParams(vmem_limit_bytes=48 * 1024 * 1024)
-
-
-def group_rows(rows, head):
-    group = head // (QHEADS // KVHEADS)
-    own = rows[head * HEAD_DIM : (head + 1) * HEAD_DIM]
-    blank = jnp.zeros_like(own)
-    return jnp.concatenate([own if g == group else blank for g in range(KVHEADS)], axis=0)
 
 
 def plain_dot(left, right):
     return jnp.dot(left, right, preferred_element_type=jnp.float32)
+
+
+def head_span(head):
+    return slice(head * HEAD_DIM, (head + 1) * HEAD_DIM)
 
 
 def hidden_keys(rows):
@@ -96,34 +96,31 @@
     return 2 * (place_ref[0] - z) + lax.bitwise_xor(x, place_ref[1])
 
 
-def attend_kernel(place_ref, query_ref, key_ref, value_ref, out_ref, log_ref, best_ref, sum_ref):
+def attend_kernel(place_ref, query_ref, keyval_ref, keyval_cols_ref, out_ref, log_ref, best_ref, sum_ref):
     rows = query_ref.shape[1]
-    scale = log2_e / math.sqrt(HEAD_DIM)
-    group_size = QHEADS // KVHEADS
-
-    def scores_of(keys, head):
-        return plain_dot(keys, group_rows(query_ref, head)) * scale
+    scale = log2_e * score_scale
+
+    def scores_of(piece, head):
+        group = head // group_size
+        keys = keyval_ref[piece, :, 2 * group * HEAD_DIM : 2 * (group + 1) * HEAD_DIM]
+        query = query_ref[head_span(head), :]
+        return plain_dot(keys, jnp.concatenate([query, jnp.zeros_like(query)], axis=0)) * scale
 
     def values_of(piece, head):
-        group = head // group_size
-        return value_ref[piece, group * HEAD_DIM : (group + 1) * HEAD_DIM, :]
-
-    own = key_ref[0]
+        return keyval_cols_ref[piece, head_span(2 * (head // group_size) + 1), :]
+
     for head in range(QHEADS):
-        scores = jnp.where(hidden_keys(rows), masked_score, scores_of(own, head))
+        scores = jnp.where(hidden_keys(rows), masked_score, scores_of(0, head))
         best = jnp.max(scores, axis=0, keepdims=True)
         weights = jnp.exp2(scores - best)
         best_ref[head : head + 1, :] = best
         sum_ref[head : head + 1, :] = jnp.sum(weights, axis=0, keepdims=True)
-        out_ref[head * HEAD_DIM : (head + 1) * HEAD_DIM, :] = plain_dot(
-            values_of(0, head), weights.astype(jnp.bfloat16)
-        )
+        out_ref[head_span(head), :] = plain_dot(values_of(0, head), weights.astype(jnp.bfloat16))
 
     def piece_step(index, carry):
         piece = slot_of(index, place_ref)
-        keys = key_ref[piece]
         for head in range(QHEADS):
-            scores = scores_of(keys, head)
+            scores = scores_of(piece, head)
             old = best_ref[head : head + 1, :]
             best = jnp.maximum(old, jnp.max(scores, axis=0, keepdims=True))
             fade = jnp.exp2(old - best)
@@ -132,8 +129,7 @@
             sum_ref[head : head + 1, :] = sum_ref[head : head + 1, :] * fade + jnp.sum(
                 weights, axis=0, keepdims=True
             )
-            span = slice(head * HEAD_DIM, (head + 1) * HEAD_DIM)
-            out_ref[span, :] = out_ref[span, :] * fade + plain_dot(
+            out_ref[head_span(head), :] = out_ref[head_span(head), :] * fade + plain_dot(
                 values_of(piece, head), weights.astype(jnp.bfloat16)
             )
         return carry
@@ -142,17 +138,16 @@
     total = sum_ref[...]
     log_ref[...] = best_ref[...] + jnp.log2(total)
     for head in range(QHEADS):
-        span = slice(head * HEAD_DIM, (head + 1) * HEAD_DIM)
-        out_ref[span, :] = out_ref[span, :] / total[head : head + 1, :]
+        out_ref[head_span(head), :] = out_ref[head_span(head), :] / total[head : head + 1, :]
 
 
 def in_vmem(count):
     return [pl.BlockSpec(memory_space=pltpu.VMEM)] * count
 
 
-def attend(place, queries, keys, values):
+def attend(place, queries, keyvals, keyval_cols):
     rows = queries.shape[1]
-    flops = 4 * queries.size * rows * keys.shape[0]
+    flops = 4 * queries.size * rows * keyvals.shape[0]
     return pl.pallas_call(
         attend_kernel,
         out_shape=(
@@ -164,15 +159,14 @@
         scratch_shapes=[pltpu.VMEM((QHEADS, rows), jnp.float32)] * 2,
         compiler_params=compiler_room,
         cost_estimate=pl.CostEstimate(
-            flops=flops,
-            bytes_accessed=2 * (keys.size + values.size),
-            transcendentals=flops // 256,
+            flops=8 * flops, bytes_accessed=4 * keyvals.size, transcendentals=flops // 256
         ),
         name="attend",
-    )(place, queries, keys, values)
+    )(place, queries, keyvals, keyval_cols)
 
 
 def attend_back_kernel(
+    group,
     place_ref,
     query_ref,
     query_rows_ref,
@@ -180,104 +174,82 @@
     grad_rows_ref,
     out_ref,
     log_ref,
-    key_ref,
-    key_cols_ref,
-    value_ref,
+    keyval_ref,
+    keyval_cols_ref,
     grad_query_ref,
-    grad_key_ref,
+    grad_keyval_ref,
     dots_ref,
+    query_side_ref,
+    grad_side_ref,
 ):
     rows = query_ref.shape[1]
-    key_width = KVHEADS * HEAD_DIM
-    group_size = QHEADS // KVHEADS
-    scale = log2_e / math.sqrt(HEAD_DIM)
+    scale = log2_e * score_scale
     grad_query_ref[...] = jnp.zeros_like(grad_query_ref)
-    for head in range(QHEADS):
-        span = slice(head * HEAD_DIM, (head + 1) * HEAD_DIM)
-        dots_ref[head : head + 1, :] = jnp.sum(
+    for j in range(group_size):
+        span = head_span(group * group_size + j)
+        dots_ref[j : j + 1, :] = jnp.sum(
             grad_ref[span, :].astype(jnp.float32) * out_ref[span, :], axis=0, keepdims=True
         )
+        query = (query_rows_ref[:, span].astype(jnp.float32) * score_scale).astype(jnp.bfloat16)
+        grad = grad_rows_ref[:, span]
+        query_side_ref[j] = jnp.concatenate([query, jnp.zeros_like(query)], axis=1)
+        grad_side_ref[j] = jnp.concatenate([jnp.zeros_like(grad), grad], axis=1)
 
     def one_piece(piece, own):
-        keys = key_ref[piece]
-        values = value_ref[piece]
-        grad_keys = jnp.zeros((rows, key_width), jnp.float32)
-        grad_values = jnp.zeros((rows, key_width), jnp.float32)
-        for head in range(QHEADS):
-            group = head // group_size
-            scores = plain_dot(keys, group_rows(query_ref, head)) * scale
+        keyvals = keyval_ref[piece, :, 2 * group * HEAD_DIM : 2 * (group + 1) * HEAD_DIM]
+        key_cols = keyval_cols_ref[piece, head_span(2 * group), :]
+        total = jnp.zeros((rows, 2 * HEAD_DIM), jnp.float32)
+        for j in range(group_size):
+            head = group * group_size + j
+            query, grad = query_ref[head_span(head), :], grad_ref[head_span(head), :]
+            blank = jnp.zeros_like(query)
+            scores = plain_dot(keyvals, jnp.concatenate([query, blank], axis=0)) * scale
             weights = jnp.exp2(scores - log_ref[head : head + 1, :])
             if own:
                 weights = jnp.where(hidden_keys(rows), 0.0, weights)
-            grad_weights = plain_dot(values, group_rows(grad_ref, head))
-            grad_scores = (weights * (grad_weights - dots_ref[head : head + 1, :])).astype(
-                jnp.bfloat16
-            )
-            span = slice(head * HEAD_DIM, (head + 1) * HEAD_DIM)
-            grad_query_ref[span, :] += plain_dot(
-                key_cols_ref[piece, group * HEAD_DIM : (group + 1) * HEAD_DIM, :], grad_scores
-            )
-            grad_keys += plain_dot(grad_scores, query_rows_ref[head])
-            grad_values += plain_dot(weights.astype(jnp.bfloat16), grad_rows_ref[head])
-        grad_key_ref[piece, :, :key_width] = grad_keys * (1.0 / math.sqrt(HEAD_DIM))
-        grad_key_ref[piece, :, key_width:] = grad_values
+            grad_weights = plain_dot(keyvals, jnp.concatenate([blank, grad], axis=0))
+            grad_scores = (weights * (grad_weights - dots_ref[j : j + 1, :])).astype(jnp.bfloat16)
+            grad_query_ref[head_span(j), :] += plain_dot(key_cols, grad_scores)
+            total = total + plain_dot(grad_scores, query_side_ref[j])
+            total = total + plain_dot(weights.astype(jnp.bfloat16), grad_side_ref[j])
+        grad_keyval_ref[piece] = total
 
     def clear(piece, carry):
-        grad_key_ref[piece] = jnp.zeros(grad_key_ref.shape[1:], jnp.float32)
+        grad_keyval_ref[piece] = jnp.zeros(grad_keyval_ref.shape[1:], jnp.float32)
         return carry
 
     def earlier(index, carry):
         one_piece(slot_of(index, place_ref), False)
         return carry
 
-    lax.fori_loop(1, key_ref.shape[0], clear, 0)
+    lax.fori_loop(1, keyval_ref.shape[0], clear, 0)
     one_piece(0, True)
     lax.fori_loop(0, 2 * place_ref[0] + place_ref[1], earlier, 0)
-    grad_query_ref[...] = grad_query_ref[...] * (1.0 / math.sqrt(HEAD_DIM))
-
-
-def padded_heads(rows):
-    group_size = QHEADS // KVHEADS
-    heads = []
-    for head in range(QHEADS):
-        group = head // group_size
-        own = rows[:, head * HEAD_DIM : (head + 1) * HEAD_DIM]
-        after = (KVHEADS - 1 - group) * HEAD_DIM
-        heads.append(jnp.pad(own, ((0, 0), (group * HEAD_DIM, after))))
-    return jnp.stack(heads)
-
-
-def attend_back(place, queries, grads, grad_rows, outs, logs, keys, key_cols, values):
+    grad_query_ref[...] = grad_query_ref[...] * score_scale
+
+
+def attend_back(group, place, queries, query_rows, grads, grad_rows, outs, logs, keyvals, keyval_cols):
     rows = queries.shape[1]
-    flops = 10 * queries.size * rows * keys.shape[0]
+    flops = 10 * queries.size * rows * keyvals.shape[0] // KVHEADS
     return pl.pallas_call(
-        attend_back_kernel,
+        partial(attend_back_kernel, group),
         out_shape=(
-            jax.ShapeDtypeStruct(queries.shape, jnp.float32),
-            jax.ShapeDtypeStruct((*keys.shape[:2], 2 * keys.shape[2]), jnp.float32),
+            jax.ShapeDtypeStruct((group_size * HEAD_DIM, rows), jnp.float32),
+            jax.ShapeDtypeStruct((*keyvals.shape[:2], 2 * HEAD_DIM), jnp.float32),
         ),
-        in_specs=[pl.BlockSpec(memory_space=pltpu.SMEM)] + in_vmem(9),
+        in_specs=[pl.BlockSpec(memory_space=pltpu.SMEM)] + in_vmem(8),
         out_specs=tuple(in_vmem(2)),
-        scratch_shapes=[pltpu.VMEM((QHEADS, rows), jnp.float32)],
+        scratch_shapes=[
+            pltpu.VMEM((8, rows), jnp.float32),
+            pltpu.VMEM((group_size, rows, 2 * HEAD_DIM), jnp.bfloat16),
+            pltpu.VMEM((group_size, rows, 2 * HEAD_DIM), jnp.bfloat16),
+        ],
         compiler_params=compiler_room,
         cost_estimate=pl.CostEstimate(
-            flops=flops,
-            bytes_accessed=8 * keys.size,
-            transcendentals=flops // 640,
+            flops=6 * flops, bytes_accessed=4 * keyvals.size, transcendentals=flops // 640
         ),
-        name="attend_back",
-    )(
-        place,
-        queries,
-        padded_heads(queries.T),
-        grads,
-        padded_heads(grad_rows),
-        outs,
-        logs,
-        keys,
-        key_cols,
-        values,
-    )
+        name="attend_back_" + str(group),
+    )(place, queries, query_rows, grads, grad_rows, outs, logs, keyvals, keyval_cols)
 
 
 ssd_rows = 128
@@ -389,7 +361,7 @@
         out_specs=tuple(in_vmem(4)),
         compiler_params=compiler_room,
         cost_estimate=pl.CostEstimate(
-            flops=chunks * rows * inner * 2000, bytes_accessed=act.size * 16, transcendentals=0
+            flops=chunks * rows * inner * 10000, bytes_accessed=act.size * 16, transcendentals=0
         ),
         name="ssd",
     )(act, cum, jnp.swapaxes(cum, 1, 2), step_size, head_columns(MHEADS, 3))
@@ -548,7 +520,7 @@
         ],
         compiler_params=compiler_room,
         cost_estimate=pl.CostEstimate(
-            flops=chunks * rows * inner * 5000, bytes_accessed=act.size * 16, transcendentals=0
+            flops=chunks * rows * inner * 25000, bytes_accessed=act.size * 16, transcendentals=0
         ),
         name="ssd_back",
     )(
@@ -593,16 +565,22 @@
     return (lax.broadcasted_iota(jnp.int32, (width, width), 0) == usual).astype(jnp.bfloat16)
 
 
-def gather_stages(shard, first, after=None):
-    if after is not None:
-        shard, _ = lax.optimization_barrier((shard, after))
+def after(values, *others):
+    return lax.optimization_barrier((values, others))[0]
+
+
+def gather_stages(shard):
     parts = [shard] + [shifted(shard, "z", -k) for k in range(1, lax.axis_size("z"))]
     started = parts[-1]
     block = jnp.concatenate(parts, axis=0)[None, None]
-    for axis in (first, "xy".replace(first, "")):
-        parts = [block] + [shifted(block, axis, -k) for k in range(1, lax.axis_size(axis))]
-        block = jnp.concatenate(parts, axis="yx".index(axis))
-    own = block.reshape(-1, shard.shape[1])
+    middle = shard.shape[1] // 256 * 128
+    halves = []
+    for half, axes in ((block[..., :middle], "xy"), (block[..., middle:], "yx")):
+        for axis in axes:
+            parts = [half] + [shifted(half, axis, -k) for k in range(1, lax.axis_size(axis))]
+            half = jnp.concatenate(parts, axis="yx".index(axis))
+        halves.append(half.reshape(-1, half.shape[-1]))
+    own = jnp.concatenate(halves, axis=1)
     return (own, shifted(own, "core", 1)), started
 
 
@@ -615,24 +593,37 @@
     return jnp.concatenate([back_product(values, pair[0]), back_product(values, pair[1])], axis=1)
 
 
-def keep_own(total, axis, dim):
+def keep_own(total, axis, dim, received=None):
     kept = lax.index_in_dim(total, 0, dim, False)
     for step in range(1, lax.axis_size(axis)):
         part = lax.index_in_dim(total, step, dim, False)
-        kept = kept + shifted(part.astype(jnp.bfloat16), axis, step).astype(jnp.float32)
+        got = shifted(part.astype(jnp.bfloat16), axis, step)
+        if received is not None:
+            received.append(got)
+        kept = kept + got.astype(jnp.float32)
     return kept
 
 
-def scatter_product(left, right, first):
+def core_sum(left, right, received):
     half = left.shape[1] // 2
     sizes = [lax.axis_size(axis) for axis in ("y", "x", "z")]
-    sent = outer_product(left[:, half:], right).astype(jnp.bfloat16)
-    received = shifted(sent, "core", 1)
-    total = outer_product(left[:, :half], right) + received.astype(jnp.float32)
-    total = total.reshape(*sizes, -1, right.shape[1])
-    for axis, dim in ((("x", 1), ("y", 0)) if first == "x" else (("y", 0), ("x", 0))):
-        total = keep_own(total, axis, dim)
-    return keep_own(total, "z", 0)
+    got = shifted(outer_product(left[:, half:], right).astype(jnp.bfloat16), "core", 1)
+    received.append(got)
+    total = outer_product(left[:, :half], right) + got.astype(jnp.float32)
+    return total.reshape(*sizes, -1, right.shape[1])
+
+
+def side_by_side(parts):
+    return parts[0] if len(parts) == 1 else jnp.concatenate(parts, axis=-1)
+
+
+def chip_sums(by_x, by_y, received):
+    by_x = side_by_side([keep_own(total, "x", 1, received) for total in by_x])
+    by_y = side_by_side([keep_own(total, "y", 0, received) for total in by_y])
+    later = []
+    by_x = keep_own(by_x, "y", 0, later)
+    by_y = keep_own(by_y, "x", 0, later)
+    return keep_own(jnp.concatenate([by_x, by_y], axis=-1), "z", 0), later
 
 
 def sum_everywhere(values):
@@ -675,17 +666,20 @@
 
 
 def gather_keys(own):
-    slots = []
-    for step in range(lax.axis_size("z")):
-        block = moved_along(own, "z", step) if step else own
-        slots += [block, shifted(block, "x", 1)]
-    return jnp.stack(slots)
-
-
-def sum_key_grads(slots):
+    blocks = [moved_along(own, "z", step) if step else own for step in range(lax.axis_size("z"))]
+    blocks = jnp.stack(blocks)
+    slots = jnp.stack([blocks, shifted(blocks, "x", 1)], axis=1)
+    return slots.reshape(-1, *own.shape)
+
+
+def swap_key_grads(slots):
     total = slots.reshape(-1, 2, *slots.shape[1:])
     swapped = shifted(total[:, 1].astype(jnp.bfloat16), "x", 1)
-    kept = total[:, 0] + swapped.astype(jnp.float32)
+    return total[:, 0], swapped
+
+
+def sum_key_grads(kept, swapped):
+    kept = kept + swapped.astype(jnp.float32)
     own = kept[0]
     for step in range(1, kept.shape[0]):
         own = own + moved_along(kept[step].astype(jnp.bfloat16), "z", -step).astype(jnp.float32)
@@ -741,29 +735,26 @@
     )
     gate_shard = jnp.concatenate([w_in[:, :inner_width], w_query], axis=1)
     out_shard = jnp.concatenate([w_mix_out.T, w_attn_out.T], axis=1)
-    out_half = out_shard.shape[1] // 2
     down_shard = w_down.T
-    down_half = down_shard.shape[1] // 2
-    conv_pair, conv_started = gather_stages(conv_shard, "x")
-    gate_pair, gate_started = gather_stages(gate_shard, "y")
-    started = (conv_started, gate_started)
-    out_pair_a, out_started = gather_stages(out_shard[:, :out_half], "x", started)
-    out_pair_b, out_started_b = gather_stages(out_shard[:, out_half:], "y", started)
-    started = (out_started, out_started_b)
-    ff_pair_a, ff_started = gather_stages(w_gate_up[:, :FF], "x", started)
-    ff_pair_b, ff_started_b = gather_stages(w_gate_up[:, FF:], "y", started)
-    started = (ff_started, ff_started_b)
-    down_pair_a, _ = gather_stages(down_shard[:, :down_half], "x", started)
-    down_pair_b, _ = gather_stages(down_shard[:, down_half:], "y", started)
+    late_shard = jnp.concatenate([out_shard, w_gate_up, down_shard], axis=1)
+    late = lax.all_gather(late_shard, every_axis, axis=0, tiled=True)
+    full_out, full_gate, full_up, full_down = jnp.split(
+        late, [out_shard.shape[1], out_shard.shape[1] + FF, out_shard.shape[1] + 2 * FF], axis=1
+    )
+    conv_pair, started = gather_stages(conv_shard)
+    gate_pair, _ = gather_stages(after(gate_shard, started))
 
     order = width_order(width)
     inputs = plain_dot(tokens[0], order)
-    grad_output = plain_dot(cotangent[0], order).astype(jnp.bfloat16)
+    grad_output = cotangent[0]
     small = jnp.concatenate([half[:, gain_at : tap_at + tap_columns] for half in conv_pair], axis=0)
     gain_one_float = small[:, 0].astype(jnp.float32)
-    gain_two_float = small[:, 1].astype(jnp.float32)
-    tap_all = plain_dot(order, small[:, 2:]).reshape(device_count, own_rows, tap_columns)
-    tap_all = jnp.swapaxes(tap_all, 1, 2).reshape(device_count, -1)[:, : taps.size]
+    small_rows = lax.dot_general(
+        small, order, (((0,), (1,)), ((), ())), preferred_element_type=jnp.float32
+    )
+    gain_two_float = small_rows[1]
+    tap_all = small_rows[2:].reshape(tap_columns, device_count, own_rows)
+    tap_all = jnp.swapaxes(tap_all, 0, 1).reshape(device_count, -1)[:, : taps.size]
     tap_all = jnp.swapaxes(tap_all.reshape(-1, *taps.shape), 0, 1).reshape(taps.shape[0], channels)
 
     normed = rms_norm(inputs, gain_one_float).astype(jnp.bfloat16)
@@ -775,9 +766,14 @@
         row_count, dtype=jnp.int32
     )
     cosine, sine = turn_columns(positions)
-    own_keys = turn_rows(keyval_raw[:, :key_width].T, cosine, sine).T
-    own_keyval = jnp.concatenate([own_keys, keyval_raw[:, key_width:]], axis=1).astype(jnp.bfloat16)
-    all_keyval = gather_keys(own_keyval)
+    keyval_cols = keyval_raw.T
+    key_cols = turn_rows(keyval_cols[:key_width], cosine, sine)
+    by_head = (KVHEADS, 1, HEAD_DIM, row_count)
+    own_keyval = jnp.concatenate(
+        [key_cols.reshape(by_head), keyval_cols[key_width:].reshape(by_head)], axis=1
+    ).reshape(2 * key_width, row_count)
+    all_keyval = gather_keys(own_keyval.T.astype(jnp.bfloat16))
+    all_cols = jnp.swapaxes(all_keyval, 1, 2)
     border = lax.ppermute(
         conv_input[row_count - (CONV - 1) :],
         seq_axes,
@@ -800,9 +796,7 @@
     gate_projected = times_rows(normed, gate_pair)
     gate_z = gate_projected[:, :inner_width]
     query_cols = turn_rows(gate_projected[:, inner_width:].T, cosine, sine).astype(jnp.bfloat16)
-    all_keys = all_keyval[:, :, :key_width]
-    all_values = all_keyval[:, :, key_width:]
-    attended_cols, logs = attend(place, query_cols, all_keys, jnp.swapaxes(all_values, 1, 2))
+    attended_cols, logs = attend(place, query_cols, all_keyval, all_cols)
     attention_rows = attended_cols.T.astype(jnp.bfloat16)
 
     skip_row = jnp.repeat(skip_weight, MHEAD_DIM)[None, :]
@@ -815,41 +809,38 @@
     gate_sigmoid = jax.nn.sigmoid(gate_z)
     mixer = (ssm_y * gate_z * gate_sigmoid).astype(jnp.bfloat16)
     branches = jnp.concatenate([mixer, attention_rows], axis=1)
-    branches_a, branches_b = branches[:, :out_half], branches[:, out_half:]
-    hidden = (
-        inputs + times_rows_back(branches_a, out_pair_a) + times_rows_back(branches_b, out_pair_b)
-    )
+    hidden = tokens[0].astype(jnp.float32) + back_product(branches, full_out)
     normed_two = rms_norm(hidden, gain_two_float).astype(jnp.bfloat16)
-    gate_part = times_rows(normed_two, ff_pair_a)
-    up_part = times_rows(normed_two, ff_pair_b)
+    gate_part = plain_dot(normed_two, full_gate)
+    up_part = plain_dot(normed_two, full_up)
     activated = (jax.nn.silu(gate_part) * up_part).astype(jnp.bfloat16)
-    active_a, active_b = activated[:, :down_half], activated[:, down_half:]
-    result = (
-        hidden + times_rows_back(active_a, down_pair_a) + times_rows_back(active_b, down_pair_b)
-    )
-    output = back_product(result.astype(jnp.bfloat16), order).astype(jnp.bfloat16)[None]
-
-    grad_activated = jnp.concatenate(
-        [times_rows(grad_output, down_pair_a), times_rows(grad_output, down_pair_b)], axis=1
-    )
-    grad_down_a = scatter_product(grad_output, active_a, "x")
-    grad_down_b = scatter_product(grad_output, active_b, "y")
+    result = hidden + back_product(activated, full_down)
+    output = result.astype(jnp.bfloat16)[None]
+
+    def reordered(rows):
+        return plain_dot(rows, order).astype(jnp.bfloat16)
+
+    grad_activated = plain_dot(grad_output, full_down)
+    core_got = []
+    grad_output_rows = reordered(grad_output)
+    down_half = FF // 2
+    normed_two_rows = reordered(normed_two)
     ff_sigmoid = jax.nn.sigmoid(gate_part)
     grad_gate = grad_activated * up_part * ff_sigmoid * (1.0 + gate_part * (1.0 - ff_sigmoid))
     grad_gate = grad_gate.astype(jnp.bfloat16)
     grad_up = (grad_activated * gate_part * ff_sigmoid).astype(jnp.bfloat16)
-    grad_ff_a = scatter_product(normed_two, grad_gate, "x")
-    grad_ff_b = scatter_product(normed_two, grad_up, "y")
-    grad_normed_two = times_rows_back(grad_gate, ff_pair_a) + times_rows_back(grad_up, ff_pair_b)
+    gate_total = core_sum(normed_two_rows, grad_gate, core_got)
+    up_total = core_sum(normed_two_rows, grad_up, core_got)
+    down_a = core_sum(grad_output_rows, activated[:, :down_half], [])
+    down_b = core_sum(grad_output_rows, activated[:, down_half:], [])
+    ff_got = []
+    ff_sums, ff_later = chip_sums([gate_total, down_a], [up_total, down_b], ff_got)
+    grad_normed_two = back_product(after(grad_gate, *core_got), full_gate) + back_product(grad_up, full_up)
     _, pull_two = jax.vjp(rms_norm, hidden, gain_two_float)
     grad_hidden_norm, grad_gain_two = pull_two(grad_normed_two)
     grad_hidden = grad_output.astype(jnp.float32) + grad_hidden_norm
     grad_branch = grad_hidden.astype(jnp.bfloat16)
-    grad_branches = jnp.concatenate(
-        [times_rows(grad_branch, out_pair_a), times_rows(grad_branch, out_pair_b)], axis=1
-    )
-    grad_out_a = scatter_product(grad_branch, branches_a, "x")
-    grad_out_b = scatter_product(grad_branch, branches_b, "y")
+    grad_branches = after(plain_dot(grad_branch, full_out), ff_got[1], ff_got[3])
     grad_mixer = grad_branches[:, :inner_width]
     grad_y = grad_mixer * gate_z * gate_sigmoid
     grad_gate_z = grad_mixer * ssm_y * gate_sigmoid * (1.0 + gate_z * (1.0 - gate_sigmoid))
@@ -857,26 +848,50 @@
     grad_end = carried(from_output, tail, -1)
 
     grad_attention = grad_branches[:, inner_width:].astype(jnp.bfloat16)
-    grad_query_cols, grad_slots = attend_back(
-        place,
-        query_cols,
-        grad_attention.T,
-        grad_attention,
-        attended_cols,
-        logs,
-        all_keys,
-        jnp.swapaxes(all_keys, 1, 2),
-        all_values,
-    )
-    own_grads = sum_key_grads(grad_slots)
+    out_got = []
+    out_total = core_sum(reordered(grad_branch), branches, out_got)
+    in_gate_total = core_sum(normed, grad_gate_z.astype(jnp.bfloat16), out_got)
+    grad_cols = grad_attention.T
+    query_rows = query_cols.T
+    def one_group(group, grad_cols):
+        return attend_back(
+            group,
+            place,
+            query_cols,
+            query_rows,
+            grad_cols,
+            grad_attention,
+            attended_cols,
+            logs,
+            all_keyval,
+            all_cols,
+        )
+
+    query_a, slots_a = one_group(0, after(grad_cols, gate_total, up_total))
+    query_a, slots_a = after((query_a, slots_a), ff_got[0], ff_got[2])
+    kept_a, swapped_a = swap_key_grads(slots_a)
+    query_b, slots_b = one_group(1, after(grad_cols, ff_got[0], ff_got[2], *out_got))
+    before_ssd = (query_b, *ff_later, swapped_a)
+    query_b, slots_b, kept_a, swapped_a = after((query_b, slots_b, kept_a, swapped_a), *before_ssd)
+    own_a = sum_key_grads(kept_a, swapped_a)
+    kept_b, swapped_b = swap_key_grads(slots_b)
+    own_b = sum_key_grads(kept_b, swapped_b)
+    own_grads = [own_a, own_b]
+    key_got = [swapped_b]
+    grad_query_cols = jnp.concatenate([query_a, query_b], axis=0)
+    mid_got = []
+    mid_sums, mid_later = chip_sums([in_gate_total], [out_total], mid_got)
     grad_query = turn_rows(grad_query_cols, cosine, -sine).T.astype(jnp.bfloat16)
-    grad_keys = turn_rows(own_grads[:, :key_width].T, cosine, -sine).T
-    grad_keyval = jnp.concatenate([grad_keys, own_grads[:, key_width:]], axis=1).astype(
-        jnp.bfloat16
-    )
+    own_cols = jnp.concatenate(own_grads, axis=1).T.reshape(KVHEADS, 2, HEAD_DIM, row_count)
+    grad_keys = turn_rows(own_cols[:, 0].reshape(key_width, row_count), cosine, -sine)
+    grad_keyval = jnp.concatenate([grad_keys, own_cols[:, 1].reshape(key_width, row_count)], axis=0)
+    grad_keyval = grad_keyval.T.astype(jnp.bfloat16)
 
     grad_act, grad_step_size, grad_log, grad_skip = ssd_back(
-        act, cum, step_size, grad_y, carry_state, grad_end, skip_row
+        act, cum, step_size, after(grad_y, *before_ssd), carry_state, grad_end, skip_row
+    )
+    grad_act, grad_step_size, grad_log = after(
+        (grad_act, grad_step_size, grad_log), *mid_got, *key_got
     )
     grad_step_size = grad_step_size - grad_log * jnp.exp(mamba_heads[0])[None, :]
     grad_step_raw = grad_step_size * jax.nn.sigmoid(step_raw + mamba_heads[1][None, :])
@@ -890,30 +905,30 @@
     grad_conv_input = grad_extended[CONV - 1 :] + jnp.pad(
         rim_back, ((row_count - (CONV - 1), 0), (0, 0))
     )
+    grad_conv_low = after(grad_conv_input.astype(jnp.bfloat16), ff_sums)
+    grad_step_low = jnp.pad(
+        grad_step_raw.astype(jnp.bfloat16), ((0, 0), (0, conv_shard.shape[1] - gain_at))
+    )
+    grad_few = jnp.concatenate([grad_query, grad_keyval, grad_step_low], axis=1)
+    last_core_got, last_got = [], []
+    conv_total = core_sum(normed, grad_conv_low, last_core_got)
+    few_total = core_sum(normed, grad_few, [])
+    last_sums, _ = chip_sums([conv_total], [few_total], last_got)
     grad_gate_half = jnp.concatenate([grad_gate_z.astype(jnp.bfloat16), grad_query], axis=1)
-    grad_conv_half = jnp.concatenate(
-        [
-            grad_conv_input.astype(jnp.bfloat16),
-            grad_keyval,
-            grad_step_raw.astype(jnp.bfloat16),
-            jnp.zeros((row_count, conv_shard.shape[1] - gain_at), jnp.bfloat16),
-        ],
-        axis=1,
-    )
-    grad_in_gate = scatter_product(normed, grad_gate_half, "y")
-    grad_in_conv = scatter_product(normed, grad_conv_half, "x")
+    grad_conv_half = jnp.concatenate([grad_conv_low, grad_keyval, grad_step_low], axis=1)
     grad_normed = times_rows_back(grad_gate_half, gate_pair) + times_rows_back(
         grad_conv_half, conv_pair
     )
     _, pull_one = jax.vjp(rms_norm, inputs, gain_one_float)
     grad_input_norm, grad_gain_one = pull_one(grad_normed)
     input_grad = lax.dot_general(
-        grad_hidden + grad_input_norm,
+        grad_input_norm,
         order.astype(jnp.float32),
         (((1,), (1,)), ((), ())),
         precision=lax.Precision.HIGH,
         preferred_element_type=jnp.float32,
-    )[None]
+    )
+    input_grad = (grad_hidden + input_grad)[None]
 
     def usual_gain(grad):
         rows = jnp.broadcast_to(grad[None], (8, width))
@@ -932,40 +947,44 @@
         axis=1,
     )
     summed = sum_everywhere(
-        jnp.concatenate(
+        after(jnp.concatenate(
             [
                 grad_conv_weight,
                 grad_conv_bias[None],
-                padded(usual_gain(grad_gain_two)),
+                padded(grad_gain_two[None]),
+                padded(usual_gain(grad_gain_one)),
                 padded(head_row),
             ],
             axis=0,
-        )
-    )
-    summed_gain = sum_everywhere(usual_gain(grad_gain_one))
+        ), *last_core_got)
+    )
     device = lax.axis_index(every_axis)
     own_channels = conv_weight.shape[1]
     own_taps = lax.dynamic_slice_in_dim(summed[: CONV + 1], device * own_channels, own_channels, 1)
     own_gain_two = lax.dynamic_slice_in_dim(summed[CONV + 1], device * own_rows, own_rows)
-    own_gain_one = lax.dynamic_slice_in_dim(summed_gain[0], device * own_rows, own_rows)
-    head_sums_row = summed[CONV + 2]
+    own_gain_one = lax.dynamic_slice_in_dim(summed[CONV + 2], device * own_rows, own_rows)
+    head_sums_row = summed[CONV + 3]
+    query_at = channels + query_width
+    step_from = query_at + w_keyval.shape[1]
     return (
         output,
         input_grad,
         own_gain_one,
-        jnp.concatenate([grad_in_gate[:, :inner_width], grad_in_conv[:, :channels]], axis=1),
-        grad_in_conv[:, step_at:gain_at],
+        jnp.concatenate([mid_sums[:, :inner_width], last_sums[:, :channels]], axis=1),
+        last_sums[:, step_from : step_from + w_step.shape[1]],
         own_taps[:CONV],
         own_taps[CONV],
         head_sums_row[: 2 * MHEADS].reshape(2, MHEADS),
         head_sums_row[2 * MHEADS : 3 * MHEADS],
-        grad_in_gate[:, inner_width:],
-        grad_in_conv[:, channels:step_at],
-        jnp.concatenate([grad_out_a, grad_out_b], axis=1)[:, inner_width:].T,
-        jnp.concatenate([grad_out_a, grad_out_b], axis=1)[:, :inner_width].T,
+        last_sums[:, channels:query_at],
+        last_sums[:, query_at:step_from],
+        mid_sums[:, 2 * inner_width :].T,
+        mid_sums[:, inner_width : 2 * inner_width].T,
         own_gain_two,
-        jnp.concatenate([grad_ff_a, grad_ff_b], axis=1),
-        jnp.concatenate([grad_down_a, grad_down_b], axis=1).T,
+        jnp.concatenate([ff_sums[:, :FF], ff_sums[:, FF + down_half : 2 * FF + down_half]], axis=1),
+        jnp.concatenate(
+            [ff_sums[:, FF : FF + down_half], ff_sums[:, 2 * FF + down_half :]], axis=1
+        ).T,
     )
 
 

time: 793 us -> 675 us (0.85)
  waiting for transfers between devices: 292 us -> 191 us
  matrix products: 133 us -> 111 us
  between operations: 4.8 us -> 17.6 us
  other arithmetic: 75.4 us -> 65.6 us
    ppermute x105 -> x54, waiting for transfers between devices: 215 us -> 137 us  [shifted(): lax.ppermute(block, axis, [(i, (i + distance) % count) for i in range(cou...]
    ppermute x12 -> x15, starting transfers between devices: 18.9 us -> 55.1 us  [moved_along(): return lax.ppermute(block, axis, route)]
    ppermute x105 -> x54, starting transfers between devices: 124 us -> 93.8 us  [shifted(): lax.ppermute(block, axis, [(i, (i + distance) % count) for i in range(cou...]
    ppermute x12 -> x15, waiting for transfers between devices: 70.3 us -> 43 us  [moved_along(): return lax.ppermute(block, axis, route)]
    concatenate x21 -> x16, other arithmetic: 21 us -> 8.74 us  [the longest x2 3.24 us: gather_stages(): own = jnp.concatenate(halves, axis=1)]
    add x16 -> x18, other arithmetic: 6.17 us -> 15.4 us  [the longest x17 15 us: keep_own(): kept = kept + got.astype(jnp.float32)]
    dot_general x17 -> x8, matrix products: 40.1 us -> 30.9 us  [back_product(): lax.dot_general(grad_rows, weight_matrix, (((1,), (1,)), ((), ())), prefe...]
    unnamed x380 -> x348, local copies, waits for them, and re-layouts: 34.2 us -> 40.3 us
  transfers between devices with their start and end apart: 129 -> 77, of which waited for: 55 -> 39; matrix products, arithmetic and copies ran while one was open for 31% -> 27% of each run, Pallas kernels for 4% -> 5%
where the time goes in v3:
time: 675 us; the launch traced here: 666 us
  waiting for transfers between devices  191 us (28%)
  starting transfers between devices  163 us (24%)
  matrix products  111 us (16%)
  local copies, waits for them, and re-layouts  84.8 us (13%)
  other arithmetic  65.6 us (10%)
  Pallas kernels  32.3 us (5%)
  between operations  17.6 us (3%)
    ppermute x54, waiting for transfers between devices, shifted(): lax.ppermute(block, axis, [(i, (i + distance) % count) for i in range(cou...  137 us
    ppermute x54, starting transfers between devices, shifted(): lax.ppermute(block, axis, [(i, (i + distance) % count) for i in range(cou...  93.8 us
    ppermute x15, starting transfers between devices, moved_along(): return lax.ppermute(block, axis, route)  55.1 us
    ppermute x15, waiting for transfers between devices, moved_along(): return lax.ppermute(block, axis, route)  43 us
    dot_general x13, matrix products, plain_dot(): return jnp.dot(left, right, preferred_element_type=jnp.float32)  42 us
    unnamed x348, local copies, waits for them, and re-layouts  40.3 us
    dot_general x8, matrix products, back_product(): lax.dot_general(grad_rows, weight_matrix, (((1,), (1,)), ((), ())), prefe...  30.9 us
    dot_general x17, matrix products, outer_product(): lax.dot_general(left, right, (((0,), (0,)), ((), ())), preferred_element_...  28.8 us
  transfers between devices with their start and end apart: 77, of which 39 were waited for; matrix products, arithmetic and copies ran while one was open for 27% of the time, Pallas kernels for 5%

profile of v3, /device:TPU:0, one launch (start us, length us, event | category | flops | bytes accessed | tf_op | source)
XLA Modules:
  0.0 666.0 jit_solution(7847276917112797408)
XLA Ops:
  45.5 8.9 %collective-permute-start.16 = (bf16[32,2048]{1,0:T(8,128)(2,1)}, bf16[32,2048]{1,0:T(8,128)(2,1)}, u32[]{:S(2)}, u32[]{:S(2)}) collective-permute-start(bf16[32,2048]{1,0:T(8,128)(2,1)} %pad_maximum_fusion.46), channel_id=1, source_target_pairs={{0,2},{2,4},{4,6},{6,0},{1,3},{3,5},{5,7},{7,1},{8,10},{10,12},{12... | collective-permute-start | bytes 393224 | tf_op jit(solution)/shard_map/ppermute | solution.py:543
  59.6 5.9 collective-permute-done.4
  83.5 9.0 %collective-permute-done.20 = bf16[2,1,128,1024]{3,2,1,0:T(8,128)(2,1)S(1)} collective-permute-done((bf16[2,1,128,1024]{3,2,1,0:T(8,128)(2,1)S(1)}, bf16[2,1,128,1024]{3,2,1,0:T(8,128)(2,1)S(1)}, u32[]{:S(2)}, u32[]{:S(2)}) %collective-permute-start.20) | collective-permute-done | bytes 524320 | tf_op jit(solution)/shard_map/ppermute | solution.py:543
  104.2 23.3 %collective-permute-start.24 = (bf16[384,256]{0,1:T(8,128)(2,1)}, bf16[384,256]{0,1:T(8,128)(2,1)}, u32[]{:S(2)}, u32[]{:S(2)}) collective-permute-start(bf16[384,256]{0,1:T(8,128)(2,1)} %bitcast.37), channel_id=1, source_target_pairs={{0,6},{1,7},{8,14},{9,15},{16,22},{17,23},{24,30},{25,31}} | collective-permute-start | bytes 589832 | tf_op jit(solution)/shard_map/ppermute | solution.py:549
  145.9 6.5 ssd.1
  153.4 5.7 collective-permute-start.9
  164.6 5.0 collective-permute-done.9
  171.9 12.2 %collective-permute-start.11 = (bf16[136,768]{1,0:T(8,128)(2,1)}, bf16[136,768]{1,0:T(8,128)(2,1)}, u32[]{:S(2)}, u32[]{:S(2)}) collective-permute-start(bf16[136,768]{1,0:T(8,128)(2,1)} %fusion.144), channel_id=1, source_target_pairs={{0,4},{2,6},{1,5},{3,7},{8,12},{10,14},{9,13},{11,15},{16,20},{18,... | collective-permute-start | bytes 626696 | tf_op jit(solution)/shard_map/ppermute | solution.py:549
  208.5 4.9 multiply_convert_fusion.2
  213.5 8.5 %collective-permute-done.25 = bf16[4,384,256]{1,2,0:T(8,128)(2,1)S(1)} collective-permute-done((bf16[4,384,256]{1,2,0:T(8,128)(2,1)S(1)}, bf16[4,384,256]{1,2,0:T(8,128)(2,1)S(1)}, u32[]{:S(2)}, u32[]{:S(2)}) %collective-permute-start.25) | collective-permute-done | bytes 786464 | tf_op jit(solution)/shard_map/ppermute | solution.py:543
  228.5 4.8 multiply_reduce_fusion.7
  244.9 4.7 fusion.44
  254.9 4.9 fusion.90
  270.1 6.0 collective-permute-done.29
  279.6 5.0 multiply_reduce_fusion.5
  306.3 8.2 %collective-permute-done.39 = bf16[136,1536]{1,0:T(8,128)(2,1)S(1)} collective-permute-done((bf16[136,1536]{1,0:T(8,128)(2,1)S(1)}, bf16[136,1536]{1,0:T(8,128)(2,1)S(1)}, u32[]{:S(2)}, u32[]{:S(2)}) %collective-permute-start.39) | collective-permute-done | bytes 417824 | tf_op jit(solution)/shard_map/ppermute | solution.py:543
  327.5 16.5 %collective-permute-done.41 = bf16[136,768]{1,0:T(8,128)(2,1)} collective-permute-done((bf16[136,768]{1,0:T(8,128)(2,1)}, bf16[136,768]{1,0:T(8,128)(2,1)}, u32[]{:S(2)}, u32[]{:S(2)}) %collective-permute-start.41) | collective-permute-done | bytes 208928 | tf_op jit(solution)/shard_map/ppermute | solution.py:549
  346.6 5.0 collective-permute-done.42
  388.4 7.1 %collective-permute-done.38 = bf16[4,32,3072]{2,1,0:T(8,128)(2,1)} collective-permute-done((bf16[4,32,3072]{2,1,0:T(8,128)(2,1)}, bf16[4,32,3072]{2,1,0:T(8,128)(2,1)}, u32[]{:S(2)}, u32[]{:S(2)}) %collective-permute-start.38) | collective-permute-done | bytes 786464 | tf_op jit(solution)/shard_map/ppermute | solution.py:543
  398.4 13.9 %collective-permute-start.50 = (bf16[32,6144]{1,0:T(8,128)(2,1)}, bf16[32,6144]{1,0:T(8,128)(2,1)}, u32[]{:S(2)}, u32[]{:S(2)}) collective-permute-start(bf16[32,6144]{1,0:T(8,128)(2,1)} %get-tuple-element.166), channel_id=1, source_target_pairs={{0,6},{2,0},{4,2},{6,4},{1,7},{3,1},{5,3},{7,5},{8,14},{10,8},{12,... | collective-permute-start | bytes 1179656 | tf_op jit(solution)/shard_map/ppermute | solution.py:543
  436.5 13.8 %ssd_back.1 = (f32[3,128,1792]{2,1,0:T(8,128)}, f32[3,128,24]{2,1,0:T(8,128)S(1)}, f32[3,128,24]{2,1,0:T(8,128)S(1)}, f32[1,1536]{1,0:T(1,128)S(1)}) custom-call(f32[3,128,1792]{2,1,0:T(8,128)} %bitcast.373, f32[3,128,24]{2,1,0:T(8,128)S(1)} %copy-done.28, f32[3,24,128]{2,1,0:T(8,128)S(1)} %copy-done.32, f32[3,128,24]{2,1,0:T(8,128)S(1)} %bitcast.350, ...), custom_call_target="tpu_custom_call" | custom-call | flops 14745600000 | bytes 11010048 | tf_op jit(solution)/shard_map/ssd_back/pallas_call | solution.py:506
  453.4 5.3 fusion.96
  480.1 12.5 %collective-permute-done.44 = bf16[2,4,32,1536]{3,2,1,0:T(8,128)(2,1)S(1)} collective-permute-done((bf16[2,4,32,1536]{3,2,1,0:T(8,128)(2,1)}, bf16[2,4,32,1536]{3,2,1,0:T(8,128)(2,1)S(1)}, u32[]{:S(2)}, u32[]{:S(2)}) %collective-permute-start.44) | collective-permute-done | bytes 786464 | tf_op jit(solution)/shard_map/ppermute | solution.py:543
  502.7 15.0 %collective-permute-done.56 = bf16[384,128]{0,1:T(8,128)(2,1)S(1)} collective-permute-done((bf16[384,128]{0,1:T(8,128)(2,1)S(1)}, bf16[384,128]{0,1:T(8,128)(2,1)S(1)}, u32[]{:S(2)}, u32[]{:S(2)}) %collective-permute-start.56) | collective-permute-done | bytes 98336 | tf_op jit(solution)/shard_map/ppermute | solution.py:549
  544.5 5.0 add_bitcast_fusion
  553.7 6.9 %collective-permute-start.67 = (bf16[32,3584]{1,0:T(8,128)(2,1)}, bf16[32,3584]{1,0:T(8,128)(2,1)}, u32[]{:S(2)}, u32[]{:S(2)}) collective-permute-start(bf16[32,3584]{1,0:T(8,128)(2,1)} %get-tuple-element.169), channel_id=1, source_target_pairs={{0,6},{2,0},{4,2},{6,4},{1,7},{3,1},{5,3},{7,5},{8,14},{10,8},{12,... | collective-permute-start | bytes 688136 | tf_op jit(solution)/shard_map/ppermute | solution.py:543
  566.9 12.1 %collective-permute-done.66 = bf16[32,3584]{1,0:T(8,128)(2,1)} collective-permute-done((bf16[32,3584]{1,0:T(8,128)(2,1)}, bf16[32,3584]{1,0:T(8,128)(2,1)}, u32[]{:S(2)}, u32[]{:S(2)}) %collective-permute-start.66) | collective-permute-done | bytes 229408 | tf_op jit(solution)/shard_map/ppermute | solution.py:543
  584.3 9.7 %collective-permute-done.71 = bf16[2,4,32,896]{3,2,1,0:T(8,128)(2,1)S(1)} collective-permute-done((bf16[2,4,32,896]{3,2,1,0:T(8,128)(2,1)S(1)}, bf16[2,4,32,896]{3,2,1,0:T(8,128)(2,1)S(1)}, u32[]{:S(2)}, u32[]{:S(2)}) %collective-permute-start.71) | collective-permute-done | bytes 458784 | tf_op jit(solution)/shard_map/ppermute | solution.py:543
  612.8 4.6 collective-permute-start.62
  620.1 6.4 collective-permute-done.68
  630.8 7.0 %collective-permute-done.69 = bf16[4,32,1792]{2,1,0:T(8,128)(2,1)S(1)} collective-permute-done((bf16[4,32,1792]{2,1,0:T(8,128)(2,1)S(1)}, bf16[4,32,1792]{2,1,0:T(8,128)(2,1)S(1)}, u32[]{:S(2)}, u32[]{:S(2)}) %collective-permute-start.69) | collective-permute-done | bytes 458784 | tf_op jit(solution)/shard_map/ppermute | solution.py:543
  645.4 10.5 %collective-permute-done.74 = bf16[32,2688]{1,0:T(8,128)(2,1)S(1)} collective-permute-done((bf16[32,2688]{1,0:T(8,128)(2,1)S(1)}, bf16[32,2688]{1,0:T(8,128)(2,1)S(1)}, u32[]{:S(2)}, u32[]{:S(2)}) %collective-permute-start.74) | collective-permute-done | bytes 172064 | tf_op jit(solution)/shard_map/ppermute | solution.py:543
  (761 shorter events, 373.4 us)
Async XLA Ops:
  7.2 221.3 %all-gather.2.cloned.1.call-start = ((), (), s32[]{:S(2)}) async-start(), calls=%async_computation | async-start | bytes 17301504 | tf_op jit(solution)/shard_map/all_gather | solution.py:740
  43.3 22.2 %collective-permute-start.4 = (bf16[2,1,128,1152]{3,2,1,0:T(8,128)(2,1)S(1)}, bf16[2,1,128,1152]{3,2,1,0:T(8,128)(2,1)}, u32[]{:S(2)}, u32[]{:S(2)}) collective-permute-start(bf16[2,1,128,1152]{3,2,1,0:T(8,128)(2,1)S(1)} %pad_maximum_fusion.22), channel_id=1, source_target_pairs={{0,1},{1,0},{2,3},{3,2},{4,5},{5,4},{6,7},{7,6},{8,9},{9,8},{10,11... | collective-permute-start | bytes 1769480 | tf_op jit(solution)/shard_map/ppermute | solution.py:543
  45.5 23.7 %collective-permute-start.16 = (bf16[32,2048]{1,0:T(8,128)(2,1)}, bf16[32,2048]{1,0:T(8,128)(2,1)}, u32[]{:S(2)}, u32[]{:S(2)}) collective-permute-start(bf16[32,2048]{1,0:T(8,128)(2,1)} %pad_maximum_fusion.46), channel_id=1, source_target_pairs={{0,2},{2,4},{4,6},{6,0},{1,3},{3,5},{5,7},{7,1},{8,10},{10,12},{12... | collective-permute-start | bytes 393224 | tf_op jit(solution)/shard_map/ppermute | solution.py:543
  69.2 25.1 %collective-permute-start.7 = (bf16[512,2176]{0,1:T(8,128)(2,1)}, bf16[512,2176]{0,1:T(8,128)(2,1)}, u32[]{:S(2)}, u32[]{:S(2)}) collective-permute-start(bf16[512,2176]{0,1:T(8,128)(2,1)} %pad_maximum_fusion.2), channel_id=1, source_target_pairs={{0,8},{8,0},{1,9},{9,1},{2,10},{10,2},{3,11},{11,3},{4,12},{12,4},... | collective-permute-start | bytes 6684680 | tf_op jit(solution)/shard_map/ppermute | solution.py:543
  94.3 64.7 %collective-permute-start.21 = (bf16[512,2048]{1,0:T(8,128)(2,1)}, bf16[512,2048]{1,0:T(8,128)(2,1)}, u32[]{:S(2)}, u32[]{:S(2)}) collective-permute-start(bf16[512,2048]{1,0:T(8,128)(2,1)} %pad_maximum_fusion.3), channel_id=1, source_target_pairs={{0,8},{8,0},{1,9},{9,1},{2,10},{10,2},{3,11},{11,3},{4,12},{12,4},... | collective-permute-start | bytes 6291464 | tf_op jit(solution)/shard_map/ppermute | solution.py:543
  104.2 95.5 %collective-permute-start.24 = (bf16[384,256]{0,1:T(8,128)(2,1)}, bf16[384,256]{0,1:T(8,128)(2,1)}, u32[]{:S(2)}, u32[]{:S(2)}) collective-permute-start(bf16[384,256]{0,1:T(8,128)(2,1)} %bitcast.37), channel_id=1, source_target_pairs={{0,6},{1,7},{8,14},{9,15},{16,22},{17,23},{24,30},{25,31}} | collective-permute-start | bytes 589832 | tf_op jit(solution)/shard_map/ppermute | solution.py:549
  127.5 72.2 %collective-permute-start.23 = (bf16[384,256]{0,1:T(8,128)(2,1)}, bf16[384,256]{0,1:T(8,128)(2,1)}, u32[]{:S(2)}, u32[]{:S(2)}) collective-permute-start(bf16[384,256]{0,1:T(8,128)(2,1)} %bitcast.37), channel_id=1, source_target_pairs={{0,4},{2,6},{1,5},{3,7},{8,12},{10,14},{9,13},{11,15},{16,20},{18,... | collective-permute-start | bytes 589832 | tf_op jit(solution)/shard_map/ppermute | solution.py:549
  202.1 19.9 %collective-permute-start.25 = (bf16[4,384,256]{1,2,0:T(8,128)(2,1)S(1)}, bf16[4,384,256]{1,2,0:T(8,128)(2,1)S(1)}, u32[]{:S(2)}, u32[]{:S(2)}) collective-permute-start(bf16[4,384,256]{1,2,0:T(8,128)(2,1)S(1)} %get-tuple-element.184), channel_id=1, source_target_pairs={{0,1},{1,0},{2,3},{3,2},{4,5},{5,4},{6,7},{7,6},{8,9},{9,8},{10,11... | collective-permute-start | bytes 2359304 | tf_op jit(solution)/shard_map/ppermute | solution.py:543
  250.8 28.7 %collective-permute-start.26 = (bf16[512,2048]{1,0:T(8,128)(2,1)S(1)}, bf16[512,2048]{1,0:T(8,128)(2,1)S(1)}, u32[]{:S(2)}, u32[]{:S(2)}) collective-permute-start(bf16[512,2048]{1,0:T(8,128)(2,1)S(1)} %convolution_convert_fusion.4), channel_id=1, source_target_pairs={{0,8},{8,0},{1,9},{9,1},{2,10},{10,2},{3,11},{11,3},{4,12},{12,4},... | collective-permute-start | bytes 6291464 | tf_op jit(solution)/shard_map/ppermute | solution.py:543
  253.5 26.1 %collective-permute-start.27 = (bf16[512,2048]{1,0:T(8,128)(2,1)S(1)}, bf16[512,2048]{1,0:T(8,128)(2,1)S(1)}, u32[]{:S(2)}, u32[]{:S(2)}) collective-permute-start(bf16[512,2048]{1,0:T(8,128)(2,1)S(1)} %convolution_convert_fusion.3), channel_id=1, source_target_pairs={{0,8},{8,0},{1,9},{9,1},{2,10},{10,2},{3,11},{11,3},{4,12},{12,4},... | collective-permute-start | bytes 6291464 | tf_op jit(solution)/shard_map/ppermute | solution.py:543
  316.6 27.5 %collective-permute-start.41 = (bf16[136,768]{1,0:T(8,128)(2,1)}, bf16[136,768]{1,0:T(8,128)(2,1)}, u32[]{:S(2)}, u32[]{:S(2)}) collective-permute-start(bf16[136,768]{1,0:T(8,128)(2,1)} %fusion.141), channel_id=1, source_target_pairs={{4,0},{6,2},{5,1},{7,3},{12,8},{14,10},{13,9},{15,11},{20,16},{22,... | collective-permute-start | bytes 626696 | tf_op jit(solution)/shard_map/ppermute | solution.py:549
  317.9 27.2 %collective-permute-start.40 = (bf16[136,768]{1,0:T(8,128)(2,1)}, bf16[136,768]{1,0:T(8,128)(2,1)}, u32[]{:S(2)}, u32[]{:S(2)}) collective-permute-start(bf16[136,768]{1,0:T(8,128)(2,1)} %fusion.141), channel_id=1, source_target_pairs={{2,0},{4,2},{6,4},{3,1},{5,3},{7,5},{10,8},{12,10},{14,12},{11,9},... | collective-permute-start | bytes 626696 | tf_op jit(solution)/shard_map/ppermute | solution.py:549
  319.2 32.4 %collective-permute-start.42 = (bf16[136,768]{1,0:T(8,128)(2,1)}, bf16[136,768]{1,0:T(8,128)(2,1)}, u32[]{:S(2)}, u32[]{:S(2)}) collective-permute-start(bf16[136,768]{1,0:T(8,128)(2,1)} %fusion.141), channel_id=1, source_target_pairs={{6,0},{7,1},{14,8},{15,9},{22,16},{23,17},{30,24},{31,25}} | collective-permute-start | bytes 626696 | tf_op jit(solution)/shard_map/ppermute | solution.py:549
  323.3 42.4 %collective-permute-start.32 = (bf16[2,4,32,2048]{3,2,1,0:T(8,128)(2,1)}, bf16[2,4,32,2048]{3,2,1,0:T(8,128)(2,1)}, u32[]{:S(2)}, u32[]{:S(2)}) collective-permute-start(bf16[2,4,32,2048]{3,2,1,0:T(8,128)(2,1)} %fusion.93), channel_id=1, source_target_pairs={{0,1},{1,0},{2,3},{3,2},{4,5},{5,4},{6,7},{7,6},{8,9},{9,8},{10,11... | collective-permute-start | bytes 3145736 | tf_op jit(solution)/shard_map/ppermute | solution.py:543
  324.5 42.8 %collective-permute-start.33 = (bf16[2,4,32,2048]{3,2,1,0:T(8,128)(2,1)}, bf16[2,4,32,2048]{3,2,1,0:T(8,128)(2,1)}, u32[]{:S(2)}, u32[]{:S(2)}) collective-permute-start(bf16[2,4,32,2048]{3,2,1,0:T(8,128)(2,1)} %bitcast.64), channel_id=1, source_target_pairs={{0,16},{16,0},{1,17},{17,1},{2,18},{18,2},{3,19},{19,3},{4,20},{20... | collective-permute-start | bytes 3145736 | tf_op jit(solution)/shard_map/ppermute | solution.py:543
  344.1 68.8 %collective-permute-start.34 = (bf16[512,2048]{1,0:T(8,128)(2,1)}, bf16[512,2048]{1,0:T(8,128)(2,1)}, u32[]{:S(2)}, u32[]{:S(2)}) collective-permute-start(bf16[512,2048]{1,0:T(8,128)(2,1)} %convolution_convert_fusion.2), channel_id=1, source_target_pairs={{0,8},{8,0},{1,9},{9,1},{2,10},{10,2},{3,11},{11,3},{4,12},{12,4},... | collective-permute-start | bytes 6291464 | tf_op jit(solution)/shard_map/ppermute | solution.py:543
  345.1 35.9 %collective-permute-start.35 = (bf16[512,1536]{1,0:T(8,128)(2,1)}, bf16[512,1536]{1,0:T(8,128)(2,1)}, u32[]{:S(2)}, u32[]{:S(2)}) collective-permute-start(bf16[512,1536]{1,0:T(8,128)(2,1)} %convolution_convert_fusion.1), channel_id=1, source_target_pairs={{0,8},{8,0},{1,9},{9,1},{2,10},{10,2},{3,11},{11,3},{4,12},{12,4},... | collective-permute-start | bytes 4718600 | tf_op jit(solution)/shard_map/ppermute | solution.py:543
  374.3 21.2 %collective-permute-start.38 = (bf16[4,32,3072]{2,1,0:T(8,128)(2,1)}, bf16[4,32,3072]{2,1,0:T(8,128)(2,1)}, u32[]{:S(2)}, u32[]{:S(2)}) collective-permute-start(bf16[4,32,3072]{2,1,0:T(8,128)(2,1)} %fusion.104), channel_id=1, source_target_pairs={{0,1},{1,0},{2,3},{3,2},{4,5},{5,4},{6,7},{7,6},{8,9},{9,8},{10,11... | collective-permute-start | bytes 2359304 | tf_op jit(solution)/shard_map/ppermute | solution.py:543
  378.7 46.4 %collective-permute-start.36 = (bf16[4,384,128]{1,2,0:T(8,128)(2,1)}, bf16[4,384,128]{1,2,0:T(8,128)(2,1)}, u32[]{:S(2)}, u32[]{:S(2)}) collective-permute-start(bf16[4,384,128]{1,2,0:T(8,128)(2,1)} %bitcast.394), channel_id=1, source_target_pairs={{0,1},{1,0},{2,3},{3,2},{4,5},{5,4},{6,7},{7,6},{8,9},{9,8},{10,11... | collective-permute-start | bytes 1179656 | tf_op jit(solution)/shard_map/ppermute | solution.py:543
  398.4 77.9 %collective-permute-start.50 = (bf16[32,6144]{1,0:T(8,128)(2,1)}, bf16[32,6144]{1,0:T(8,128)(2,1)}, u32[]{:S(2)}, u32[]{:S(2)}) collective-permute-start(bf16[32,6144]{1,0:T(8,128)(2,1)} %get-tuple-element.166), channel_id=1, source_target_pairs={{0,6},{2,0},{4,2},{6,4},{1,7},{3,1},{5,3},{7,5},{8,14},{10,8},{12,... | collective-permute-start | bytes 1179656 | tf_op jit(solution)/shard_map/ppermute | solution.py:543
  412.3 64.5 %collective-permute-start.49 = (bf16[32,6144]{1,0:T(8,128)(2,1)}, bf16[32,6144]{1,0:T(8,128)(2,1)}, u32[]{:S(2)}, u32[]{:S(2)}) collective-permute-start(bf16[32,6144]{1,0:T(8,128)(2,1)} %get-tuple-element.167), channel_id=1, source_target_pairs={{0,4},{2,6},{4,0},{6,2},{1,5},{3,7},{5,1},{7,3},{8,12},{10,14},{12... | collective-permute-start | bytes 1179656 | tf_op jit(solution)/shard_map/ppermute | solution.py:543
  412.3 64.5 %collective-permute-start.48 = (bf16[32,6144]{1,0:T(8,128)(2,1)}, bf16[32,6144]{1,0:T(8,128)(2,1)}, u32[]{:S(2)}, u32[]{:S(2)}) collective-permute-start(bf16[32,6144]{1,0:T(8,128)(2,1)} %get-tuple-element.165), channel_id=1, source_target_pairs={{0,2},{2,4},{4,6},{6,0},{1,3},{3,5},{5,7},{7,1},{8,10},{10,12},{12... | collective-permute-start | bytes 1179656 | tf_op jit(solution)/shard_map/ppermute | solution.py:543
  427.8 30.9 %collective-permute-start.53 = (bf16[384,128]{0,1:T(8,128)(2,1)}, bf16[384,128]{0,1:T(8,128)(2,1)}, u32[]{:S(2)}, u32[]{:S(2)}) collective-permute-start(bf16[384,128]{0,1:T(8,128)(2,1)} %get-tuple-element.193), channel_id=1, source_target_pairs={{6,0},{7,1},{14,8},{15,9},{22,16},{23,17},{30,24},{31,25}} | collective-permute-start | bytes 294920 | tf_op jit(solution)/shard_map/ppermute | solution.py:549
  429.1 40.8 %collective-permute-start.52 = (bf16[384,128]{0,1:T(8,128)(2,1)}, bf16[384,128]{0,1:T(8,128)(2,1)}, u32[]{:S(2)}, u32[]{:S(2)}) collective-permute-start(bf16[384,128]{0,1:T(8,128)(2,1)} %get-tuple-element.194), channel_id=1, source_target_pairs={{4,0},{6,2},{5,1},{7,3},{12,8},{14,10},{13,9},{15,11},{20,16},{22,... | collective-permute-start | bytes 294920 | tf_op jit(solution)/shard_map/ppermute | solution.py:549
  469.9 22.7 %collective-permute-start.44 = (bf16[2,4,32,1536]{3,2,1,0:T(8,128)(2,1)}, bf16[2,4,32,1536]{3,2,1,0:T(8,128)(2,1)S(1)}, u32[]{:S(2)}, u32[]{:S(2)}) collective-permute-start(bf16[2,4,32,1536]{3,2,1,0:T(8,128)(2,1)} %fusion.102), channel_id=1, source_target_pairs={{0,1},{1,0},{2,3},{3,2},{4,5},{5,4},{6,7},{7,6},{8,9},{9,8},{10,11... | collective-permute-start | bytes 2359304 | tf_op jit(solution)/shard_map/ppermute | solution.py:543
  474.1 47.0 %collective-permute-start.45 = (bf16[2,4,32,2048]{3,2,1,0:T(8,128)(2,1)}, bf16[2,4,32,2048]{3,2,1,0:T(8,128)(2,1)}, u32[]{:S(2)}, u32[]{:S(2)}) collective-permute-start(bf16[2,4,32,2048]{3,2,1,0:T(8,128)(2,1)} %bitcast.385), channel_id=1, source_target_pairs={{0,16},{16,0},{1,17},{17,1},{2,18},{18,2},{3,19},{19,3},{4,20},{20... | collective-permute-start | bytes 3145736 | tf_op jit(solution)/shard_map/ppermute | solution.py:543
  476.3 20.6 %collective-permute-start.46 = (bf16[4,384,128]{1,2,0:T(8,128)(2,1)}, bf16[4,384,128]{1,2,0:T(8,128)(2,1)S(1)}, u32[]{:S(2)}, u32[]{:S(2)}) collective-permute-start(bf16[4,384,128]{1,2,0:T(8,128)(2,1)} %bitcast.393), channel_id=1, source_target_pairs={{0,1},{1,0},{2,3},{3,2},{4,5},{5,4},{6,7},{7,6},{8,9},{9,8},{10,11... | collective-permute-start | bytes 1179656 | tf_op jit(solution)/shard_map/ppermute | solution.py:543
  497.0 20.7 %collective-permute-start.56 = (bf16[384,128]{0,1:T(8,128)(2,1)S(1)}, bf16[384,128]{0,1:T(8,128)(2,1)S(1)}, u32[]{:S(2)}, u32[]{:S(2)}) collective-permute-start(bf16[384,128]{0,1:T(8,128)(2,1)S(1)} %get-tuple-element.196), channel_id=1, source_target_pairs={{6,0},{7,1},{14,8},{15,9},{22,16},{23,17},{30,24},{31,25}} | collective-permute-start | bytes 294920 | tf_op jit(solution)/shard_map/ppermute | solution.py:549
  532.8 47.6 %collective-permute-start.70 = (bf16[512,896]{1,0:T(8,128)(2,1)}, bf16[512,896]{1,0:T(8,128)(2,1)}, u32[]{:S(2)}, u32[]{:S(2)}) collective-permute-start(bf16[512,896]{1,0:T(8,128)(2,1)} %convolution_convert_fusion.8), channel_id=1, source_target_pairs={{0,8},{8,0},{1,9},{9,1},{2,10},{10,2},{3,11},{11,3},{4,12},{12,4},... | collective-permute-start | bytes 2752520 | tf_op jit(solution)/shard_map/ppermute | solution.py:543
  563.7 30.4 %collective-permute-start.57 = (bf16[512,1792]{1,0:T(8,128)(2,1)}, bf16[512,1792]{1,0:T(8,128)(2,1)}, u32[]{:S(2)}, u32[]{:S(2)}) collective-permute-start(bf16[512,1792]{1,0:T(8,128)(2,1)} %convolution_convert_fusion), channel_id=1, source_target_pairs={{0,8},{8,0},{1,9},{9,1},{2,10},{10,2},{3,11},{11,3},{4,12},{12,4},... | collective-permute-start | bytes 5505032 | tf_op jit(solution)/shard_map/ppermute | solution.py:543
  594.3 23.1 %collective-permute-start.72 = (bf16[4,32,896]{2,1,0:T(8,128)(2,1)S(1)}, bf16[4,32,896]{2,1,0:T(8,128)(2,1)S(1)}, u32[]{:S(2)}, u32[]{:S(2)}) collective-permute-start(bf16[4,32,896]{2,1,0:T(8,128)(2,1)S(1)} %fusion.177), channel_id=1, source_target_pairs={{0,1},{1,0},{2,3},{3,2},{4,5},{5,4},{6,7},{7,6},{8,9},{9,8},{10,11... | collective-permute-start | bytes 688136 | tf_op jit(solution)/shard_map/ppermute | solution.py:543
  604.8 21.7 %collective-permute-start.68 = (bf16[2,4,32,1792]{3,2,1,0:T(8,128)(2,1)S(1)}, bf16[2,4,32,1792]{3,2,1,0:T(8,128)(2,1)S(1)}, u32[]{:S(2)}, u32[]{:S(2)}) collective-permute-start(bf16[2,4,32,1792]{3,2,1,0:T(8,128)(2,1)S(1)} %fusion.98), channel_id=1, source_target_pairs={{0,1},{1,0},{2,3},{3,2},{4,5},{5,4},{6,7},{7,6},{8,9},{9,8},{10,11... | collective-permute-start | bytes 2752520 | tf_op jit(solution)/shard_map/ppermute | solution.py:543
  (219 other events, 2362.6 us)
Sparse Core Ops, SparseCore 0:
  11.6 143.4 all-gather.1

commit v4 on v3

--- a/solution.py
+++ b/solution.py
@@ -571,7 +571,6 @@
 
 def gather_stages(shard):
     parts = [shard] + [shifted(shard, "z", -k) for k in range(1, lax.axis_size("z"))]
-    started = parts[-1]
     block = jnp.concatenate(parts, axis=0)[None, None]
     middle = shard.shape[1] // 256 * 128
     halves = []
@@ -581,7 +580,7 @@
             half = jnp.concatenate(parts, axis="yx".index(axis))
         halves.append(half.reshape(-1, half.shape[-1]))
     own = jnp.concatenate(halves, axis=1)
-    return (own, shifted(own, "core", 1)), started
+    return own, shifted(own, "core", 1)
 
 
 def times_rows(values, pair):
@@ -593,13 +592,14 @@
     return jnp.concatenate([back_product(values, pair[0]), back_product(values, pair[1])], axis=1)
 
 
-def keep_own(total, axis, dim, received=None):
+def keep_own(total, axis, dim, received, hold=()):
     kept = lax.index_in_dim(total, 0, dim, False)
     for step in range(1, lax.axis_size(axis)):
         part = lax.index_in_dim(total, step, dim, False)
         got = shifted(part.astype(jnp.bfloat16), axis, step)
-        if received is not None:
-            received.append(got)
+        received.append(got)
+        if hold:
+            got = after(got, *hold)
         kept = kept + got.astype(jnp.float32)
     return kept
 
@@ -617,17 +617,31 @@
     return parts[0] if len(parts) == 1 else jnp.concatenate(parts, axis=-1)
 
 
-def chip_sums(by_x, by_y, received):
+def first_sums(by_x, by_y, received):
     by_x = side_by_side([keep_own(total, "x", 1, received) for total in by_x])
     by_y = side_by_side([keep_own(total, "y", 0, received) for total in by_y])
-    later = []
-    by_x = keep_own(by_x, "y", 0, later)
-    by_y = keep_own(by_y, "x", 0, later)
-    return keep_own(jnp.concatenate([by_x, by_y], axis=-1), "z", 0), later
-
-
-def sum_everywhere(values):
+    return by_x, by_y
+
+
+def layer_sums(by_x, by_y, received, hold=()):
+    by_x = keep_own(by_x, "y", 0, received, hold)
+    by_y = keep_own(by_y, "x", 0, received, hold)
+    return jnp.concatenate([by_x, by_y], axis=-1)
+
+
+def send_layers(total):
+    parts = [total[step].astype(jnp.bfloat16) for step in range(1, total.shape[0])]
+    return [total[0]] + [shifted(part, "z", step + 1) for step, part in enumerate(parts)]
+
+
+def sum_layers(parts):
+    return sum(part.astype(jnp.float32) for part in parts)
+
+
+def sum_everywhere(values, holds):
     for axis in ("core", "x", "y", "z"):
+        if axis in holds:
+            values = after(values, *holds[axis])
         count = lax.axis_size(axis)
         step = 1
         while step < count:
@@ -636,40 +650,54 @@
     return values
 
 
-def carried(state, tail, direction):
+def send_states(state, tail, direction):
     depth, width = state.shape
     half = width // 2
     at_x = lax.axis_index("x")
     is_second = (at_x == 1) if direction == 1 else (at_x == 0)
     packed = jnp.concatenate([state, tail], axis=0).astype(jnp.bfloat16)
-    other = shifted(packed, "x", 1).astype(jnp.float32)
+    other = shifted(packed, "x", 1)
     own = packed.astype(jnp.float32)
-    first = jnp.where(is_second, other, own)
-    second = jnp.where(is_second, own, other)
-    first_state, first_tail = first[:depth], first[depth : depth + 1]
-    second_tail = second[depth : depth + 1]
+    first = jnp.where(is_second, other.astype(jnp.float32), own)
+    second = jnp.where(is_second, own, other.astype(jnp.float32))
     pair = jnp.concatenate(
-        [second_tail * first_state + second[:depth], first[depth:] * second[depth:]], axis=0
+        [
+            second[depth : depth + 1] * first[:depth] + second[:depth],
+            first[depth:] * second[depth:],
+        ],
+        axis=0,
     )
     mine = jnp.where(at_x == 0, pair[:, :half], pair[:, half:]).astype(jnp.bfloat16)
+    steps = range(1, lax.axis_size("z"))
+    passed = [moved_along(mine, "z", direction * step) for step in steps]
+    return jnp.where(is_second, first, 0.0), other, passed
+
+
+def carried(behind, passed, direction):
+    depth, half = behind.shape[0] - 8, behind.shape[1] // 2
+    at_x = lax.axis_index("x")
+    is_second = (at_x == 1) if direction == 1 else (at_x == 0)
     total = jnp.zeros((depth, half), jnp.float32)
     fade = jnp.ones((1, half), jnp.float32)
-    for step in range(1, lax.axis_size("z")):
-        got = moved_along(mine, "z", direction * step).astype(jnp.float32)
+    for got in passed:
+        got = got.astype(jnp.float32)
         total = total + fade * got[:depth]
         fade = fade * got[depth : depth + 1]
     total = total.astype(jnp.bfloat16)
     rest = shifted(total, "x", 1)
     left, right = jnp.where(at_x == 0, total, rest), jnp.where(at_x == 0, rest, total)
     carry = jnp.concatenate([left, right], axis=1).astype(jnp.float32)
-    return jnp.where(is_second, first_tail * carry + first_state, carry)
-
-
-def gather_keys(own):
-    blocks = [moved_along(own, "z", step) if step else own for step in range(lax.axis_size("z"))]
+    return jnp.where(is_second, behind[depth : depth + 1], 1.0) * carry + behind[:depth]
+
+
+def keys_behind(own):
+    return [moved_along(own, "z", step) if step else own for step in range(lax.axis_size("z"))]
+
+
+def all_slots(blocks):
     blocks = jnp.stack(blocks)
     slots = jnp.stack([blocks, shifted(blocks, "x", 1)], axis=1)
-    return slots.reshape(-1, *own.shape)
+    return slots.reshape(-1, *blocks.shape[1:])
 
 
 def swap_key_grads(slots):
@@ -678,11 +706,13 @@
     return total[:, 0], swapped
 
 
-def sum_key_grads(kept, swapped):
+def sum_key_grads(kept, swapped, received):
     kept = kept + swapped.astype(jnp.float32)
     own = kept[0]
     for step in range(1, kept.shape[0]):
-        own = own + moved_along(kept[step].astype(jnp.bfloat16), "z", -step).astype(jnp.float32)
+        got = moved_along(kept[step].astype(jnp.bfloat16), "z", -step)
+        received.append(got)
+        own = own + got.astype(jnp.float32)
     return own
 
 
@@ -718,13 +748,15 @@
     taps = jnp.concatenate([conv_weight, conv_bias[None]], axis=0)
     tap_columns = -(-taps.size // own_rows)
     tap_shard = jnp.pad(taps.reshape(-1), (0, tap_columns * own_rows - taps.size))
-    step_at = channels + w_keyval.shape[1]
+    query_at = channels + w_keyval.shape[1]
+    step_at = query_at + query_width
     gain_at = step_at + w_step.shape[1]
     tap_at = gain_at + 2
     conv_shard = jnp.concatenate(
         [
             w_in[:, inner_width:],
             w_keyval,
+            w_query,
             w_step,
             gain_one[:, None],
             gain_two[:, None],
@@ -733,34 +765,33 @@
         ],
         axis=1,
     )
-    gate_shard = jnp.concatenate([w_in[:, :inner_width], w_query], axis=1)
-    out_shard = jnp.concatenate([w_mix_out.T, w_attn_out.T], axis=1)
-    down_shard = w_down.T
-    late_shard = jnp.concatenate([out_shard, w_gate_up, down_shard], axis=1)
-    late = lax.all_gather(late_shard, every_axis, axis=0, tiled=True)
-    full_out, full_gate, full_up, full_down = jnp.split(
-        late, [out_shard.shape[1], out_shard.shape[1] + FF, out_shard.shape[1] + 2 * FF], axis=1
-    )
-    conv_pair, started = gather_stages(conv_shard)
-    gate_pair, _ = gather_stages(after(gate_shard, started))
-
-    order = width_order(width)
-    inputs = plain_dot(tokens[0], order)
+    late_shards = [w_in[:, :inner_width], w_mix_out.T, w_attn_out.T, w_gate_up, w_down.T]
+    late = lax.all_gather(jnp.concatenate(late_shards, axis=1), every_axis, axis=0, tiled=True)
+    out_at = inner_width
+    ff_at = out_at + inner_width + query_width
+    full_gate_z, full_out, full_gate, full_up, full_down = jnp.split(
+        late, [out_at, ff_at, ff_at + FF, ff_at + 2 * FF], axis=1
+    )
+    conv_pair = gather_stages(conv_shard)
+
+    order = lax.optimization_barrier(width_order(width))
+    inputs = tokens[0].astype(jnp.float32)
+    inputs_rows = plain_dot(tokens[0], order)
     grad_output = cotangent[0]
     small = jnp.concatenate([half[:, gain_at : tap_at + tap_columns] for half in conv_pair], axis=0)
-    gain_one_float = small[:, 0].astype(jnp.float32)
     small_rows = lax.dot_general(
         small, order, (((0,), (1,)), ((), ())), preferred_element_type=jnp.float32
     )
-    gain_two_float = small_rows[1]
+    gain_one_float, gain_two_float = small_rows[0], small_rows[1]
     tap_all = small_rows[2:].reshape(tap_columns, device_count, own_rows)
     tap_all = jnp.swapaxes(tap_all, 0, 1).reshape(device_count, -1)[:, : taps.size]
     tap_all = jnp.swapaxes(tap_all.reshape(-1, *taps.shape), 0, 1).reshape(taps.shape[0], channels)
 
-    normed = rms_norm(inputs, gain_one_float).astype(jnp.bfloat16)
+    normed = rms_norm(inputs_rows, small[:, 0].astype(jnp.float32)).astype(jnp.bfloat16)
     conv_projected = times_rows(normed, conv_pair)
     conv_input = conv_projected[:, :channels].astype(jnp.bfloat16)
-    keyval_raw = conv_projected[:, channels:step_at]
+    keyval_raw = conv_projected[:, channels:query_at]
+    query_raw = conv_projected[:, query_at:step_at]
     step_raw = conv_projected[:, step_at:gain_at]
     positions = (at_z * lax.axis_size("x") + at_x) * row_count + jnp.arange(
         row_count, dtype=jnp.int32
@@ -772,8 +803,8 @@
     own_keyval = jnp.concatenate(
         [key_cols.reshape(by_head), keyval_cols[key_width:].reshape(by_head)], axis=1
     ).reshape(2 * key_width, row_count)
-    all_keyval = gather_keys(own_keyval.T.astype(jnp.bfloat16))
-    all_cols = jnp.swapaxes(all_keyval, 1, 2)
+    key_blocks = keys_behind(own_keyval.T.astype(jnp.bfloat16))
+    query_cols = turn_rows(query_raw.T, cosine, sine).astype(jnp.bfloat16)
     border = lax.ppermute(
         conv_input[row_count - (CONV - 1) :],
         seq_axes,
@@ -788,15 +819,18 @@
     lower = jnp.tril(jnp.ones((chunk_rows, chunk_rows), jnp.float32))
     cum = jnp.stack([jnp.dot(lower, c, precision=highest_precision) for c in by_chunk])
     cum = cum.reshape(log_decay.shape)
-    y_local, grown, fresh_state, tail = ssd_local(act, cum, step_size)
+    y_local, grown, fresh_state, tail, *key_blocks = after(
+        (*ssd_local(act, cum, step_size), *key_blocks)
+    )
+    all_keyval = all_slots(key_blocks)
+    all_cols = jnp.swapaxes(all_keyval, 1, 2)
     y_local = y_local.reshape(row_count, inner_width)
     grown = grown.reshape(row_count, inner_width)
-    carry_state = carried(fresh_state, tail, 1)
-
-    gate_projected = times_rows(normed, gate_pair)
-    gate_z = gate_projected[:, :inner_width]
-    query_cols = turn_rows(gate_projected[:, inner_width:].T, cosine, sine).astype(jnp.bfloat16)
-    attended_cols, logs = attend(place, query_cols, all_keyval, all_cols)
+    behind, other_state, passed = send_states(fresh_state, tail, 1)
+    attended_cols, logs = attend(place, after(query_cols, other_state), all_keyval, all_cols)
+    attended_cols, logs, *passed = after((attended_cols, logs, *passed))
+    carry_state = carried(behind, passed, 1)
+    gate_z = plain_dot(back_product(normed, order).astype(jnp.bfloat16), full_gate_z)
     attention_rows = attended_cols.T.astype(jnp.bfloat16)
 
     skip_row = jnp.repeat(skip_weight, MHEAD_DIM)[None, :]
@@ -809,7 +843,7 @@
     gate_sigmoid = jax.nn.sigmoid(gate_z)
     mixer = (ssm_y * gate_z * gate_sigmoid).astype(jnp.bfloat16)
     branches = jnp.concatenate([mixer, attention_rows], axis=1)
-    hidden = tokens[0].astype(jnp.float32) + back_product(branches, full_out)
+    hidden = inputs + back_product(branches, full_out)
     normed_two = rms_norm(hidden, gain_two_float).astype(jnp.bfloat16)
     gate_part = plain_dot(normed_two, full_gate)
     up_part = plain_dot(normed_two, full_up)
@@ -834,7 +868,10 @@
     down_a = core_sum(grad_output_rows, activated[:, :down_half], [])
     down_b = core_sum(grad_output_rows, activated[:, down_half:], [])
     ff_got = []
-    ff_sums, ff_later = chip_sums([gate_total, down_a], [up_total, down_b], ff_got)
+    ff_later = []
+    ff_parts = send_layers(
+        layer_sums(*first_sums([gate_total, down_a], [up_total, down_b], ff_got), ff_later)
+    )
     grad_normed_two = back_product(after(grad_gate, *core_got), full_gate) + back_product(grad_up, full_up)
     _, pull_two = jax.vjp(rms_norm, hidden, gain_two_float)
     grad_hidden_norm, grad_gain_two = pull_two(grad_normed_two)
@@ -845,14 +882,17 @@
     grad_y = grad_mixer * gate_z * gate_sigmoid
     grad_gate_z = grad_mixer * ssm_y * gate_sigmoid * (1.0 + gate_z * (1.0 - gate_sigmoid))
     from_output = outer_product(output_low, (grown * grad_y).astype(jnp.bfloat16))
-    grad_end = carried(from_output, tail, -1)
+    behind, _, passed = send_states(from_output, tail, -1)
 
     grad_attention = grad_branches[:, inner_width:].astype(jnp.bfloat16)
     out_got = []
     out_total = core_sum(reordered(grad_branch), branches, out_got)
-    in_gate_total = core_sum(normed, grad_gate_z.astype(jnp.bfloat16), out_got)
+    grad_gate_low = grad_gate_z.astype(jnp.bfloat16)
+    in_gate_total = core_sum(normed, grad_gate_low, out_got)
+    grad_normed_part = back_product(grad_gate_low, full_gate_z)
     grad_cols = grad_attention.T
     query_rows = query_cols.T
+
     def one_group(group, grad_cols):
         return attend_back(
             group,
@@ -872,31 +912,37 @@
     kept_a, swapped_a = swap_key_grads(slots_a)
     query_b, slots_b = one_group(1, after(grad_cols, ff_got[0], ff_got[2], *out_got))
     before_ssd = (query_b, *ff_later, swapped_a)
-    query_b, slots_b, kept_a, swapped_a = after((query_b, slots_b, kept_a, swapped_a), *before_ssd)
-    own_a = sum_key_grads(kept_a, swapped_a)
+    query_b, slots_b, kept_a, swapped_a, *passed = after(
+        (query_b, slots_b, kept_a, swapped_a, *passed), *before_ssd
+    )
+    grad_end = carried(behind, passed, -1)
+    key_got = []
+    own_a = sum_key_grads(kept_a, swapped_a, key_got)
     kept_b, swapped_b = swap_key_grads(slots_b)
-    own_b = sum_key_grads(kept_b, swapped_b)
+    own_b = sum_key_grads(kept_b, swapped_b, key_got)
     own_grads = [own_a, own_b]
-    key_got = [swapped_b]
     grad_query_cols = jnp.concatenate([query_a, query_b], axis=0)
     mid_got = []
-    mid_sums, mid_later = chip_sums([in_gate_total], [out_total], mid_got)
+    mid_both = first_sums([in_gate_total], [out_total], mid_got)
     grad_query = turn_rows(grad_query_cols, cosine, -sine).T.astype(jnp.bfloat16)
     own_cols = jnp.concatenate(own_grads, axis=1).T.reshape(KVHEADS, 2, HEAD_DIM, row_count)
     grad_keys = turn_rows(own_cols[:, 0].reshape(key_width, row_count), cosine, -sine)
     grad_keyval = jnp.concatenate([grad_keys, own_cols[:, 1].reshape(key_width, row_count)], axis=0)
     grad_keyval = grad_keyval.T.astype(jnp.bfloat16)
 
+    ssd_grad = after(
+        grad_y, *before_ssd, swapped_b, *out_got, grad_normed_part
+    )
     grad_act, grad_step_size, grad_log, grad_skip = ssd_back(
-        act, cum, step_size, after(grad_y, *before_ssd), carry_state, grad_end, skip_row
-    )
-    grad_act, grad_step_size, grad_log = after(
-        (grad_act, grad_step_size, grad_log), *mid_got, *key_got
-    )
+        act, cum, step_size, ssd_grad, carry_state, grad_end, skip_row
+    )
+    grad_act, grad_step_size, grad_log = after((grad_act, grad_step_size, grad_log), *key_got)
     grad_step_size = grad_step_size - grad_log * jnp.exp(mamba_heads[0])[None, :]
     grad_step_raw = grad_step_size * jax.nn.sigmoid(step_raw + mamba_heads[1][None, :])
     grad_heads = jnp.stack([jnp.sum(grad_log * log_decay, axis=0), jnp.sum(grad_step_raw, axis=0)])
     grad_extended, grad_conv_weight, grad_conv_bias = pull_conv(grad_act)
+    grad_extended, *ff_parts = after((grad_extended, *ff_parts), *mid_got)
+    ff_sums = sum_layers(ff_parts)
     rim_back = lax.ppermute(
         grad_extended[: CONV - 1],
         seq_axes,
@@ -905,39 +951,31 @@
     grad_conv_input = grad_extended[CONV - 1 :] + jnp.pad(
         rim_back, ((row_count - (CONV - 1), 0), (0, 0))
     )
-    grad_conv_low = after(grad_conv_input.astype(jnp.bfloat16), ff_sums)
     grad_step_low = jnp.pad(
         grad_step_raw.astype(jnp.bfloat16), ((0, 0), (0, conv_shard.shape[1] - gain_at))
     )
-    grad_few = jnp.concatenate([grad_query, grad_keyval, grad_step_low], axis=1)
-    last_core_got, last_got = [], []
+    grad_few = jnp.concatenate([grad_keyval, grad_query, grad_step_low], axis=1)
+    few_core_got, last_core_got = [], []
+    few_total = core_sum(normed, grad_few, few_core_got)
+    grad_conv_low = after(grad_conv_input.astype(jnp.bfloat16), *few_core_got)
     conv_total = core_sum(normed, grad_conv_low, last_core_got)
-    few_total = core_sum(normed, grad_few, [])
-    last_sums, _ = chip_sums([conv_total], [few_total], last_got)
-    grad_gate_half = jnp.concatenate([grad_gate_z.astype(jnp.bfloat16), grad_query], axis=1)
-    grad_conv_half = jnp.concatenate([grad_conv_low, grad_keyval, grad_step_low], axis=1)
-    grad_normed = times_rows_back(grad_gate_half, gate_pair) + times_rows_back(
-        grad_conv_half, conv_pair
-    )
-    _, pull_one = jax.vjp(rms_norm, inputs, gain_one_float)
-    grad_input_norm, grad_gain_one = pull_one(grad_normed)
-    input_grad = lax.dot_general(
-        grad_input_norm,
+    last_got, last_later = [], []
+    mid_parts = send_layers(layer_sums(*mid_both, [], last_core_got))
+    last_parts = send_layers(
+        layer_sums(*first_sums([conv_total], [few_total], last_got), last_later)
+    )
+    last_parts, *mid_parts = after((tuple(last_parts), *mid_parts), *last_later)
+    last_sums, mid_sums = sum_layers(last_parts), sum_layers(mid_parts)
+    grad_normed = lax.dot_general(
+        times_rows_back(jnp.concatenate([grad_conv_low, grad_few], axis=1), conv_pair),
         order.astype(jnp.float32),
         (((1,), (1,)), ((), ())),
         precision=lax.Precision.HIGH,
         preferred_element_type=jnp.float32,
     )
-    input_grad = (grad_hidden + input_grad)[None]
-
-    def usual_gain(grad):
-        rows = jnp.broadcast_to(grad[None], (8, width))
-        return lax.dot_general(
-            rows,
-            order.astype(jnp.float32),
-            (((1,), (1,)), ((), ())),
-            precision=highest_precision,
-        )[:1]
+    _, pull_one = jax.vjp(rms_norm, inputs, gain_one_float)
+    grad_input_norm, grad_gain_one = pull_one(grad_normed + grad_normed_part)
+    input_grad = (grad_hidden + grad_input_norm)[None]
 
     def padded(row):
         return jnp.pad(row, ((0, 0), (0, channels - row.shape[1])))
@@ -947,16 +985,20 @@
         axis=1,
     )
     summed = sum_everywhere(
-        after(jnp.concatenate(
-            [
-                grad_conv_weight,
-                grad_conv_bias[None],
-                padded(grad_gain_two[None]),
-                padded(usual_gain(grad_gain_one)),
-                padded(head_row),
-            ],
-            axis=0,
-        ), *last_core_got)
+        after(
+            jnp.concatenate(
+                [
+                    grad_conv_weight,
+                    grad_conv_bias[None],
+                    padded(grad_gain_two[None]),
+                    padded(grad_gain_one[None]),
+                    padded(head_row),
+                ],
+                axis=0,
+            ),
+            *last_core_got,
+        ),
+        {"y": last_got, "z": last_later},
     )
     device = lax.axis_index(every_axis)
     own_channels = conv_weight.shape[1]
@@ -964,20 +1006,18 @@
     own_gain_two = lax.dynamic_slice_in_dim(summed[CONV + 1], device * own_rows, own_rows)
     own_gain_one = lax.dynamic_slice_in_dim(summed[CONV + 2], device * own_rows, own_rows)
     head_sums_row = summed[CONV + 3]
-    query_at = channels + query_width
-    step_from = query_at + w_keyval.shape[1]
     return (
         output,
         input_grad,
         own_gain_one,
         jnp.concatenate([mid_sums[:, :inner_width], last_sums[:, :channels]], axis=1),
-        last_sums[:, step_from : step_from + w_step.shape[1]],
+        last_sums[:, step_at:gain_at],
         own_taps[:CONV],
         own_taps[CONV],
         head_sums_row[: 2 * MHEADS].reshape(2, MHEADS),
         head_sums_row[2 * MHEADS : 3 * MHEADS],
+        last_sums[:, query_at:step_at],
         last_sums[:, channels:query_at],
-        last_sums[:, query_at:step_from],
         mid_sums[:, 2 * inner_width :].T,
         mid_sums[:, inner_width : 2 * inner_width].T,
         own_gain_two,

time: 675 us -> 648 us (0.960)
  waiting for transfers between devices: 191 us -> 169 us
  other arithmetic: 65.6 us -> 82.3 us
  starting transfers between devices: 163 us -> 151 us
  matrix products: 111 us -> 99.5 us
    ppermute x15, waiting for transfers between devices: 43 us -> 10.9 us  [moved_along(): return lax.ppermute(block, axis, route)]
    ppermute x5, waiting for transfers between devices: 11.5 us -> 38.7 us  [sum_everywhere(): lax.ppermute(values, axis, [(i, i ^ step) for i in range(count)])]
    ppermute x54 -> x46, waiting for transfers between devices: 137 us -> 120 us  [shifted(): lax.ppermute(block, axis, [(i, (i + distance) % count) for i in range(cou...]
    unnamed x348 -> x264, local copies, waits for them, and re-layouts: 40.3 us -> 31.4 us
    ppermute x54 -> x46, starting transfers between devices: 93.8 us -> 90.2 us  [shifted(): lax.ppermute(block, axis, [(i, (i + distance) % count) for i in range(cou...]
    dot_general x8 -> x7, matrix products: 30.9 us -> 27.3 us  [back_product(): lax.dot_general(grad_rows, weight_matrix, (((1,), (1,)), ((), ())), prefe...]
    dot_general x13 -> x12, matrix products: 42 us -> 40.3 us  [plain_dot(): return jnp.dot(left, right, preferred_element_type=jnp.float32)]
    add x17 -> x14, other arithmetic: 15 us -> 14.4 us  [keep_own(): kept = kept + got.astype(jnp.float32)]
  transfers between devices with their start and end apart: 77 -> 69, of which waited for: 39 -> 24; matrix products, arithmetic and copies ran while one was open for 27% -> 30% of each run, Pallas kernels for 5% -> 5%
where the time goes in v4:
time: 648 us; the launch traced here: 638 us
  waiting for transfers between devices  169 us (26%)
  starting transfers between devices  151 us (23%)
  matrix products  99.5 us (15%)
  local copies, waits for them, and re-layouts  87.5 us (14%)
  other arithmetic  82.3 us (13%)
  Pallas kernels  32 us (5%)
  between operations  17 us (3%)
    ppermute x46, waiting for transfers between devices, shifted(): lax.ppermute(block, axis, [(i, (i + distance) % count) for i in range(cou...  120 us
    ppermute x46, starting transfers between devices, shifted(): lax.ppermute(block, axis, [(i, (i + distance) % count) for i in range(cou...  90.2 us
    ppermute x15, starting transfers between devices, moved_along(): return lax.ppermute(block, axis, route)  50 us
    dot_general x12, matrix products, plain_dot(): return jnp.dot(left, right, preferred_element_type=jnp.float32)  40.3 us
    ppermute x5, waiting for transfers between devices, sum_everywhere(): lax.ppermute(values, axis, [(i, i ^ step) for i in range(count)])  38.7 us
    unnamed x264, local copies, waits for them, and re-layouts  31.4 us
    dot_general x7, matrix products, back_product(): lax.dot_general(grad_rows, weight_matrix, (((1,), (1,)), ((), ())), prefe...  27.3 us
    dot_general x17, matrix products, outer_product(): lax.dot_general(left, right, (((0,), (0,)), ((), ())), preferred_element_...  27.2 us
  transfers between devices with their start and end apart: 69, of which 24 were waited for; matrix products, arithmetic and copies ran while one was open for 30% of the time, Pallas kernels for 5%

profile of v4, /device:TPU:0, one launch (start us, length us, event | category | flops | bytes accessed | tf_op | source)
XLA Modules:
  0.0 638.2 jit_solution(371615469876078813)
XLA Ops:
  28.0 14.1 %collective-permute-done.1 = bf16[32,2688]{1,0:T(8,128)(2,1)S(1)} collective-permute-done((bf16[32,2688]{1,0:T(8,128)(2,1)S(1)}, bf16[32,2688]{1,0:T(8,128)(2,1)S(1)}, u32[]{:S(2)}, u32[]{:S(2)}) %collective-permute-start.1) | collective-permute-done | bytes 172064 | tf_op jit(solution)/shard_map/ppermute | solution.py:543
  45.1 6.1 collective-permute-done.5
  56.4 19.8 %collective-permute-done.6 = bf16[1,2,128,1280]{3,2,1,0:T(8,128)(2,1)S(1)} collective-permute-done((bf16[1,2,128,1280]{3,2,1,0:T(8,128)(2,1)S(1)}, bf16[1,2,128,1280]{3,2,1,0:T(8,128)(2,1)S(1)}, u32[]{:S(2)}, u32[]{:S(2)}) %collective-permute-start.6) | collective-permute-done | bytes 655392 | tf_op jit(solution)/shard_map/ppermute | solution.py:543
  79.8 6.2 collective-permute-done.4
  104.1 4.6 fusion.246
  111.3 11.0 %collective-permute-start.9 = (bf16[384,256]{0,1:T(8,128)(2,1)S(1)}, bf16[384,256]{0,1:T(8,128)(2,1)}, u32[]{:S(2)}, u32[]{:S(2)}) collective-permute-start(bf16[384,256]{0,1:T(8,128)(2,1)S(1)} %bitcast.356), channel_id=1, source_target_pairs={{0,2},{2,4},{4,6},{1,3},{3,5},{5,7},{8,10},{10,12},{12,14},{9,11},... | collective-permute-start | bytes 589832 | tf_op jit(solution)/shard_map/ppermute | solution.py:549
  144.0 6.5 %ssd.1 = (f32[3,128,1536]{2,1,0:T(8,128)S(1)}, f32[3,128,1536]{2,1,0:T(8,128)S(1)}, f32[128,1536]{1,0:T(8,128)S(1)}, f32[8,1536]{1,0:T(8,128)S(1)}) custom-call(f32[3,128,1792]{2,1,0:T(8,128)} %bitcast.342, f32[3,128,24]{2,1,0:T(8,128)S(1)} %copy.112.cum_ref, f32[3,24,128]{2,1,0:T(8,128)S(1)} %get-tuple-element.277.cum_rows_ref, ...), custom_call_target="tpu_custom_call" | custom-call | flops 5898240000 | bytes 11010048 | tf_op jit(solution)/shard_map/ssd/pallas_call | solution.py:352
  153.5 9.5 %collective-permute-start.12 = (bf16[136,1536]{1,0:T(8,128)(2,1)S(1)}, bf16[136,1536]{1,0:T(8,128)(2,1)S(1)}, u32[]{:S(2)}, u32[]{:S(2)}) collective-permute-start(bf16[136,1536]{1,0:T(8,128)(2,1)S(1)} %pad_maximum_fusion.17), channel_id=1, source_target_pairs={{0,1},{1,0},{2,3},{3,2},{4,5},{5,4},{6,7},{7,6},{8,9},{9,8},{10,11... | collective-permute-start | bytes 1253384 | tf_op jit(solution)/shard_map/ppermute | solution.py:543
  166.0 7.5 %collective-permute-done.12 = bf16[136,1536]{1,0:T(8,128)(2,1)S(1)} collective-permute-done((bf16[136,1536]{1,0:T(8,128)(2,1)S(1)}, bf16[136,1536]{1,0:T(8,128)(2,1)S(1)}, u32[]{:S(2)}, u32[]{:S(2)}) %collective-permute-start.12) | collective-permute-done | bytes 417824 | tf_op jit(solution)/shard_map/ppermute | solution.py:543
  174.7 15.2 %collective-permute-start.14 = (bf16[136,768]{1,0:T(8,128)(2,1)}, bf16[136,768]{1,0:T(8,128)(2,1)}, u32[]{:S(2)}, u32[]{:S(2)}) collective-permute-start(bf16[136,768]{1,0:T(8,128)(2,1)} %fusion.132), channel_id=1, source_target_pairs={{0,2},{2,4},{4,6},{1,3},{3,5},{5,7},{8,10},{10,12},{12,14},{9,11},... | collective-permute-start | bytes 626696 | tf_op jit(solution)/shard_map/ppermute | solution.py:549
  189.9 5.3 collective-permute-start.15
  213.6 7.2 %fusion.50 = f32[384,1536]{1,0:T(8,128)} fusion(bf16[1024,9728]{1,0:T(8,128)(2,1)} %all-gather.2.cloned.1.call-done, bf16[1024,1024]{1,0:T(8,128)(2,1)} %copy-done.50, f32[1024,384]{1,0:T(8,128)} %copy-done.83, f32[1024]{0:T(1024)} %bitcast.377, f32[384]{0:T(512)} %copy-done.119), kind=kOutput, calls=%fused_computation.115 | convolution fusion | flops 2014838784 | bytes 9181184 | tf_op jit(solution)/shard_map/dot_general | solution.py:81
  225.2 4.5 multiply_reduce_fusion.6
  240.4 5.1 fusion.45
  251.1 4.9 fusion.92
  265.1 5.6 collective-permute-done.21
  274.2 4.9 multiply_reduce_fusion.4
  317.8 4.6 fusion.48
  322.4 9.4 %collective-permute-done.31 = bf16[136,1536]{1,0:T(8,128)(2,1)S(1)} collective-permute-done((bf16[136,1536]{1,0:T(8,128)(2,1)S(1)}, bf16[136,1536]{1,0:T(8,128)(2,1)S(1)}, u32[]{:S(2)}, u32[]{:S(2)}) %collective-permute-start.31) | collective-permute-done | bytes 417824 | tf_op jit(solution)/shard_map/ppermute | solution.py:543
  354.3 4.6 collective-permute-done.28
  361.5 5.0 collective-permute-done.29
  381.8 17.6 %collective-permute-start.43 = (bf16[32,6144]{1,0:T(8,128)(2,1)}, bf16[32,6144]{1,0:T(8,128)(2,1)}, u32[]{:S(2)}, u32[]{:S(2)}) collective-permute-start(bf16[32,6144]{1,0:T(8,128)(2,1)} %get-tuple-element.233), channel_id=1, source_target_pairs={{0,2},{2,4},{4,6},{6,0},{1,3},{3,5},{5,7},{7,1},{8,10},{10,12},{12... | collective-permute-start | bytes 1179656 | tf_op jit(solution)/shard_map/ppermute | solution.py:543
  422.1 10.8 %collective-permute-done.37 = bf16[384,128]{0,1:T(8,128)(2,1)} collective-permute-done((bf16[384,128]{0,1:T(8,128)(2,1)}, bf16[384,128]{0,1:T(8,128)(2,1)}, u32[]{:S(2)}, u32[]{:S(2)}) %collective-permute-start.37) | collective-permute-done | bytes 98336 | tf_op jit(solution)/shard_map/ppermute | solution.py:549
  432.9 11.2 %collective-permute-start.44 = (bf16[32,6144]{1,0:T(8,128)(2,1)}, bf16[32,6144]{1,0:T(8,128)(2,1)}, u32[]{:S(2)}, u32[]{:S(2)}) collective-permute-start(bf16[32,6144]{1,0:T(8,128)(2,1)} %get-tuple-element.232), channel_id=1, source_target_pairs={{0,4},{2,6},{4,0},{6,2},{1,5},{3,7},{5,1},{7,3},{8,12},{10,14},{12... | collective-permute-start | bytes 1179656 | tf_op jit(solution)/shard_map/ppermute | solution.py:543
  449.9 8.5 %collective-permute-done.36 = bf16[128,768]{1,0:T(8,128)(2,1)S(1)} collective-permute-done((bf16[128,768]{1,0:T(8,128)(2,1)S(1)}, bf16[128,768]{1,0:T(8,128)(2,1)S(1)}, u32[]{:S(2)}, u32[]{:S(2)}) %collective-permute-start.36) | collective-permute-done | bytes 196640 | tf_op jit(solution)/shard_map/ppermute | solution.py:543
  467.9 14.3 %ssd_back.1 = (f32[3,128,1792]{2,1,0:T(8,128)}, f32[3,128,24]{2,1,0:T(8,128)S(1)}, f32[3,128,24]{2,1,0:T(8,128)S(1)}, f32[1,1536]{1,0:T(1,128)S(1)}) custom-call(f32[3,128,1792]{2,1,0:T(8,128)} %bitcast.343, f32[3,128,24]{2,1,0:T(8,128)S(1)} %copy-done.24, f32[3,24,128]{2,1,0:T(8,128)S(1)} %copy-done.28, f32[3,128,24]{2,1,0:T(8,128)S(1)} %bitcast.327, ...), custom_call_target="tpu_custom_call" | custom-call | flops 14745600000 | bytes 11010048 | tf_op jit(solution)/shard_map/ssd_back/pallas_call | solution.py:506
  483.9 7.9 %collective-permute-start.45 = (bf16[32,6144]{1,0:T(8,128)(2,1)}, bf16[32,6144]{1,0:T(8,128)(2,1)}, u32[]{:S(2)}, u32[]{:S(2)}) collective-permute-start(bf16[32,6144]{1,0:T(8,128)(2,1)} %get-tuple-element.231), channel_id=1, source_target_pairs={{0,6},{2,0},{4,2},{6,4},{1,7},{3,1},{5,3},{7,5},{8,14},{10,8},{12,... | collective-permute-start | bytes 1179656 | tf_op jit(solution)/shard_map/ppermute | solution.py:543
  502.1 6.8 %multiply_reduce_fusion.3 = (f32[1792]{0:T(1024)S(1)}, f32[1792]{0:T(1024)S(1)}, f32[1792]{0:T(1024)S(1)}, f32[1792]{0:T(1024)S(1)}, f32[1792]{0:T(1024)S(1)}, /*index=5*/f32[384,1792]{1,0:T(8,128)S(1)}) fusion(f32[387,1792]{1,0:T(8,128)} %copy-done.33, f32[384,1792]{1,0:T(8,128)} %get-tuple-element.222, f32[384,1792]{1,0:T(8,128)S(1)} %bitcast.347), kind=kLoop, calls=%fused_computation.123 | loop fusion | flops 12377344 | bytes 19303424 | tf_op jit(solution)/shard_map/transpose(jvp())/reduce_sum | solution.py:70
  560.7 19.4 %collective-permute-done.52 = f32[8,1792]{1,0:T(8,128)S(1)} collective-permute-done((f32[8,1792]{1,0:T(8,128)S(1)}, f32[8,1792]{1,0:T(8,128)S(1)}, u32[]{:S(2)}, u32[]{:S(2)}) %collective-permute-start.52) | collective-permute-done | bytes 57376 | tf_op jit(solution)/shard_map/ppermute | solution.py:648
  586.5 7.8 %collective-permute-done.56 = bf16[4,32,1792]{2,1,0:T(8,128)(2,1)S(1)} collective-permute-done((bf16[4,32,1792]{2,1,0:T(8,128)(2,1)S(1)}, bf16[4,32,1792]{2,1,0:T(8,128)(2,1)S(1)}, u32[]{:S(2)}, u32[]{:S(2)}) %collective-permute-start.56) | collective-permute-done | bytes 458784 | tf_op jit(solution)/shard_map/ppermute | solution.py:543
  595.6 6.5 %collective-permute-done.58 = f32[8,1792]{1,0:T(8,128)S(1)} collective-permute-done((f32[8,1792]{1,0:T(8,128)S(1)}, f32[8,1792]{1,0:T(8,128)S(1)}, u32[]{:S(2)}, u32[]{:S(2)}) %collective-permute-start.58) | collective-permute-done | bytes 57376 | tf_op jit(solution)/shard_map/ppermute | solution.py:648
  603.0 12.8 %collective-permute-done.59 = f32[8,1792]{1,0:T(8,128)S(1)} collective-permute-done((f32[8,1792]{1,0:T(8,128)S(1)}, f32[8,1792]{1,0:T(8,128)S(1)}, u32[]{:S(2)}, u32[]{:S(2)}) %collective-permute-start.59) | collective-permute-done | bytes 57376 | tf_op jit(solution)/shard_map/ppermute | solution.py:648
  (652 shorter events, 336.2 us)
Async XLA Ops:
  7.2 206.4 %all-gather.2.cloned.1.call-start = ((), (), s32[]{:S(2)}) async-start(), calls=%async_computation | async-start | bytes 20545536 | tf_op jit(solution)/shard_map/all_gather | solution.py:769
  51.3 24.9 %collective-permute-start.6 = (bf16[1,2,128,1280]{3,2,1,0:T(8,128)(2,1)S(1)}, bf16[1,2,128,1280]{3,2,1,0:T(8,128)(2,1)S(1)}, u32[]{:S(2)}, u32[]{:S(2)}) collective-permute-start(bf16[1,2,128,1280]{3,2,1,0:T(8,128)(2,1)S(1)} %pad_maximum_fusion.15), channel_id=1, source_target_pairs={{0,16},{16,0},{1,17},{17,1},{2,18},{18,2},{3,19},{19,3},{4,20},{20... | collective-permute-start | bytes 1966088 | tf_op jit(solution)/shard_map/ppermute | solution.py:543
  54.8 31.1 %collective-permute-start.4 = (bf16[2,1,128,1408]{3,2,1,0:T(8,128)(2,1)}, bf16[2,1,128,1408]{3,2,1,0:T(8,128)(2,1)}, u32[]{:S(2)}, u32[]{:S(2)}) collective-permute-start(bf16[2,1,128,1408]{3,2,1,0:T(8,128)(2,1)} %pad_maximum_fusion.13), channel_id=1, source_target_pairs={{0,1},{1,0},{2,3},{3,2},{4,5},{5,4},{6,7},{7,6},{8,9},{9,8},{10,11... | collective-permute-start | bytes 2162696 | tf_op jit(solution)/shard_map/ppermute | solution.py:543
  111.3 42.1 %collective-permute-start.9 = (bf16[384,256]{0,1:T(8,128)(2,1)S(1)}, bf16[384,256]{0,1:T(8,128)(2,1)}, u32[]{:S(2)}, u32[]{:S(2)}) collective-permute-start(bf16[384,256]{0,1:T(8,128)(2,1)S(1)} %bitcast.356), channel_id=1, source_target_pairs={{0,2},{2,4},{4,6},{1,3},{3,5},{5,7},{8,10},{10,12},{12,14},{9,11},... | collective-permute-start | bytes 589832 | tf_op jit(solution)/shard_map/ppermute | solution.py:549
  122.3 31.2 %collective-permute-start.10 = (bf16[384,256]{0,1:T(8,128)(2,1)S(1)}, bf16[384,256]{0,1:T(8,128)(2,1)}, u32[]{:S(2)}, u32[]{:S(2)}) collective-permute-start(bf16[384,256]{0,1:T(8,128)(2,1)S(1)} %bitcast.357), channel_id=1, source_target_pairs={{0,4},{2,6},{1,5},{3,7},{8,12},{10,14},{9,13},{11,15},{16,20},{18,... | collective-permute-start | bytes 589832 | tf_op jit(solution)/shard_map/ppermute | solution.py:549
  124.9 28.5 %collective-permute-start.11 = (bf16[384,256]{0,1:T(8,128)(2,1)S(1)}, bf16[384,256]{0,1:T(8,128)(2,1)}, u32[]{:S(2)}, u32[]{:S(2)}) collective-permute-start(bf16[384,256]{0,1:T(8,128)(2,1)S(1)} %bitcast.358), channel_id=1, source_target_pairs={{0,6},{1,7},{8,14},{9,15},{16,22},{17,23},{24,30},{25,31}} | collective-permute-start | bytes 589832 | tf_op jit(solution)/shard_map/ppermute | solution.py:549
  165.9 31.9 %collective-permute-start.13 = (bf16[4,384,256]{1,2,0:T(8,128)(2,1)S(1)}, bf16[4,384,256]{1,2,0:T(8,128)(2,1)S(1)}, u32[]{:S(2)}, u32[]{:S(2)}) collective-permute-start(bf16[4,384,256]{1,2,0:T(8,128)(2,1)S(1)} %get-tuple-element.252), channel_id=1, source_target_pairs={{0,1},{1,0},{2,3},{3,2},{4,5},{5,4},{6,7},{7,6},{8,9},{9,8},{10,11... | collective-permute-start | bytes 2359304 | tf_op jit(solution)/shard_map/ppermute | solution.py:543
  174.7 28.2 %collective-permute-start.14 = (bf16[136,768]{1,0:T(8,128)(2,1)}, bf16[136,768]{1,0:T(8,128)(2,1)}, u32[]{:S(2)}, u32[]{:S(2)}) collective-permute-start(bf16[136,768]{1,0:T(8,128)(2,1)} %fusion.132), channel_id=1, source_target_pairs={{0,2},{2,4},{4,6},{1,3},{3,5},{5,7},{8,10},{10,12},{12,14},{9,11},... | collective-permute-start | bytes 626696 | tf_op jit(solution)/shard_map/ppermute | solution.py:549
  247.0 27.1 %collective-permute-start.18 = (bf16[512,2048]{1,0:T(8,128)(2,1)S(1)}, bf16[512,2048]{1,0:T(8,128)(2,1)S(1)}, u32[]{:S(2)}, u32[]{:S(2)}) collective-permute-start(bf16[512,2048]{1,0:T(8,128)(2,1)S(1)} %convolution_convert_fusion.4), channel_id=1, source_target_pairs={{0,8},{8,0},{1,9},{9,1},{2,10},{10,2},{3,11},{11,3},{4,12},{12,4},... | collective-permute-start | bytes 6291464 | tf_op jit(solution)/shard_map/ppermute | solution.py:543
  249.7 24.5 %collective-permute-start.19 = (bf16[512,2048]{1,0:T(8,128)(2,1)S(1)}, bf16[512,2048]{1,0:T(8,128)(2,1)S(1)}, u32[]{:S(2)}, u32[]{:S(2)}) collective-permute-start(bf16[512,2048]{1,0:T(8,128)(2,1)S(1)} %convolution_convert_fusion.3), channel_id=1, source_target_pairs={{0,8},{8,0},{1,9},{9,1},{2,10},{10,2},{3,11},{11,3},{4,12},{12,4},... | collective-permute-start | bytes 6291464 | tf_op jit(solution)/shard_map/ppermute | solution.py:543
  298.7 36.4 %collective-permute-start.24 = (bf16[2,4,32,2048]{3,2,1,0:T(8,128)(2,1)}, bf16[2,4,32,2048]{3,2,1,0:T(8,128)(2,1)}, u32[]{:S(2)}, u32[]{:S(2)}) collective-permute-start(bf16[2,4,32,2048]{3,2,1,0:T(8,128)(2,1)} %fusion.95), channel_id=1, source_target_pairs={{0,1},{1,0},{2,3},{3,2},{4,5},{5,4},{6,7},{7,6},{8,9},{9,8},{10,11... | collective-permute-start | bytes 3145736 | tf_op jit(solution)/shard_map/ppermute | solution.py:543
  299.5 38.7 %collective-permute-start.25 = (bf16[2,4,32,2048]{3,2,1,0:T(8,128)(2,1)}, bf16[2,4,32,2048]{3,2,1,0:T(8,128)(2,1)}, u32[]{:S(2)}, u32[]{:S(2)}) collective-permute-start(bf16[2,4,32,2048]{3,2,1,0:T(8,128)(2,1)} %bitcast.60), channel_id=1, source_target_pairs={{0,16},{16,0},{1,17},{17,1},{2,18},{18,2},{3,19},{19,3},{4,20},{20... | collective-permute-start | bytes 3145736 | tf_op jit(solution)/shard_map/ppermute | solution.py:543
  303.6 66.9 %collective-permute-start.26 = (bf16[512,2048]{1,0:T(8,128)(2,1)}, bf16[512,2048]{1,0:T(8,128)(2,1)}, u32[]{:S(2)}, u32[]{:S(2)}) collective-permute-start(bf16[512,2048]{1,0:T(8,128)(2,1)} %convolution_convert_fusion.2), channel_id=1, source_target_pairs={{0,8},{8,0},{1,9},{9,1},{2,10},{10,2},{3,11},{11,3},{4,12},{12,4},... | collective-permute-start | bytes 6291464 | tf_op jit(solution)/shard_map/ppermute | solution.py:543
  305.8 43.5 %collective-permute-start.27 = (bf16[512,1536]{1,0:T(8,128)(2,1)}, bf16[512,1536]{1,0:T(8,128)(2,1)}, u32[]{:S(2)}, u32[]{:S(2)}) collective-permute-start(bf16[512,1536]{1,0:T(8,128)(2,1)} %convolution_convert_fusion.1), channel_id=1, source_target_pairs={{0,8},{8,0},{1,9},{9,1},{2,10},{10,2},{3,11},{11,3},{4,12},{12,4},... | collective-permute-start | bytes 4718600 | tf_op jit(solution)/shard_map/ppermute | solution.py:543
  333.1 48.7 %collective-permute-start.32 = (bf16[136,768]{1,0:T(8,128)(2,1)}, bf16[136,768]{1,0:T(8,128)(2,1)}, u32[]{:S(2)}, u32[]{:S(2)}) collective-permute-start(bf16[136,768]{1,0:T(8,128)(2,1)} %fusion.129), channel_id=1, source_target_pairs={{2,0},{4,2},{6,4},{3,1},{5,3},{7,5},{10,8},{12,10},{14,12},{11,9},... | collective-permute-start | bytes 626696 | tf_op jit(solution)/shard_map/ppermute | solution.py:549
  335.0 64.4 %collective-permute-start.33 = (bf16[136,768]{1,0:T(8,128)(2,1)}, bf16[136,768]{1,0:T(8,128)(2,1)}, u32[]{:S(2)}, u32[]{:S(2)}) collective-permute-start(bf16[136,768]{1,0:T(8,128)(2,1)} %fusion.129), channel_id=1, source_target_pairs={{4,0},{6,2},{5,1},{7,3},{12,8},{14,10},{13,9},{15,11},{20,16},{22,... | collective-permute-start | bytes 626696 | tf_op jit(solution)/shard_map/ppermute | solution.py:549
  358.8 40.6 %collective-permute-start.34 = (bf16[136,768]{1,0:T(8,128)(2,1)}, bf16[136,768]{1,0:T(8,128)(2,1)}, u32[]{:S(2)}, u32[]{:S(2)}) collective-permute-start(bf16[136,768]{1,0:T(8,128)(2,1)} %fusion.129), channel_id=1, source_target_pairs={{6,0},{7,1},{14,8},{15,9},{22,16},{23,17},{30,24},{31,25}} | collective-permute-start | bytes 626696 | tf_op jit(solution)/shard_map/ppermute | solution.py:549
  366.4 33.0 %collective-permute-start.30 = (bf16[4,384,128]{1,2,0:T(8,128)(2,1)}, bf16[4,384,128]{1,2,0:T(8,128)(2,1)}, u32[]{:S(2)}, u32[]{:S(2)}) collective-permute-start(bf16[4,384,128]{1,2,0:T(8,128)(2,1)} %bitcast.277), channel_id=1, source_target_pairs={{0,1},{1,0},{2,3},{3,2},{4,5},{5,4},{6,7},{7,6},{8,9},{9,8},{10,11... | collective-permute-start | bytes 1179656 | tf_op jit(solution)/shard_map/ppermute | solution.py:543
  370.5 89.2 %collective-permute-start.46 = (bf16[2,4,32,1536]{3,2,1,0:T(8,128)(2,1)}, bf16[2,4,32,1536]{3,2,1,0:T(8,128)(2,1)}, u32[]{:S(2)}, u32[]{:S(2)}) collective-permute-start(bf16[2,4,32,1536]{3,2,1,0:T(8,128)(2,1)} %fusion.100), channel_id=1, source_target_pairs={{0,1},{1,0},{2,3},{3,2},{4,5},{5,4},{6,7},{7,6},{8,9},{9,8},{10,11... | collective-permute-start | bytes 2359304 | tf_op jit(solution)/shard_map/ppermute | solution.py:543
  381.8 132.8 %collective-permute-start.43 = (bf16[32,6144]{1,0:T(8,128)(2,1)}, bf16[32,6144]{1,0:T(8,128)(2,1)}, u32[]{:S(2)}, u32[]{:S(2)}) collective-permute-start(bf16[32,6144]{1,0:T(8,128)(2,1)} %get-tuple-element.233), channel_id=1, source_target_pairs={{0,2},{2,4},{4,6},{6,0},{1,3},{3,5},{5,7},{7,1},{8,10},{10,12},{12... | collective-permute-start | bytes 1179656 | tf_op jit(solution)/shard_map/ppermute | solution.py:543
  414.8 29.4 %collective-permute-start.38 = (bf16[384,128]{0,1:T(8,128)(2,1)}, bf16[384,128]{0,1:T(8,128)(2,1)}, u32[]{:S(2)}, u32[]{:S(2)}) collective-permute-start(bf16[384,128]{0,1:T(8,128)(2,1)} %get-tuple-element.262), channel_id=1, source_target_pairs={{4,0},{6,2},{5,1},{7,3},{12,8},{14,10},{13,9},{15,11},{20,16},{22,... | collective-permute-start | bytes 294920 | tf_op jit(solution)/shard_map/ppermute | solution.py:549
  416.1 31.9 %collective-permute-start.39 = (bf16[384,128]{0,1:T(8,128)(2,1)}, bf16[384,128]{0,1:T(8,128)(2,1)}, u32[]{:S(2)}, u32[]{:S(2)}) collective-permute-start(bf16[384,128]{0,1:T(8,128)(2,1)} %get-tuple-element.261), channel_id=1, source_target_pairs={{6,0},{7,1},{14,8},{15,9},{22,16},{23,17},{30,24},{31,25}} | collective-permute-start | bytes 294920 | tf_op jit(solution)/shard_map/ppermute | solution.py:549
  432.9 81.7 %collective-permute-start.44 = (bf16[32,6144]{1,0:T(8,128)(2,1)}, bf16[32,6144]{1,0:T(8,128)(2,1)}, u32[]{:S(2)}, u32[]{:S(2)}) collective-permute-start(bf16[32,6144]{1,0:T(8,128)(2,1)} %get-tuple-element.232), channel_id=1, source_target_pairs={{0,4},{2,6},{4,0},{6,2},{1,5},{3,7},{5,1},{7,3},{8,12},{10,14},{12... | collective-permute-start | bytes 1179656 | tf_op jit(solution)/shard_map/ppermute | solution.py:543
  465.0 26.7 %collective-permute-start.41 = (bf16[384,128]{0,1:T(8,128)(2,1)}, bf16[384,128]{0,1:T(8,128)(2,1)}, u32[]{:S(2)}, u32[]{:S(2)}) collective-permute-start(bf16[384,128]{0,1:T(8,128)(2,1)} %get-tuple-element.259), channel_id=1, source_target_pairs={{4,0},{6,2},{5,1},{7,3},{12,8},{14,10},{13,9},{15,11},{20,16},{22,... | collective-permute-start | bytes 294920 | tf_op jit(solution)/shard_map/ppermute | solution.py:549
  466.3 27.4 %collective-permute-start.42 = (bf16[384,128]{0,1:T(8,128)(2,1)}, bf16[384,128]{0,1:T(8,128)(2,1)}, u32[]{:S(2)}, u32[]{:S(2)}) collective-permute-start(bf16[384,128]{0,1:T(8,128)(2,1)} %get-tuple-element.258), channel_id=1, source_target_pairs={{6,0},{7,1},{14,8},{15,9},{22,16},{23,17},{30,24},{31,25}} | collective-permute-start | bytes 294920 | tf_op jit(solution)/shard_map/ppermute | solution.py:549
  483.9 30.8 %collective-permute-start.45 = (bf16[32,6144]{1,0:T(8,128)(2,1)}, bf16[32,6144]{1,0:T(8,128)(2,1)}, u32[]{:S(2)}, u32[]{:S(2)}) collective-permute-start(bf16[32,6144]{1,0:T(8,128)(2,1)} %get-tuple-element.231), channel_id=1, source_target_pairs={{0,6},{2,0},{4,2},{6,4},{1,7},{3,1},{5,3},{7,5},{8,14},{10,8},{12,... | collective-permute-start | bytes 1179656 | tf_op jit(solution)/shard_map/ppermute | solution.py:543
  491.7 25.5 %collective-permute-start.47 = (bf16[2,4,32,2048]{3,2,1,0:T(8,128)(2,1)}, bf16[2,4,32,2048]{3,2,1,0:T(8,128)(2,1)}, u32[]{:S(2)}, u32[]{:S(2)}) collective-permute-start(bf16[2,4,32,2048]{3,2,1,0:T(8,128)(2,1)} %bitcast.355), channel_id=1, source_target_pairs={{0,16},{16,0},{1,17},{17,1},{2,18},{18,2},{3,19},{19,3},{4,20},{20... | collective-permute-start | bytes 3145736 | tf_op jit(solution)/shard_map/ppermute | solution.py:543
  493.7 63.9 %collective-permute-start.63 = (bf16[4,32,1536]{2,1,0:T(8,128)(2,1)}, bf16[4,32,1536]{2,1,0:T(8,128)(2,1)}, u32[]{:S(2)}, u32[]{:S(2)}) collective-permute-start(bf16[4,32,1536]{2,1,0:T(8,128)(2,1)} %fusion.133), channel_id=1, source_target_pairs={{0,16},{16,0},{1,17},{17,1},{2,18},{18,2},{3,19},{19,3},{4,20},{20... | collective-permute-start | bytes 1179656 | tf_op jit(solution)/shard_map/ppermute | solution.py:543
  521.5 35.0 %collective-permute-start.64 = (bf16[4,32,2048]{2,1,0:T(8,128)(2,1)}, bf16[4,32,2048]{2,1,0:T(8,128)(2,1)}, u32[]{:S(2)}, u32[]{:S(2)}) collective-permute-start(bf16[4,32,2048]{2,1,0:T(8,128)(2,1)} %fusion.120), channel_id=1, source_target_pairs={{0,1},{1,0},{2,3},{3,2},{4,5},{5,4},{6,7},{7,6},{8,9},{9,8},{10,11... | collective-permute-start | bytes 1572872 | tf_op jit(solution)/shard_map/ppermute | solution.py:543
  582.6 36.2 %collective-permute-start.65 = (bf16[32,3584]{1,0:T(8,128)(2,1)S(1)}, bf16[32,3584]{1,0:T(8,128)(2,1)S(1)}, u32[]{:S(2)}, u32[]{:S(2)}) collective-permute-start(bf16[32,3584]{1,0:T(8,128)(2,1)S(1)} %get-tuple-element.236), channel_id=1, source_target_pairs={{0,2},{2,4},{4,6},{6,0},{1,3},{3,5},{5,7},{7,1},{8,10},{10,12},{12... | collective-permute-start | bytes 688136 | tf_op jit(solution)/shard_map/ppermute | solution.py:543
  583.8 35.6 %collective-permute-start.66 = (bf16[32,3584]{1,0:T(8,128)(2,1)S(1)}, bf16[32,3584]{1,0:T(8,128)(2,1)S(1)}, u32[]{:S(2)}, u32[]{:S(2)}) collective-permute-start(bf16[32,3584]{1,0:T(8,128)(2,1)S(1)} %get-tuple-element.235), channel_id=1, source_target_pairs={{0,4},{2,6},{4,0},{6,2},{1,5},{3,7},{5,1},{7,3},{8,12},{10,14},{12... | collective-permute-start | bytes 688136 | tf_op jit(solution)/shard_map/ppermute | solution.py:543
  583.8 35.6 %collective-permute-start.67 = (bf16[32,3584]{1,0:T(8,128)(2,1)S(1)}, bf16[32,3584]{1,0:T(8,128)(2,1)S(1)}, u32[]{:S(2)}, u32[]{:S(2)}) collective-permute-start(bf16[32,3584]{1,0:T(8,128)(2,1)S(1)} %get-tuple-element.234), channel_id=1, source_target_pairs={{0,6},{2,0},{4,2},{6,4},{1,7},{3,1},{5,3},{7,5},{8,14},{10,8},{12,... | collective-permute-start | bytes 688136 | tf_op jit(solution)/shard_map/ppermute | solution.py:543
  (165 other events, 1473.6 us)
Sparse Core Ops, SparseCore 0:
  12.7 160.2 all-gather.1

commit v5 on v4

--- a/solution.py
+++ b/solution.py
@@ -177,7 +177,8 @@
     keyval_ref,
     keyval_cols_ref,
     grad_query_ref,
-    grad_keyval_ref,
+    grad_own_ref,
+    grad_other_ref,
     dots_ref,
     query_side_ref,
     grad_side_ref,
@@ -212,17 +213,29 @@
             grad_query_ref[head_span(j), :] += plain_dot(key_cols, grad_scores)
             total = total + plain_dot(grad_scores, query_side_ref[j])
             total = total + plain_dot(weights.astype(jnp.bfloat16), grad_side_ref[j])
-        grad_keyval_ref[piece] = total
-
-    def clear(piece, carry):
-        grad_keyval_ref[piece] = jnp.zeros(grad_keyval_ref.shape[1:], jnp.float32)
+        behind = lax.shift_right_logical(piece, 1) if not own else 0
+        if own:
+            grad_own_ref[0] = total
+            return
+
+        @pl.when(lax.bitwise_and(piece, 1) == 0)
+        def _():
+            grad_own_ref[behind] = total
+
+        @pl.when(lax.bitwise_and(piece, 1) == 1)
+        def _():
+            grad_other_ref[behind] = total.astype(jnp.bfloat16)
+
+    def clear(step, carry):
+        grad_own_ref[step] = jnp.zeros(grad_own_ref.shape[1:], jnp.float32)
+        grad_other_ref[step] = jnp.zeros(grad_other_ref.shape[1:], jnp.bfloat16)
         return carry
 
     def earlier(index, carry):
         one_piece(slot_of(index, place_ref), False)
         return carry
 
-    lax.fori_loop(1, keyval_ref.shape[0], clear, 0)
+    lax.fori_loop(0, grad_own_ref.shape[0], clear, 0)
     one_piece(0, True)
     lax.fori_loop(0, 2 * place_ref[0] + place_ref[1], earlier, 0)
     grad_query_ref[...] = grad_query_ref[...] * score_scale
@@ -235,10 +248,11 @@
         partial(attend_back_kernel, group),
         out_shape=(
             jax.ShapeDtypeStruct((group_size * HEAD_DIM, rows), jnp.float32),
-            jax.ShapeDtypeStruct((*keyvals.shape[:2], 2 * HEAD_DIM), jnp.float32),
+            jax.ShapeDtypeStruct((keyvals.shape[0] // 2, rows, 2 * HEAD_DIM), jnp.float32),
+            jax.ShapeDtypeStruct((keyvals.shape[0] // 2, rows, 2 * HEAD_DIM), jnp.bfloat16),
         ),
         in_specs=[pl.BlockSpec(memory_space=pltpu.SMEM)] + in_vmem(8),
-        out_specs=tuple(in_vmem(2)),
+        out_specs=tuple(in_vmem(3)),
         scratch_shapes=[
             pltpu.VMEM((8, rows), jnp.float32),
             pltpu.VMEM((group_size, rows, 2 * HEAD_DIM), jnp.bfloat16),
@@ -549,17 +563,38 @@
     return lax.ppermute(block, axis, route)
 
 
-def width_order(width):
+def own_half_first(values):
+    cuts = 2 * lax.axis_size("y")
+    width = values.shape[1] // cuts
+    blocks = [values[:, i * width : (i + 1) * width] for i in range(cuts)]
+    first = lax.axis_index("core") == 0
+    own = [jnp.where(first, a, b) for a, b in zip(blocks[0::2], blocks[1::2])]
+    other = [jnp.where(first, b, a) for a, b in zip(blocks[0::2], blocks[1::2])]
+    return jnp.concatenate(own + other, axis=1)
+
+
+def usual_order(values):
+    cuts = 2 * lax.axis_size("y")
+    width = values.shape[1] // cuts
+    blocks = [values[:, i * width : (i + 1) * width] for i in range(cuts)]
+    first = lax.axis_index("core") == 0
+    merged = []
+    for own, other in zip(blocks[: cuts // 2], blocks[cuts // 2 :]):
+        merged += [jnp.where(first, own, other), jnp.where(first, other, own)]
+    return jnp.concatenate(merged, axis=1)
+
+
+def width_order(width, first):
     sizes = {axis: lax.axis_size(axis) for axis in every_axis}
     rows = width // math.prod(sizes.values())
     rest = lax.broadcasted_iota(jnp.int32, (width, width), 1)
     inside, rest = rest % rows, rest // rows
     owner = {}
-    for axis in ("z", "x", "y", "core"):
+    for axis in ("z", "xy".replace(first, ""), first):
         owner[axis] = (rest % sizes[axis] + lax.axis_index(axis)) % sizes[axis]
         rest = rest // sizes[axis]
-    usual = owner["y"]
-    for axis in ("core", "z", "x"):
+    usual = rest
+    for axis in ("y", "z", "x"):
         usual = usual * sizes[axis] + owner[axis]
     usual = usual * rows + inside
     return (lax.broadcasted_iota(jnp.int32, (width, width), 0) == usual).astype(jnp.bfloat16)
@@ -569,18 +604,17 @@
     return lax.optimization_barrier((values, others))[0]
 
 
-def gather_stages(shard):
+def gather_stages(shard, middle):
     parts = [shard] + [shifted(shard, "z", -k) for k in range(1, lax.axis_size("z"))]
-    block = jnp.concatenate(parts, axis=0)[None, None]
-    middle = shard.shape[1] // 256 * 128
-    halves = []
-    for half, axes in ((block[..., :middle], "xy"), (block[..., middle:], "yx")):
-        for axis in axes:
-            parts = [half] + [shifted(half, axis, -k) for k in range(1, lax.axis_size(axis))]
-            half = jnp.concatenate(parts, axis="yx".index(axis))
-        halves.append(half.reshape(-1, half.shape[-1]))
-    own = jnp.concatenate(halves, axis=1)
-    return own, shifted(own, "core", 1)
+    block = jnp.concatenate(parts, axis=0)
+    halves = [block[:, :middle], block[:, middle:]]
+    for axes in ("xy", "yx"):
+        got = [
+            [half] + [shifted(half, axis, -k) for k in range(1, lax.axis_size(axis))]
+            for half, axis in zip(halves, axes)
+        ]
+        halves = [jnp.concatenate(parts, axis=0) for parts in lax.optimization_barrier(got)]
+    return [(half, shifted(half, "core", 1)) for half in halves]
 
 
 def times_rows(values, pair):
@@ -592,11 +626,10 @@
     return jnp.concatenate([back_product(values, pair[0]), back_product(values, pair[1])], axis=1)
 
 
-def keep_own(total, axis, dim, received, hold=()):
-    kept = lax.index_in_dim(total, 0, dim, False)
+def keep_own(total, axis, received, hold=()):
+    kept = total[0]
     for step in range(1, lax.axis_size(axis)):
-        part = lax.index_in_dim(total, step, dim, False)
-        got = shifted(part.astype(jnp.bfloat16), axis, step)
+        got = shifted(total[step].astype(jnp.bfloat16), axis, step)
         received.append(got)
         if hold:
             got = after(got, *hold)
@@ -604,9 +637,9 @@
     return kept
 
 
-def core_sum(left, right, received):
+def core_sum(left, right, first, received):
     half = left.shape[1] // 2
-    sizes = [lax.axis_size(axis) for axis in ("y", "x", "z")]
+    sizes = [lax.axis_size(axis) for axis in (first, "xy".replace(first, ""), "z")]
     got = shifted(outer_product(left[:, half:], right).astype(jnp.bfloat16), "core", 1)
     received.append(got)
     total = outer_product(left[:, :half], right) + got.astype(jnp.float32)
@@ -618,14 +651,14 @@
 
 
 def first_sums(by_x, by_y, received):
-    by_x = side_by_side([keep_own(total, "x", 1, received) for total in by_x])
-    by_y = side_by_side([keep_own(total, "y", 0, received) for total in by_y])
+    by_x = side_by_side([keep_own(total, "x", received) for total in by_x])
+    by_y = side_by_side([keep_own(total, "y", received) for total in by_y])
     return by_x, by_y
 
 
 def layer_sums(by_x, by_y, received, hold=()):
-    by_x = keep_own(by_x, "y", 0, received, hold)
-    by_y = keep_own(by_y, "x", 0, received, hold)
+    by_x = keep_own(by_x, "y", received, hold)
+    by_y = keep_own(by_y, "x", received, hold)
     return jnp.concatenate([by_x, by_y], axis=-1)
 
 
@@ -680,9 +713,8 @@
     total = jnp.zeros((depth, half), jnp.float32)
     fade = jnp.ones((1, half), jnp.float32)
     for got in passed:
-        got = got.astype(jnp.float32)
-        total = total + fade * got[:depth]
-        fade = fade * got[depth : depth + 1]
+        total = total + fade * got[:depth].astype(jnp.float32)
+        fade = fade * got[depth : depth + 1].astype(jnp.float32)
     total = total.astype(jnp.bfloat16)
     rest = shifted(total, "x", 1)
     left, right = jnp.where(at_x == 0, total, rest), jnp.where(at_x == 0, rest, total)
@@ -696,14 +728,9 @@
 
 def all_slots(blocks):
     blocks = jnp.stack(blocks)
-    slots = jnp.stack([blocks, shifted(blocks, "x", 1)], axis=1)
-    return slots.reshape(-1, *blocks.shape[1:])
-
-
-def swap_key_grads(slots):
-    total = slots.reshape(-1, 2, *slots.shape[1:])
-    swapped = shifted(total[:, 1].astype(jnp.bfloat16), "x", 1)
-    return total[:, 0], swapped
+    swapped = shifted(blocks, "x", 1)
+    slots = jnp.stack([blocks, swapped], axis=1)
+    return slots.reshape(-1, *blocks.shape[1:]), swapped
 
 
 def sum_key_grads(kept, swapped, received):
@@ -765,34 +792,44 @@
         ],
         axis=1,
     )
-    late_shards = [w_in[:, :inner_width], w_mix_out.T, w_attn_out.T, w_gate_up, w_down.T]
-    late = lax.all_gather(jnp.concatenate(late_shards, axis=1), every_axis, axis=0, tiled=True)
+    conv_shard = after(conv_shard)
+    late_shards = [w_in[:, :inner_width], w_mix_out.T, w_attn_out.T, w_gate_up, after(w_down.T, conv_shard)]
+    late = lax.all_gather(jnp.concatenate(late_shards, axis=1), ("y", "z", "x"), axis=0, tiled=True)
+    middle = conv_shard.shape[1] // 256 * 128
+    pair_a, pair_b = gather_stages(conv_shard, middle)
     out_at = inner_width
     ff_at = out_at + inner_width + query_width
-    full_gate_z, full_out, full_gate, full_up, full_down = jnp.split(
-        late, [out_at, ff_at, ff_at + FF, ff_at + 2 * FF], axis=1
-    )
-    conv_pair = gather_stages(conv_shard)
-
-    order = lax.optimization_barrier(width_order(width))
-    inputs = tokens[0].astype(jnp.float32)
-    inputs_rows = plain_dot(tokens[0], order)
-    grad_output = cotangent[0]
-    small = jnp.concatenate([half[:, gain_at : tap_at + tap_columns] for half in conv_pair], axis=0)
+    order_x, order_y = lax.optimization_barrier((width_order(width, "x"), width_order(width, "y")))
+    inputs = own_half_first(tokens[0]).astype(jnp.float32)
+    grad_output = own_half_first(cotangent[0])
+    small = jnp.concatenate(
+        [half[:, gain_at - middle : tap_at + tap_columns - middle] for half in pair_b], axis=0
+    )
     small_rows = lax.dot_general(
-        small, order, (((0,), (1,)), ((), ())), preferred_element_type=jnp.float32
+        small, order_x, (((0,), (1,)), ((), ())), preferred_element_type=jnp.float32
     )
     gain_one_float, gain_two_float = small_rows[0], small_rows[1]
-    tap_all = small_rows[2:].reshape(tap_columns, device_count, own_rows)
+    tap_all = usual_order(small_rows[2:]).reshape(tap_columns, device_count, own_rows)
     tap_all = jnp.swapaxes(tap_all, 0, 1).reshape(device_count, -1)[:, : taps.size]
     tap_all = jnp.swapaxes(tap_all.reshape(-1, *taps.shape), 0, 1).reshape(taps.shape[0], channels)
 
-    normed = rms_norm(inputs_rows, small[:, 0].astype(jnp.float32)).astype(jnp.bfloat16)
-    conv_projected = times_rows(normed, conv_pair)
-    conv_input = conv_projected[:, :channels].astype(jnp.bfloat16)
-    keyval_raw = conv_projected[:, channels:query_at]
-    query_raw = conv_projected[:, query_at:step_at]
-    step_raw = conv_projected[:, step_at:gain_at]
+    def reordered(rows, order):
+        return plain_dot(rows, order).astype(jnp.bfloat16)
+
+    normed = rms_norm(inputs, gain_one_float).astype(jnp.bfloat16)
+    normed_x, normed_y = reordered(normed, order_x), reordered(normed, order_y)
+    projected_a = times_rows(normed_y, pair_a)
+    projected_b = times_rows(normed_x, pair_b)
+    conv_input = jnp.concatenate(
+        [
+            projected_a.astype(jnp.bfloat16),
+            projected_b[:, : channels - middle].astype(jnp.bfloat16),
+        ],
+        axis=1,
+    )
+    keyval_raw = projected_b[:, channels - middle : query_at - middle]
+    query_raw = projected_b[:, query_at - middle : step_at - middle]
+    step_raw = projected_b[:, step_at - middle : gain_at - middle]
     positions = (at_z * lax.axis_size("x") + at_x) * row_count + jnp.arange(
         row_count, dtype=jnp.int32
     )
@@ -822,15 +859,21 @@
     y_local, grown, fresh_state, tail, *key_blocks = after(
         (*ssd_local(act, cum, step_size), *key_blocks)
     )
-    all_keyval = all_slots(key_blocks)
+    all_keyval, keys_swapped = all_slots(key_blocks)
     all_cols = jnp.swapaxes(all_keyval, 1, 2)
     y_local = y_local.reshape(row_count, inner_width)
     grown = grown.reshape(row_count, inner_width)
     behind, other_state, passed = send_states(fresh_state, tail, 1)
+    late = after(late, keys_swapped)
+    late = (late, shifted(late, "core", 1))
+    cuts = (0, out_at, ff_at, ff_at + FF, ff_at + 2 * FF, late[0].shape[1])
+    full_gate_z, full_out, full_gate, full_up, full_down = (
+        tuple(half[:, low:high] for half in late) for low, high in zip(cuts[:-1], cuts[1:])
+    )
     attended_cols, logs = attend(place, after(query_cols, other_state), all_keyval, all_cols)
     attended_cols, logs, *passed = after((attended_cols, logs, *passed))
     carry_state = carried(behind, passed, 1)
-    gate_z = plain_dot(back_product(normed, order).astype(jnp.bfloat16), full_gate_z)
+    gate_z = times_rows(normed, full_gate_z)
     attention_rows = attended_cols.T.astype(jnp.bfloat16)
 
     skip_row = jnp.repeat(skip_weight, MHEAD_DIM)[None, :]
@@ -843,41 +886,38 @@
     gate_sigmoid = jax.nn.sigmoid(gate_z)
     mixer = (ssm_y * gate_z * gate_sigmoid).astype(jnp.bfloat16)
     branches = jnp.concatenate([mixer, attention_rows], axis=1)
-    hidden = inputs + back_product(branches, full_out)
+    hidden = inputs + times_rows_back(branches, full_out)
     normed_two = rms_norm(hidden, gain_two_float).astype(jnp.bfloat16)
-    gate_part = plain_dot(normed_two, full_gate)
-    up_part = plain_dot(normed_two, full_up)
+    gate_part = times_rows(normed_two, full_gate)
+    up_part = times_rows(normed_two, full_up)
     activated = (jax.nn.silu(gate_part) * up_part).astype(jnp.bfloat16)
-    result = hidden + back_product(activated, full_down)
-    output = result.astype(jnp.bfloat16)[None]
-
-    def reordered(rows):
-        return plain_dot(rows, order).astype(jnp.bfloat16)
-
-    grad_activated = plain_dot(grad_output, full_down)
+    result = hidden + times_rows_back(activated, full_down)
+    output = usual_order(result.astype(jnp.bfloat16))[None]
+
+    grad_activated = times_rows(grad_output, full_down)
     core_got = []
-    grad_output_rows = reordered(grad_output)
     down_half = FF // 2
-    normed_two_rows = reordered(normed_two)
     ff_sigmoid = jax.nn.sigmoid(gate_part)
     grad_gate = grad_activated * up_part * ff_sigmoid * (1.0 + gate_part * (1.0 - ff_sigmoid))
     grad_gate = grad_gate.astype(jnp.bfloat16)
     grad_up = (grad_activated * gate_part * ff_sigmoid).astype(jnp.bfloat16)
-    gate_total = core_sum(normed_two_rows, grad_gate, core_got)
-    up_total = core_sum(normed_two_rows, grad_up, core_got)
-    down_a = core_sum(grad_output_rows, activated[:, :down_half], [])
-    down_b = core_sum(grad_output_rows, activated[:, down_half:], [])
+    gate_total = core_sum(reordered(normed_two, order_x), grad_gate, "x", core_got)
+    up_total = core_sum(reordered(normed_two, order_y), grad_up, "y", core_got)
+    down_a = core_sum(reordered(grad_output, order_x), activated[:, :down_half], "x", [])
+    down_b = core_sum(reordered(grad_output, order_y), activated[:, down_half:], "y", [])
     ff_got = []
     ff_later = []
     ff_parts = send_layers(
         layer_sums(*first_sums([gate_total, down_a], [up_total, down_b], ff_got), ff_later)
     )
-    grad_normed_two = back_product(after(grad_gate, *core_got), full_gate) + back_product(grad_up, full_up)
+    grad_normed_two = times_rows_back(after(grad_gate, *core_got), full_gate) + times_rows_back(
+        grad_up, full_up
+    )
     _, pull_two = jax.vjp(rms_norm, hidden, gain_two_float)
     grad_hidden_norm, grad_gain_two = pull_two(grad_normed_two)
     grad_hidden = grad_output.astype(jnp.float32) + grad_hidden_norm
     grad_branch = grad_hidden.astype(jnp.bfloat16)
-    grad_branches = after(plain_dot(grad_branch, full_out), ff_got[1], ff_got[3])
+    grad_branches = after(times_rows(grad_branch, full_out), ff_got[1], ff_got[3])
     grad_mixer = grad_branches[:, :inner_width]
     grad_y = grad_mixer * gate_z * gate_sigmoid
     grad_gate_z = grad_mixer * ssm_y * gate_sigmoid * (1.0 + gate_z * (1.0 - gate_sigmoid))
@@ -886,14 +926,14 @@
 
     grad_attention = grad_branches[:, inner_width:].astype(jnp.bfloat16)
     out_got = []
-    out_total = core_sum(reordered(grad_branch), branches, out_got)
+    out_total = core_sum(reordered(grad_branch, order_y), branches, "y", out_got)
     grad_gate_low = grad_gate_z.astype(jnp.bfloat16)
-    in_gate_total = core_sum(normed, grad_gate_low, out_got)
-    grad_normed_part = back_product(grad_gate_low, full_gate_z)
+    in_gate_total = core_sum(normed_x, grad_gate_low, "x", out_got)
+    grad_normed_part = times_rows_back(grad_gate_low, full_gate_z)
     grad_cols = grad_attention.T
     query_rows = query_cols.T
 
-    def one_group(group, grad_cols):
+    def one_group(group, place):
         return attend_back(
             group,
             place,
@@ -907,18 +947,18 @@
             all_cols,
         )
 
-    query_a, slots_a = one_group(0, after(grad_cols, gate_total, up_total))
-    query_a, slots_a = after((query_a, slots_a), ff_got[0], ff_got[2])
-    kept_a, swapped_a = swap_key_grads(slots_a)
-    query_b, slots_b = one_group(1, after(grad_cols, ff_got[0], ff_got[2], *out_got))
+    query_a, kept_a, other_a = one_group(0, after(place, gate_total, up_total))
+    query_a, kept_a, other_a = after((query_a, kept_a, other_a), ff_got[0], ff_got[2])
+    swapped_a = shifted(other_a, "x", 1)
+    query_b, kept_b, other_b = one_group(1, after(place, ff_got[0], ff_got[2], *out_got))
     before_ssd = (query_b, *ff_later, swapped_a)
-    query_b, slots_b, kept_a, swapped_a, *passed = after(
-        (query_b, slots_b, kept_a, swapped_a, *passed), *before_ssd
+    query_b, kept_b, other_b, kept_a, swapped_a, *passed = after(
+        (query_b, kept_b, other_b, kept_a, swapped_a, *passed), *before_ssd
     )
     grad_end = carried(behind, passed, -1)
     key_got = []
     own_a = sum_key_grads(kept_a, swapped_a, key_got)
-    kept_b, swapped_b = swap_key_grads(slots_b)
+    swapped_b = shifted(other_b, "x", 1)
     own_b = sum_key_grads(kept_b, swapped_b, key_got)
     own_grads = [own_a, own_b]
     grad_query_cols = jnp.concatenate([query_a, query_b], axis=0)
@@ -930,11 +970,11 @@
     grad_keyval = jnp.concatenate([grad_keys, own_cols[:, 1].reshape(key_width, row_count)], axis=0)
     grad_keyval = grad_keyval.T.astype(jnp.bfloat16)
 
-    ssd_grad = after(
-        grad_y, *before_ssd, swapped_b, *out_got, grad_normed_part
+    ssd_skip = after(
+        skip_row, *before_ssd, swapped_b, *out_got, grad_normed_part
     )
     grad_act, grad_step_size, grad_log, grad_skip = ssd_back(
-        act, cum, step_size, ssd_grad, carry_state, grad_end, skip_row
+        act, cum, step_size, grad_y, carry_state, grad_end, ssd_skip
     )
     grad_act, grad_step_size, grad_log = after((grad_act, grad_step_size, grad_log), *key_got)
     grad_step_size = grad_step_size - grad_log * jnp.exp(mamba_heads[0])[None, :]
@@ -956,9 +996,9 @@
     )
     grad_few = jnp.concatenate([grad_keyval, grad_query, grad_step_low], axis=1)
     few_core_got, last_core_got = [], []
-    few_total = core_sum(normed, grad_few, few_core_got)
+    few_total = core_sum(normed_y, grad_few, "y", few_core_got)
     grad_conv_low = after(grad_conv_input.astype(jnp.bfloat16), *few_core_got)
-    conv_total = core_sum(normed, grad_conv_low, last_core_got)
+    conv_total = core_sum(normed_x, grad_conv_low, "x", last_core_got)
     last_got, last_later = [], []
     mid_parts = send_layers(layer_sums(*mid_both, [], last_core_got))
     last_parts = send_layers(
@@ -967,15 +1007,24 @@
     last_parts, *mid_parts = after((tuple(last_parts), *mid_parts), *last_later)
     last_sums, mid_sums = sum_layers(last_parts), sum_layers(mid_parts)
     grad_normed = lax.dot_general(
-        times_rows_back(jnp.concatenate([grad_conv_low, grad_few], axis=1), conv_pair),
-        order.astype(jnp.float32),
+        jnp.concatenate(
+            [
+                times_rows_back(grad_conv_low[:, :middle], pair_a),
+                times_rows_back(
+                    jnp.concatenate([grad_conv_low[:, middle:], grad_few], axis=1), pair_b
+                ),
+            ],
+            axis=1,
+        ),
+        jnp.concatenate([order_y, order_x], axis=1).astype(jnp.float32),
         (((1,), (1,)), ((), ())),
         precision=lax.Precision.HIGH,
         preferred_element_type=jnp.float32,
     )
     _, pull_one = jax.vjp(rms_norm, inputs, gain_one_float)
     grad_input_norm, grad_gain_one = pull_one(grad_normed + grad_normed_part)
-    input_grad = (grad_hidden + grad_input_norm)[None]
+    input_grad = usual_order(grad_hidden + grad_input_norm)[None]
+    gain_grads = usual_order(jnp.stack([grad_gain_two, grad_gain_one]))
 
     def padded(row):
         return jnp.pad(row, ((0, 0), (0, channels - row.shape[1])))
@@ -990,8 +1039,7 @@
                 [
                     grad_conv_weight,
                     grad_conv_bias[None],
-                    padded(grad_gain_two[None]),
-                    padded(grad_gain_one[None]),
+                    padded(gain_grads),
                     padded(head_row),
                 ],
                 axis=0,

time: 648 us -> 655 us (1.011)
  starting transfers between devices: 151 us -> 175 us
  local copies, waits for them, and re-layouts: 87.5 us -> 76.5 us
  matrix products: 99.5 us -> 109 us
  waiting for transfers between devices: 169 us -> 160 us
    ppermute x15, starting transfers between devices: 50 us -> 61.4 us  [moved_along(): return lax.ppermute(block, axis, route)]
    ppermute x5, waiting for transfers between devices: 38.7 us -> 28.1 us  [sum_everywhere(): lax.ppermute(values, axis, [(i, i ^ step) for i in range(count)])]
    ppermute x46 -> x48, starting transfers between devices: 90.2 us -> 99.4 us  [shifted(): lax.ppermute(block, axis, [(i, (i + distance) % count) for i in range(cou...]
    concatenate x6 -> x5, other arithmetic: 9.07 us -> 0.09 us  [the longest x1 0.03 us: on_device(): jnp.concatenate([grad_conv_weight, grad_conv_bias[None], padded(gain_grad...]
    ppermute x15, waiting for transfers between devices: 10.9 us -> 2.76 us  [moved_along(): return lax.ppermute(block, axis, route)]
    ppermute x1, waiting for transfers between devices: 0.01 us -> 7.9 us  [on_device(): lax.ppermute(grad_extended[:CONV - 1], seq_axes, [(i + 1, i) for i in ran...]
    dot_general x12 -> x22, matrix products: 40.3 us -> 47 us  [plain_dot(): return jnp.dot(left, right, preferred_element_type=jnp.float32)]
    unnamed x264 -> x336, local copies, waits for them, and re-layouts: 31.4 us -> 27.6 us
  transfers between devices with their start and end apart: 69 -> 71, of which waited for: 24 -> 22; matrix products, arithmetic and copies ran while one was open for 30% -> 26% of each run, Pallas kernels for 5% -> 5%
where the time goes in v5:
time: 655 us; the launch traced here: 646 us
  starting transfers between devices  175 us (27%)
  waiting for transfers between devices  160 us (24%)
  matrix products  109 us (17%)
  other arithmetic  77.2 us (12%)
  local copies, waits for them, and re-layouts  76.5 us (12%)
  Pallas kernels  31.1 us (5%)
  between operations  17.8 us (3%)
    ppermute x48, waiting for transfers between devices, shifted(): lax.ppermute(block, axis, [(i, (i + distance) % count) for i in range(cou...  122 us
    ppermute x48, starting transfers between devices, shifted(): lax.ppermute(block, axis, [(i, (i + distance) % count) for i in range(cou...  99.4 us
    ppermute x15, starting transfers between devices, moved_along(): return lax.ppermute(block, axis, route)  61.4 us
    dot_general x22, matrix products, plain_dot(): return jnp.dot(left, right, preferred_element_type=jnp.float32)  47 us
    dot_general x14, matrix products, back_product(): lax.dot_general(grad_rows, weight_matrix, (((1,), (1,)), ((), ())), prefe...  30.7 us
    ppermute x5, waiting for transfers between devices, sum_everywhere(): lax.ppermute(values, axis, [(i, i ^ step) for i in range(count)])  28.1 us
    unnamed x336, local copies, waits for them, and re-layouts  27.6 us
    dot_general x17, matrix products, outer_product(): lax.dot_general(left, right, (((0,), (0,)), ((), ())), preferred_element_...  25.7 us
  transfers between devices with their start and end apart: 71, of which 22 were waited for; matrix products, arithmetic and copies ran while one was open for 26% of the time, Pallas kernels for 5%

profile of v5, /device:TPU:0, one launch (start us, length us, event | category | flops | bytes accessed | tf_op | source)
XLA Modules:
  0.0 646.2 jit_solution(18259179466421212309)
XLA Ops:
  24.7 3.7 fusion.31
  28.5 9.0 %collective-permute-done.1 = bf16[32,2688]{1,0:T(8,128)(2,1)S(1)} collective-permute-done((bf16[32,2688]{1,0:T(8,128)(2,1)S(1)}, bf16[32,2688]{1,0:T(8,128)(2,1)S(1)}, u32[]{:S(2)}, u32[]{:S(2)}) %collective-permute-start.1) | collective-permute-done | bytes 172064 | tf_op jit(solution)/shard_map/ppermute | solution.py:557
  42.2 7.0 %collective-permute-done.3 = bf16[128,1280]{1,0:T(8,128)(2,1)S(1)} collective-permute-done((bf16[128,1280]{1,0:T(8,128)(2,1)S(1)}, bf16[128,1280]{1,0:T(8,128)(2,1)S(1)}, u32[]{:S(2)}, u32[]{:S(2)}) %collective-permute-start.3) | collective-permute-done | bytes 327712 | tf_op jit(solution)/shard_map/ppermute | solution.py:557
  52.2 22.2 %collective-permute-done.5 = bf16[256,1280]{1,0:T(8,128)(2,1)S(1)} collective-permute-done((bf16[256,1280]{1,0:T(8,128)(2,1)S(1)}, bf16[256,1280]{1,0:T(8,128)(2,1)S(1)}, u32[]{:S(2)}, u32[]{:S(2)}) %collective-permute-start.5) | collective-permute-done | bytes 655392 | tf_op jit(solution)/shard_map/ppermute | solution.py:557
  99.4 21.1 %collective-permute-start.12 = (bf16[384,256]{0,1:T(8,128)(2,1)}, bf16[384,256]{0,1:T(8,128)(2,1)}, u32[]{:S(2)}, u32[]{:S(2)}) collective-permute-start(bf16[384,256]{0,1:T(8,128)(2,1)} %bitcast.23), channel_id=1, source_target_pairs={{0,6},{1,7},{8,14},{9,15},{16,22},{17,23},{24,30},{25,31}} | collective-permute-start | bytes 589832 | tf_op jit(solution)/shard_map/ppermute | solution.py:563
  133.1 3.9 collective-permute-start.9
  143.6 6.1 ssd.1
  155.0 8.3 %collective-permute-start.14 = (bf16[4,384,256]{1,2,0:T(8,128)(2,1)S(1)}, bf16[4,384,256]{1,2,0:T(8,128)(2,1)}, u32[]{:S(2)}, u32[]{:S(2)}) collective-permute-start(bf16[4,384,256]{1,2,0:T(8,128)(2,1)S(1)} %get-tuple-element.337), channel_id=1, source_target_pairs={{0,1},{1,0},{2,3},{3,2},{4,5},{5,4},{6,7},{7,6},{8,9},{9,8},{10,11... | collective-permute-start | bytes 2359304 | tf_op jit(solution)/shard_map/ppermute | solution.py:557
  163.2 17.0 %collective-permute-done.14 = bf16[4,384,256]{1,2,0:T(8,128)(2,1)} collective-permute-done((bf16[4,384,256]{1,2,0:T(8,128)(2,1)S(1)}, bf16[4,384,256]{1,2,0:T(8,128)(2,1)}, u32[]{:S(2)}, u32[]{:S(2)}) %collective-permute-start.14) | collective-permute-done | bytes 786464 | tf_op jit(solution)/shard_map/ppermute | solution.py:557
  187.2 8.8 %collective-permute-done.13 = bf16[136,1536]{1,0:T(8,128)(2,1)} collective-permute-done((bf16[136,1536]{1,0:T(8,128)(2,1)S(1)}, bf16[136,1536]{1,0:T(8,128)(2,1)}, u32[]{:S(2)}, u32[]{:S(2)}) %collective-permute-start.13) | collective-permute-done | bytes 417824 | tf_op jit(solution)/shard_map/ppermute | solution.py:557
  198.9 5.4 collective-permute-start.17
  204.4 16.6 %collective-permute-start.16 = (bf16[136,768]{1,0:T(8,128)(2,1)}, bf16[136,768]{1,0:T(8,128)(2,1)}, u32[]{:S(2)}, u32[]{:S(2)}) collective-permute-start(bf16[136,768]{1,0:T(8,128)(2,1)} %fusion.140), channel_id=1, source_target_pairs={{0,4},{2,6},{1,5},{3,7},{8,12},{10,14},{9,13},{11,15},{16,20},{18,... | collective-permute-start | bytes 626696 | tf_op jit(solution)/shard_map/ppermute | solution.py:563
  246.0 4.5 multiply_convert_fusion.4
  267.5 3.8 multiply_convert_fusion.1
  291.1 8.6 %collective-permute-done.25 = bf16[2,4,32,1024]{3,2,1,0:T(8,128)(2,1)S(1)} collective-permute-done((bf16[2,4,32,1024]{3,2,1,0:T(8,128)(2,1)S(1)}, bf16[2,4,32,1024]{3,2,1,0:T(8,128)(2,1)S(1)}, u32[]{:S(2)}, u32[]{:S(2)}) %collective-permute-start.25) | collective-permute-done | bytes 524320 | tf_op jit(solution)/shard_map/ppermute | solution.py:557
  347.8 4.2 attend_back_0.1
  362.5 12.3 %collective-permute-done.27 = bf16[2,4,32,2048]{3,2,1,0:T(8,128)(2,1)S(1)} collective-permute-done((bf16[2,4,32,2048]{3,2,1,0:T(8,128)(2,1)}, bf16[2,4,32,2048]{3,2,1,0:T(8,128)(2,1)S(1)}, u32[]{:S(2)}, u32[]{:S(2)}) %collective-permute-start.27) | collective-permute-done | bytes 1048608 | tf_op jit(solution)/shard_map/ppermute | solution.py:557
  383.8 10.2 %collective-permute-done.36 = bf16[4,32,3072]{2,1,0:T(8,128)(2,1)S(1)} collective-permute-done((bf16[4,32,3072]{2,1,0:T(8,128)(2,1)S(1)}, bf16[4,32,3072]{2,1,0:T(8,128)(2,1)S(1)}, u32[]{:S(2)}, u32[]{:S(2)}) %collective-permute-start.36) | collective-permute-done | bytes 786464 | tf_op jit(solution)/shard_map/ppermute | solution.py:557
  401.9 3.8 attend_back_1.1
  411.5 24.1 %collective-permute-start.47 = (bf16[32,6144]{1,0:T(8,128)(2,1)}, bf16[32,6144]{1,0:T(8,128)(2,1)}, u32[]{:S(2)}, u32[]{:S(2)}) collective-permute-start(bf16[32,6144]{1,0:T(8,128)(2,1)} %get-tuple-element.307), channel_id=1, source_target_pairs={{0,6},{2,0},{4,2},{6,4},{1,7},{3,1},{5,3},{7,5},{8,14},{10,8},{12,... | collective-permute-start | bytes 1179656 | tf_op jit(solution)/shard_map/ppermute | solution.py:557
  454.5 4.6 collective-permute-done.37
  468.6 13.6 %ssd_back.1 = (f32[3,128,1792]{2,1,0:T(8,128)}, f32[3,128,24]{2,1,0:T(8,128)S(1)}, f32[3,128,24]{2,1,0:T(8,128)S(1)}, f32[1,1536]{1,0:T(1,128)S(1)}) custom-call(f32[3,128,1792]{2,1,0:T(8,128)} %bitcast.280, f32[3,128,24]{2,1,0:T(8,128)S(1)} %copy-done.17, f32[3,24,128]{2,1,0:T(8,128)S(1)} %copy-done.21, f32[3,128,24]{2,1,0:T(8,128)S(1)} %bitcast.268, ...), custom_call_target="tpu_custom_call" | custom-call | flops 14745600000 | bytes 11010048 | tf_op jit(solution)/shard_map/ssd_back/pallas_call | solution.py:520
  483.0 6.5 %collective-permute-start.45 = (bf16[32,6144]{1,0:T(8,128)(2,1)}, bf16[32,6144]{1,0:T(8,128)(2,1)}, u32[]{:S(2)}, u32[]{:S(2)}) collective-permute-start(bf16[32,6144]{1,0:T(8,128)(2,1)} %get-tuple-element.309), channel_id=1, source_target_pairs={{0,2},{2,4},{4,6},{6,0},{1,3},{3,5},{5,7},{7,1},{8,10},{10,12},{12... | collective-permute-start | bytes 1179656 | tf_op jit(solution)/shard_map/ppermute | solution.py:557
  493.4 9.0 %multiply_reduce_fusion.3 = (f32[1792]{0:T(1024)S(1)}, f32[1792]{0:T(1024)S(1)}, f32[1792]{0:T(1024)S(1)}, f32[1792]{0:T(1024)S(1)}, f32[1792]{0:T(1024)S(1)}, /*index=5*/f32[384,1792]{1,0:T(8,128)}) fusion(f32[387,1792]{1,0:T(8,128)} %copy-done.28, f32[384,1792]{1,0:T(8,128)} %get-tuple-element.294, f32[384,1792]{1,0:T(8,128)} %bitcast.283), kind=kLoop, calls=%fused_computation.121 | loop fusion | flops 12377344 | bytes 19303424 | tf_op jit(solution)/shard_map/transpose(jvp())/reduce_sum | solution.py:70
  526.3 7.9 %collective-permute-done.50 = f32[3,1792]{1,0:T(4,128)S(1)} collective-permute-done((f32[3,1792]{1,0:T(4,128)S(1)}, f32[3,1792]{1,0:T(4,128)S(1)}, u32[]{:S(2)}, u32[]{:S(2)}) %collective-permute-start.50) | collective-permute-done | bytes 21536 | tf_op jit(solution)/shard_map/ppermute | solution.py:986
  547.2 3.9 fusion.82
  554.5 6.6 %collective-permute-done.59 = bf16[4,32,896]{2,1,0:T(8,128)(2,1)S(1)} collective-permute-done((bf16[4,32,896]{2,1,0:T(8,128)(2,1)S(1)}, bf16[4,32,896]{2,1,0:T(8,128)(2,1)S(1)}, u32[]{:S(2)}, u32[]{:S(2)}) %collective-permute-start.59) | collective-permute-done | bytes 229408 | tf_op jit(solution)/shard_map/ppermute | solution.py:557
  566.2 21.6 %collective-permute-done.54 = f32[8,1792]{1,0:T(8,128)S(1)} collective-permute-done((f32[8,1792]{1,0:T(8,128)S(1)}, f32[8,1792]{1,0:T(8,128)S(1)}, u32[]{:S(2)}, u32[]{:S(2)}) %collective-permute-start.54) | collective-permute-done | bytes 57376 | tf_op jit(solution)/shard_map/ppermute | solution.py:681
  595.9 6.0 collective-permute-done.58
  604.1 4.6 collective-permute-done.60
  620.2 9.9 %collective-permute-start.62 = (bf16[32,2688]{1,0:T(8,128)(2,1)S(1)}, bf16[32,2688]{1,0:T(8,128)(2,1)S(1)}, u32[]{:S(2)}, u32[]{:S(2)}) collective-permute-start(bf16[32,2688]{1,0:T(8,128)(2,1)S(1)} %get-tuple-element.344), channel_id=1, source_target_pairs={{0,2},{2,4},{4,6},{6,0},{1,3},{3,5},{5,7},{7,1},{8,10},{10,12},{12... | collective-permute-start | bytes 516104 | tf_op jit(solution)/shard_map/ppermute | solution.py:557
  630.6 4.0 collective-permute-done.62
  (759 shorter events, 329.7 us)
Async XLA Ops:
  7.2 173.0 %all-gather.2.cloned.1.call-start = ((), (), s32[]{:S(2)}) async-start(), calls=%async_computation | async-start | bytes 10584064 | tf_op jit(solution)/shard_map/all_gather | solution.py:797
  49.3 26.1 %collective-permute-start.6 = (bf16[256,1408]{1,0:T(8,128)(2,1)S(1)}, bf16[256,1408]{1,0:T(8,128)(2,1)S(1)}, u32[]{:S(2)}, u32[]{:S(2)}) collective-permute-start(bf16[256,1408]{1,0:T(8,128)(2,1)S(1)} %constant_dynamic-update-slice_fusion.2), channel_id=1, source_target_pairs={{0,1},{1,0},{2,3},{3,2},{4,5},{5,4},{6,7},{7,6},{8,9},{9,8},{10,11... | collective-permute-start | bytes 2162696 | tf_op jit(solution)/shard_map/ppermute | solution.py:557
  84.2 44.5 %collective-permute-start.8 = (bf16[512,1280]{1,0:T(8,128)(2,1)}, bf16[512,1280]{1,0:T(8,128)(2,1)}, u32[]{:S(2)}, u32[]{:S(2)}) collective-permute-start(bf16[512,1280]{1,0:T(8,128)(2,1)} %constant_dynamic-update-slice_fusion.6), channel_id=1, source_target_pairs={{0,8},{8,0},{1,9},{9,1},{2,10},{10,2},{3,11},{11,3},{4,12},{12,4},... | collective-permute-start | bytes 3932168 | tf_op jit(solution)/shard_map/ppermute | solution.py:557
  99.4 53.2 %collective-permute-start.12 = (bf16[384,256]{0,1:T(8,128)(2,1)}, bf16[384,256]{0,1:T(8,128)(2,1)}, u32[]{:S(2)}, u32[]{:S(2)}) collective-permute-start(bf16[384,256]{0,1:T(8,128)(2,1)} %bitcast.23), channel_id=1, source_target_pairs={{0,6},{1,7},{8,14},{9,15},{16,22},{17,23},{24,30},{25,31}} | collective-permute-start | bytes 589832 | tf_op jit(solution)/shard_map/ppermute | solution.py:563
  120.5 32.1 %collective-permute-start.11 = (bf16[384,256]{0,1:T(8,128)(2,1)}, bf16[384,256]{0,1:T(8,128)(2,1)}, u32[]{:S(2)}, u32[]{:S(2)}) collective-permute-start(bf16[384,256]{0,1:T(8,128)(2,1)} %bitcast.23), channel_id=1, source_target_pairs={{0,4},{2,6},{1,5},{3,7},{8,12},{10,14},{9,13},{11,15},{16,20},{18,... | collective-permute-start | bytes 589832 | tf_op jit(solution)/shard_map/ppermute | solution.py:563
  122.5 30.1 %collective-permute-start.10 = (bf16[384,256]{0,1:T(8,128)(2,1)}, bf16[384,256]{0,1:T(8,128)(2,1)}, u32[]{:S(2)}, u32[]{:S(2)}) collective-permute-start(bf16[384,256]{0,1:T(8,128)(2,1)} %bitcast.23), channel_id=1, source_target_pairs={{0,2},{2,4},{4,6},{1,3},{3,5},{5,7},{8,10},{10,12},{12,14},{9,11},... | collective-permute-start | bytes 589832 | tf_op jit(solution)/shard_map/ppermute | solution.py:563
  155.0 25.2 %collective-permute-start.14 = (bf16[4,384,256]{1,2,0:T(8,128)(2,1)S(1)}, bf16[4,384,256]{1,2,0:T(8,128)(2,1)}, u32[]{:S(2)}, u32[]{:S(2)}) collective-permute-start(bf16[4,384,256]{1,2,0:T(8,128)(2,1)S(1)} %get-tuple-element.337), channel_id=1, source_target_pairs={{0,1},{1,0},{2,3},{3,2},{4,5},{5,4},{6,7},{7,6},{8,9},{9,8},{10,11... | collective-permute-start | bytes 2359304 | tf_op jit(solution)/shard_map/ppermute | solution.py:557
  180.2 60.4 %collective-permute-start.19 = (bf16[512,9728]{1,0:T(8,128)(2,1)}, bf16[512,9728]{1,0:T(8,128)(2,1)}, u32[]{:S(2)}, u32[]{:S(2)}) collective-permute-start(bf16[512,9728]{1,0:T(8,128)(2,1)} %all-gather.2.cloned.1.call-done), channel_id=1, source_target_pairs={{0,8},{8,0},{1,9},{9,1},{2,10},{10,2},{3,11},{11,3},{4,12},{12,4},... | collective-permute-start | bytes 29884424 | tf_op jit(solution)/shard_map/ppermute | solution.py:557
  198.9 30.5 %collective-permute-start.17 = (bf16[136,768]{1,0:T(8,128)(2,1)}, bf16[136,768]{1,0:T(8,128)(2,1)}, u32[]{:S(2)}, u32[]{:S(2)}) collective-permute-start(bf16[136,768]{1,0:T(8,128)(2,1)} %fusion.140), channel_id=1, source_target_pairs={{0,6},{1,7},{8,14},{9,15},{16,22},{17,23},{24,30},{25,31}} | collective-permute-start | bytes 626696 | tf_op jit(solution)/shard_map/ppermute | solution.py:563
  204.4 25.1 %collective-permute-start.16 = (bf16[136,768]{1,0:T(8,128)(2,1)}, bf16[136,768]{1,0:T(8,128)(2,1)}, u32[]{:S(2)}, u32[]{:S(2)}) collective-permute-start(bf16[136,768]{1,0:T(8,128)(2,1)} %fusion.140), channel_id=1, source_target_pairs={{0,4},{2,6},{1,5},{3,7},{8,12},{10,14},{9,13},{11,15},{16,20},{18,... | collective-permute-start | bytes 626696 | tf_op jit(solution)/shard_map/ppermute | solution.py:563
  281.8 23.8 %collective-permute-start.20 = (bf16[512,2048]{1,0:T(8,128)(2,1)S(1)}, bf16[512,2048]{1,0:T(8,128)(2,1)S(1)}, u32[]{:S(2)}, u32[]{:S(2)}) collective-permute-start(bf16[512,2048]{1,0:T(8,128)(2,1)S(1)} %convolution_convert_fusion.4), channel_id=1, source_target_pairs={{0,8},{8,0},{1,9},{9,1},{2,10},{10,2},{3,11},{11,3},{4,12},{12,4},... | collective-permute-start | bytes 6291464 | tf_op jit(solution)/shard_map/ppermute | solution.py:557
  330.3 29.1 %collective-permute-start.28 = (bf16[2,4,32,2048]{3,2,1,0:T(8,128)(2,1)}, bf16[2,4,32,2048]{3,2,1,0:T(8,128)(2,1)}, u32[]{:S(2)}, u32[]{:S(2)}) collective-permute-start(bf16[2,4,32,2048]{3,2,1,0:T(8,128)(2,1)} %bitcast.51), channel_id=1, source_target_pairs={{0,16},{16,0},{1,17},{17,1},{2,18},{18,2},{3,19},{19,3},{4,20},{20... | collective-permute-start | bytes 3145736 | tf_op jit(solution)/shard_map/ppermute | solution.py:557
  335.3 65.8 %collective-permute-start.29 = (bf16[512,2048]{1,0:T(8,128)(2,1)}, bf16[512,2048]{1,0:T(8,128)(2,1)}, u32[]{:S(2)}, u32[]{:S(2)}) collective-permute-start(bf16[512,2048]{1,0:T(8,128)(2,1)} %convolution_convert_fusion.2), channel_id=1, source_target_pairs={{0,8},{8,0},{1,9},{9,1},{2,10},{10,2},{3,11},{11,3},{4,12},{12,4},... | collective-permute-start | bytes 6291464 | tf_op jit(solution)/shard_map/ppermute | solution.py:557
  342.1 36.3 %collective-permute-start.30 = (bf16[512,1536]{1,0:T(8,128)(2,1)}, bf16[512,1536]{1,0:T(8,128)(2,1)}, u32[]{:S(2)}, u32[]{:S(2)}) collective-permute-start(bf16[512,1536]{1,0:T(8,128)(2,1)} %convolution_convert_fusion.1), channel_id=1, source_target_pairs={{0,8},{8,0},{1,9},{9,1},{2,10},{10,2},{3,11},{11,3},{4,12},{12,4},... | collective-permute-start | bytes 4718600 | tf_op jit(solution)/shard_map/ppermute | solution.py:557
  342.3 32.6 %collective-permute-start.27 = (bf16[2,4,32,2048]{3,2,1,0:T(8,128)(2,1)}, bf16[2,4,32,2048]{3,2,1,0:T(8,128)(2,1)S(1)}, u32[]{:S(2)}, u32[]{:S(2)}) collective-permute-start(bf16[2,4,32,2048]{3,2,1,0:T(8,128)(2,1)} %bitcast.292), channel_id=1, source_target_pairs={{0,1},{1,0},{2,3},{3,2},{4,5},{5,4},{6,7},{7,6},{8,9},{9,8},{10,11... | collective-permute-start | bytes 3145736 | tf_op jit(solution)/shard_map/ppermute | solution.py:557
  357.4 54.1 %collective-permute-start.34 = (bf16[136,768]{1,0:T(8,128)(2,1)}, bf16[136,768]{1,0:T(8,128)(2,1)}, u32[]{:S(2)}, u32[]{:S(2)}) collective-permute-start(bf16[136,768]{1,0:T(8,128)(2,1)} %fusion.137), channel_id=1, source_target_pairs={{6,0},{7,1},{14,8},{15,9},{22,16},{23,17},{30,24},{31,25}} | collective-permute-start | bytes 626696 | tf_op jit(solution)/shard_map/ppermute | solution.py:563
  359.4 76.1 %collective-permute-start.33 = (bf16[136,768]{1,0:T(8,128)(2,1)}, bf16[136,768]{1,0:T(8,128)(2,1)}, u32[]{:S(2)}, u32[]{:S(2)}) collective-permute-start(bf16[136,768]{1,0:T(8,128)(2,1)} %fusion.137), channel_id=1, source_target_pairs={{4,0},{6,2},{5,1},{7,3},{12,8},{14,10},{13,9},{15,11},{20,16},{22,... | collective-permute-start | bytes 626696 | tf_op jit(solution)/shard_map/ppermute | solution.py:563
  394.0 41.5 %collective-permute-start.32 = (bf16[136,768]{1,0:T(8,128)(2,1)}, bf16[136,768]{1,0:T(8,128)(2,1)S(1)}, u32[]{:S(2)}, u32[]{:S(2)}) collective-permute-start(bf16[136,768]{1,0:T(8,128)(2,1)} %fusion.137), channel_id=1, source_target_pairs={{2,0},{4,2},{6,4},{3,1},{5,3},{7,5},{10,8},{12,10},{14,12},{11,9},... | collective-permute-start | bytes 626696 | tf_op jit(solution)/shard_map/ppermute | solution.py:563
  397.4 38.2 %collective-permute-start.31 = (bf16[4,384,128]{2,1,0:T(8,128)(2,1)S(1)}, bf16[4,384,128]{2,1,0:T(8,128)(2,1)S(1)}, u32[]{:S(2)}, u32[]{:S(2)}) collective-permute-start(bf16[4,384,128]{2,1,0:T(8,128)(2,1)S(1)} %get-tuple-element.137), channel_id=1, source_target_pairs={{0,1},{1,0},{2,3},{3,2},{4,5},{5,4},{6,7},{7,6},{8,9},{9,8},{10,11... | collective-permute-start | bytes 1179656 | tf_op jit(solution)/shard_map/ppermute | solution.py:557
  401.0 59.3 %collective-permute-start.48 = (bf16[2,4,32,1536]{3,2,1,0:T(8,128)(2,1)}, bf16[2,4,32,1536]{3,2,1,0:T(8,128)(2,1)}, u32[]{:S(2)}, u32[]{:S(2)}) collective-permute-start(bf16[2,4,32,1536]{3,2,1,0:T(8,128)(2,1)} %bitcast.76), channel_id=1, source_target_pairs={{0,1},{1,0},{2,3},{3,2},{4,5},{5,4},{6,7},{7,6},{8,9},{9,8},{10,11... | collective-permute-start | bytes 2359304 | tf_op jit(solution)/shard_map/ppermute | solution.py:557
  411.5 108.1 %collective-permute-start.47 = (bf16[32,6144]{1,0:T(8,128)(2,1)}, bf16[32,6144]{1,0:T(8,128)(2,1)}, u32[]{:S(2)}, u32[]{:S(2)}) collective-permute-start(bf16[32,6144]{1,0:T(8,128)(2,1)} %get-tuple-element.307), channel_id=1, source_target_pairs={{0,6},{2,0},{4,2},{6,4},{1,7},{3,1},{5,3},{7,5},{8,14},{10,8},{12,... | collective-permute-start | bytes 1179656 | tf_op jit(solution)/shard_map/ppermute | solution.py:557
  447.0 74.7 %collective-permute-start.46 = (bf16[32,6144]{1,0:T(8,128)(2,1)}, bf16[32,6144]{1,0:T(8,128)(2,1)}, u32[]{:S(2)}, u32[]{:S(2)}) collective-permute-start(bf16[32,6144]{1,0:T(8,128)(2,1)} %get-tuple-element.308), channel_id=1, source_target_pairs={{0,4},{2,6},{4,0},{6,2},{1,5},{3,7},{5,1},{7,3},{8,12},{10,14},{12... | collective-permute-start | bytes 1179656 | tf_op jit(solution)/shard_map/ppermute | solution.py:557
  466.0 23.5 %collective-permute-start.43 = (bf16[384,128]{1,0:T(8,128)(2,1)S(1)}, bf16[384,128]{1,0:T(8,128)(2,1)S(1)}, u32[]{:S(2)}, u32[]{:S(2)}) collective-permute-start(bf16[384,128]{1,0:T(8,128)(2,1)S(1)} %get-tuple-element.348), channel_id=1, source_target_pairs={{4,0},{6,2},{5,1},{7,3},{12,8},{14,10},{13,9},{15,11},{20,16},{22,... | collective-permute-start | bytes 294920 | tf_op jit(solution)/shard_map/ppermute | solution.py:563
  483.0 38.8 %collective-permute-start.45 = (bf16[32,6144]{1,0:T(8,128)(2,1)}, bf16[32,6144]{1,0:T(8,128)(2,1)}, u32[]{:S(2)}, u32[]{:S(2)}) collective-permute-start(bf16[32,6144]{1,0:T(8,128)(2,1)} %get-tuple-element.309), channel_id=1, source_target_pairs={{0,2},{2,4},{4,6},{6,0},{1,3},{3,5},{5,7},{7,1},{8,10},{10,12},{12... | collective-permute-start | bytes 1179656 | tf_op jit(solution)/shard_map/ppermute | solution.py:557
  489.4 27.7 %collective-permute-start.49 = (bf16[2,4,32,2048]{3,2,1,0:T(8,128)(2,1)}, bf16[2,4,32,2048]{3,2,1,0:T(8,128)(2,1)}, u32[]{:S(2)}, u32[]{:S(2)}) collective-permute-start(bf16[2,4,32,2048]{3,2,1,0:T(8,128)(2,1)} %bitcast.291), channel_id=1, source_target_pairs={{0,16},{16,0},{1,17},{17,1},{2,18},{18,2},{3,19},{19,3},{4,20},{20... | collective-permute-start | bytes 3145736 | tf_op jit(solution)/shard_map/ppermute | solution.py:557
  490.0 71.2 %collective-permute-start.65 = (bf16[4,32,1536]{2,1,0:T(8,128)(2,1)}, bf16[4,32,1536]{2,1,0:T(8,128)(2,1)}, u32[]{:S(2)}, u32[]{:S(2)}) collective-permute-start(bf16[4,32,1536]{2,1,0:T(8,128)(2,1)} %fusion.141), channel_id=1, source_target_pairs={{0,16},{16,0},{1,17},{17,1},{2,18},{18,2},{3,19},{19,3},{4,20},{20... | collective-permute-start | bytes 1179656 | tf_op jit(solution)/shard_map/ppermute | solution.py:557
  519.6 41.5 %collective-permute-start.66 = (bf16[4,32,2048]{2,1,0:T(8,128)(2,1)S(1)}, bf16[4,32,2048]{2,1,0:T(8,128)(2,1)S(1)}, u32[]{:S(2)}, u32[]{:S(2)}) collective-permute-start(bf16[4,32,2048]{2,1,0:T(8,128)(2,1)S(1)} %fusion.130), channel_id=1, source_target_pairs={{0,1},{1,0},{2,3},{3,2},{4,5},{5,4},{6,7},{7,6},{8,9},{9,8},{10,11... | collective-permute-start | bytes 1572872 | tf_op jit(solution)/shard_map/ppermute | solution.py:557
  563.7 24.1 %collective-permute-start.55 = (bf16[2,4,32,1792]{3,2,1,0:T(8,128)(2,1)S(1)}, bf16[2,4,32,1792]{3,2,1,0:T(8,128)(2,1)S(1)}, u32[]{:S(2)}, u32[]{:S(2)}) collective-permute-start(bf16[2,4,32,1792]{3,2,1,0:T(8,128)(2,1)S(1)} %bitcast.293), channel_id=1, source_target_pairs={{0,1},{1,0},{2,3},{3,2},{4,5},{5,4},{6,7},{7,6},{8,9},{9,8},{10,11... | collective-permute-start | bytes 2752520 | tf_op jit(solution)/shard_map/ppermute | solution.py:557
  564.2 23.6 %collective-permute-start.54 = (f32[8,1792]{1,0:T(8,128)S(1)}, f32[8,1792]{1,0:T(8,128)S(1)}, u32[]{:S(2)}, u32[]{:S(2)}) collective-permute-start(f32[8,1792]{1,0:T(8,128)S(1)} %add.573), channel_id=1, source_target_pairs={{0,1},{1,0},{2,3},{3,2},{4,5},{5,4},{6,7},{7,6},{8,9},{9,8},{10,11... | collective-permute-start | bytes 172040 | tf_op jit(solution)/shard_map/ppermute | solution.py:681
  590.2 30.0 %collective-permute-start.69 = (bf16[32,3584]{1,0:T(8,128)(2,1)S(1)}, bf16[32,3584]{1,0:T(8,128)(2,1)S(1)}, u32[]{:S(2)}, u32[]{:S(2)}) collective-permute-start(bf16[32,3584]{1,0:T(8,128)(2,1)S(1)} %get-tuple-element.311), channel_id=1, source_target_pairs={{0,6},{2,0},{4,2},{6,4},{1,7},{3,1},{5,3},{7,5},{8,14},{10,8},{12,... | collective-permute-start | bytes 688136 | tf_op jit(solution)/shard_map/ppermute | solution.py:557
  593.3 37.3 %collective-permute-start.68 = (bf16[32,3584]{1,0:T(8,128)(2,1)S(1)}, bf16[32,3584]{1,0:T(8,128)(2,1)S(1)}, u32[]{:S(2)}, u32[]{:S(2)}) collective-permute-start(bf16[32,3584]{1,0:T(8,128)(2,1)S(1)} %get-tuple-element.312), channel_id=1, source_target_pairs={{0,4},{2,6},{4,0},{6,2},{1,5},{3,7},{5,1},{7,3},{8,12},{10,14},{12... | collective-permute-start | bytes 688136 | tf_op jit(solution)/shard_map/ppermute | solution.py:557
  593.9 36.7 %collective-permute-start.67 = (bf16[32,3584]{1,0:T(8,128)(2,1)S(1)}, bf16[32,3584]{1,0:T(8,128)(2,1)S(1)}, u32[]{:S(2)}, u32[]{:S(2)}) collective-permute-start(bf16[32,3584]{1,0:T(8,128)(2,1)S(1)} %get-tuple-element.313), channel_id=1, source_target_pairs={{0,2},{2,4},{4,6},{6,0},{1,3},{3,5},{5,7},{7,1},{8,10},{10,12},{12... | collective-permute-start | bytes 688136 | tf_op jit(solution)/shard_map/ppermute | solution.py:557
  (209 other events, 1778.5 us)
Sparse Core Ops, SparseCore 0:
  17.7 156.2 all-gather.1

commit v6 on v5

--- a/solution.py
+++ b/solution.py
@@ -166,7 +166,6 @@
 
 
 def attend_back_kernel(
-    group,
     place_ref,
     query_ref,
     query_rows_ref,
@@ -186,45 +185,50 @@
     rows = query_ref.shape[1]
     scale = log2_e * score_scale
     grad_query_ref[...] = jnp.zeros_like(grad_query_ref)
-    for j in range(group_size):
-        span = head_span(group * group_size + j)
-        dots_ref[j : j + 1, :] = jnp.sum(
+    for head in range(QHEADS):
+        span = head_span(head)
+        dots_ref[head : head + 1, :] = jnp.sum(
             grad_ref[span, :].astype(jnp.float32) * out_ref[span, :], axis=0, keepdims=True
         )
         query = (query_rows_ref[:, span].astype(jnp.float32) * score_scale).astype(jnp.bfloat16)
         grad = grad_rows_ref[:, span]
-        query_side_ref[j] = jnp.concatenate([query, jnp.zeros_like(query)], axis=1)
-        grad_side_ref[j] = jnp.concatenate([jnp.zeros_like(grad), grad], axis=1)
+        query_side_ref[head] = jnp.concatenate([query, jnp.zeros_like(query)], axis=1)
+        grad_side_ref[head] = jnp.concatenate([jnp.zeros_like(grad), grad], axis=1)
 
     def one_piece(piece, own):
-        keyvals = keyval_ref[piece, :, 2 * group * HEAD_DIM : 2 * (group + 1) * HEAD_DIM]
-        key_cols = keyval_cols_ref[piece, head_span(2 * group), :]
-        total = jnp.zeros((rows, 2 * HEAD_DIM), jnp.float32)
-        for j in range(group_size):
-            head = group * group_size + j
-            query, grad = query_ref[head_span(head), :], grad_ref[head_span(head), :]
-            blank = jnp.zeros_like(query)
-            scores = plain_dot(keyvals, jnp.concatenate([query, blank], axis=0)) * scale
-            weights = jnp.exp2(scores - log_ref[head : head + 1, :])
+        for group in range(KVHEADS):
+            both = slice(2 * group * HEAD_DIM, 2 * (group + 1) * HEAD_DIM)
+            keyvals = keyval_ref[piece, :, both]
+            key_cols = keyval_cols_ref[piece, head_span(2 * group), :]
+            total = jnp.zeros((rows, 2 * HEAD_DIM), jnp.float32)
+            for head in range(group * group_size, (group + 1) * group_size):
+                query, grad = query_ref[head_span(head), :], grad_ref[head_span(head), :]
+                blank = jnp.zeros_like(query)
+                scores = plain_dot(keyvals, jnp.concatenate([query, blank], axis=0)) * scale
+                weights = jnp.exp2(scores - log_ref[head : head + 1, :])
+                if own:
+                    weights = jnp.where(hidden_keys(rows), 0.0, weights)
+                grad_weights = plain_dot(keyvals, jnp.concatenate([blank, grad], axis=0))
+                grad_scores = weights * (grad_weights - dots_ref[head : head + 1, :])
+                grad_scores = grad_scores.astype(jnp.bfloat16)
+                grad_query_ref[head_span(head), :] += plain_dot(key_cols, grad_scores)
+                total = total + plain_dot(grad_scores, query_side_ref[head])
+                total = total + plain_dot(weights.astype(jnp.bfloat16), grad_side_ref[head])
             if own:
-                weights = jnp.where(hidden_keys(rows), 0.0, weights)
-            grad_weights = plain_dot(keyvals, jnp.concatenate([blank, grad], axis=0))
-            grad_scores = (weights * (grad_weights - dots_ref[j : j + 1, :])).astype(jnp.bfloat16)
-            grad_query_ref[head_span(j), :] += plain_dot(key_cols, grad_scores)
-            total = total + plain_dot(grad_scores, query_side_ref[j])
-            total = total + plain_dot(weights.astype(jnp.bfloat16), grad_side_ref[j])
-        behind = lax.shift_right_logical(piece, 1) if not own else 0
-        if own:
-            grad_own_ref[0] = total
-            return
+                grad_own_ref[0, :, both] = total
+            else:
+                put_piece(piece, both, total)
+
+    def put_piece(piece, both, total):
+        behind = lax.shift_right_logical(piece, 1)
 
         @pl.when(lax.bitwise_and(piece, 1) == 0)
         def _():
-            grad_own_ref[behind] = total
+            grad_own_ref[behind, :, both] = total
 
         @pl.when(lax.bitwise_and(piece, 1) == 1)
         def _():
-            grad_other_ref[behind] = total.astype(jnp.bfloat16)
+            grad_other_ref[behind, :, both] = total.astype(jnp.bfloat16)
 
     def clear(step, carry):
         grad_own_ref[step] = jnp.zeros(grad_own_ref.shape[1:], jnp.float32)
@@ -241,28 +245,28 @@
     grad_query_ref[...] = grad_query_ref[...] * score_scale
 
 
-def attend_back(group, place, queries, query_rows, grads, grad_rows, outs, logs, keyvals, keyval_cols):
-    rows = queries.shape[1]
-    flops = 10 * queries.size * rows * keyvals.shape[0] // KVHEADS
+def attend_back(place, queries, query_rows, grads, grad_rows, outs, logs, keyvals, keyval_cols):
+    slots, rows, width = keyvals.shape
+    flops = 10 * queries.size * rows * slots
     return pl.pallas_call(
-        partial(attend_back_kernel, group),
+        attend_back_kernel,
         out_shape=(
-            jax.ShapeDtypeStruct((group_size * HEAD_DIM, rows), jnp.float32),
-            jax.ShapeDtypeStruct((keyvals.shape[0] // 2, rows, 2 * HEAD_DIM), jnp.float32),
-            jax.ShapeDtypeStruct((keyvals.shape[0] // 2, rows, 2 * HEAD_DIM), jnp.bfloat16),
+            jax.ShapeDtypeStruct(queries.shape, jnp.float32),
+            jax.ShapeDtypeStruct((slots // 2, rows, width), jnp.float32),
+            jax.ShapeDtypeStruct((slots // 2, rows, width), jnp.bfloat16),
         ),
         in_specs=[pl.BlockSpec(memory_space=pltpu.SMEM)] + in_vmem(8),
         out_specs=tuple(in_vmem(3)),
         scratch_shapes=[
-            pltpu.VMEM((8, rows), jnp.float32),
-            pltpu.VMEM((group_size, rows, 2 * HEAD_DIM), jnp.bfloat16),
-            pltpu.VMEM((group_size, rows, 2 * HEAD_DIM), jnp.bfloat16),
+            pltpu.VMEM((QHEADS, rows), jnp.float32),
+            pltpu.VMEM((QHEADS, rows, 2 * HEAD_DIM), jnp.bfloat16),
+            pltpu.VMEM((QHEADS, rows, 2 * HEAD_DIM), jnp.bfloat16),
         ],
         compiler_params=compiler_room,
         cost_estimate=pl.CostEstimate(
             flops=6 * flops, bytes_accessed=4 * keyvals.size, transcendentals=flops // 640
         ),
-        name="attend_back_" + str(group),
+        name="attend_back",
     )(place, queries, query_rows, grads, grad_rows, outs, logs, keyvals, keyval_cols)
 
 
@@ -563,38 +567,17 @@
     return lax.ppermute(block, axis, route)
 
 
-def own_half_first(values):
-    cuts = 2 * lax.axis_size("y")
-    width = values.shape[1] // cuts
-    blocks = [values[:, i * width : (i + 1) * width] for i in range(cuts)]
-    first = lax.axis_index("core") == 0
-    own = [jnp.where(first, a, b) for a, b in zip(blocks[0::2], blocks[1::2])]
-    other = [jnp.where(first, b, a) for a, b in zip(blocks[0::2], blocks[1::2])]
-    return jnp.concatenate(own + other, axis=1)
-
-
-def usual_order(values):
-    cuts = 2 * lax.axis_size("y")
-    width = values.shape[1] // cuts
-    blocks = [values[:, i * width : (i + 1) * width] for i in range(cuts)]
-    first = lax.axis_index("core") == 0
-    merged = []
-    for own, other in zip(blocks[: cuts // 2], blocks[cuts // 2 :]):
-        merged += [jnp.where(first, own, other), jnp.where(first, other, own)]
-    return jnp.concatenate(merged, axis=1)
-
-
 def width_order(width, first):
     sizes = {axis: lax.axis_size(axis) for axis in every_axis}
     rows = width // math.prod(sizes.values())
     rest = lax.broadcasted_iota(jnp.int32, (width, width), 1)
     inside, rest = rest % rows, rest // rows
     owner = {}
-    for axis in ("z", "xy".replace(first, ""), first):
+    for axis in ("z", "xy".replace(first, ""), first, "core"):
         owner[axis] = (rest % sizes[axis] + lax.axis_index(axis)) % sizes[axis]
         rest = rest // sizes[axis]
-    usual = rest
-    for axis in ("y", "z", "x"):
+    usual = owner["y"]
+    for axis in ("core", "z", "x"):
         usual = usual * sizes[axis] + owner[axis]
     usual = usual * rows + inside
     return (lax.broadcasted_iota(jnp.int32, (width, width), 0) == usual).astype(jnp.bfloat16)
@@ -608,13 +591,15 @@
     parts = [shard] + [shifted(shard, "z", -k) for k in range(1, lax.axis_size("z"))]
     block = jnp.concatenate(parts, axis=0)
     halves = [block[:, :middle], block[:, middle:]]
+    arrived = []
     for axes in ("xy", "yx"):
         got = [
             [half] + [shifted(half, axis, -k) for k in range(1, lax.axis_size(axis))]
             for half, axis in zip(halves, axes)
         ]
+        arrived += [parts[1] for parts in got]
         halves = [jnp.concatenate(parts, axis=0) for parts in lax.optimization_barrier(got)]
-    return [(half, shifted(half, "core", 1)) for half in halves]
+    return [(half, shifted(half, "core", 1)) for half in halves], arrived[:2]
 
 
 def times_rows(values, pair):
@@ -728,9 +713,8 @@
 
 def all_slots(blocks):
     blocks = jnp.stack(blocks)
-    swapped = shifted(blocks, "x", 1)
-    slots = jnp.stack([blocks, swapped], axis=1)
-    return slots.reshape(-1, *blocks.shape[1:]), swapped
+    slots = jnp.stack([blocks, shifted(blocks, "x", 1)], axis=1)
+    return slots.reshape(-1, *blocks.shape[1:])
 
 
 def sum_key_grads(kept, swapped, received):
@@ -792,16 +776,20 @@
         ],
         axis=1,
     )
-    conv_shard = after(conv_shard)
-    late_shards = [w_in[:, :inner_width], w_mix_out.T, w_attn_out.T, w_gate_up, after(w_down.T, conv_shard)]
-    late = lax.all_gather(jnp.concatenate(late_shards, axis=1), ("y", "z", "x"), axis=0, tiled=True)
     middle = conv_shard.shape[1] // 256 * 128
-    pair_a, pair_b = gather_stages(conv_shard, middle)
+    (pair_a, pair_b), arrived = gather_stages(conv_shard, middle)
+    late_shards = [w_in[:, :inner_width], w_mix_out.T, w_attn_out.T, w_gate_up, w_down.T]
+    late_shard = after(jnp.concatenate(late_shards, axis=1), *arrived)
+    late = lax.all_gather(late_shard, every_axis, axis=0, tiled=True)
     out_at = inner_width
     ff_at = out_at + inner_width + query_width
+    full_gate_z, full_out, full_gate, full_up, full_down = jnp.split(
+        late, [out_at, ff_at, ff_at + FF, ff_at + 2 * FF], axis=1
+    )
+
     order_x, order_y = lax.optimization_barrier((width_order(width, "x"), width_order(width, "y")))
-    inputs = own_half_first(tokens[0]).astype(jnp.float32)
-    grad_output = own_half_first(cotangent[0])
+    inputs = tokens[0].astype(jnp.float32)
+    grad_output = cotangent[0]
     small = jnp.concatenate(
         [half[:, gain_at - middle : tap_at + tap_columns - middle] for half in pair_b], axis=0
     )
@@ -809,7 +797,7 @@
         small, order_x, (((0,), (1,)), ((), ())), preferred_element_type=jnp.float32
     )
     gain_one_float, gain_two_float = small_rows[0], small_rows[1]
-    tap_all = usual_order(small_rows[2:]).reshape(tap_columns, device_count, own_rows)
+    tap_all = small_rows[2:].reshape(tap_columns, device_count, own_rows)
     tap_all = jnp.swapaxes(tap_all, 0, 1).reshape(device_count, -1)[:, : taps.size]
     tap_all = jnp.swapaxes(tap_all.reshape(-1, *taps.shape), 0, 1).reshape(taps.shape[0], channels)
 
@@ -859,21 +847,15 @@
     y_local, grown, fresh_state, tail, *key_blocks = after(
         (*ssd_local(act, cum, step_size), *key_blocks)
     )
-    all_keyval, keys_swapped = all_slots(key_blocks)
+    all_keyval = all_slots(key_blocks)
     all_cols = jnp.swapaxes(all_keyval, 1, 2)
     y_local = y_local.reshape(row_count, inner_width)
     grown = grown.reshape(row_count, inner_width)
     behind, other_state, passed = send_states(fresh_state, tail, 1)
-    late = after(late, keys_swapped)
-    late = (late, shifted(late, "core", 1))
-    cuts = (0, out_at, ff_at, ff_at + FF, ff_at + 2 * FF, late[0].shape[1])
-    full_gate_z, full_out, full_gate, full_up, full_down = (
-        tuple(half[:, low:high] for half in late) for low, high in zip(cuts[:-1], cuts[1:])
-    )
     attended_cols, logs = attend(place, after(query_cols, other_state), all_keyval, all_cols)
     attended_cols, logs, *passed = after((attended_cols, logs, *passed))
     carry_state = carried(behind, passed, 1)
-    gate_z = times_rows(normed, full_gate_z)
+    gate_z = plain_dot(normed, full_gate_z)
     attention_rows = attended_cols.T.astype(jnp.bfloat16)
 
     skip_row = jnp.repeat(skip_weight, MHEAD_DIM)[None, :]
@@ -886,15 +868,15 @@
     gate_sigmoid = jax.nn.sigmoid(gate_z)
     mixer = (ssm_y * gate_z * gate_sigmoid).astype(jnp.bfloat16)
     branches = jnp.concatenate([mixer, attention_rows], axis=1)
-    hidden = inputs + times_rows_back(branches, full_out)
+    hidden = inputs + back_product(branches, full_out)
     normed_two = rms_norm(hidden, gain_two_float).astype(jnp.bfloat16)
-    gate_part = times_rows(normed_two, full_gate)
-    up_part = times_rows(normed_two, full_up)
+    gate_part = plain_dot(normed_two, full_gate)
+    up_part = plain_dot(normed_two, full_up)
     activated = (jax.nn.silu(gate_part) * up_part).astype(jnp.bfloat16)
-    result = hidden + times_rows_back(activated, full_down)
-    output = usual_order(result.astype(jnp.bfloat16))[None]
-
-    grad_activated = times_rows(grad_output, full_down)
+    result = hidden + back_product(activated, full_down)
+    output = result.astype(jnp.bfloat16)[None]
+
+    grad_activated = plain_dot(grad_output, full_down)
     core_got = []
     down_half = FF // 2
     ff_sigmoid = jax.nn.sigmoid(gate_part)
@@ -910,78 +892,69 @@
     ff_parts = send_layers(
         layer_sums(*first_sums([gate_total, down_a], [up_total, down_b], ff_got), ff_later)
     )
-    grad_normed_two = times_rows_back(after(grad_gate, *core_got), full_gate) + times_rows_back(
+    grad_normed_two = back_product(after(grad_gate, *core_got), full_gate) + back_product(
         grad_up, full_up
     )
     _, pull_two = jax.vjp(rms_norm, hidden, gain_two_float)
     grad_hidden_norm, grad_gain_two = pull_two(grad_normed_two)
     grad_hidden = grad_output.astype(jnp.float32) + grad_hidden_norm
     grad_branch = grad_hidden.astype(jnp.bfloat16)
-    grad_branches = after(times_rows(grad_branch, full_out), ff_got[1], ff_got[3])
+    grad_branches = after(plain_dot(grad_branch, full_out), ff_got[1], ff_got[3])
     grad_mixer = grad_branches[:, :inner_width]
     grad_y = grad_mixer * gate_z * gate_sigmoid
     grad_gate_z = grad_mixer * ssm_y * gate_sigmoid * (1.0 + gate_z * (1.0 - gate_sigmoid))
     from_output = outer_product(output_low, (grown * grad_y).astype(jnp.bfloat16))
-    behind, _, passed = send_states(from_output, tail, -1)
+    behind, other_state, passed = send_states(from_output, tail, -1)
 
     grad_attention = grad_branches[:, inner_width:].astype(jnp.bfloat16)
     out_got = []
     out_total = core_sum(reordered(grad_branch, order_y), branches, "y", out_got)
     grad_gate_low = grad_gate_z.astype(jnp.bfloat16)
     in_gate_total = core_sum(normed_x, grad_gate_low, "x", out_got)
-    grad_normed_part = times_rows_back(grad_gate_low, full_gate_z)
+    grad_normed_part = back_product(grad_gate_low, full_gate_z)
     grad_cols = grad_attention.T
     query_rows = query_cols.T
 
-    def one_group(group, place):
-        return attend_back(
-            group,
-            place,
-            query_cols,
-            query_rows,
-            grad_cols,
-            grad_attention,
-            attended_cols,
-            logs,
-            all_keyval,
-            all_cols,
-        )
-
-    query_a, kept_a, other_a = one_group(0, after(place, gate_total, up_total))
-    query_a, kept_a, other_a = after((query_a, kept_a, other_a), ff_got[0], ff_got[2])
-    swapped_a = shifted(other_a, "x", 1)
-    query_b, kept_b, other_b = one_group(1, after(place, ff_got[0], ff_got[2], *out_got))
-    before_ssd = (query_b, *ff_later, swapped_a)
-    query_b, kept_b, other_b, kept_a, swapped_a, *passed = after(
-        (query_b, kept_b, other_b, kept_a, swapped_a, *passed), *before_ssd
+    grad_query_cols, kept, other = attend_back(
+        after(place, gate_total, up_total, other_state),
+        query_cols,
+        query_rows,
+        grad_cols,
+        grad_attention,
+        attended_cols,
+        logs,
+        all_keyval,
+        all_cols,
+    )
+    grad_query_cols, kept, other, *passed = after(
+        (grad_query_cols, kept, other, *passed), ff_got[0], ff_got[2], *out_got
     )
     grad_end = carried(behind, passed, -1)
+    swapped = shifted(other, "x", 1)
     key_got = []
-    own_a = sum_key_grads(kept_a, swapped_a, key_got)
-    swapped_b = shifted(other_b, "x", 1)
-    own_b = sum_key_grads(kept_b, swapped_b, key_got)
-    own_grads = [own_a, own_b]
-    grad_query_cols = jnp.concatenate([query_a, query_b], axis=0)
+    own_grads = sum_key_grads(kept, swapped, key_got)
     mid_got = []
     mid_both = first_sums([in_gate_total], [out_total], mid_got)
     grad_query = turn_rows(grad_query_cols, cosine, -sine).T.astype(jnp.bfloat16)
-    own_cols = jnp.concatenate(own_grads, axis=1).T.reshape(KVHEADS, 2, HEAD_DIM, row_count)
+    own_cols = own_grads.T.reshape(KVHEADS, 2, HEAD_DIM, row_count)
     grad_keys = turn_rows(own_cols[:, 0].reshape(key_width, row_count), cosine, -sine)
     grad_keyval = jnp.concatenate([grad_keys, own_cols[:, 1].reshape(key_width, row_count)], axis=0)
     grad_keyval = grad_keyval.T.astype(jnp.bfloat16)
 
     ssd_skip = after(
-        skip_row, *before_ssd, swapped_b, *out_got, grad_normed_part
+        skip_row, grad_normed_part
     )
     grad_act, grad_step_size, grad_log, grad_skip = ssd_back(
         act, cum, step_size, grad_y, carry_state, grad_end, ssd_skip
     )
-    grad_act, grad_step_size, grad_log = after((grad_act, grad_step_size, grad_log), *key_got)
+    grad_act, grad_step_size, grad_log = after(
+        (grad_act, grad_step_size, grad_log), *ff_later, *mid_got, swapped
+    )
     grad_step_size = grad_step_size - grad_log * jnp.exp(mamba_heads[0])[None, :]
     grad_step_raw = grad_step_size * jax.nn.sigmoid(step_raw + mamba_heads[1][None, :])
     grad_heads = jnp.stack([jnp.sum(grad_log * log_decay, axis=0), jnp.sum(grad_step_raw, axis=0)])
     grad_extended, grad_conv_weight, grad_conv_bias = pull_conv(grad_act)
-    grad_extended, *ff_parts = after((grad_extended, *ff_parts), *mid_got)
+    grad_extended, *ff_parts = after((grad_extended, *ff_parts), *key_got)
     ff_sums = sum_layers(ff_parts)
     rim_back = lax.ppermute(
         grad_extended[: CONV - 1],
@@ -1023,8 +996,8 @@
     )
     _, pull_one = jax.vjp(rms_norm, inputs, gain_one_float)
     grad_input_norm, grad_gain_one = pull_one(grad_normed + grad_normed_part)
-    input_grad = usual_order(grad_hidden + grad_input_norm)[None]
-    gain_grads = usual_order(jnp.stack([grad_gain_two, grad_gain_one]))
+    input_grad = (grad_hidden + grad_input_norm)[None]
+    gain_grads = jnp.stack([grad_gain_two, grad_gain_one])
 
     def padded(row):
         return jnp.pad(row, ((0, 0), (0, channels - row.shape[1])))

time: 655 us -> 607 us (0.927)
  starting transfers between devices: 175 us -> 121 us
  waiting for transfers between devices: 160 us -> 190 us
  other arithmetic: 77.2 us -> 59.6 us
    ppermute x15 -> x12, starting transfers between devices: 61.4 us -> 24.4 us  [moved_along(): return lax.ppermute(block, axis, route)]
    ppermute x15 -> x12, waiting for transfers between devices: 2.76 us -> 27.1 us  [moved_along(): return lax.ppermute(block, axis, route)]
    ppermute x48 -> x46, starting transfers between devices: 99.4 us -> 89.4 us  [shifted(): lax.ppermute(block, axis, [(i, (i + distance) % count) for i in range(cou...]
    ppermute x5, waiting for transfers between devices: 28.1 us -> 34.9 us  [sum_everywhere(): lax.ppermute(values, axis, [(i, i ^ step) for i in range(count)])]
    unnamed x336 -> x264, local copies, waits for them, and re-layouts: 27.6 us -> 21.5 us
    ppermute x48 -> x46, waiting for transfers between devices: 122 us -> 124 us  [shifted(): lax.ppermute(block, axis, [(i, (i + distance) % count) for i in range(cou...]
    dot_general x14 -> x9, matrix products: 30.7 us -> 31.6 us  [back_product(): lax.dot_general(grad_rows, weight_matrix, (((1,), (1,)), ((), ())), prefe...]
    dot_general x22 -> x17, matrix products: 47 us -> 47.3 us  [plain_dot(): return jnp.dot(left, right, preferred_element_type=jnp.float32)]
  transfers between devices with their start and end apart: 71 -> 66, of which waited for: 22 -> 26; matrix products, arithmetic and copies ran while one was open for 26% -> 29% of each run, Pallas kernels for 5% -> 5%
where the time goes in v6:
time: 607 us; the launch traced here: 597 us
  waiting for transfers between devices  190 us (31%)
  starting transfers between devices  121 us (20%)
  matrix products  108 us (18%)
  local copies, waits for them, and re-layouts  71.8 us (12%)
  other arithmetic  59.6 us (10%)
  Pallas kernels  30.3 us (5%)
  between operations  17.1 us (3%)
    ppermute x46, waiting for transfers between devices, shifted(): lax.ppermute(block, axis, [(i, (i + distance) % count) for i in range(cou...  124 us
    ppermute x46, starting transfers between devices, shifted(): lax.ppermute(block, axis, [(i, (i + distance) % count) for i in range(cou...  89.4 us
    dot_general x17, matrix products, plain_dot(): return jnp.dot(left, right, preferred_element_type=jnp.float32)  47.3 us
    ppermute x5, waiting for transfers between devices, sum_everywhere(): lax.ppermute(values, axis, [(i, i ^ step) for i in range(count)])  34.9 us
    dot_general x9, matrix products, back_product(): lax.dot_general(grad_rows, weight_matrix, (((1,), (1,)), ((), ())), prefe...  31.6 us
    ppermute x12, waiting for transfers between devices, moved_along(): return lax.ppermute(block, axis, route)  27.1 us
    ppermute x12, starting transfers between devices, moved_along(): return lax.ppermute(block, axis, route)  24.4 us
    dot_general x17, matrix products, outer_product(): lax.dot_general(left, right, (((0,), (0,)), ((), ())), preferred_element_...  23.8 us
  transfers between devices with their start and end apart: 66, of which 26 were waited for; matrix products, arithmetic and copies ran while one was open for 29% of the time, Pallas kernels for 5%

profile of v6, /device:TPU:0, one launch (start us, length us, event | category | flops | bytes accessed | tf_op | source)
XLA Modules:
  0.0 597.3 jit_solution(9368326273609357015)
XLA Ops:
  22.9 6.4 %collective-permute-done.1 = bf16[32,2688]{1,0:T(8,128)(2,1)S(1)} collective-permute-done((bf16[32,2688]{1,0:T(8,128)(2,1)S(1)}, bf16[32,2688]{1,0:T(8,128)(2,1)S(1)}, u32[]{:S(2)}, u32[]{:S(2)}) %collective-permute-start.1) | collective-permute-done | bytes 172064 | tf_op jit(solution)/shard_map/ppermute | solution.py:561
  32.5 6.4 %collective-permute-done.3 = bf16[128,1280]{1,0:T(8,128)(2,1)S(1)} collective-permute-done((bf16[128,1280]{1,0:T(8,128)(2,1)S(1)}, bf16[128,1280]{1,0:T(8,128)(2,1)S(1)}, u32[]{:S(2)}, u32[]{:S(2)}) %collective-permute-start.3) | collective-permute-done | bytes 327712 | tf_op jit(solution)/shard_map/ppermute | solution.py:561
  53.2 14.9 %collective-permute-done.5 = bf16[256,1280]{1,0:T(8,128)(2,1)S(1)} collective-permute-done((bf16[256,1280]{1,0:T(8,128)(2,1)S(1)}, bf16[256,1280]{1,0:T(8,128)(2,1)S(1)}, u32[]{:S(2)}, u32[]{:S(2)}) %collective-permute-start.5) | collective-permute-done | bytes 655392 | tf_op jit(solution)/shard_map/ppermute | solution.py:561
  72.0 4.0 fusion.106
  97.1 5.8 collective-permute-start.12
  134.1 6.3 %ssd.1 = (f32[3,128,1536]{2,1,0:T(8,128)S(1)}, f32[3,128,1536]{2,1,0:T(8,128)S(1)}, f32[128,1536]{1,0:T(8,128)S(1)}, f32[8,1536]{1,0:T(8,128)S(1)}) custom-call(f32[3,128,1792]{2,1,0:T(8,128)} %bitcast.292, f32[3,128,24]{2,1,0:T(8,128)S(1)} %copy.127.cum_ref, f32[3,24,128]{2,1,0:T(8,128)S(1)} %get-tuple-element.316.cum_rows_ref, ...), custom_call_target="tpu_custom_call" | custom-call | flops 5898240000 | bytes 11010048 | tf_op jit(solution)/shard_map/ssd/pallas_call | solution.py:370
  147.3 17.1 %collective-permute-done.13 = bf16[136,1536]{1,0:T(8,128)(2,1)} collective-permute-done((bf16[136,1536]{1,0:T(8,128)(2,1)}, bf16[136,1536]{1,0:T(8,128)(2,1)}, u32[]{:S(2)}, u32[]{:S(2)}) %collective-permute-start.13) | collective-permute-done | bytes 417824 | tf_op jit(solution)/shard_map/ppermute | solution.py:561
  173.2 12.6 %collective-permute-done.14 = bf16[4,384,256]{1,2,0:T(8,128)(2,1)S(1)} collective-permute-done((bf16[4,384,256]{1,2,0:T(8,128)(2,1)S(1)}, bf16[4,384,256]{1,2,0:T(8,128)(2,1)S(1)}, u32[]{:S(2)}, u32[]{:S(2)}) %collective-permute-start.14) | collective-permute-done | bytes 786464 | tf_op jit(solution)/shard_map/ppermute | solution.py:561
  197.9 3.9 collective-permute-done.18
  208.9 4.5 multiply_reduce_fusion.6
  217.8 4.0 fusion.37
  221.7 4.0 fusion.47
  225.7 5.1 fusion.64
  236.7 4.9 fusion.107
  246.8 4.0 fusion.41
  250.8 5.5 collective-permute-done.24
  263.4 4.9 multiply_reduce_fusion.4
  270.0 4.7 fusion.49
  290.0 4.5 fusion.68
  303.8 6.9 %attend_back.1 = (f32[512,384]{1,0:T(8,128)S(1)}, f32[4,384,256]{2,1,0:T(8,128)S(1)}, bf16[4,384,256]{2,1,0:T(8,128)(2,1)S(1)}) custom-call(s32[2]{0:T(128)S(1)} %pad_add_fusion.2.place_ref, bf16[512,384]{1,0:T(8,128)(2,1)S(1)} %bitcast.277, bf16[384,512]{1,0:T(8,128)(2,1)S(1)} %bitcast.279, bf16[512,384]{1,0:T(8,128)(2,1)S(1)} %copy.137.grad_ref, ...), custom_call_target="tpu_custom_call" | custom-call | flops 36238786560 | bytes 3145728 | tf_op jit(solution)/shard_map/attend_back/pallas_call | solution.py:251
  313.9 9.1 %collective-permute-done.29 = bf16[2,4,32,2048]{3,2,1,0:T(8,128)(2,1)S(1)} collective-permute-done((bf16[2,4,32,2048]{3,2,1,0:T(8,128)(2,1)S(1)}, bf16[2,4,32,2048]{3,2,1,0:T(8,128)(2,1)S(1)}, u32[]{:S(2)}, u32[]{:S(2)}) %collective-permute-start.29) | collective-permute-done | bytes 1048608 | tf_op jit(solution)/shard_map/ppermute | solution.py:561
  332.7 9.4 %collective-permute-done.35 = bf16[4,32,3072]{2,1,0:T(8,128)(2,1)S(1)} collective-permute-done((bf16[4,32,3072]{2,1,0:T(8,128)(2,1)S(1)}, bf16[4,32,3072]{2,1,0:T(8,128)(2,1)S(1)}, u32[]{:S(2)}, u32[]{:S(2)}) %collective-permute-start.35) | collective-permute-done | bytes 786464 | tf_op jit(solution)/shard_map/ppermute | solution.py:561
  349.3 43.0 %collective-permute-start.41 = (bf16[32,6144]{1,0:T(8,128)(2,1)}, bf16[32,6144]{1,0:T(8,128)(2,1)}, u32[]{:S(2)}, u32[]{:S(2)}) collective-permute-start(bf16[32,6144]{1,0:T(8,128)(2,1)} %get-tuple-element.273), channel_id=1, source_target_pairs={{0,6},{2,0},{4,2},{6,4},{1,7},{3,1},{5,3},{7,5},{8,14},{10,8},{12,... | collective-permute-start | bytes 1179656 | tf_op jit(solution)/shard_map/ppermute | solution.py:561
  411.1 13.6 %ssd_back.1 = (f32[3,128,1792]{2,1,0:T(8,128)}, f32[3,128,24]{2,1,0:T(8,128)S(1)}, f32[3,128,24]{2,1,0:T(8,128)S(1)}, f32[1,1536]{1,0:T(1,128)S(1)}) custom-call(f32[3,128,1792]{2,1,0:T(8,128)} %bitcast.293, f32[3,128,24]{2,1,0:T(8,128)S(1)} %copy-done.18, f32[3,24,128]{2,1,0:T(8,128)S(1)} %copy-done.22, f32[3,128,24]{2,1,0:T(8,128)S(1)} %bitcast.283, ...), custom_call_target="tpu_custom_call" | custom-call | flops 14745600000 | bytes 11010048 | tf_op jit(solution)/shard_map/ssd_back/pallas_call | solution.py:524
  434.9 4.4 collective-permute-done.42
  445.6 19.0 %collective-permute-done.43 = bf16[384,256]{1,0:T(8,128)(2,1)S(1)} collective-permute-done((bf16[384,256]{1,0:T(8,128)(2,1)S(1)}, bf16[384,256]{1,0:T(8,128)(2,1)S(1)}, u32[]{:S(2)}, u32[]{:S(2)}) %collective-permute-start.43) | collective-permute-done | bytes 196640 | tf_op jit(solution)/shard_map/ppermute | solution.py:567
  468.9 4.1 multiply_reduce_fusion.3
  508.9 7.0 %collective-permute-done.54 = bf16[4,32,896]{2,1,0:T(8,128)(2,1)S(1)} collective-permute-done((bf16[4,32,896]{2,1,0:T(8,128)(2,1)S(1)}, bf16[4,32,896]{2,1,0:T(8,128)(2,1)S(1)}, u32[]{:S(2)}, u32[]{:S(2)}) %collective-permute-start.54) | collective-permute-done | bytes 229408 | tf_op jit(solution)/shard_map/ppermute | solution.py:561
  521.0 21.6 %collective-permute-done.49 = f32[8,1792]{1,0:T(8,128)S(1)} collective-permute-done((f32[8,1792]{1,0:T(8,128)S(1)}, f32[8,1792]{1,0:T(8,128)S(1)}, u32[]{:S(2)}, u32[]{:S(2)}) %collective-permute-start.49) | collective-permute-done | bytes 57376 | tf_op jit(solution)/shard_map/ppermute | solution.py:666
  547.5 8.9 %collective-permute-done.53 = bf16[4,32,1792]{2,1,0:T(8,128)(2,1)S(1)} collective-permute-done((bf16[4,32,1792]{2,1,0:T(8,128)(2,1)S(1)}, bf16[4,32,1792]{2,1,0:T(8,128)(2,1)S(1)}, u32[]{:S(2)}, u32[]{:S(2)}) %collective-permute-start.53) | collective-permute-done | bytes 458784 | tf_op jit(solution)/shard_map/ppermute | solution.py:561
  556.6 9.2 %collective-permute-done.55 = f32[8,1792]{1,0:T(8,128)S(1)} collective-permute-done((f32[8,1792]{1,0:T(8,128)S(1)}, f32[8,1792]{1,0:T(8,128)S(1)}, u32[]{:S(2)}, u32[]{:S(2)}) %collective-permute-start.55) | collective-permute-done | bytes 57376 | tf_op jit(solution)/shard_map/ppermute | solution.py:666
  575.2 10.6 %collective-permute-done.58 = bf16[32,2688]{1,0:T(8,128)(2,1)S(1)} collective-permute-done((bf16[32,2688]{1,0:T(8,128)(2,1)S(1)}, bf16[32,2688]{1,0:T(8,128)(2,1)S(1)}, u32[]{:S(2)}, u32[]{:S(2)}) %collective-permute-start.58) | collective-permute-done | bytes 172064 | tf_op jit(solution)/shard_map/ppermute | solution.py:561
  (643 shorter events, 289.5 us)
Async XLA Ops:
  7.2 194.9 %all-gather.2.cloned.1.call-start = ((), (), s32[]{:S(2)}) async-start(), calls=%async_computation | async-start | bytes 20545536 | tf_op jit(solution)/shard_map/all_gather | solution.py:783
  80.2 34.4 %collective-permute-start.8 = (bf16[512,1280]{1,0:T(8,128)(2,1)}, bf16[512,1280]{1,0:T(8,128)(2,1)}, u32[]{:S(2)}, u32[]{:S(2)}) collective-permute-start(bf16[512,1280]{1,0:T(8,128)(2,1)} %constant_dynamic-update-slice_fusion.6), channel_id=1, source_target_pairs={{0,8},{8,0},{1,9},{9,1},{2,10},{10,2},{3,11},{11,3},{4,12},{12,4},... | collective-permute-start | bytes 3932168 | tf_op jit(solution)/shard_map/ppermute | solution.py:561
  97.1 44.7 %collective-permute-start.12 = (bf16[384,256]{0,1:T(8,128)(2,1)}, bf16[384,256]{0,1:T(8,128)(2,1)}, u32[]{:S(2)}, u32[]{:S(2)}) collective-permute-start(bf16[384,256]{0,1:T(8,128)(2,1)} %bitcast.24), channel_id=1, source_target_pairs={{0,6},{1,7},{8,14},{9,15},{16,22},{17,23},{24,30},{25,31}} | collective-permute-start | bytes 589832 | tf_op jit(solution)/shard_map/ppermute | solution.py:567
  102.9 38.9 %collective-permute-start.11 = (bf16[384,256]{0,1:T(8,128)(2,1)}, bf16[384,256]{0,1:T(8,128)(2,1)}, u32[]{:S(2)}, u32[]{:S(2)}) collective-permute-start(bf16[384,256]{0,1:T(8,128)(2,1)} %bitcast.24), channel_id=1, source_target_pairs={{0,4},{2,6},{1,5},{3,7},{8,12},{10,14},{9,13},{11,15},{16,20},{18,... | collective-permute-start | bytes 589832 | tf_op jit(solution)/shard_map/ppermute | solution.py:567
  104.9 36.9 %collective-permute-start.10 = (bf16[384,256]{0,1:T(8,128)(2,1)}, bf16[384,256]{0,1:T(8,128)(2,1)}, u32[]{:S(2)}, u32[]{:S(2)}) collective-permute-start(bf16[384,256]{0,1:T(8,128)(2,1)} %bitcast.24), channel_id=1, source_target_pairs={{0,2},{2,4},{4,6},{1,3},{3,5},{5,7},{8,10},{10,12},{12,14},{9,11},... | collective-permute-start | bytes 589832 | tf_op jit(solution)/shard_map/ppermute | solution.py:567
  142.7 21.7 %collective-permute-start.13 = (bf16[136,1536]{1,0:T(8,128)(2,1)}, bf16[136,1536]{1,0:T(8,128)(2,1)}, u32[]{:S(2)}, u32[]{:S(2)}) collective-permute-start(bf16[136,1536]{1,0:T(8,128)(2,1)} %pad_maximum_fusion.11), channel_id=1, source_target_pairs={{0,1},{1,0},{2,3},{3,2},{4,5},{5,4},{6,7},{7,6},{8,9},{9,8},{10,11... | collective-permute-start | bytes 1253384 | tf_op jit(solution)/shard_map/ppermute | solution.py:561
  146.0 39.9 %collective-permute-start.14 = (bf16[4,384,256]{1,2,0:T(8,128)(2,1)S(1)}, bf16[4,384,256]{1,2,0:T(8,128)(2,1)S(1)}, u32[]{:S(2)}, u32[]{:S(2)}) collective-permute-start(bf16[4,384,256]{1,2,0:T(8,128)(2,1)S(1)} %get-tuple-element.297), channel_id=1, source_target_pairs={{0,1},{1,0},{2,3},{3,2},{4,5},{5,4},{6,7},{7,6},{8,9},{9,8},{10,11... | collective-permute-start | bytes 2359304 | tf_op jit(solution)/shard_map/ppermute | solution.py:561
  166.7 24.5 %collective-permute-start.17 = (bf16[136,768]{1,0:T(8,128)(2,1)}, bf16[136,768]{1,0:T(8,128)(2,1)}, u32[]{:S(2)}, u32[]{:S(2)}) collective-permute-start(bf16[136,768]{1,0:T(8,128)(2,1)} %fusion.150), channel_id=1, source_target_pairs={{0,6},{1,7},{8,14},{9,15},{16,22},{17,23},{24,30},{25,31}} | collective-permute-start | bytes 626696 | tf_op jit(solution)/shard_map/ppermute | solution.py:567
  168.6 22.5 %collective-permute-start.16 = (bf16[136,768]{1,0:T(8,128)(2,1)}, bf16[136,768]{1,0:T(8,128)(2,1)}, u32[]{:S(2)}, u32[]{:S(2)}) collective-permute-start(bf16[136,768]{1,0:T(8,128)(2,1)} %fusion.150), channel_id=1, source_target_pairs={{0,4},{2,6},{1,5},{3,7},{8,12},{10,14},{9,13},{11,15},{16,20},{18,... | collective-permute-start | bytes 626696 | tf_op jit(solution)/shard_map/ppermute | solution.py:567
  234.8 25.0 %collective-permute-start.20 = (bf16[512,2048]{1,0:T(8,128)(2,1)S(1)}, bf16[512,2048]{1,0:T(8,128)(2,1)S(1)}, u32[]{:S(2)}, u32[]{:S(2)}) collective-permute-start(bf16[512,2048]{1,0:T(8,128)(2,1)S(1)} %convolution_convert_fusion.3), channel_id=1, source_target_pairs={{0,8},{8,0},{1,9},{9,1},{2,10},{10,2},{3,11},{11,3},{4,12},{12,4},... | collective-permute-start | bytes 6291464 | tf_op jit(solution)/shard_map/ppermute | solution.py:561
  236.2 27.2 %collective-permute-start.19 = (bf16[512,2048]{1,0:T(8,128)(2,1)S(1)}, bf16[512,2048]{1,0:T(8,128)(2,1)S(1)}, u32[]{:S(2)}, u32[]{:S(2)}) collective-permute-start(bf16[512,2048]{1,0:T(8,128)(2,1)S(1)} %convolution_convert_fusion.4), channel_id=1, source_target_pairs={{0,8},{8,0},{1,9},{9,1},{2,10},{10,2},{3,11},{11,3},{4,12},{12,4},... | collective-permute-start | bytes 6291464 | tf_op jit(solution)/shard_map/ppermute | solution.py:561
  280.0 30.7 %collective-permute-start.30 = (bf16[2,4,32,2048]{3,2,1,0:T(8,128)(2,1)}, bf16[2,4,32,2048]{3,2,1,0:T(8,128)(2,1)}, u32[]{:S(2)}, u32[]{:S(2)}) collective-permute-start(bf16[2,4,32,2048]{3,2,1,0:T(8,128)(2,1)} %bitcast.58), channel_id=1, source_target_pairs={{0,16},{16,0},{1,17},{17,1},{2,18},{18,2},{3,19},{19,3},{4,20},{20... | collective-permute-start | bytes 3145736 | tf_op jit(solution)/shard_map/ppermute | solution.py:561
  283.2 66.1 %collective-permute-start.31 = (bf16[512,2048]{1,0:T(8,128)(2,1)}, bf16[512,2048]{1,0:T(8,128)(2,1)}, u32[]{:S(2)}, u32[]{:S(2)}) collective-permute-start(bf16[512,2048]{1,0:T(8,128)(2,1)} %convolution_convert_fusion.2), channel_id=1, source_target_pairs={{0,8},{8,0},{1,9},{9,1},{2,10},{10,2},{3,11},{11,3},{4,12},{12,4},... | collective-permute-start | bytes 6291464 | tf_op jit(solution)/shard_map/ppermute | solution.py:561
  297.1 29.4 %collective-permute-start.32 = (bf16[512,1536]{1,0:T(8,128)(2,1)S(1)}, bf16[512,1536]{1,0:T(8,128)(2,1)}, u32[]{:S(2)}, u32[]{:S(2)}) collective-permute-start(bf16[512,1536]{1,0:T(8,128)(2,1)S(1)} %convolution_convert_fusion.1), channel_id=1, source_target_pairs={{0,8},{8,0},{1,9},{9,1},{2,10},{10,2},{3,11},{11,3},{4,12},{12,4},... | collective-permute-start | bytes 4718600 | tf_op jit(solution)/shard_map/ppermute | solution.py:561
  297.4 25.5 %collective-permute-start.29 = (bf16[2,4,32,2048]{3,2,1,0:T(8,128)(2,1)S(1)}, bf16[2,4,32,2048]{3,2,1,0:T(8,128)(2,1)S(1)}, u32[]{:S(2)}, u32[]{:S(2)}) collective-permute-start(bf16[2,4,32,2048]{3,2,1,0:T(8,128)(2,1)S(1)} %bitcast.299), channel_id=1, source_target_pairs={{0,1},{1,0},{2,3},{3,2},{4,5},{5,4},{6,7},{7,6},{8,9},{9,8},{10,11... | collective-permute-start | bytes 3145736 | tf_op jit(solution)/shard_map/ppermute | solution.py:561
  302.3 95.2 %collective-permute-start.28 = (bf16[136,768]{1,0:T(8,128)(2,1)S(1)}, bf16[136,768]{1,0:T(8,128)(2,1)}, u32[]{:S(2)}, u32[]{:S(2)}) collective-permute-start(bf16[136,768]{1,0:T(8,128)(2,1)S(1)} %fusion.147), channel_id=1, source_target_pairs={{6,0},{7,1},{14,8},{15,9},{22,16},{23,17},{30,24},{31,25}} | collective-permute-start | bytes 626696 | tf_op jit(solution)/shard_map/ppermute | solution.py:567
  310.7 88.2 %collective-permute-start.27 = (bf16[136,768]{1,0:T(8,128)(2,1)S(1)}, bf16[136,768]{1,0:T(8,128)(2,1)S(1)}, u32[]{:S(2)}, u32[]{:S(2)}) collective-permute-start(bf16[136,768]{1,0:T(8,128)(2,1)S(1)} %fusion.147), channel_id=1, source_target_pairs={{4,0},{6,2},{5,1},{7,3},{12,8},{14,10},{13,9},{15,11},{20,16},{22,... | collective-permute-start | bytes 626696 | tf_op jit(solution)/shard_map/ppermute | solution.py:567
  342.1 56.8 %collective-permute-start.26 = (bf16[136,768]{1,0:T(8,128)(2,1)S(1)}, bf16[136,768]{1,0:T(8,128)(2,1)S(1)}, u32[]{:S(2)}, u32[]{:S(2)}) collective-permute-start(bf16[136,768]{1,0:T(8,128)(2,1)S(1)} %fusion.147), channel_id=1, source_target_pairs={{2,0},{4,2},{6,4},{3,1},{5,3},{7,5},{10,8},{12,10},{14,12},{11,9},... | collective-permute-start | bytes 626696 | tf_op jit(solution)/shard_map/ppermute | solution.py:567
  345.5 80.8 %collective-permute-start.36 = (bf16[2,4,32,1536]{3,2,1,0:T(8,128)(2,1)}, bf16[2,4,32,1536]{3,2,1,0:T(8,128)(2,1)}, u32[]{:S(2)}, u32[]{:S(2)}) collective-permute-start(bf16[2,4,32,1536]{3,2,1,0:T(8,128)(2,1)} %bitcast.68), channel_id=1, source_target_pairs={{0,1},{1,0},{2,3},{3,2},{4,5},{5,4},{6,7},{7,6},{8,9},{9,8},{10,11... | collective-permute-start | bytes 2359304 | tf_op jit(solution)/shard_map/ppermute | solution.py:561
  349.3 125.4 %collective-permute-start.41 = (bf16[32,6144]{1,0:T(8,128)(2,1)}, bf16[32,6144]{1,0:T(8,128)(2,1)}, u32[]{:S(2)}, u32[]{:S(2)}) collective-permute-start(bf16[32,6144]{1,0:T(8,128)(2,1)} %get-tuple-element.273), channel_id=1, source_target_pairs={{0,6},{2,0},{4,2},{6,4},{1,7},{3,1},{5,3},{7,5},{8,14},{10,8},{12,... | collective-permute-start | bytes 1179656 | tf_op jit(solution)/shard_map/ppermute | solution.py:561
  397.5 71.3 %collective-permute-start.37 = (bf16[2,4,32,2048]{3,2,1,0:T(8,128)(2,1)}, bf16[2,4,32,2048]{3,2,1,0:T(8,128)(2,1)}, u32[]{:S(2)}, u32[]{:S(2)}) collective-permute-start(bf16[2,4,32,2048]{3,2,1,0:T(8,128)(2,1)} %bitcast.69), channel_id=1, source_target_pairs={{0,16},{16,0},{1,17},{17,1},{2,18},{18,2},{3,19},{19,3},{4,20},{20... | collective-permute-start | bytes 3145736 | tf_op jit(solution)/shard_map/ppermute | solution.py:561
  403.7 24.5 %collective-permute-start.38 = (bf16[4,384,256]{2,1,0:T(8,128)(2,1)}, bf16[4,384,256]{2,1,0:T(8,128)(2,1)}, u32[]{:S(2)}, u32[]{:S(2)}) collective-permute-start(bf16[4,384,256]{2,1,0:T(8,128)(2,1)} %copy-done.23), channel_id=1, source_target_pairs={{0,1},{1,0},{2,3},{3,2},{4,5},{5,4},{6,7},{7,6},{8,9},{9,8},{10,11... | collective-permute-start | bytes 2359304 | tf_op jit(solution)/shard_map/ppermute | solution.py:561
  432.8 31.8 %collective-permute-start.43 = (bf16[384,256]{1,0:T(8,128)(2,1)S(1)}, bf16[384,256]{1,0:T(8,128)(2,1)S(1)}, u32[]{:S(2)}, u32[]{:S(2)}) collective-permute-start(bf16[384,256]{1,0:T(8,128)(2,1)S(1)} %get-tuple-element.295), channel_id=1, source_target_pairs={{4,0},{6,2},{5,1},{7,3},{12,8},{14,10},{13,9},{15,11},{20,16},{22,... | collective-permute-start | bytes 589832 | tf_op jit(solution)/shard_map/ppermute | solution.py:567
  439.3 35.3 %collective-permute-start.40 = (bf16[32,6144]{1,0:T(8,128)(2,1)}, bf16[32,6144]{1,0:T(8,128)(2,1)}, u32[]{:S(2)}, u32[]{:S(2)}) collective-permute-start(bf16[32,6144]{1,0:T(8,128)(2,1)} %get-tuple-element.274), channel_id=1, source_target_pairs={{0,4},{2,6},{4,0},{6,2},{1,5},{3,7},{5,1},{7,3},{8,12},{10,14},{12... | collective-permute-start | bytes 1179656 | tf_op jit(solution)/shard_map/ppermute | solution.py:561
  445.6 29.1 %collective-permute-start.39 = (bf16[32,6144]{1,0:T(8,128)(2,1)}, bf16[32,6144]{1,0:T(8,128)(2,1)}, u32[]{:S(2)}, u32[]{:S(2)}) collective-permute-start(bf16[32,6144]{1,0:T(8,128)(2,1)} %get-tuple-element.275), channel_id=1, source_target_pairs={{0,2},{2,4},{4,6},{6,0},{1,3},{3,5},{5,7},{7,1},{8,10},{10,12},{12... | collective-permute-start | bytes 1179656 | tf_op jit(solution)/shard_map/ppermute | solution.py:561
  464.6 51.5 %collective-permute-start.60 = (bf16[4,32,1536]{2,1,0:T(8,128)(2,1)}, bf16[4,32,1536]{2,1,0:T(8,128)(2,1)}, u32[]{:S(2)}, u32[]{:S(2)}) collective-permute-start(bf16[4,32,1536]{2,1,0:T(8,128)(2,1)} %fusion.151), channel_id=1, source_target_pairs={{0,16},{16,0},{1,17},{17,1},{2,18},{18,2},{3,19},{19,3},{4,20},{20... | collective-permute-start | bytes 1179656 | tf_op jit(solution)/shard_map/ppermute | solution.py:561
  478.3 37.6 %collective-permute-start.61 = (bf16[4,32,2048]{2,1,0:T(8,128)(2,1)S(1)}, bf16[4,32,2048]{2,1,0:T(8,128)(2,1)S(1)}, u32[]{:S(2)}, u32[]{:S(2)}) collective-permute-start(bf16[4,32,2048]{2,1,0:T(8,128)(2,1)S(1)} %fusion.139), channel_id=1, source_target_pairs={{0,1},{1,0},{2,3},{3,2},{4,5},{5,4},{6,7},{7,6},{8,9},{9,8},{10,11... | collective-permute-start | bytes 1572872 | tf_op jit(solution)/shard_map/ppermute | solution.py:561
  518.6 24.1 %collective-permute-start.50 = (bf16[2,4,32,1792]{3,2,1,0:T(8,128)(2,1)S(1)}, bf16[2,4,32,1792]{3,2,1,0:T(8,128)(2,1)S(1)}, u32[]{:S(2)}, u32[]{:S(2)}) collective-permute-start(bf16[2,4,32,1792]{3,2,1,0:T(8,128)(2,1)S(1)} %bitcast.300), channel_id=1, source_target_pairs={{0,1},{1,0},{2,3},{3,2},{4,5},{5,4},{6,7},{7,6},{8,9},{9,8},{10,11... | collective-permute-start | bytes 2752520 | tf_op jit(solution)/shard_map/ppermute | solution.py:561
  519.6 23.0 %collective-permute-start.49 = (f32[8,1792]{1,0:T(8,128)S(1)}, f32[8,1792]{1,0:T(8,128)S(1)}, u32[]{:S(2)}, u32[]{:S(2)}) collective-permute-start(f32[8,1792]{1,0:T(8,128)S(1)} %add.561), channel_id=1, source_target_pairs={{0,1},{1,0},{2,3},{3,2},{4,5},{5,4},{6,7},{7,6},{8,9},{9,8},{10,11... | collective-permute-start | bytes 172040 | tf_op jit(solution)/shard_map/ppermute | solution.py:666
  545.0 29.6 %collective-permute-start.64 = (bf16[32,3584]{1,0:T(8,128)(2,1)S(1)}, bf16[32,3584]{1,0:T(8,128)(2,1)S(1)}, u32[]{:S(2)}, u32[]{:S(2)}) collective-permute-start(bf16[32,3584]{1,0:T(8,128)(2,1)S(1)} %get-tuple-element.276), channel_id=1, source_target_pairs={{0,6},{2,0},{4,2},{6,4},{1,7},{3,1},{5,3},{7,5},{8,14},{10,8},{12,... | collective-permute-start | bytes 688136 | tf_op jit(solution)/shard_map/ppermute | solution.py:561
  545.1 30.1 %collective-permute-start.63 = (bf16[32,3584]{1,0:T(8,128)(2,1)S(1)}, bf16[32,3584]{1,0:T(8,128)(2,1)S(1)}, u32[]{:S(2)}, u32[]{:S(2)}) collective-permute-start(bf16[32,3584]{1,0:T(8,128)(2,1)S(1)} %get-tuple-element.277), channel_id=1, source_target_pairs={{0,4},{2,6},{4,0},{6,2},{1,5},{3,7},{5,1},{7,3},{8,12},{10,14},{12... | collective-permute-start | bytes 688136 | tf_op jit(solution)/shard_map/ppermute | solution.py:561
  546.1 29.1 %collective-permute-start.62 = (bf16[32,3584]{1,0:T(8,128)(2,1)S(1)}, bf16[32,3584]{1,0:T(8,128)(2,1)S(1)}, u32[]{:S(2)}, u32[]{:S(2)}) collective-permute-start(bf16[32,3584]{1,0:T(8,128)(2,1)S(1)} %get-tuple-element.278), channel_id=1, source_target_pairs={{0,2},{2,4},{4,6},{6,0},{1,3},{3,5},{5,7},{7,1},{8,10},{10,12},{12... | collective-permute-start | bytes 688136 | tf_op jit(solution)/shard_map/ppermute | solution.py:561
  (167 other events, 1658.4 us)
Sparse Core Ops, SparseCore 0:
  41.1 160.7 all-gather.1

commit v7 on v6

--- a/solution.py
+++ b/solution.py
@@ -611,13 +611,11 @@
     return jnp.concatenate([back_product(values, pair[0]), back_product(values, pair[1])], axis=1)
 
 
-def keep_own(total, axis, received, hold=()):
+def keep_own(total, axis, received):
     kept = total[0]
     for step in range(1, lax.axis_size(axis)):
         got = shifted(total[step].astype(jnp.bfloat16), axis, step)
         received.append(got)
-        if hold:
-            got = after(got, *hold)
         kept = kept + got.astype(jnp.float32)
     return kept
 
@@ -641,9 +639,9 @@
     return by_x, by_y
 
 
-def layer_sums(by_x, by_y, received, hold=()):
-    by_x = keep_own(by_x, "y", received, hold)
-    by_y = keep_own(by_y, "x", received, hold)
+def layer_sums(by_x, by_y, received):
+    by_x = keep_own(by_x, "y", received)
+    by_y = keep_own(by_y, "x", received)
     return jnp.concatenate([by_x, by_y], axis=-1)
 
 
@@ -657,7 +655,7 @@
 
 
 def sum_everywhere(values, holds):
-    for axis in ("core", "x", "y", "z"):
+    for axis in ("core", "y", "x", "z"):
         if axis in holds:
             values = after(values, *holds[axis])
         count = lax.axis_size(axis)
@@ -691,7 +689,7 @@
     return jnp.where(is_second, first, 0.0), other, passed
 
 
-def carried(behind, passed, direction):
+def carried(behind, passed, direction, received):
     depth, half = behind.shape[0] - 8, behind.shape[1] // 2
     at_x = lax.axis_index("x")
     is_second = (at_x == 1) if direction == 1 else (at_x == 0)
@@ -702,6 +700,7 @@
         fade = fade * got[depth : depth + 1].astype(jnp.float32)
     total = total.astype(jnp.bfloat16)
     rest = shifted(total, "x", 1)
+    received.append(rest)
     left, right = jnp.where(at_x == 0, total, rest), jnp.where(at_x == 0, rest, total)
     carry = jnp.concatenate([left, right], axis=1).astype(jnp.float32)
     return jnp.where(is_second, behind[depth : depth + 1], 1.0) * carry + behind[:depth]
@@ -854,7 +853,7 @@
     behind, other_state, passed = send_states(fresh_state, tail, 1)
     attended_cols, logs = attend(place, after(query_cols, other_state), all_keyval, all_cols)
     attended_cols, logs, *passed = after((attended_cols, logs, *passed))
-    carry_state = carried(behind, passed, 1)
+    carry_state = carried(behind, passed, 1, [])
     gate_z = plain_dot(normed, full_gate_z)
     attention_rows = attended_cols.T.astype(jnp.bfloat16)
 
@@ -929,12 +928,17 @@
     grad_query_cols, kept, other, *passed = after(
         (grad_query_cols, kept, other, *passed), ff_got[0], ff_got[2], *out_got
     )
-    grad_end = carried(behind, passed, -1)
+    rested = []
+    grad_end = carried(behind, passed, -1, rested)
     swapped = shifted(other, "x", 1)
     key_got = []
     own_grads = sum_key_grads(kept, swapped, key_got)
     mid_got = []
-    mid_both = first_sums([in_gate_total], [out_total], mid_got)
+    mid_both = first_sums(
+        [after(in_gate_total, *rested)], [after(out_total, *rested)], mid_got
+    )
+    mid_later = []
+    mid_parts = send_layers(layer_sums(*mid_both, mid_later))
     grad_query = turn_rows(grad_query_cols, cosine, -sine).T.astype(jnp.bfloat16)
     own_cols = own_grads.T.reshape(KVHEADS, 2, HEAD_DIM, row_count)
     grad_keys = turn_rows(own_cols[:, 0].reshape(key_width, row_count), cosine, -sine)
@@ -948,13 +952,13 @@
         act, cum, step_size, grad_y, carry_state, grad_end, ssd_skip
     )
     grad_act, grad_step_size, grad_log = after(
-        (grad_act, grad_step_size, grad_log), *ff_later, *mid_got, swapped
+        (grad_act, grad_step_size, grad_log), *ff_later, swapped
     )
     grad_step_size = grad_step_size - grad_log * jnp.exp(mamba_heads[0])[None, :]
     grad_step_raw = grad_step_size * jax.nn.sigmoid(step_raw + mamba_heads[1][None, :])
     grad_heads = jnp.stack([jnp.sum(grad_log * log_decay, axis=0), jnp.sum(grad_step_raw, axis=0)])
     grad_extended, grad_conv_weight, grad_conv_bias = pull_conv(grad_act)
-    grad_extended, *ff_parts = after((grad_extended, *ff_parts), *key_got)
+    grad_extended, *ff_parts = after((grad_extended, *ff_parts), *key_got, *mid_got)
     ff_sums = sum_layers(ff_parts)
     rim_back = lax.ppermute(
         grad_extended[: CONV - 1],
@@ -970,13 +974,13 @@
     grad_few = jnp.concatenate([grad_keyval, grad_query, grad_step_low], axis=1)
     few_core_got, last_core_got = [], []
     few_total = core_sum(normed_y, grad_few, "y", few_core_got)
-    grad_conv_low = after(grad_conv_input.astype(jnp.bfloat16), *few_core_got)
+    grad_conv_low = after(
+        grad_conv_input.astype(jnp.bfloat16), *few_core_got, *mid_later
+    )
     conv_total = core_sum(normed_x, grad_conv_low, "x", last_core_got)
     last_got, last_later = [], []
-    mid_parts = send_layers(layer_sums(*mid_both, [], last_core_got))
-    last_parts = send_layers(
-        layer_sums(*first_sums([conv_total], [few_total], last_got), last_later)
-    )
+    last_both = after(first_sums([conv_total], [few_total], last_got), *last_got)
+    last_parts = send_layers(layer_sums(*last_both, last_later))
     last_parts, *mid_parts = after((tuple(last_parts), *mid_parts), *last_later)
     last_sums, mid_sums = sum_layers(last_parts), sum_layers(mid_parts)
     grad_normed = lax.dot_general(
@@ -1019,7 +1023,7 @@
             ),
             *last_core_got,
         ),
-        {"y": last_got, "z": last_later},
+        {"x": last_got, "z": last_later},
     )
     device = lax.axis_index(every_axis)
     own_channels = conv_weight.shape[1]

time: 607 us -> 604 us (level)
  waiting for transfers between devices: 190 us -> 165 us
  starting transfers between devices: 121 us -> 136 us
    ppermute x5, waiting for transfers between devices: 34.9 us -> 10.5 us  [sum_everywhere(): lax.ppermute(values, axis, [(i, i ^ step) for i in range(count)])]
    ppermute x12, waiting for transfers between devices: 27.1 us -> 11.8 us  [moved_along(): return lax.ppermute(block, axis, route)]
    ppermute x46, starting transfers between devices: 89.4 us -> 102 us  [shifted(): lax.ppermute(block, axis, [(i, (i + distance) % count) for i in range(cou...]
    ppermute x46, waiting for transfers between devices: 124 us -> 137 us  [shifted(): lax.ppermute(block, axis, [(i, (i + distance) % count) for i in range(cou...]
    unnamed x264 -> x252, local copies, waits for them, and re-layouts: 21.5 us -> 20.6 us
  transfers between devices with their start and end apart: 66 -> 66, of which waited for: 26 -> 29; matrix products, arithmetic and copies ran while one was open for 29% -> 30% of each run, Pallas kernels for 5% -> 5%
where the time goes in v7:
time: 604 us; the launch traced here: 593 us
  waiting for transfers between devices  165 us (27%)
  starting transfers between devices  136 us (23%)
  matrix products  113 us (19%)
  local copies, waits for them, and re-layouts  72.7 us (12%)
  other arithmetic  58.7 us (10%)
  Pallas kernels  30.7 us (5%)
  between operations  16.9 us (3%)
    ppermute x46, waiting for transfers between devices, shifted(): lax.ppermute(block, axis, [(i, (i + distance) % count) for i in range(cou...  137 us
    ppermute x46, starting transfers between devices, shifted(): lax.ppermute(block, axis, [(i, (i + distance) % count) for i in range(cou...  102 us
    dot_general x17, matrix products, plain_dot(): return jnp.dot(left, right, preferred_element_type=jnp.float32)  47.3 us
    dot_general x9, matrix products, back_product(): lax.dot_general(grad_rows, weight_matrix, (((1,), (1,)), ((), ())), prefe...  31.6 us
    dot_general x17, matrix products, outer_product(): lax.dot_general(left, right, (((0,), (0,)), ((), ())), preferred_element_...  29.1 us
    ppermute x12, starting transfers between devices, moved_along(): return lax.ppermute(block, axis, route)  24.4 us
    unnamed x252, local copies, waits for them, and re-layouts  20.6 us
    pallas_call x1, Pallas kernels, ssd_back(): pl.pallas_call(ssd_back_kernel, out_shape=(jax.ShapeDtypeStruct(act.shape...  13.9 us
  transfers between devices with their start and end apart: 66, of which 29 were waited for; matrix products, arithmetic and copies ran while one was open for 30% of the time, Pallas kernels for 5%

profile of v7, /device:TPU:0, one launch (start us, length us, event | category | flops | bytes accessed | tf_op | source)
XLA Modules:
  0.0 593.4 jit_solution(14249096445604371265)
XLA Ops:
  22.9 6.4 %collective-permute-done.1 = bf16[32,2688]{1,0:T(8,128)(2,1)S(1)} collective-permute-done((bf16[32,2688]{1,0:T(8,128)(2,1)S(1)}, bf16[32,2688]{1,0:T(8,128)(2,1)S(1)}, u32[]{:S(2)}, u32[]{:S(2)}) %collective-permute-start.1) | collective-permute-done | bytes 172064 | tf_op jit(solution)/shard_map/ppermute | solution.py:561
  32.5 6.4 %collective-permute-done.3 = bf16[128,1280]{1,0:T(8,128)(2,1)S(1)} collective-permute-done((bf16[128,1280]{1,0:T(8,128)(2,1)S(1)}, bf16[128,1280]{1,0:T(8,128)(2,1)S(1)}, u32[]{:S(2)}, u32[]{:S(2)}) %collective-permute-start.3) | collective-permute-done | bytes 327712 | tf_op jit(solution)/shard_map/ppermute | solution.py:561
  53.2 15.0 %collective-permute-done.5 = bf16[256,1280]{1,0:T(8,128)(2,1)S(1)} collective-permute-done((bf16[256,1280]{1,0:T(8,128)(2,1)S(1)}, bf16[256,1280]{1,0:T(8,128)(2,1)S(1)}, u32[]{:S(2)}, u32[]{:S(2)}) %collective-permute-start.5) | collective-permute-done | bytes 655392 | tf_op jit(solution)/shard_map/ppermute | solution.py:561
  72.0 4.0 fusion.106
  97.1 5.9 collective-permute-start.12
  134.0 6.3 %ssd.1 = (f32[3,128,1536]{2,1,0:T(8,128)S(1)}, f32[3,128,1536]{2,1,0:T(8,128)S(1)}, f32[128,1536]{1,0:T(8,128)S(1)}, f32[8,1536]{1,0:T(8,128)S(1)}) custom-call(f32[3,128,1792]{2,1,0:T(8,128)} %bitcast.296, f32[3,128,24]{2,1,0:T(8,128)S(1)} %copy.127.cum_ref, f32[3,24,128]{2,1,0:T(8,128)S(1)} %get-tuple-element.320.cum_rows_ref, ...), custom_call_target="tpu_custom_call" | custom-call | flops 5898240000 | bytes 11010048 | tf_op jit(solution)/shard_map/ssd/pallas_call | solution.py:370
  147.2 17.1 %collective-permute-done.13 = bf16[136,1536]{1,0:T(8,128)(2,1)} collective-permute-done((bf16[136,1536]{1,0:T(8,128)(2,1)}, bf16[136,1536]{1,0:T(8,128)(2,1)}, u32[]{:S(2)}, u32[]{:S(2)}) %collective-permute-start.13) | collective-permute-done | bytes 417824 | tf_op jit(solution)/shard_map/ppermute | solution.py:561
  173.2 12.7 %collective-permute-done.14 = bf16[4,384,256]{1,2,0:T(8,128)(2,1)S(1)} collective-permute-done((bf16[4,384,256]{1,2,0:T(8,128)(2,1)S(1)}, bf16[4,384,256]{1,2,0:T(8,128)(2,1)S(1)}, u32[]{:S(2)}, u32[]{:S(2)}) %collective-permute-start.14) | collective-permute-done | bytes 786464 | tf_op jit(solution)/shard_map/ppermute | solution.py:561
  208.9 4.5 multiply_reduce_fusion.6
  225.7 5.1 fusion.64
  236.7 4.9 fusion.107
  246.8 4.0 fusion.41
  250.8 5.5 collective-permute-done.24
  263.5 4.9 multiply_reduce_fusion.4
  270.0 4.7 fusion.49
  289.3 4.5 fusion.68
  302.8 6.9 %attend_back.1 = (f32[512,384]{1,0:T(8,128)S(1)}, f32[4,384,256]{2,1,0:T(8,128)S(1)}, bf16[4,384,256]{2,1,0:T(8,128)(2,1)S(1)}) custom-call(s32[2]{0:T(128)S(1)} %pad_add_fusion.2.place_ref, bf16[512,384]{1,0:T(8,128)(2,1)S(1)} %bitcast.279, bf16[384,512]{1,0:T(8,128)(2,1)S(1)} %bitcast.281, bf16[512,384]{1,0:T(8,128)(2,1)S(1)} %copy-done.9, ...), custom_call_target="tpu_custom_call" | custom-call | flops 36238786560 | bytes 3145728 | tf_op jit(solution)/shard_map/attend_back/pallas_call | solution.py:251
  312.8 9.9 %collective-permute-done.29 = bf16[2,4,32,2048]{3,2,1,0:T(8,128)(2,1)S(1)} collective-permute-done((bf16[2,4,32,2048]{3,2,1,0:T(8,128)(2,1)S(1)}, bf16[2,4,32,2048]{3,2,1,0:T(8,128)(2,1)S(1)}, u32[]{:S(2)}, u32[]{:S(2)}) %collective-permute-start.29) | collective-permute-done | bytes 1048608 | tf_op jit(solution)/shard_map/ppermute | solution.py:561
  326.7 4.1 convert_add_fusion.5
  330.8 10.8 %collective-permute-done.35 = bf16[4,32,3072]{2,1,0:T(8,128)(2,1)S(1)} collective-permute-done((bf16[4,32,3072]{2,1,0:T(8,128)(2,1)S(1)}, bf16[4,32,3072]{2,1,0:T(8,128)(2,1)S(1)}, u32[]{:S(2)}, u32[]{:S(2)}) %collective-permute-start.35) | collective-permute-done | bytes 786464 | tf_op jit(solution)/shard_map/ppermute | solution.py:561
  346.5 42.2 %collective-permute-start.39 = (bf16[32,6144]{1,0:T(8,128)(2,1)}, bf16[32,6144]{1,0:T(8,128)(2,1)}, u32[]{:S(2)}, u32[]{:S(2)}) collective-permute-start(bf16[32,6144]{1,0:T(8,128)(2,1)} %get-tuple-element.277), channel_id=1, source_target_pairs={{0,6},{2,0},{4,2},{6,4},{1,7},{3,1},{5,3},{7,5},{8,14},{10,8},{12,... | collective-permute-start | bytes 1179656 | tf_op jit(solution)/shard_map/ppermute | solution.py:561
  393.7 5.4 convert_add_fusion
  400.9 13.9 %ssd_back.1 = (f32[3,128,1792]{2,1,0:T(8,128)}, f32[3,128,24]{2,1,0:T(8,128)S(1)}, f32[3,128,24]{2,1,0:T(8,128)S(1)}, f32[1,1536]{1,0:T(1,128)S(1)}) custom-call(f32[3,128,1792]{2,1,0:T(8,128)} %bitcast.297, f32[3,128,24]{2,1,0:T(8,128)S(1)} %copy-done.13, f32[3,24,128]{2,1,0:T(8,128)S(1)} %copy-done.17, f32[3,128,24]{2,1,0:T(8,128)S(1)} %bitcast.285, ...), custom_call_target="tpu_custom_call" | custom-call | flops 14745600000 | bytes 11010048 | tf_op jit(solution)/shard_map/ssd_back/pallas_call | solution.py:524
  421.9 7.5 %multiply_reduce_fusion.3 = (f32[1792]{0:T(1024)S(1)}, f32[1792]{0:T(1024)S(1)}, f32[1792]{0:T(1024)S(1)}, f32[1792]{0:T(1024)S(1)}, f32[1792]{0:T(1024)S(1)}, /*index=5*/f32[384,1792]{1,0:T(8,128)S(1)}) fusion(f32[387,1792]{1,0:T(8,128)} %copy-done.23, f32[384,1792]{1,0:T(8,128)} %get-tuple-element.268, f32[384,1792]{1,0:T(8,128)} %bitcast.299), kind=kLoop, calls=%fused_computation.151 | loop fusion | flops 12377344 | bytes 19303424 | tf_op jit(solution)/shard_map/transpose(jvp())/reduce_sum | solution.py:70
  438.4 5.0 collective-permute-done.40
  446.6 10.9 %collective-permute-start.37 = (bf16[32,6144]{1,0:T(8,128)(2,1)}, bf16[32,6144]{1,0:T(8,128)(2,1)}, u32[]{:S(2)}, u32[]{:S(2)}) collective-permute-start(bf16[32,6144]{1,0:T(8,128)(2,1)} %get-tuple-element.279), channel_id=1, source_target_pairs={{0,2},{2,4},{4,6},{6,0},{1,3},{3,5},{5,7},{7,1},{8,10},{10,12},{12... | collective-permute-start | bytes 1179656 | tf_op jit(solution)/shard_map/ppermute | solution.py:561
  472.1 4.8 collective-permute-done.38
  476.9 10.6 %collective-permute-done.44 = bf16[2,4,32,2048]{3,2,1,0:T(8,128)(2,1)} collective-permute-done((bf16[2,4,32,2048]{3,2,1,0:T(8,128)(2,1)}, bf16[2,4,32,2048]{3,2,1,0:T(8,128)(2,1)}, u32[]{:S(2)}, u32[]{:S(2)}) %collective-permute-start.44) | collective-permute-done | bytes 1048608 | tf_op jit(solution)/shard_map/ppermute | solution.py:561
  494.8 5.3 collective-permute-done.45
  526.6 16.9 %collective-permute-done.52 = bf16[2,4,32,1792]{3,2,1,0:T(8,128)(2,1)S(1)} collective-permute-done((bf16[2,4,32,1792]{3,2,1,0:T(8,128)(2,1)S(1)}, bf16[2,4,32,1792]{3,2,1,0:T(8,128)(2,1)S(1)}, u32[]{:S(2)}, u32[]{:S(2)}) %collective-permute-start.52) | collective-permute-done | bytes 917536 | tf_op jit(solution)/shard_map/ppermute | solution.py:561
  552.3 5.3 collective-permute-done.55
  573.0 5.9 collective-permute-start.59
  (627 shorter events, 299.0 us)
Async XLA Ops:
  7.2 194.9 %all-gather.2.cloned.1.call-start = ((), (), s32[]{:S(2)}) async-start(), calls=%async_computation | async-start | bytes 20545536 | tf_op jit(solution)/shard_map/all_gather | solution.py:782
  47.9 21.3 %collective-permute-start.6 = (bf16[256,1408]{1,0:T(8,128)(2,1)S(1)}, bf16[256,1408]{1,0:T(8,128)(2,1)S(1)}, u32[]{:S(2)}, u32[]{:S(2)}) collective-permute-start(bf16[256,1408]{1,0:T(8,128)(2,1)S(1)} %constant_dynamic-update-slice_fusion.2), channel_id=1, source_target_pairs={{0,1},{1,0},{2,3},{3,2},{4,5},{5,4},{6,7},{7,6},{8,9},{9,8},{10,11... | collective-permute-start | bytes 2162696 | tf_op jit(solution)/shard_map/ppermute | solution.py:561
  80.2 34.4 %collective-permute-start.8 = (bf16[512,1280]{1,0:T(8,128)(2,1)}, bf16[512,1280]{1,0:T(8,128)(2,1)}, u32[]{:S(2)}, u32[]{:S(2)}) collective-permute-start(bf16[512,1280]{1,0:T(8,128)(2,1)} %constant_dynamic-update-slice_fusion.6), channel_id=1, source_target_pairs={{0,8},{8,0},{1,9},{9,1},{2,10},{10,2},{3,11},{11,3},{4,12},{12,4},... | collective-permute-start | bytes 3932168 | tf_op jit(solution)/shard_map/ppermute | solution.py:561
  97.1 44.7 %collective-permute-start.12 = (bf16[384,256]{0,1:T(8,128)(2,1)}, bf16[384,256]{0,1:T(8,128)(2,1)}, u32[]{:S(2)}, u32[]{:S(2)}) collective-permute-start(bf16[384,256]{0,1:T(8,128)(2,1)} %bitcast.24), channel_id=1, source_target_pairs={{0,6},{1,7},{8,14},{9,15},{16,22},{17,23},{24,30},{25,31}} | collective-permute-start | bytes 589832 | tf_op jit(solution)/shard_map/ppermute | solution.py:567
  103.0 38.8 %collective-permute-start.11 = (bf16[384,256]{0,1:T(8,128)(2,1)}, bf16[384,256]{0,1:T(8,128)(2,1)}, u32[]{:S(2)}, u32[]{:S(2)}) collective-permute-start(bf16[384,256]{0,1:T(8,128)(2,1)} %bitcast.24), channel_id=1, source_target_pairs={{0,4},{2,6},{1,5},{3,7},{8,12},{10,14},{9,13},{11,15},{16,20},{18,... | collective-permute-start | bytes 589832 | tf_op jit(solution)/shard_map/ppermute | solution.py:567
  104.9 36.8 %collective-permute-start.10 = (bf16[384,256]{0,1:T(8,128)(2,1)}, bf16[384,256]{0,1:T(8,128)(2,1)}, u32[]{:S(2)}, u32[]{:S(2)}) collective-permute-start(bf16[384,256]{0,1:T(8,128)(2,1)} %bitcast.24), channel_id=1, source_target_pairs={{0,2},{2,4},{4,6},{1,3},{3,5},{5,7},{8,10},{10,12},{12,14},{9,11},... | collective-permute-start | bytes 589832 | tf_op jit(solution)/shard_map/ppermute | solution.py:567
  142.6 21.7 %collective-permute-start.13 = (bf16[136,1536]{1,0:T(8,128)(2,1)}, bf16[136,1536]{1,0:T(8,128)(2,1)}, u32[]{:S(2)}, u32[]{:S(2)}) collective-permute-start(bf16[136,1536]{1,0:T(8,128)(2,1)} %pad_maximum_fusion.11), channel_id=1, source_target_pairs={{0,1},{1,0},{2,3},{3,2},{4,5},{5,4},{6,7},{7,6},{8,9},{9,8},{10,11... | collective-permute-start | bytes 1253384 | tf_op jit(solution)/shard_map/ppermute | solution.py:561
  145.9 39.9 %collective-permute-start.14 = (bf16[4,384,256]{1,2,0:T(8,128)(2,1)S(1)}, bf16[4,384,256]{1,2,0:T(8,128)(2,1)S(1)}, u32[]{:S(2)}, u32[]{:S(2)}) collective-permute-start(bf16[4,384,256]{1,2,0:T(8,128)(2,1)S(1)} %get-tuple-element.301), channel_id=1, source_target_pairs={{0,1},{1,0},{2,3},{3,2},{4,5},{5,4},{6,7},{7,6},{8,9},{9,8},{10,11... | collective-permute-start | bytes 2359304 | tf_op jit(solution)/shard_map/ppermute | solution.py:561
  166.6 24.5 %collective-permute-start.17 = (bf16[136,768]{1,0:T(8,128)(2,1)}, bf16[136,768]{1,0:T(8,128)(2,1)}, u32[]{:S(2)}, u32[]{:S(2)}) collective-permute-start(bf16[136,768]{1,0:T(8,128)(2,1)} %fusion.150), channel_id=1, source_target_pairs={{0,6},{1,7},{8,14},{9,15},{16,22},{17,23},{24,30},{25,31}} | collective-permute-start | bytes 626696 | tf_op jit(solution)/shard_map/ppermute | solution.py:567
  168.6 22.5 %collective-permute-start.16 = (bf16[136,768]{1,0:T(8,128)(2,1)}, bf16[136,768]{1,0:T(8,128)(2,1)}, u32[]{:S(2)}, u32[]{:S(2)}) collective-permute-start(bf16[136,768]{1,0:T(8,128)(2,1)} %fusion.150), channel_id=1, source_target_pairs={{0,4},{2,6},{1,5},{3,7},{8,12},{10,14},{9,13},{11,15},{16,20},{18,... | collective-permute-start | bytes 626696 | tf_op jit(solution)/shard_map/ppermute | solution.py:567
  234.7 25.1 %collective-permute-start.20 = (bf16[512,2048]{1,0:T(8,128)(2,1)S(1)}, bf16[512,2048]{1,0:T(8,128)(2,1)S(1)}, u32[]{:S(2)}, u32[]{:S(2)}) collective-permute-start(bf16[512,2048]{1,0:T(8,128)(2,1)S(1)} %convolution_convert_fusion.3), channel_id=1, source_target_pairs={{0,8},{8,0},{1,9},{9,1},{2,10},{10,2},{3,11},{11,3},{4,12},{12,4},... | collective-permute-start | bytes 6291464 | tf_op jit(solution)/shard_map/ppermute | solution.py:561
  236.2 27.3 %collective-permute-start.19 = (bf16[512,2048]{1,0:T(8,128)(2,1)S(1)}, bf16[512,2048]{1,0:T(8,128)(2,1)S(1)}, u32[]{:S(2)}, u32[]{:S(2)}) collective-permute-start(bf16[512,2048]{1,0:T(8,128)(2,1)S(1)} %convolution_convert_fusion.4), channel_id=1, source_target_pairs={{0,8},{8,0},{1,9},{9,1},{2,10},{10,2},{3,11},{11,3},{4,12},{12,4},... | collective-permute-start | bytes 6291464 | tf_op jit(solution)/shard_map/ppermute | solution.py:561
  280.1 29.6 %collective-permute-start.30 = (bf16[2,4,32,2048]{3,2,1,0:T(8,128)(2,1)}, bf16[2,4,32,2048]{3,2,1,0:T(8,128)(2,1)}, u32[]{:S(2)}, u32[]{:S(2)}) collective-permute-start(bf16[2,4,32,2048]{3,2,1,0:T(8,128)(2,1)} %bitcast.58), channel_id=1, source_target_pairs={{0,16},{16,0},{1,17},{17,1},{2,18},{18,2},{3,19},{19,3},{4,20},{20... | collective-permute-start | bytes 3145736 | tf_op jit(solution)/shard_map/ppermute | solution.py:561
  283.2 105.6 %collective-permute-start.31 = (bf16[512,2048]{1,0:T(8,128)(2,1)}, bf16[512,2048]{1,0:T(8,128)(2,1)}, u32[]{:S(2)}, u32[]{:S(2)}) collective-permute-start(bf16[512,2048]{1,0:T(8,128)(2,1)} %convolution_convert_fusion.2), channel_id=1, source_target_pairs={{0,8},{8,0},{1,9},{9,1},{2,10},{10,2},{3,11},{11,3},{4,12},{12,4},... | collective-permute-start | bytes 6291464 | tf_op jit(solution)/shard_map/ppermute | solution.py:561
  297.1 28.0 %collective-permute-start.32 = (bf16[512,1536]{1,0:T(8,128)(2,1)S(1)}, bf16[512,1536]{1,0:T(8,128)(2,1)}, u32[]{:S(2)}, u32[]{:S(2)}) collective-permute-start(bf16[512,1536]{1,0:T(8,128)(2,1)S(1)} %convolution_convert_fusion.1), channel_id=1, source_target_pairs={{0,8},{8,0},{1,9},{9,1},{2,10},{10,2},{3,11},{11,3},{4,12},{12,4},... | collective-permute-start | bytes 4718600 | tf_op jit(solution)/shard_map/ppermute | solution.py:561
  297.4 25.3 %collective-permute-start.29 = (bf16[2,4,32,2048]{3,2,1,0:T(8,128)(2,1)S(1)}, bf16[2,4,32,2048]{3,2,1,0:T(8,128)(2,1)S(1)}, u32[]{:S(2)}, u32[]{:S(2)}) collective-permute-start(bf16[2,4,32,2048]{3,2,1,0:T(8,128)(2,1)S(1)} %bitcast.303), channel_id=1, source_target_pairs={{0,1},{1,0},{2,3},{3,2},{4,5},{5,4},{6,7},{7,6},{8,9},{9,8},{10,11... | collective-permute-start | bytes 3145736 | tf_op jit(solution)/shard_map/ppermute | solution.py:561
  301.3 87.5 %collective-permute-start.28 = (bf16[136,768]{1,0:T(8,128)(2,1)S(1)}, bf16[136,768]{1,0:T(8,128)(2,1)}, u32[]{:S(2)}, u32[]{:S(2)}) collective-permute-start(bf16[136,768]{1,0:T(8,128)(2,1)S(1)} %fusion.147), channel_id=1, source_target_pairs={{6,0},{7,1},{14,8},{15,9},{22,16},{23,17},{30,24},{31,25}} | collective-permute-start | bytes 626696 | tf_op jit(solution)/shard_map/ppermute | solution.py:567
  309.7 79.0 %collective-permute-start.27 = (bf16[136,768]{1,0:T(8,128)(2,1)S(1)}, bf16[136,768]{1,0:T(8,128)(2,1)S(1)}, u32[]{:S(2)}, u32[]{:S(2)}) collective-permute-start(bf16[136,768]{1,0:T(8,128)(2,1)S(1)} %fusion.147), channel_id=1, source_target_pairs={{4,0},{6,2},{5,1},{7,3},{12,8},{14,10},{13,9},{15,11},{20,16},{22,... | collective-permute-start | bytes 626696 | tf_op jit(solution)/shard_map/ppermute | solution.py:567
  341.7 47.1 %collective-permute-start.26 = (bf16[136,768]{1,0:T(8,128)(2,1)S(1)}, bf16[136,768]{1,0:T(8,128)(2,1)S(1)}, u32[]{:S(2)}, u32[]{:S(2)}) collective-permute-start(bf16[136,768]{1,0:T(8,128)(2,1)S(1)} %fusion.147), channel_id=1, source_target_pairs={{2,0},{4,2},{6,4},{3,1},{5,3},{7,5},{10,8},{12,10},{14,12},{11,9},... | collective-permute-start | bytes 626696 | tf_op jit(solution)/shard_map/ppermute | solution.py:567
  346.5 125.5 %collective-permute-start.39 = (bf16[32,6144]{1,0:T(8,128)(2,1)}, bf16[32,6144]{1,0:T(8,128)(2,1)}, u32[]{:S(2)}, u32[]{:S(2)}) collective-permute-start(bf16[32,6144]{1,0:T(8,128)(2,1)} %get-tuple-element.277), channel_id=1, source_target_pairs={{0,6},{2,0},{4,2},{6,4},{1,7},{3,1},{5,3},{7,5},{8,14},{10,8},{12,... | collective-permute-start | bytes 1179656 | tf_op jit(solution)/shard_map/ppermute | solution.py:561
  393.3 28.6 %collective-permute-start.36 = (bf16[4,384,256]{2,1,0:T(8,128)(2,1)}, bf16[4,384,256]{2,1,0:T(8,128)(2,1)}, u32[]{:S(2)}, u32[]{:S(2)}) collective-permute-start(bf16[4,384,256]{2,1,0:T(8,128)(2,1)} %copy-done.18), channel_id=1, source_target_pairs={{0,1},{1,0},{2,3},{3,2},{4,5},{5,4},{6,7},{7,6},{8,9},{9,8},{10,11... | collective-permute-start | bytes 2359304 | tf_op jit(solution)/shard_map/ppermute | solution.py:561
  417.4 48.2 %collective-permute-start.43 = (bf16[2,4,32,1536]{3,2,1,0:T(8,128)(2,1)}, bf16[2,4,32,1536]{3,2,1,0:T(8,128)(2,1)}, u32[]{:S(2)}, u32[]{:S(2)}) collective-permute-start(bf16[2,4,32,1536]{3,2,1,0:T(8,128)(2,1)} %fusion.121), channel_id=1, source_target_pairs={{0,1},{1,0},{2,3},{3,2},{4,5},{5,4},{6,7},{7,6},{8,9},{9,8},{10,11... | collective-permute-start | bytes 2359304 | tf_op jit(solution)/shard_map/ppermute | solution.py:561
  435.3 25.8 %collective-permute-start.41 = (bf16[384,256]{1,0:T(8,128)(2,1)S(1)}, bf16[384,256]{1,0:T(8,128)(2,1)S(1)}, u32[]{:S(2)}, u32[]{:S(2)}) collective-permute-start(bf16[384,256]{1,0:T(8,128)(2,1)S(1)} %get-tuple-element.299), channel_id=1, source_target_pairs={{4,0},{6,2},{5,1},{7,3},{12,8},{14,10},{13,9},{15,11},{20,16},{22,... | collective-permute-start | bytes 589832 | tf_op jit(solution)/shard_map/ppermute | solution.py:567
  443.4 33.5 %collective-permute-start.38 = (bf16[32,6144]{1,0:T(8,128)(2,1)}, bf16[32,6144]{1,0:T(8,128)(2,1)}, u32[]{:S(2)}, u32[]{:S(2)}) collective-permute-start(bf16[32,6144]{1,0:T(8,128)(2,1)} %get-tuple-element.278), channel_id=1, source_target_pairs={{0,4},{2,6},{4,0},{6,2},{1,5},{3,7},{5,1},{7,3},{8,12},{10,14},{12... | collective-permute-start | bytes 1179656 | tf_op jit(solution)/shard_map/ppermute | solution.py:561
  446.6 30.3 %collective-permute-start.37 = (bf16[32,6144]{1,0:T(8,128)(2,1)}, bf16[32,6144]{1,0:T(8,128)(2,1)}, u32[]{:S(2)}, u32[]{:S(2)}) collective-permute-start(bf16[32,6144]{1,0:T(8,128)(2,1)} %get-tuple-element.279), channel_id=1, source_target_pairs={{0,2},{2,4},{4,6},{6,0},{1,3},{3,5},{5,7},{7,1},{8,10},{10,12},{12... | collective-permute-start | bytes 1179656 | tf_op jit(solution)/shard_map/ppermute | solution.py:561
  461.1 26.4 %collective-permute-start.44 = (bf16[2,4,32,2048]{3,2,1,0:T(8,128)(2,1)}, bf16[2,4,32,2048]{3,2,1,0:T(8,128)(2,1)}, u32[]{:S(2)}, u32[]{:S(2)}) collective-permute-start(bf16[2,4,32,2048]{3,2,1,0:T(8,128)(2,1)} %fusion.110), channel_id=1, source_target_pairs={{0,16},{16,0},{1,17},{17,1},{2,18},{18,2},{3,19},{19,3},{4,20},{20... | collective-permute-start | bytes 3145736 | tf_op jit(solution)/shard_map/ppermute | solution.py:561
  469.3 31.1 %collective-permute-start.47 = (bf16[4,32,1536]{2,1,0:T(8,128)(2,1)}, bf16[4,32,1536]{2,1,0:T(8,128)(2,1)}, u32[]{:S(2)}, u32[]{:S(2)}) collective-permute-start(bf16[4,32,1536]{2,1,0:T(8,128)(2,1)} %fusion.151), channel_id=1, source_target_pairs={{0,16},{16,0},{1,17},{17,1},{2,18},{18,2},{3,19},{19,3},{4,20},{20... | collective-permute-start | bytes 1179656 | tf_op jit(solution)/shard_map/ppermute | solution.py:561
  472.0 30.2 %collective-permute-start.46 = (bf16[512,896]{1,0:T(8,128)(2,1)S(1)}, bf16[512,896]{1,0:T(8,128)(2,1)S(1)}, u32[]{:S(2)}, u32[]{:S(2)}) collective-permute-start(bf16[512,896]{1,0:T(8,128)(2,1)S(1)} %convolution_convert_fusion.8), channel_id=1, source_target_pairs={{0,8},{8,0},{1,9},{9,1},{2,10},{10,2},{3,11},{11,3},{4,12},{12,4},... | collective-permute-start | bytes 2752520 | tf_op jit(solution)/shard_map/ppermute | solution.py:561
  501.8 71.2 %collective-permute-start.64 = (bf16[32,3584]{1,0:T(8,128)(2,1)S(1)}, bf16[32,3584]{1,0:T(8,128)(2,1)S(1)}, u32[]{:S(2)}, u32[]{:S(2)}) collective-permute-start(bf16[32,3584]{1,0:T(8,128)(2,1)S(1)} %get-tuple-element.280), channel_id=1, source_target_pairs={{0,6},{2,0},{4,2},{6,4},{1,7},{3,1},{5,3},{7,5},{8,14},{10,8},{12,... | collective-permute-start | bytes 688136 | tf_op jit(solution)/shard_map/ppermute | solution.py:561
  502.1 77.4 %collective-permute-start.63 = (bf16[32,3584]{1,0:T(8,128)(2,1)S(1)}, bf16[32,3584]{1,0:T(8,128)(2,1)S(1)}, u32[]{:S(2)}, u32[]{:S(2)}) collective-permute-start(bf16[32,3584]{1,0:T(8,128)(2,1)S(1)} %get-tuple-element.281), channel_id=1, source_target_pairs={{0,4},{2,6},{4,0},{6,2},{1,5},{3,7},{5,1},{7,3},{8,12},{10,14},{12... | collective-permute-start | bytes 688136 | tf_op jit(solution)/shard_map/ppermute | solution.py:561
  520.7 22.8 %collective-permute-start.52 = (bf16[2,4,32,1792]{3,2,1,0:T(8,128)(2,1)S(1)}, bf16[2,4,32,1792]{3,2,1,0:T(8,128)(2,1)S(1)}, u32[]{:S(2)}, u32[]{:S(2)}) collective-permute-start(bf16[2,4,32,1792]{3,2,1,0:T(8,128)(2,1)S(1)} %bitcast.304), channel_id=1, source_target_pairs={{0,1},{1,0},{2,3},{3,2},{4,5},{5,4},{6,7},{7,6},{8,9},{9,8},{10,11... | collective-permute-start | bytes 2752520 | tf_op jit(solution)/shard_map/ppermute | solution.py:561
  548.6 30.8 %collective-permute-start.62 = (bf16[32,3584]{1,0:T(8,128)(2,1)S(1)}, bf16[32,3584]{1,0:T(8,128)(2,1)S(1)}, u32[]{:S(2)}, u32[]{:S(2)}) collective-permute-start(bf16[32,3584]{1,0:T(8,128)(2,1)S(1)} %get-tuple-element.282), channel_id=1, source_target_pairs={{0,2},{2,4},{4,6},{6,0},{1,3},{3,5},{5,7},{7,1},{8,10},{10,12},{12... | collective-permute-start | bytes 688136 | tf_op jit(solution)/shard_map/ppermute | solution.py:561
  (159 other events, 1607.2 us)
Sparse Core Ops, SparseCore 0:
  41.1 160.5 all-gather.1

commit v8 on v7

--- a/solution.py
+++ b/solution.py
@@ -938,7 +938,7 @@
         [after(in_gate_total, *rested)], [after(out_total, *rested)], mid_got
     )
     mid_later = []
-    mid_parts = send_layers(layer_sums(*mid_both, mid_later))
+    mid_layer = layer_sums(*mid_both, mid_later)
     grad_query = turn_rows(grad_query_cols, cosine, -sine).T.astype(jnp.bfloat16)
     own_cols = own_grads.T.reshape(KVHEADS, 2, HEAD_DIM, row_count)
     grad_keys = turn_rows(own_cols[:, 0].reshape(key_width, row_count), cosine, -sine)
@@ -979,6 +979,7 @@
     )
     conv_total = core_sum(normed_x, grad_conv_low, "x", last_core_got)
     last_got, last_later = [], []
+    mid_parts = send_layers(after(mid_layer, *last_core_got))
     last_both = after(first_sums([conv_total], [few_total], last_got), *last_got)
     last_parts = send_layers(layer_sums(*last_both, last_later))
     last_parts, *mid_parts = after((tuple(last_parts), *mid_parts), *last_later)

time: 604 us -> 621 us (1.028)
  waiting for transfers between devices: 165 us -> 193 us
  starting transfers between devices: 136 us -> 122 us
    ppermute x12, waiting for transfers between devices: 11.8 us -> 30.3 us  [moved_along(): return lax.ppermute(block, axis, route)]
    ppermute x46, starting transfers between devices: 102 us -> 91.9 us  [shifted(): lax.ppermute(block, axis, [(i, (i + distance) % count) for i in range(cou...]
    unnamed x252 -> x268, local copies, waits for them, and re-layouts: 20.6 us -> 21.4 us
  transfers between devices with their start and end apart: 66 -> 66, of which waited for: 29 -> 27; matrix products, arithmetic and copies ran while one was open for 30% -> 29% of each run, Pallas kernels for 5% -> 5%
where the time goes in v8:
time: 621 us; the launch traced here: 610 us
  waiting for transfers between devices  193 us (31%)
  starting transfers between devices  122 us (20%)
  matrix products  114 us (18%)
  local copies, waits for them, and re-layouts  74.1 us (12%)
  other arithmetic  59.2 us (10%)
  Pallas kernels  30.3 us (5%)
  between operations  17.1 us (3%)
    ppermute x46, waiting for transfers between devices, shifted(): lax.ppermute(block, axis, [(i, (i + distance) % count) for i in range(cou...  141 us
    ppermute x46, starting transfers between devices, shifted(): lax.ppermute(block, axis, [(i, (i + distance) % count) for i in range(cou...  91.9 us
    dot_general x17, matrix products, plain_dot(): return jnp.dot(left, right, preferred_element_type=jnp.float32)  47.3 us
    dot_general x9, matrix products, back_product(): lax.dot_general(grad_rows, weight_matrix, (((1,), (1,)), ((), ())), prefe...  31.6 us
    ppermute x12, waiting for transfers between devices, moved_along(): return lax.ppermute(block, axis, route)  30.3 us
    dot_general x17, matrix products, outer_product(): lax.dot_general(left, right, (((0,), (0,)), ((), ())), preferred_element_...  29.7 us
    ppermute x12, starting transfers between devices, moved_along(): return lax.ppermute(block, axis, route)  24.4 us
    unnamed x268, local copies, waits for them, and re-layouts  21.4 us
  transfers between devices with their start and end apart: 66, of which 27 were waited for; matrix products, arithmetic and copies ran while one was open for 29% of the time, Pallas kernels for 5%

profile of v8, /device:TPU:0, one launch (start us, length us, event | category | flops | bytes accessed | tf_op | source)
XLA Modules:
  0.0 610.5 jit_solution(2629717043751401039)
XLA Ops:
  22.9 6.4 %collective-permute-done.1 = bf16[32,2688]{1,0:T(8,128)(2,1)S(1)} collective-permute-done((bf16[32,2688]{1,0:T(8,128)(2,1)S(1)}, bf16[32,2688]{1,0:T(8,128)(2,1)S(1)}, u32[]{:S(2)}, u32[]{:S(2)}) %collective-permute-start.1) | collective-permute-done | bytes 172064 | tf_op jit(solution)/shard_map/ppermute | solution.py:561
  32.5 6.4 %collective-permute-done.3 = bf16[128,1280]{1,0:T(8,128)(2,1)S(1)} collective-permute-done((bf16[128,1280]{1,0:T(8,128)(2,1)S(1)}, bf16[128,1280]{1,0:T(8,128)(2,1)S(1)}, u32[]{:S(2)}, u32[]{:S(2)}) %collective-permute-start.3) | collective-permute-done | bytes 327712 | tf_op jit(solution)/shard_map/ppermute | solution.py:561
  53.2 14.9 %collective-permute-done.5 = bf16[256,1280]{1,0:T(8,128)(2,1)S(1)} collective-permute-done((bf16[256,1280]{1,0:T(8,128)(2,1)S(1)}, bf16[256,1280]{1,0:T(8,128)(2,1)S(1)}, u32[]{:S(2)}, u32[]{:S(2)}) %collective-permute-start.5) | collective-permute-done | bytes 655392 | tf_op jit(solution)/shard_map/ppermute | solution.py:561
  97.1 5.8 collective-permute-start.12
  134.1 6.3 %ssd.1 = (f32[3,128,1536]{2,1,0:T(8,128)S(1)}, f32[3,128,1536]{2,1,0:T(8,128)S(1)}, f32[128,1536]{1,0:T(8,128)S(1)}, f32[8,1536]{1,0:T(8,128)S(1)}) custom-call(f32[3,128,1792]{2,1,0:T(8,128)} %bitcast.296, f32[3,128,24]{2,1,0:T(8,128)S(1)} %copy.127.cum_ref, f32[3,24,128]{2,1,0:T(8,128)S(1)} %get-tuple-element.322.cum_rows_ref, ...), custom_call_target="tpu_custom_call" | custom-call | flops 5898240000 | bytes 11010048 | tf_op jit(solution)/shard_map/ssd/pallas_call | solution.py:370
  147.3 17.1 %collective-permute-done.13 = bf16[136,1536]{1,0:T(8,128)(2,1)} collective-permute-done((bf16[136,1536]{1,0:T(8,128)(2,1)}, bf16[136,1536]{1,0:T(8,128)(2,1)}, u32[]{:S(2)}, u32[]{:S(2)}) %collective-permute-start.13) | collective-permute-done | bytes 417824 | tf_op jit(solution)/shard_map/ppermute | solution.py:561
  173.2 12.6 %collective-permute-done.14 = bf16[4,384,256]{1,2,0:T(8,128)(2,1)S(1)} collective-permute-done((bf16[4,384,256]{1,2,0:T(8,128)(2,1)S(1)}, bf16[4,384,256]{1,2,0:T(8,128)(2,1)S(1)}, u32[]{:S(2)}, u32[]{:S(2)}) %collective-permute-start.14) | collective-permute-done | bytes 786464 | tf_op jit(solution)/shard_map/ppermute | solution.py:561
  208.9 4.5 multiply_reduce_fusion.6
  225.7 5.1 fusion.64
  236.7 4.9 fusion.106
  250.8 5.5 collective-permute-done.24
  263.4 4.9 multiply_reduce_fusion.4
  270.0 4.7 fusion.49
  290.0 4.5 fusion.68
  303.6 6.9 %attend_back.1 = (f32[512,384]{1,0:T(8,128)S(1)}, f32[4,384,256]{2,1,0:T(8,128)S(1)}, bf16[4,384,256]{2,1,0:T(8,128)(2,1)S(1)}) custom-call(s32[2]{0:T(128)S(1)} %pad_add_fusion.2.place_ref, bf16[512,384]{1,0:T(8,128)(2,1)S(1)} %bitcast.279, bf16[384,512]{1,0:T(8,128)(2,1)S(1)} %bitcast.281, bf16[512,384]{1,0:T(8,128)(2,1)S(1)} %copy.137.grad_ref, ...), custom_call_target="tpu_custom_call" | custom-call | flops 36238786560 | bytes 3145728 | tf_op jit(solution)/shard_map/attend_back/pallas_call | solution.py:251
  313.7 10.1 %collective-permute-done.29 = bf16[2,4,32,2048]{3,2,1,0:T(8,128)(2,1)S(1)} collective-permute-done((bf16[2,4,32,2048]{3,2,1,0:T(8,128)(2,1)S(1)}, bf16[2,4,32,2048]{3,2,1,0:T(8,128)(2,1)S(1)}, u32[]{:S(2)}, u32[]{:S(2)}) %collective-permute-start.29) | collective-permute-done | bytes 1048608 | tf_op jit(solution)/shard_map/ppermute | solution.py:561
  328.2 4.1 convert_add_fusion.5
  332.3 10.4 %collective-permute-done.35 = bf16[4,32,3072]{2,1,0:T(8,128)(2,1)S(1)} collective-permute-done((bf16[4,32,3072]{2,1,0:T(8,128)(2,1)S(1)}, bf16[4,32,3072]{2,1,0:T(8,128)(2,1)S(1)}, u32[]{:S(2)}, u32[]{:S(2)}) %collective-permute-start.35) | collective-permute-done | bytes 786464 | tf_op jit(solution)/shard_map/ppermute | solution.py:561
  348.1 42.1 %collective-permute-start.39 = (bf16[32,6144]{1,0:T(8,128)(2,1)}, bf16[32,6144]{1,0:T(8,128)(2,1)}, u32[]{:S(2)}, u32[]{:S(2)}) collective-permute-start(bf16[32,6144]{1,0:T(8,128)(2,1)} %get-tuple-element.279), channel_id=1, source_target_pairs={{0,6},{2,0},{4,2},{6,4},{1,7},{3,1},{5,3},{7,5},{8,14},{10,8},{12,... | collective-permute-start | bytes 1179656 | tf_op jit(solution)/shard_map/ppermute | solution.py:561
  394.0 4.9 convert_add_fusion
  404.3 13.6 %ssd_back.1 = (f32[3,128,1792]{2,1,0:T(8,128)}, f32[3,128,24]{2,1,0:T(8,128)S(1)}, f32[3,128,24]{2,1,0:T(8,128)S(1)}, f32[1,1536]{1,0:T(1,128)S(1)}) custom-call(f32[3,128,1792]{2,1,0:T(8,128)} %bitcast.297, f32[3,128,24]{2,1,0:T(8,128)S(1)} %copy-done.18, f32[3,24,128]{2,1,0:T(8,128)S(1)} %copy-done.22, f32[3,128,24]{2,1,0:T(8,128)S(1)} %bitcast.285, ...), custom_call_target="tpu_custom_call" | custom-call | flops 14745600000 | bytes 11010048 | tf_op jit(solution)/shard_map/ssd_back/pallas_call | solution.py:524
  426.6 4.3 multiply_reduce_fusion.3
  440.0 7.0 %collective-permute-done.40 = bf16[384,256]{1,0:T(8,128)(2,1)S(1)} collective-permute-done((bf16[384,256]{1,0:T(8,128)(2,1)S(1)}, bf16[384,256]{1,0:T(8,128)(2,1)S(1)}, u32[]{:S(2)}, u32[]{:S(2)}) %collective-permute-start.40) | collective-permute-done | bytes 196640 | tf_op jit(solution)/shard_map/ppermute | solution.py:567
  447.1 23.2 %collective-permute-done.41 = bf16[384,256]{1,0:T(8,128)(2,1)S(1)} collective-permute-done((bf16[384,256]{1,0:T(8,128)(2,1)S(1)}, bf16[384,256]{1,0:T(8,128)(2,1)S(1)}, u32[]{:S(2)}, u32[]{:S(2)}) %collective-permute-start.41) | collective-permute-done | bytes 196640 | tf_op jit(solution)/shard_map/ppermute | solution.py:567
  481.3 15.4 %collective-permute-done.44 = bf16[2,4,32,2048]{3,2,1,0:T(8,128)(2,1)} collective-permute-done((bf16[2,4,32,2048]{3,2,1,0:T(8,128)(2,1)}, bf16[2,4,32,2048]{3,2,1,0:T(8,128)(2,1)}, u32[]{:S(2)}, u32[]{:S(2)}) %collective-permute-start.44) | collective-permute-done | bytes 1048608 | tf_op jit(solution)/shard_map/ppermute | solution.py:561
  503.6 5.8 collective-permute-done.45
  537.1 18.0 %collective-permute-done.52 = bf16[2,4,32,1792]{3,2,1,0:T(8,128)(2,1)S(1)} collective-permute-done((bf16[2,4,32,1792]{3,2,1,0:T(8,128)(2,1)S(1)}, bf16[2,4,32,1792]{3,2,1,0:T(8,128)(2,1)S(1)}, u32[]{:S(2)}, u32[]{:S(2)}) %collective-permute-start.52) | collective-permute-done | bytes 917536 | tf_op jit(solution)/shard_map/ppermute | solution.py:561
  563.3 5.3 collective-permute-done.55
  568.8 7.4 %collective-permute-done.57 = f32[8,1792]{1,0:T(8,128)S(1)} collective-permute-done((f32[8,1792]{1,0:T(8,128)S(1)}, f32[8,1792]{1,0:T(8,128)S(1)}, u32[]{:S(2)}, u32[]{:S(2)}) %collective-permute-start.57) | collective-permute-done | bytes 57376 | tf_op jit(solution)/shard_map/ppermute | solution.py:664
  578.0 4.2 collective-permute-done.58
  585.3 9.1 %collective-permute-start.59 = (bf16[32,2688]{1,0:T(8,128)(2,1)S(1)}, bf16[32,2688]{1,0:T(8,128)(2,1)S(1)}, u32[]{:S(2)}, u32[]{:S(2)}) collective-permute-start(bf16[32,2688]{1,0:T(8,128)(2,1)S(1)} %get-tuple-element.306), channel_id=1, source_target_pairs={{0,2},{2,4},{4,6},{6,0},{1,3},{3,5},{5,7},{7,1},{8,10},{10,12},{12... | collective-permute-start | bytes 516104 | tf_op jit(solution)/shard_map/ppermute | solution.py:561
  594.9 4.0 collective-permute-done.59
  (645 shorter events, 293.7 us)
Async XLA Ops:
  7.2 194.9 %all-gather.2.cloned.1.call-start = ((), (), s32[]{:S(2)}) async-start(), calls=%async_computation | async-start | bytes 20545536 | tf_op jit(solution)/shard_map/all_gather | solution.py:782
  47.9 21.3 %collective-permute-start.6 = (bf16[256,1408]{1,0:T(8,128)(2,1)S(1)}, bf16[256,1408]{1,0:T(8,128)(2,1)S(1)}, u32[]{:S(2)}, u32[]{:S(2)}) collective-permute-start(bf16[256,1408]{1,0:T(8,128)(2,1)S(1)} %constant_dynamic-update-slice_fusion.2), channel_id=1, source_target_pairs={{0,1},{1,0},{2,3},{3,2},{4,5},{5,4},{6,7},{7,6},{8,9},{9,8},{10,11... | collective-permute-start | bytes 2162696 | tf_op jit(solution)/shard_map/ppermute | solution.py:561
  80.2 34.4 %collective-permute-start.8 = (bf16[512,1280]{1,0:T(8,128)(2,1)}, bf16[512,1280]{1,0:T(8,128)(2,1)}, u32[]{:S(2)}, u32[]{:S(2)}) collective-permute-start(bf16[512,1280]{1,0:T(8,128)(2,1)} %constant_dynamic-update-slice_fusion.6), channel_id=1, source_target_pairs={{0,8},{8,0},{1,9},{9,1},{2,10},{10,2},{3,11},{11,3},{4,12},{12,4},... | collective-permute-start | bytes 3932168 | tf_op jit(solution)/shard_map/ppermute | solution.py:561
  97.1 44.7 %collective-permute-start.12 = (bf16[384,256]{0,1:T(8,128)(2,1)}, bf16[384,256]{0,1:T(8,128)(2,1)}, u32[]{:S(2)}, u32[]{:S(2)}) collective-permute-start(bf16[384,256]{0,1:T(8,128)(2,1)} %bitcast.24), channel_id=1, source_target_pairs={{0,6},{1,7},{8,14},{9,15},{16,22},{17,23},{24,30},{25,31}} | collective-permute-start | bytes 589832 | tf_op jit(solution)/shard_map/ppermute | solution.py:567
  102.9 38.9 %collective-permute-start.11 = (bf16[384,256]{0,1:T(8,128)(2,1)}, bf16[384,256]{0,1:T(8,128)(2,1)}, u32[]{:S(2)}, u32[]{:S(2)}) collective-permute-start(bf16[384,256]{0,1:T(8,128)(2,1)} %bitcast.24), channel_id=1, source_target_pairs={{0,4},{2,6},{1,5},{3,7},{8,12},{10,14},{9,13},{11,15},{16,20},{18,... | collective-permute-start | bytes 589832 | tf_op jit(solution)/shard_map/ppermute | solution.py:567
  104.9 36.9 %collective-permute-start.10 = (bf16[384,256]{0,1:T(8,128)(2,1)}, bf16[384,256]{0,1:T(8,128)(2,1)}, u32[]{:S(2)}, u32[]{:S(2)}) collective-permute-start(bf16[384,256]{0,1:T(8,128)(2,1)} %bitcast.24), channel_id=1, source_target_pairs={{0,2},{2,4},{4,6},{1,3},{3,5},{5,7},{8,10},{10,12},{12,14},{9,11},... | collective-permute-start | bytes 589832 | tf_op jit(solution)/shard_map/ppermute | solution.py:567
  142.7 21.7 %collective-permute-start.13 = (bf16[136,1536]{1,0:T(8,128)(2,1)}, bf16[136,1536]{1,0:T(8,128)(2,1)}, u32[]{:S(2)}, u32[]{:S(2)}) collective-permute-start(bf16[136,1536]{1,0:T(8,128)(2,1)} %pad_maximum_fusion.11), channel_id=1, source_target_pairs={{0,1},{1,0},{2,3},{3,2},{4,5},{5,4},{6,7},{7,6},{8,9},{9,8},{10,11... | collective-permute-start | bytes 1253384 | tf_op jit(solution)/shard_map/ppermute | solution.py:561
  146.0 39.9 %collective-permute-start.14 = (bf16[4,384,256]{1,2,0:T(8,128)(2,1)S(1)}, bf16[4,384,256]{1,2,0:T(8,128)(2,1)S(1)}, u32[]{:S(2)}, u32[]{:S(2)}) collective-permute-start(bf16[4,384,256]{1,2,0:T(8,128)(2,1)S(1)} %get-tuple-element.303), channel_id=1, source_target_pairs={{0,1},{1,0},{2,3},{3,2},{4,5},{5,4},{6,7},{7,6},{8,9},{9,8},{10,11... | collective-permute-start | bytes 2359304 | tf_op jit(solution)/shard_map/ppermute | solution.py:561
  166.7 24.5 %collective-permute-start.17 = (bf16[136,768]{1,0:T(8,128)(2,1)}, bf16[136,768]{1,0:T(8,128)(2,1)}, u32[]{:S(2)}, u32[]{:S(2)}) collective-permute-start(bf16[136,768]{1,0:T(8,128)(2,1)} %fusion.147), channel_id=1, source_target_pairs={{0,6},{1,7},{8,14},{9,15},{16,22},{17,23},{24,30},{25,31}} | collective-permute-start | bytes 626696 | tf_op jit(solution)/shard_map/ppermute | solution.py:567
  168.6 22.5 %collective-permute-start.16 = (bf16[136,768]{1,0:T(8,128)(2,1)}, bf16[136,768]{1,0:T(8,128)(2,1)}, u32[]{:S(2)}, u32[]{:S(2)}) collective-permute-start(bf16[136,768]{1,0:T(8,128)(2,1)} %fusion.147), channel_id=1, source_target_pairs={{0,4},{2,6},{1,5},{3,7},{8,12},{10,14},{9,13},{11,15},{16,20},{18,... | collective-permute-start | bytes 626696 | tf_op jit(solution)/shard_map/ppermute | solution.py:567
  234.8 25.0 %collective-permute-start.20 = (bf16[512,2048]{1,0:T(8,128)(2,1)S(1)}, bf16[512,2048]{1,0:T(8,128)(2,1)S(1)}, u32[]{:S(2)}, u32[]{:S(2)}) collective-permute-start(bf16[512,2048]{1,0:T(8,128)(2,1)S(1)} %convolution_convert_fusion.3), channel_id=1, source_target_pairs={{0,8},{8,0},{1,9},{9,1},{2,10},{10,2},{3,11},{11,3},{4,12},{12,4},... | collective-permute-start | bytes 6291464 | tf_op jit(solution)/shard_map/ppermute | solution.py:561
  236.2 27.2 %collective-permute-start.19 = (bf16[512,2048]{1,0:T(8,128)(2,1)S(1)}, bf16[512,2048]{1,0:T(8,128)(2,1)S(1)}, u32[]{:S(2)}, u32[]{:S(2)}) collective-permute-start(bf16[512,2048]{1,0:T(8,128)(2,1)S(1)} %convolution_convert_fusion.4), channel_id=1, source_target_pairs={{0,8},{8,0},{1,9},{9,1},{2,10},{10,2},{3,11},{11,3},{4,12},{12,4},... | collective-permute-start | bytes 6291464 | tf_op jit(solution)/shard_map/ppermute | solution.py:561
  280.0 30.6 %collective-permute-start.30 = (bf16[2,4,32,2048]{3,2,1,0:T(8,128)(2,1)}, bf16[2,4,32,2048]{3,2,1,0:T(8,128)(2,1)}, u32[]{:S(2)}, u32[]{:S(2)}) collective-permute-start(bf16[2,4,32,2048]{3,2,1,0:T(8,128)(2,1)} %bitcast.58), channel_id=1, source_target_pairs={{0,16},{16,0},{1,17},{17,1},{2,18},{18,2},{3,19},{19,3},{4,20},{20... | collective-permute-start | bytes 3145736 | tf_op jit(solution)/shard_map/ppermute | solution.py:561
  283.2 107.0 %collective-permute-start.31 = (bf16[512,2048]{1,0:T(8,128)(2,1)}, bf16[512,2048]{1,0:T(8,128)(2,1)}, u32[]{:S(2)}, u32[]{:S(2)}) collective-permute-start(bf16[512,2048]{1,0:T(8,128)(2,1)} %convolution_convert_fusion.2), channel_id=1, source_target_pairs={{0,8},{8,0},{1,9},{9,1},{2,10},{10,2},{3,11},{11,3},{4,12},{12,4},... | collective-permute-start | bytes 6291464 | tf_op jit(solution)/shard_map/ppermute | solution.py:561
  298.2 28.4 %collective-permute-start.32 = (bf16[512,1536]{1,0:T(8,128)(2,1)}, bf16[512,1536]{1,0:T(8,128)(2,1)}, u32[]{:S(2)}, u32[]{:S(2)}) collective-permute-start(bf16[512,1536]{1,0:T(8,128)(2,1)} %convolution_convert_fusion.1), channel_id=1, source_target_pairs={{0,8},{8,0},{1,9},{9,1},{2,10},{10,2},{3,11},{11,3},{4,12},{12,4},... | collective-permute-start | bytes 4718600 | tf_op jit(solution)/shard_map/ppermute | solution.py:561
  298.5 25.3 %collective-permute-start.29 = (bf16[2,4,32,2048]{3,2,1,0:T(8,128)(2,1)S(1)}, bf16[2,4,32,2048]{3,2,1,0:T(8,128)(2,1)S(1)}, u32[]{:S(2)}, u32[]{:S(2)}) collective-permute-start(bf16[2,4,32,2048]{3,2,1,0:T(8,128)(2,1)S(1)} %bitcast.303), channel_id=1, source_target_pairs={{0,1},{1,0},{2,3},{3,2},{4,5},{5,4},{6,7},{7,6},{8,9},{9,8},{10,11... | collective-permute-start | bytes 3145736 | tf_op jit(solution)/shard_map/ppermute | solution.py:561
  302.2 88.0 %collective-permute-start.28 = (bf16[136,768]{1,0:T(8,128)(2,1)S(1)}, bf16[136,768]{1,0:T(8,128)(2,1)}, u32[]{:S(2)}, u32[]{:S(2)}) collective-permute-start(bf16[136,768]{1,0:T(8,128)(2,1)S(1)} %fusion.144), channel_id=1, source_target_pairs={{6,0},{7,1},{14,8},{15,9},{22,16},{23,17},{30,24},{31,25}} | collective-permute-start | bytes 626696 | tf_op jit(solution)/shard_map/ppermute | solution.py:567
  310.6 79.6 %collective-permute-start.27 = (bf16[136,768]{1,0:T(8,128)(2,1)S(1)}, bf16[136,768]{1,0:T(8,128)(2,1)S(1)}, u32[]{:S(2)}, u32[]{:S(2)}) collective-permute-start(bf16[136,768]{1,0:T(8,128)(2,1)S(1)} %fusion.144), channel_id=1, source_target_pairs={{4,0},{6,2},{5,1},{7,3},{12,8},{14,10},{13,9},{15,11},{20,16},{22,... | collective-permute-start | bytes 626696 | tf_op jit(solution)/shard_map/ppermute | solution.py:567
  342.7 47.4 %collective-permute-start.26 = (bf16[136,768]{1,0:T(8,128)(2,1)S(1)}, bf16[136,768]{1,0:T(8,128)(2,1)S(1)}, u32[]{:S(2)}, u32[]{:S(2)}) collective-permute-start(bf16[136,768]{1,0:T(8,128)(2,1)S(1)} %fusion.144), channel_id=1, source_target_pairs={{2,0},{4,2},{6,4},{3,1},{5,3},{7,5},{10,8},{12,10},{14,12},{11,9},... | collective-permute-start | bytes 626696 | tf_op jit(solution)/shard_map/ppermute | solution.py:567
  348.1 133.2 %collective-permute-start.39 = (bf16[32,6144]{1,0:T(8,128)(2,1)}, bf16[32,6144]{1,0:T(8,128)(2,1)}, u32[]{:S(2)}, u32[]{:S(2)}) collective-permute-start(bf16[32,6144]{1,0:T(8,128)(2,1)} %get-tuple-element.279), channel_id=1, source_target_pairs={{0,6},{2,0},{4,2},{6,4},{1,7},{3,1},{5,3},{7,5},{8,14},{10,8},{12,... | collective-permute-start | bytes 1179656 | tf_op jit(solution)/shard_map/ppermute | solution.py:561
  401.8 24.7 %collective-permute-start.36 = (bf16[4,384,256]{2,1,0:T(8,128)(2,1)}, bf16[4,384,256]{2,1,0:T(8,128)(2,1)}, u32[]{:S(2)}, u32[]{:S(2)}) collective-permute-start(bf16[4,384,256]{2,1,0:T(8,128)(2,1)} %copy-done.23), channel_id=1, source_target_pairs={{0,1},{1,0},{2,3},{3,2},{4,5},{5,4},{6,7},{7,6},{8,9},{9,8},{10,11... | collective-permute-start | bytes 2359304 | tf_op jit(solution)/shard_map/ppermute | solution.py:561
  421.8 52.9 %collective-permute-start.43 = (bf16[2,4,32,1536]{3,2,1,0:T(8,128)(2,1)}, bf16[2,4,32,1536]{3,2,1,0:T(8,128)(2,1)}, u32[]{:S(2)}, u32[]{:S(2)}) collective-permute-start(bf16[2,4,32,1536]{3,2,1,0:T(8,128)(2,1)} %fusion.120), channel_id=1, source_target_pairs={{0,1},{1,0},{2,3},{3,2},{4,5},{5,4},{6,7},{7,6},{8,9},{9,8},{10,11... | collective-permute-start | bytes 2359304 | tf_op jit(solution)/shard_map/ppermute | solution.py:561
  436.8 33.5 %collective-permute-start.41 = (bf16[384,256]{1,0:T(8,128)(2,1)S(1)}, bf16[384,256]{1,0:T(8,128)(2,1)S(1)}, u32[]{:S(2)}, u32[]{:S(2)}) collective-permute-start(bf16[384,256]{1,0:T(8,128)(2,1)S(1)} %get-tuple-element.301), channel_id=1, source_target_pairs={{4,0},{6,2},{5,1},{7,3},{12,8},{14,10},{13,9},{15,11},{20,16},{22,... | collective-permute-start | bytes 589832 | tf_op jit(solution)/shard_map/ppermute | solution.py:567
  447.0 34.4 %collective-permute-start.38 = (bf16[32,6144]{1,0:T(8,128)(2,1)}, bf16[32,6144]{1,0:T(8,128)(2,1)}, u32[]{:S(2)}, u32[]{:S(2)}) collective-permute-start(bf16[32,6144]{1,0:T(8,128)(2,1)} %get-tuple-element.280), channel_id=1, source_target_pairs={{0,4},{2,6},{4,0},{6,2},{1,5},{3,7},{5,1},{7,3},{8,12},{10,14},{12... | collective-permute-start | bytes 1179656 | tf_op jit(solution)/shard_map/ppermute | solution.py:561
  447.1 34.3 %collective-permute-start.37 = (bf16[32,6144]{1,0:T(8,128)(2,1)}, bf16[32,6144]{1,0:T(8,128)(2,1)}, u32[]{:S(2)}, u32[]{:S(2)}) collective-permute-start(bf16[32,6144]{1,0:T(8,128)(2,1)} %get-tuple-element.281), channel_id=1, source_target_pairs={{0,2},{2,4},{4,6},{6,0},{1,3},{3,5},{5,7},{7,1},{8,10},{10,12},{12... | collective-permute-start | bytes 1179656 | tf_op jit(solution)/shard_map/ppermute | solution.py:561
  470.3 26.4 %collective-permute-start.44 = (bf16[2,4,32,2048]{3,2,1,0:T(8,128)(2,1)}, bf16[2,4,32,2048]{3,2,1,0:T(8,128)(2,1)}, u32[]{:S(2)}, u32[]{:S(2)}) collective-permute-start(bf16[2,4,32,2048]{3,2,1,0:T(8,128)(2,1)} %fusion.109), channel_id=1, source_target_pairs={{0,16},{16,0},{1,17},{17,1},{2,18},{18,2},{3,19},{19,3},{4,20},{20... | collective-permute-start | bytes 3145736 | tf_op jit(solution)/shard_map/ppermute | solution.py:561
  478.5 31.1 %collective-permute-start.47 = (bf16[4,32,1536]{2,1,0:T(8,128)(2,1)}, bf16[4,32,1536]{2,1,0:T(8,128)(2,1)}, u32[]{:S(2)}, u32[]{:S(2)}) collective-permute-start(bf16[4,32,1536]{2,1,0:T(8,128)(2,1)} %fusion.148), channel_id=1, source_target_pairs={{0,16},{16,0},{1,17},{17,1},{2,18},{18,2},{3,19},{19,3},{4,20},{20... | collective-permute-start | bytes 1179656 | tf_op jit(solution)/shard_map/ppermute | solution.py:561
  481.2 29.8 %collective-permute-start.46 = (bf16[512,896]{1,0:T(8,128)(2,1)S(1)}, bf16[512,896]{1,0:T(8,128)(2,1)S(1)}, u32[]{:S(2)}, u32[]{:S(2)}) collective-permute-start(bf16[512,896]{1,0:T(8,128)(2,1)S(1)} %convolution_convert_fusion.8), channel_id=1, source_target_pairs={{0,8},{8,0},{1,9},{9,1},{2,10},{10,2},{3,11},{11,3},{4,12},{12,4},... | collective-permute-start | bytes 2752520 | tf_op jit(solution)/shard_map/ppermute | solution.py:561
  532.8 22.3 %collective-permute-start.52 = (bf16[2,4,32,1792]{3,2,1,0:T(8,128)(2,1)S(1)}, bf16[2,4,32,1792]{3,2,1,0:T(8,128)(2,1)S(1)}, u32[]{:S(2)}, u32[]{:S(2)}) collective-permute-start(bf16[2,4,32,1792]{3,2,1,0:T(8,128)(2,1)S(1)} %bitcast.304), channel_id=1, source_target_pairs={{0,1},{1,0},{2,3},{3,2},{4,5},{5,4},{6,7},{7,6},{8,9},{9,8},{10,11... | collective-permute-start | bytes 2752520 | tf_op jit(solution)/shard_map/ppermute | solution.py:561
  558.2 27.1 %collective-permute-start.64 = (bf16[32,3584]{1,0:T(8,128)(2,1)S(1)}, bf16[32,3584]{1,0:T(8,128)(2,1)S(1)}, u32[]{:S(2)}, u32[]{:S(2)}) collective-permute-start(bf16[32,3584]{1,0:T(8,128)(2,1)S(1)} %get-tuple-element.282), channel_id=1, source_target_pairs={{0,6},{2,0},{4,2},{6,4},{1,7},{3,1},{5,3},{7,5},{8,14},{10,8},{12,... | collective-permute-start | bytes 688136 | tf_op jit(solution)/shard_map/ppermute | solution.py:561
  558.3 36.7 %collective-permute-start.63 = (bf16[32,3584]{1,0:T(8,128)(2,1)S(1)}, bf16[32,3584]{1,0:T(8,128)(2,1)S(1)}, u32[]{:S(2)}, u32[]{:S(2)}) collective-permute-start(bf16[32,3584]{1,0:T(8,128)(2,1)S(1)} %get-tuple-element.283), channel_id=1, source_target_pairs={{0,4},{2,6},{4,0},{6,2},{1,5},{3,7},{5,1},{7,3},{8,12},{10,14},{12... | collective-permute-start | bytes 688136 | tf_op jit(solution)/shard_map/ppermute | solution.py:561
  560.2 34.7 %collective-permute-start.62 = (bf16[32,3584]{1,0:T(8,128)(2,1)S(1)}, bf16[32,3584]{1,0:T(8,128)(2,1)S(1)}, u32[]{:S(2)}, u32[]{:S(2)}) collective-permute-start(bf16[32,3584]{1,0:T(8,128)(2,1)S(1)} %get-tuple-element.284), channel_id=1, source_target_pairs={{0,2},{2,4},{4,6},{6,0},{1,3},{3,5},{5,7},{7,1},{8,10},{10,12},{12... | collective-permute-start | bytes 688136 | tf_op jit(solution)/shard_map/ppermute | solution.py:561
  (168 other events, 1663.6 us)
Sparse Core Ops, SparseCore 0:
  41.1 160.7 all-gather.1
